TPU v7x, 32 devices: a whole 2x2x4 slice. The times are simulated.
32 devices in a mesh: seq: 8 (over z, x), batch: 4 (over y, core).
Axes of the slice: x: 2, y: 2, z: 4, core: 2. Of those that a mesh axis runs over, the one named last changes fastest.
Arguments:
- queries: bfloat16 [4, 1024, 1024], P('batch', 'seq'), may hold values from -6 to 6
- keys: bfloat16 [4, 1024, 1024], P('batch', 'seq'), may hold values from -6 to 6
- values: bfloat16 [4, 1024, 1024], P('batch', 'seq'), may hold values from -6 to 6
- gates: bfloat16 [4, 1024, 1024], P('batch', 'seq'), may hold values from -6 to 6
- out_grad: bfloat16 [4, 1024, 1024], P('batch', 'seq'), may hold values from -6 to 6
- w_out: bfloat16 [1024, 1024], replicated, may hold values from -0.1875 to 0.1875
- hist_lengths: int32 [4, 4], P('batch'), may hold values from 1 to 682, 1024 in all within a row
Outputs:
- output: bfloat16 [4, 1024, 1024], P('batch', 'seq')
- grad_queries: bfloat16 [4, 1024, 1024], P('batch', 'seq')
- grad_keys: bfloat16 [4, 1024, 1024], P('batch', 'seq')
- grad_values: bfloat16 [4, 1024, 1024], P('batch', 'seq')
- grad_gates: bfloat16 [4, 1024, 1024], P('batch', 'seq')
- grad_weight: float32 [1024, 1024], P('batch')
Inputs may be any that keep to these rules, and one draw needn't show every extreme that they name: `hist_lengths`: each group's 4 lengths sum to 1024, and the longest of each group is exactly 682.
All inputs are finite; a program needn't handle non-finite values.
Results may differ from a plain program's by a relative error of at most 0.0058.
Values may be sent and summed in bfloat16 or wider, within the bound.
No kernel may reach another device: no remote copies, remote signals or barrier semaphores. Data moves between devices by JAX's collectives and lax.ppermute only.
A program may use at most 64 MiB of HBM per device.

v0:
```python
import jax
import jax.numpy as jnp
from jax import lax
from jax.sharding import PartitionSpec as P

HEADS = 8
WINDOW = 256
REACH = 2


def shifted(block, axis, distance):
    devices = range(lax.axis_size(axis))
    route = [(i - distance, i) for i in devices if i - distance in devices]
    return lax.ppermute(block, axis, route)


def segment_start(positions, lengths):
    seg_ends = jnp.cumsum(lengths)
    seg_begins = seg_ends - lengths
    inside = (seg_begins[None, :] <= positions[:, None]) & (positions[:, None] < seg_ends[None, :])
    return jnp.sum(jnp.where(inside, seg_begins[None, :], 0), axis=1)


def silu_slope(scores):
    logistic = jax.nn.sigmoid(scores)
    return logistic * (1.0 + scores * (1.0 - logistic))


def causal_mask(query_pos, query_start, key_pos):
    inside = (key_pos[None, :] >= query_start[:, None]) & (key_pos[None, :] <= query_pos[:, None])
    return inside & (key_pos[None, :] > query_pos[:, None] - WINDOW)


def on_device(queries, keys, values, gates, out_grad, w_out, hist_lengths):
    query_rows = queries[0]
    key_rows = keys[0]
    value_rows = values[0]
    gate_rows = gates[0]
    grad_rows = out_grad[0]
    lengths = hist_lengths[0]
    row_total, model_width = query_rows.shape
    head_dim = model_width // HEADS
    score_scale = head_dim ** (-0.5)
    device = lax.axis_index("seq")
    local_iota = jnp.arange(row_total, dtype=jnp.int32)
    local_pos = device * row_total + local_iota
    local_start = segment_start(local_pos, lengths)
    stacked = jnp.stack((key_rows, value_rows))
    panels = [stacked]
    current = stacked
    for distance in range(REACH):
        current = shifted(current, "seq", 1)
        panels.append(current)
    window = jnp.concatenate(panels, axis=1)
    key_pos = jnp.concatenate(
        [(device - distance) * row_total + local_iota for distance in range(REACH + 1)]
    )
    key_heads = window[0].reshape(-1, HEADS, head_dim)
    value_heads = window[1].reshape(-1, HEADS, head_dim)
    query_heads = query_rows.reshape(row_total, HEADS, head_dim)
    scores = (
        jnp.einsum("ihe,jhe->hij", query_heads, key_heads, preferred_element_type=jnp.float32)
        * score_scale
    )
    allowed = causal_mask(local_pos, local_start, key_pos)[None]
    attention = jnp.where(allowed, jax.nn.silu(scores), 0.0).astype(jnp.bfloat16)
    mixed = jnp.einsum(
        "hij,jhe->ihe", attention, value_heads, preferred_element_type=jnp.float32
    ).reshape(row_total, model_width)
    centered = mixed - jnp.mean(mixed, axis=1, keepdims=True)
    inv_std = lax.rsqrt(jnp.mean(centered * centered, axis=1, keepdims=True) + 1e-05)
    normed = centered * inv_std
    hidden = (normed * gate_rows.astype(jnp.float32)).astype(jnp.bfloat16)
    output = jnp.dot(hidden, w_out, preferred_element_type=jnp.float32).astype(jnp.bfloat16)
    grad_hidden = lax.dot_general(
        grad_rows, w_out, (((1,), (1,)), ((), ())), preferred_element_type=jnp.float32
    )
    grad_gates = (grad_hidden * normed).astype(jnp.bfloat16)
    grad_norm = grad_hidden * gate_rows.astype(jnp.float32)
    grad_mix = (
        (
            grad_norm
            - jnp.mean(grad_norm, axis=1, keepdims=True)
            - normed * jnp.mean(grad_norm * normed, axis=1, keepdims=True)
        )
        * inv_std
    ).astype(jnp.bfloat16)
    mix_heads = grad_mix.reshape(row_total, HEADS, head_dim)
    grad_attention = jnp.einsum(
        "ihe,jhe->hij", mix_heads, value_heads, preferred_element_type=jnp.float32
    )
    grad_scores = jnp.where(allowed, grad_attention * silu_slope(scores) * score_scale, 0.0).astype(
        jnp.bfloat16
    )
    grad_queries = (
        jnp.einsum("hij,jhe->ihe", grad_scores, key_heads, preferred_element_type=jnp.float32)
        .reshape(row_total, model_width)
        .astype(jnp.bfloat16)
    )
    grad_key_all = jnp.einsum(
        "hij,ihe->jhe", grad_scores, query_heads, preferred_element_type=jnp.float32
    ).reshape(-1, model_width)
    grad_value_all = jnp.einsum(
        "hij,ihe->jhe", attention, mix_heads, preferred_element_type=jnp.float32
    ).reshape(-1, model_width)
    totals = jnp.stack((grad_key_all[:row_total], grad_value_all[:row_total]))
    for distance in range(1, REACH + 1):
        partial_grads = jnp.stack(
            (
                grad_key_all[distance * row_total : (distance + 1) * row_total],
                grad_value_all[distance * row_total : (distance + 1) * row_total],
            )
        )
        totals = totals + shifted(partial_grads, "seq", -distance)
    grad_keys = totals[0].astype(jnp.bfloat16)
    grad_values = totals[1].astype(jnp.bfloat16)
    weight_share = lax.psum_scatter(
        lax.dot_general(
            hidden, grad_rows, (((0,), (0,)), ((), ())), preferred_element_type=jnp.float32
        ),
        "batch",
        scatter_dimension=0,
        tiled=True,
    )
    token_total = row_total * lax.axis_size("seq") * lax.axis_size("batch")
    grad_weight = lax.psum(weight_share, "seq") * token_total ** (-0.5)
    return (
        output[None],
        grad_queries[None],
        grad_keys[None],
        grad_values[None],
        grad_gates[None],
        grad_weight,
    )


def solution(mesh):
    placed = (
        P("batch", "seq", None),
        P("batch", "seq", None),
        P("batch", "seq", None),
        P("batch", "seq", None),
        P("batch", "seq", None),
        P(),
        P("batch", None),
    )
    return jax.shard_map(
        on_device,
        mesh=mesh,
        in_specs=placed,
        out_specs=(
            P("batch", "seq", None),
            P("batch", "seq", None),
            P("batch", "seq", None),
            P("batch", "seq", None),
            P("batch", "seq", None),
            P("batch", None),
        ),
        check_vma=False,
    )
```

profile of v0, /device:TPU:0, one launch (start us, length us, event | category | flops | bytes accessed | tf_op | source)
XLA Modules:
  0.0 196.9 jit_solution(17917129115491223885)
XLA Ops:
  7.2 1.3 copy.56
  8.5 1.1 copy.57
  9.7 0.8 pad_maximum_fusion.3
  10.5 5.6 %collective-permute-start = (bf16[2,128,1024]{1,2,0:T(8,128)(2,1)}, bf16[2,128,1024]{1,2,0:T(8,128)(2,1)}, u32[]{:S(2)}, u32[]{:S(2)}) collective-permute-start(bf16[2,128,1024]{1,2,0:T(8,128)(2,1)} %pad_maximum_fusion.3), channel_id=1, source_target_pairs={{0,4},{4,8},{8,12},{12,16},{16,20},{20,24},{24,28},{1,5},{5,9},{9,... | collective-permute-start | bytes 1572872 | tf_op jit(solution)/shard_map/ppermute | solution.py:14
  16.1 0.2 copy.85
  16.3 0.9 copy.76
  17.3 0.2 reduce-window.4
  17.5 9.4 %collective-permute-done = bf16[2,128,1024]{1,2,0:T(8,128)(2,1)} collective-permute-done((bf16[2,128,1024]{1,2,0:T(8,128)(2,1)}, bf16[2,128,1024]{1,2,0:T(8,128)(2,1)}, u32[]{:S(2)}, u32[]{:S(2)}) %collective-permute-start) | collective-permute-done | bytes 524320 | tf_op jit(solution)/shard_map/ppermute | solution.py:14
  26.8 4.4 %collective-permute-start.1 = (bf16[2,128,1024]{1,2,0:T(8,128)(2,1)}, bf16[2,128,1024]{1,2,0:T(8,128)(2,1)S(1)}, u32[]{:S(2)}, u32[]{:S(2)}) collective-permute-start(bf16[2,128,1024]{1,2,0:T(8,128)(2,1)} %collective-permute-done), channel_id=1, source_target_pairs={{0,4},{4,8},{8,12},{12,16},{16,20},{20,24},{24,28},{1,5},{5,9},{9,... | collective-permute-start | bytes 1572872 | tf_op jit(solution)/shard_map/ppermute | solution.py:14
  31.3 0.1 select_reduce_fusion
  31.3 0.1 compare_and_fusion
  31.5 10.3 %collective-permute-done.1 = bf16[2,128,1024]{1,2,0:T(8,128)(2,1)S(1)} collective-permute-done((bf16[2,128,1024]{1,2,0:T(8,128)(2,1)}, bf16[2,128,1024]{1,2,0:T(8,128)(2,1)S(1)}, u32[]{:S(2)}, u32[]{:S(2)}) %collective-permute-start.1) | collective-permute-done | bytes 524320 | tf_op jit(solution)/shard_map/ppermute | solution.py:14
  41.8 1.3 pad_maximum_fusion
  43.1 0.2 fusion.28
  43.3 2.0 %fusion.4 = (bf16[8,128,384]{1,2,0:T(8,128)(2,1)S(1)}, f32[8,384,128]{2,1,0:T(8,128)}) fusion(pred[128,384]{0,1:T(8,128)(4,1)S(1)} %compare_and_fusion, bf16[384,8,128]{0,2,1:T(8,128)(2,1)S(1)} %bitcast.104, bf16[128,8,128]{0,2,1:T(8,128)(2,1)S(1)} %bitcast.115), kind=kOutput, calls=%fused_computation.8 | convolution fusion | flops 103415808 | bytes 3457024 | tf_op jit(solution)/shard_map/ihe,jhe->hij/dot_general | solution.py:62
  45.3 0.4 fusion.30
  45.7 0.2 multiply_reduce_fusion.1
  45.8 0.7 copy-done.7
  46.6 0.1 multiply_convert_fusion
  46.7 2.6 %fusion.17 = f32[1024,1024]{1,0:T(8,128)} fusion(bf16[128,1024]{0,1:T(8,128)(2,1)S(1)} %bitcast.120, bf16[1,128,1024]{2,1,0:T(8,128)(2,1)S(1)} %copy-done.9), kind=kOutput, calls=%fused_computation.39 | convolution fusion | flops 268435456 | bytes 4718592 | tf_op jit(solution)/shard_map/dot_general | solution.py:118
  49.4 0.2 copy.61
  49.6 1.9 fusion.24
  51.6 0.9 fusion.15
  52.5 0.2 copy.86
  52.7 2.7 %fusion.10 = bf16[8,128,384]{1,2,0:T(8,128)(2,1)S(1)} fusion(f32[8,384,128]{2,1,0:T(8,128)} %get-tuple-element.39, bf16[128,8,128]{0,2,1:T(8,128)(2,1)S(1)} %bitcast.117, bf16[384,8,128]{0,2,1:T(8,128)(2,1)} %bitcast.107, pred[128,384]{0,1:T(8,128)(4,1)S(1)} %compare_and_fusion), kind=kOutput, calls=%fused_computation.14 | convolution fusion | flops 104988672 | bytes 3457024 | tf_op jit(solution)/shard_map/ihe,jhe->hij/dot_general | solution.py:89
  55.4 0.5 convolution_bitcast_fusion.1
  55.9 1.2 fusion.26
  57.1 1.4 copy.74
  58.5 2.0 %copy.72 = f32[1,128,1024]{2,1,0:T(8,128)} copy(f32[1,128,1024]{1,2,0:T(8,128)} %bitcast.111) | data formatting | bytes 1048576 | tf_op jit(solution)/shard_map/stack | solution.py:108
  60.5 2.0 convolution_bitcast_fusion
  62.5 1.2 fusion.27
  63.7 2.1 %copy.75 = f32[1,128,1024]{2,1,0:T(8,128)} copy(f32[1,128,1024]{1,2,0:T(8,128)} %bitcast.114) | data formatting | bytes 1048576 | tf_op jit(solution)/shard_map/stack | solution.py:108
  65.8 2.0 %copy.73 = f32[1,128,1024]{2,1,0:T(8,128)} copy(f32[1,128,1024]{1,2,0:T(8,128)} %bitcast.112) | data formatting | bytes 1048576 | tf_op jit(solution)/shard_map/stack | solution.py:108
  67.8 2.3 %pad_maximum_fusion.1 = f32[2,128,1024]{2,1,0:T(8,128)} fusion(f32[1,128,1024]{2,1,0:T(8,128)} %copy.73, f32[1,128,1024]{2,1,0:T(8,128)} %copy.72), kind=kLoop, calls=%fused_computation.24 | loop fusion | flops 262144 | bytes 2097152 | tf_op jit(solution)/shard_map/stack | solution.py:108
  70.2 1.3 collective-permute-start.2
  71.5 1.1 pad_maximum_fusion.2
  72.5 1.3 collective-permute-start.3
  73.8 23.2 %reduce-scatter.2.cloned.1.call-done = f32[256,1024]{1,0:T(8,128)} async-done(((f32[1024,1024]{1,0:T(8,128)}), f32[256,1024]{1,0:T(8,128)}) %reduce-scatter.2.cloned.1.call-update) | async-done | bytes 1048592 | tf_op jit(solution)/shard_map/reduce_scatter | solution.py:117
  97.1 1.7 convolution_convert_fusion
  98.8 0.9 copy.77
  99.7 1.2 copy.70
  100.9 2.1 %copy.71 = f32[1,128,1024]{2,1,0:T(8,128)} copy(f32[1,128,1024]{1,2,0:T(8,128)} %bitcast.110) | data formatting | bytes 1048576 | tf_op jit(solution)/shard_map/stack | solution.py:106
  103.0 1.2 fusion.11
  104.2 27.8 %collective-permute-done.3 = f32[2,128,1024]{2,1,0:T(8,128)} collective-permute-done((f32[2,128,1024]{2,1,0:T(8,128)}, f32[2,128,1024]{2,1,0:T(8,128)}, u32[]{:S(2)}, u32[]{:S(2)}) %collective-permute-start.3) | collective-permute-done | bytes 1048608 | tf_op jit(solution)/shard_map/ppermute | solution.py:14
  132.0 1.8 fusion.13
  133.8 0.8 fusion.29
  134.7 53.1 %all-reduce.2.cloned.1.call-done = f32[256,1024]{1,0:T(8,128)} async-done(((f32[256,1024]{1,0:T(8,128)}), f32[256,1024]{1,0:T(8,128)}) %all-reduce.2.cloned.1.call-update) | async-done | bytes 1048592 | tf_op jit(solution)/shard_map/psum | solution.py:126
  187.7 2.3 %broadcast_multiply_fusion = f32[256,1024]{1,0:T(8,128)} fusion(f32[256,1024]{1,0:T(8,128)} %all-reduce.2.cloned.1.call-done), kind=kLoop, calls=%fused_computation.31 | loop fusion | flops 262144 | bytes 2097152 | tf_op jit(solution)/shard_map/mul | solution.py:126
  (42 shorter events, 0.2 us)
Async XLA Ops:
  7.2 42.5 %copy-start = (bf16[1024,1024]{1,0:T(8,128)(2,1)S(1)}, bf16[1024,1024]{1,0:T(8,128)(2,1)}, u32[]{:S(2)}) copy-start(bf16[1024,1024]{1,0:T(8,128)(2,1)} %param.12) | copy-start | bytes 6291460
  7.2 9.0 %copy-start.13 = (bf16[1,128,1024]{2,1,0:T(8,128)(2,1)S(1)}, bf16[1,128,1024]{2,1,0:T(8,128)(2,1)}, u32[]{:S(2)}) copy-start(bf16[1,128,1024]{2,1,0:T(8,128)(2,1)} %param.7) | copy-start | bytes 786436
  7.2 9.1 %copy-start.1 = (bf16[1,128,1024]{2,1,0:T(8,128)(2,1)S(1)}, bf16[1,128,1024]{2,1,0:T(8,128)(2,1)}, u32[]{:S(2)}) copy-start(bf16[1,128,1024]{2,1,0:T(8,128)(2,1)} %param.10) | copy-start | bytes 786436
  7.2 89.8 %reduce-scatter.2.cloned.1.call-start = ((), (), s32[]{:S(2)}) async-start(), calls=%async_computation.1 | async-start | bytes 5242880 | tf_op jit(solution)/shard_map/reduce_scatter | solution.py:117
  8.5 8.7 %copy-start.14 = (s32[1,4]{1,0:T(1,128)S(1)}, s32[1,4]{1,0:T(1,128)}, u32[]{:S(2)}) copy-start(s32[1,4]{1,0:T(1,128)} %param.13) | copy-start | bytes 52
  10.5 16.3 %collective-permute-start = (bf16[2,128,1024]{1,2,0:T(8,128)(2,1)}, bf16[2,128,1024]{1,2,0:T(8,128)(2,1)}, u32[]{:S(2)}, u32[]{:S(2)}) collective-permute-start(bf16[2,128,1024]{1,2,0:T(8,128)(2,1)} %pad_maximum_fusion.3), channel_id=1, source_target_pairs={{0,4},{4,8},{8,12},{12,16},{16,20},{20,24},{24,28},{1,5},{5,9},{9,... | collective-permute-start | bytes 1572872 | tf_op jit(solution)/shard_map/ppermute | solution.py:14
  16.3 26.9 %copy-start.10 = (bf16[1,128,1024]{1,2,0:T(8,128)(2,1)}, bf16[1,128,1024]{1,2,0:T(8,128)(2,1)S(1)}, u32[]{:S(2)}) copy-start(bf16[1,128,1024]{1,2,0:T(8,128)(2,1)S(1)} %copy.85) | copy-start | bytes 786436
  26.8 15.0 %collective-permute-start.1 = (bf16[2,128,1024]{1,2,0:T(8,128)(2,1)}, bf16[2,128,1024]{1,2,0:T(8,128)(2,1)S(1)}, u32[]{:S(2)}, u32[]{:S(2)}) collective-permute-start(bf16[2,128,1024]{1,2,0:T(8,128)(2,1)} %collective-permute-done), channel_id=1, source_target_pairs={{0,4},{4,8},{8,12},{12,16},{16,20},{20,24},{24,28},{1,5},{5,9},{9,... | collective-permute-start | bytes 1572872 | tf_op jit(solution)/shard_map/ppermute | solution.py:14
  43.2 2.0 %copy-start.2 = (bf16[1,384,1024]{1,2,0:T(8,128)(2,1)}, bf16[1,384,1024]{1,2,0:T(8,128)(2,1)S(1)}, u32[]{:S(2)}) copy-start(bf16[1,384,1024]{1,2,0:T(8,128)(2,1)S(1)} %get-tuple-element.32) | copy-start | bytes 2359300
  43.3 2.0 %copy-start.5 = (bf16[1,384,1024]{1,2,0:T(8,128)(2,1)}, bf16[1,384,1024]{1,2,0:T(8,128)(2,1)S(1)}, u32[]{:S(2)}) copy-start(bf16[1,384,1024]{1,2,0:T(8,128)(2,1)S(1)} %get-tuple-element.33) | copy-start | bytes 2359300
  45.3 1.4 copy-start.4
  45.3 1.3 copy-start.7
  45.3 1.4 copy-start.9
  49.4 138.4 %all-reduce.2.cloned.1.call-start = ((), (), s32[]{:S(2)}) async-start(), calls=%async_computation.2 | async-start | bytes 2097152 | tf_op jit(solution)/shard_map/psum | solution.py:126
  52.7 2.7 %copy-start.12 = (bf16[128,1024]{0,1:T(8,128)(2,1)}, bf16[128,1024]{0,1:T(8,128)(2,1)S(1)}, u32[]{:S(2)}) copy-start(bf16[128,1024]{0,1:T(8,128)(2,1)S(1)} %copy.86) | copy-start | bytes 786436
  52.7 2.7 %copy-start.11 = (bf16[1,128,1024]{1,2,0:T(8,128)(2,1)S(1)}, bf16[1,128,1024]{1,2,0:T(8,128)(2,1)}, u32[]{:S(2)}) copy-start(bf16[1,128,1024]{1,2,0:T(8,128)(2,1)} %copy-done.10) | copy-start | bytes 786436
  55.4 1.7 copy-start.3
  67.8 3.6 %copy-start.8 = (f32[1,128,1024]{2,1,0:T(8,128)S(1)}, f32[1,128,1024]{2,1,0:T(8,128)}, u32[]{:S(2)}) copy-start(f32[1,128,1024]{2,1,0:T(8,128)} %copy.75) | copy-start | bytes 1572868
  70.2 34.0 %collective-permute-start.2 = (f32[2,128,1024]{2,1,0:T(8,128)}, f32[2,128,1024]{2,1,0:T(8,128)}, u32[]{:S(2)}, u32[]{:S(2)}) collective-permute-start(f32[2,128,1024]{2,1,0:T(8,128)} %pad_maximum_fusion.1), channel_id=1, source_target_pairs={{4,0},{8,4},{12,8},{16,12},{20,16},{24,20},{28,24},{5,1},{9,5},{13... | collective-permute-start | bytes 3145736 | tf_op jit(solution)/shard_map/ppermute | solution.py:14
  72.5 59.5 %collective-permute-start.3 = (f32[2,128,1024]{2,1,0:T(8,128)}, f32[2,128,1024]{2,1,0:T(8,128)}, u32[]{:S(2)}, u32[]{:S(2)}) collective-permute-start(f32[2,128,1024]{2,1,0:T(8,128)} %pad_maximum_fusion.2), channel_id=1, source_target_pairs={{8,0},{12,4},{16,8},{20,12},{24,16},{28,20},{9,1},{13,5},{17,9},{2... | collective-permute-start | bytes 3145736 | tf_op jit(solution)/shard_map/ppermute | solution.py:14
  103.0 29.0 %copy-start.6 = (f32[1,128,1024]{2,1,0:T(8,128)S(1)}, f32[1,128,1024]{2,1,0:T(8,128)}, u32[]{:S(2)}) copy-start(f32[1,128,1024]{2,1,0:T(8,128)} %copy.71) | copy-start | bytes 1572868
Sparse Core Ops, SparseCore 0:
  49.5 47.5 reduce-scatter.1
  101.0 86.7 all-reduce.1
where the time goes:
time: 198 us; the launch traced here: 197 us
  waiting for transfers between devices  124 us (63%)
  local copies, waits for them, and re-layouts  19.8 us (10%)
  matrix products  14.9 us (8%)
  between operations  14.4 us (7%)
  starting transfers between devices  12.7 us (6%)
  other arithmetic  11.2 us (6%)
    psum x1, waiting for transfers between devices, on_device(): grad_weight = lax.psum(weight_share, 'seq') * token_total ** (-0.5)  53.1 us
    ppermute x4, waiting for transfers between devices, shifted(): return lax.ppermute(block, axis, route)  47.6 us
    reduce_scatter x1, waiting for transfers between devices, on_device(): lax.psum_scatter(lax.dot_general(hidden, grad_rows, (((0,), (0,)), ((), (...  23.2 us
    ppermute x4, starting transfers between devices, shifted(): return lax.ppermute(block, axis, route)  12.6 us
    another operation x4, local copies, waits for them, and re-layouts, on_device(): jnp.stack((grad_key_all[distance * row_total:(distance + 1) * row_total],...  7.58 us
    unnamed x33, local copies, waits for them, and re-layouts  4.07 us
  transfers between devices with their start and end apart: 6, of which 5 were waited for; matrix products, arithmetic and copies ran while one was open for 17% of the time, Pallas kernels for 0%

commit v1 on v0

v1 whole, which is shorter than its diff:
```python
import functools

import jax
import jax.numpy as jnp
from jax import lax
from jax.experimental import pallas as pl
from jax.experimental.pallas import tpu as pltpu
from jax.sharding import PartitionSpec as P

HEADS = 8
WINDOW = 256
REACH = 2

VMEM = pl.BlockSpec(memory_space=pltpu.VMEM)
SMEM = pl.BlockSpec(memory_space=pltpu.SMEM)
F32 = jnp.float32
BF16 = jnp.bfloat16
NT = (((1,), (1,)), ((), ()))
TN = (((0,), (0,)), ((), ()))


def dot(a, b):
    return jnp.dot(a, b, preferred_element_type=F32)


def dot_nt(a, b):
    return lax.dot_general(a, b, NT, preferred_element_type=F32)


def dot_tn(a, b):
    return lax.dot_general(a, b, TN, preferred_element_type=F32)


def logistic(scores):
    return 0.5 * jnp.tanh(0.5 * scores) + 0.5


def silu_slope(scores, gate):
    return gate * (1.0 + scores * (1.0 - gate))


def start_of(positions, len_ref):
    total = jnp.zeros_like(positions)
    end = jnp.int32(0)
    for k in range(len_ref.shape[1]):
        length = len_ref[0, k]
        end = end + length
        total = total + jnp.where(positions >= end, length, 0)
    return total


def allowed_block(rows, first_query, first_key, len_ref, query_dim):
    shape = (rows, rows)
    query_pos = first_query + lax.broadcasted_iota(jnp.int32, shape, query_dim)
    key_pos = first_key + lax.broadcasted_iota(jnp.int32, shape, 1 - query_dim)
    start = start_of(query_pos, len_ref)
    return (key_pos >= start) & (key_pos <= query_pos) & (key_pos > query_pos - WINDOW)


def head_slice(h, width):
    return slice(h * width, (h + 1) * width)


def cost(flops, arrays):
    total = sum(a.size * a.dtype.itemsize for a in arrays)
    return pl.CostEstimate(flops=flops, bytes_accessed=total, transcendentals=0)


def call(kernel, outs, scalars, arrays, flops, scratch=()):
    return pl.pallas_call(
        kernel,
        out_shape=outs,
        in_specs=[SMEM] * len(scalars) + [VMEM] * len(arrays),
        out_specs=[VMEM] * len(outs),
        scratch_shapes=list(scratch),
        cost_estimate=cost(flops, list(arrays) + list(outs)),
        compiler_params=pltpu.CompilerParams(vmem_limit_bytes=40 * 1024 * 1024),
    )(*scalars, *arrays)


def own_kernel(len_ref, place_ref, q, k, v, grad, w, mixed_own, grad_hidden):
    rows, width = q.shape
    size = width // HEADS
    scale = size ** (-0.5)
    first = place_ref[0] * rows
    grad_hidden[...] = dot_nt(grad[...], w[...])
    allowed = allowed_block(rows, first, first, len_ref, 0)
    for h in range(HEADS):
        cols = head_slice(h, size)
        scores = dot_nt(q[:, cols], k[:, cols]) * scale
        attention = jnp.where(allowed, scores * logistic(scores), 0.0).astype(BF16)
        mixed_own[:, cols] = dot(attention, v[:, cols])


def forward_kernel(
    groups, len_ref, place_ref, q, k1, k2, v1, v2, mixed_own, grad_hidden, gates, *rest
):
    hidden, grad_gates, grad_mix = rest[:3]
    slices = rest[3 : 3 + groups]
    mixed = rest[3 + groups]
    rows, width = q.shape
    size = width // HEADS
    scale = size ** (-0.5)
    first = place_ref[0] * rows
    masks = [allowed_block(rows, first, first - d * rows, len_ref, 0) for d in (1, 2)]
    for h in range(HEADS):
        cols = head_slice(h, size)
        total = mixed_own[:, cols]
        for mask, kd, vd in zip(masks, (k1, k2), (v1, v2)):
            scores = dot_nt(q[:, cols], kd[:, cols]) * scale
            attention = jnp.where(mask, scores * logistic(scores), 0.0).astype(BF16)
            total = total + dot(attention, vd[:, cols])
        mixed[:, cols] = total
    values = mixed[...]
    centered = values - jnp.mean(values, axis=1, keepdims=True)
    inv_std = lax.rsqrt(jnp.mean(centered * centered, axis=1, keepdims=True) + 1e-05)
    normed = centered * inv_std
    gate = gates[...].astype(F32)
    hidden[...] = (normed * gate).astype(BF16)
    gh = grad_hidden[...]
    grad_gates[...] = (gh * normed).astype(BF16)
    grad_norm = gh * gate
    grad_mix[...] = (
        (
            grad_norm
            - jnp.mean(grad_norm, axis=1, keepdims=True)
            - normed * jnp.mean(grad_norm * normed, axis=1, keepdims=True)
        )
        * inv_std
    ).astype(BF16)
    part = width // groups
    for d, ref in enumerate(slices):
        at = pl.multiple_of((place_ref[1] ^ d) * part, 128)
        ref[...] = hidden[:, pl.ds(at, part)]


def query_kernel(len_ref, place_ref, q, k0, k1, k2, v0, v1, v2, grad_mix, hidden, w, output, grad_queries):
    rows, width = q.shape
    size = width // HEADS
    scale = size ** (-0.5)
    first = place_ref[0] * rows
    output[...] = dot(hidden[...], w[...]).astype(BF16)
    masks = [allowed_block(rows, first, first - d * rows, len_ref, 0) for d in range(REACH + 1)]
    for h in range(HEADS):
        cols = head_slice(h, size)
        total = jnp.zeros((rows, size), F32)
        for mask, kd, vd in zip(masks, (k0, k1, k2), (v0, v1, v2)):
            scores = dot_nt(q[:, cols], kd[:, cols]) * scale
            grad_attention = dot_nt(grad_mix[:, cols], vd[:, cols])
            slope = silu_slope(scores, logistic(scores))
            grad_scores = jnp.where(mask, grad_attention * slope * scale, 0.0).astype(BF16)
            total = total + dot(grad_scores, kd[:, cols])
        grad_queries[:, cols] = total.astype(BF16)


def key_kernel(len_ref, place_ref, k, v, q0, q1, q2, g0, g1, g2, grad_keys, grad_values):
    rows, width = k.shape
    size = width // HEADS
    scale = size ** (-0.5)
    first = place_ref[0] * rows
    masks = [allowed_block(rows, first + d * rows, first, len_ref, 1) for d in range(REACH + 1)]
    for h in range(HEADS):
        cols = head_slice(h, size)
        keys_total = jnp.zeros((rows, size), F32)
        values_total = jnp.zeros((rows, size), F32)
        for mask, qd, gd in zip(masks, (q0, q1, q2), (g0, g1, g2)):
            scores = dot_nt(k[:, cols], qd[:, cols]) * scale
            gate = logistic(scores)
            attention = jnp.where(mask, scores * gate, 0.0).astype(BF16)
            grad_attention = dot_nt(v[:, cols], gd[:, cols])
            slope = silu_slope(scores, gate)
            grad_scores = jnp.where(mask, grad_attention * slope * scale, 0.0).astype(BF16)
            keys_total = keys_total + dot(grad_scores, qd[:, cols])
            values_total = values_total + dot(attention, gd[:, cols])
        grad_keys[:, cols] = keys_total.astype(BF16)
        grad_values[:, cols] = values_total.astype(BF16)


def weight_kernel(groups, place_ref, *refs):
    hidden = refs[:groups]
    grads = refs[groups : 2 * groups]
    own = refs[2 * groups]
    sends = refs[2 * groups + 1 : -1]
    total = refs[-1]
    acc = dot_tn(hidden[0][...], grads[0][...])
    for a, b in zip(hidden[1:], grads[1:]):
        acc = acc + dot_tn(a[...], b[...])
    total[...] = acc
    rows = own.shape[0]
    if not sends:
        own[...] = acc
        return
    own[...] = total[pl.ds(pl.multiple_of(place_ref[0] * rows, rows), rows), :]
    for e, ref in enumerate(sends):
        at = pl.multiple_of((place_ref[0] ^ (e + 1)) * rows, rows)
        ref[...] = total[pl.ds(at, rows), :].astype(BF16)


def sum_kernel(scale, own, *refs):
    total = own[...]
    for ref in refs[:-1]:
        total = total + ref[...].astype(F32)
    refs[-1][...] = (total * scale).astype(BF16)


def place_kernel(place_ref, *refs):
    out = refs[-1]
    rows = refs[0].shape[0]
    for e, ref in enumerate(refs[:-1]):
        at = pl.multiple_of((place_ref[0] ^ e) * rows, rows)
        out[pl.ds(at, rows), :] = ref[...].astype(F32)


def xor_route(size, mask):
    return [(i, i ^ mask) for i in range(size)]


def halo(block, distance, even):
    count = lax.axis_size("seq")
    route = [(i, i + distance) for i in range(count) if 0 <= i + distance < count]
    far = lax.ppermute(block, "seq", route)
    keeps = even if distance > 0 else jnp.logical_not(even)
    passed = jnp.where(keeps, block, far)
    near = lax.ppermute(passed, "seq", xor_route(count, 1))
    return near, far


def on_device(queries, keys, values, gates, out_grad, w_out, hist_lengths):
    q, k, v, gate, grad = queries[0], keys[0], values[0], gates[0], out_grad[0]
    rows, width = q.shape
    seq = lax.axis_size("seq")
    batch = lax.axis_size("batch")
    seq_at = lax.axis_index("seq")
    batch_at = lax.axis_index("batch")
    place = jnp.stack([seq_at, batch_at]).astype(jnp.int32)
    scalars = (hist_lengths, place)
    even = (seq_at & 1) == 0
    full = jax.ShapeDtypeStruct((rows, width), BF16)
    wide = jax.ShapeDtypeStruct((rows, width), F32)
    block_flops = 2 * rows * rows * width
    proj_flops = 2 * rows * width * width

    k1, k2 = halo(k, 2, even)
    v1, v2 = halo(v, 2, even)
    q1, q2 = halo(q, -2, even)
    grads = [grad] + [lax.ppermute(grad, "batch", xor_route(batch, d)) for d in range(1, batch)]

    mixed_own, grad_hidden = call(
        own_kernel, [wide, wide], scalars, (q, k, v, grad, w_out), proj_flops + 2 * block_flops
    )
    part = width // batch
    piece = jax.ShapeDtypeStruct((rows, part), BF16)
    hidden, grad_gates, grad_mix, *slices = call(
        functools.partial(forward_kernel, batch),
        [full, full, full] + [piece] * batch,
        scalars,
        (q, k1, k2, v1, v2, mixed_own, grad_hidden, gate),
        4 * block_flops,
        [pltpu.VMEM((rows, width), F32)],
    )
    hiddens = [slices[0]] + [
        lax.ppermute(slices[d], "batch", xor_route(batch, d)) for d in range(1, batch)
    ]
    g1, g2 = halo(grad_mix, -2, even)

    direct = seq == 8
    rows_w = part // seq if direct else part
    own_shape = jax.ShapeDtypeStruct((rows_w, width), F32)
    send_shape = jax.ShapeDtypeStruct((rows_w, width), BF16)
    scale = (rows * seq * batch) ** (-0.5)
    own, *sends = call(
        functools.partial(weight_kernel, batch),
        [own_shape] + ([send_shape] * (seq - 1) if direct else []),
        (place,),
        (*hiddens, *grads),
        proj_flops,
        [pltpu.VMEM((part, width), F32)],
    )
    if direct:
        got = [lax.ppermute(s, "seq", xor_route(seq, e + 1)) for e, s in enumerate(sends)]
        (mine,) = call(functools.partial(sum_kernel, scale), [send_shape], (), (own, *got), own.size * 8)
        shares = [mine] + [lax.ppermute(mine, "seq", xor_route(seq, e)) for e in range(1, seq)]
        (grad_weight,) = call(
            place_kernel,
            [jax.ShapeDtypeStruct((part, width), F32)],
            (place,),
            tuple(shares),
            part * width,
        )
    else:
        grad_weight = lax.psum(own, "seq") * scale

    output, grad_queries = call(
        query_kernel,
        [full, full],
        scalars,
        (q, k, k1, k2, v, v1, v2, grad_mix, hidden, w_out),
        proj_flops + 9 * block_flops,
    )
    grad_keys, grad_values = call(
        key_kernel, [full, full], scalars, (k, v, q, q1, q2, grad_mix, g1, g2), 12 * block_flops
    )
    return (
        output[None],
        grad_queries[None],
        grad_keys[None],
        grad_values[None],
        grad_gates[None],
        grad_weight,
    )


def solution(mesh):
    token = P("batch", "seq", None)
    return jax.shard_map(
        on_device,
        mesh=mesh,
        in_specs=(token, token, token, token, token, P(), P("batch", None)),
        out_specs=(token, token, token, token, token, P("batch", None)),
        check_vma=False,
    )
```

time: 198 us -> 101 us (0.51)
  waiting for transfers between devices: 124 us -> 21.4 us
  starting transfers between devices: 12.7 us -> 45.4 us
  Pallas kernels: 0 us -> 20 us
  matrix products: 14.9 us -> 0 us
  between operations: 14.4 us -> 0.85 us
  local copies, waits for them, and re-layouts: 19.8 us -> 10.1 us
  other arithmetic: 11.2 us -> 3.06 us
    psum x1 -> x0, waiting for transfers between devices: 53.1 us -> none  [on_device(): grad_weight = lax.psum(weight_share, 'seq') * token_total ** (-0.5)]
    ppermute x4 -> x28, starting transfers between devices: 12.6 us -> 45.4 us  [the longest x7 12.6 us: on_device(): lax.ppermute(mine, 'seq', xor_route(seq, e))]
    ppermute x4 -> x28, waiting for transfers between devices: 47.6 us -> 21.4 us  [the longest x7 8.45 us: on_device(): lax.ppermute(mine, 'seq', xor_route(seq, e))]
    reduce_scatter x1 -> x0, waiting for transfers between devices: 23.2 us -> none  [on_device(): lax.psum_scatter(lax.dot_general(hidden, grad_rows, (((0,), (0,)), ((), (...]
    pallas_call x0 -> x7, Pallas kernels: none -> 20 us  [call(): pl.pallas_call(kernel, out_shape=outs, in_specs=[SMEM] * len(scalars) + [...]
    dot_general x9 -> x0, matrix products: 14.9 us -> none  [the longest x1 2.67 us: on_device(): jnp.einsum('ihe,jhe->hij', mix_heads, value_heads, preferred_element_type...]
    another operation x7 -> x0, local copies, waits for them, and re-layouts: 11.1 us -> none  [the longest x4 7.58 us: on_device(): jnp.stack((grad_key_all[distance * row_total:(distance + 1) * row_total],...]
    another operation x5 -> x1, other arithmetic: 6.22 us -> 0.08 us  [on_device(): place = jnp.stack([seq_at, batch_at]).astype(jnp.int32)]
  transfers between devices with their start and end apart: 6 -> 28, of which waited for: 5 -> 8; matrix products, arithmetic and copies ran while one was open for 17% -> 3% of each run, Pallas kernels for 0% -> 14%
where the time goes in v1:
time: 101 us
  starting transfers between devices  45.4 us (45%)
  waiting for transfers between devices  21.4 us (21%)
  Pallas kernels  20 us (20%)
  local copies, waits for them, and re-layouts  10.1 us (10%)
  other arithmetic  3.06 us (3%)
    pallas_call x7, Pallas kernels, call(): pl.pallas_call(kernel, out_shape=outs, in_specs=[SMEM] * len(scalars) + [...  20 us
    ppermute x7, starting transfers between devices, on_device(): lax.ppermute(mine, 'seq', xor_route(seq, e))  12.6 us
    ppermute x7, starting transfers between devices, on_device(): lax.ppermute(s, 'seq', xor_route(seq, e + 1))  12.3 us
    ppermute x4, starting transfers between devices, halo(): far = lax.ppermute(block, 'seq', route)  11.1 us
    unnamed x42, local copies, waits for them, and re-layouts  10.1 us
    ppermute x7, waiting for transfers between devices, on_device(): lax.ppermute(mine, 'seq', xor_route(seq, e))  8.45 us
    ppermute x4, starting transfers between devices, halo(): near = lax.ppermute(passed, 'seq', xor_route(count, 1))  5.7 us
    ppermute x4, waiting for transfers between devices, halo(): far = lax.ppermute(block, 'seq', route)  5.41 us
  transfers between devices with their start and end apart: 28, of which 8 were waited for; matrix products, arithmetic and copies ran while one was open for 3% of the time, Pallas kernels for 14%

profile of v1, /device:TPU:0, one launch (start us, length us, event | category | flops | bytes accessed | tf_op | source)
XLA Modules:
  0.0 100.8 jit_solution(10028842575797835511)
XLA Ops:
  0.6 4.9 %collective-permute-start = (bf16[128,1024]{1,0:T(8,128)(2,1)}, bf16[128,1024]{1,0:T(8,128)(2,1)S(1)}, u32[]{:S(2)}, u32[]{:S(2)}) collective-permute-start(bf16[128,1024]{1,0:T(8,128)(2,1)} %bitcast.20), channel_id=1, source_target_pairs={{0,8},{4,12},{8,16},{12,20},{16,24},{20,28},{1,9},{5,13},{9,17},{1... | collective-permute-start | bytes 786440 | tf_op jit(solution)/shard_map/ppermute | solution.py:221
  5.6 3.5 %collective-permute-start.2 = (bf16[128,1024]{1,0:T(8,128)(2,1)}, bf16[128,1024]{1,0:T(8,128)(2,1)S(1)}, u32[]{:S(2)}, u32[]{:S(2)}) collective-permute-start(bf16[128,1024]{1,0:T(8,128)(2,1)} %bitcast.24), channel_id=1, source_target_pairs={{0,8},{4,12},{8,16},{12,20},{16,24},{20,28},{1,9},{5,13},{9,17},{1... | collective-permute-start | bytes 786440 | tf_op jit(solution)/shard_map/ppermute | solution.py:221
  9.1 3.5 %collective-permute-done.k2 = bf16[128,1024]{1,0:T(8,128)(2,1)S(1)} collective-permute-done((bf16[128,1024]{1,0:T(8,128)(2,1)}, bf16[128,1024]{1,0:T(8,128)(2,1)S(1)}, u32[]{:S(2)}, u32[]{:S(2)}) %collective-permute-start) | collective-permute-done | bytes 262176 | tf_op jit(solution)/shard_map/ppermute | solution.py:221
  12.6 1.0 broadcast_select_fusion.3
  13.6 1.6 %collective-permute-start.1 = (bf16[128,1024]{1,0:T(8,128)(2,1)S(1)}, bf16[128,1024]{1,0:T(8,128)(2,1)S(1)}, u32[]{:S(2)}, u32[]{:S(2)}) collective-permute-start(bf16[128,1024]{1,0:T(8,128)(2,1)S(1)} %broadcast_select_fusion.3), channel_id=1, source_target_pairs={{0,4},{4,0},{8,12},{12,8},{16,20},{20,16},{24,28},{28,24},{1,5},{5... | collective-permute-start | bytes 786440 | tf_op jit(solution)/shard_map/ppermute | solution.py:224
  15.1 1.9 %collective-permute-done.2.v2 = bf16[128,1024]{1,0:T(8,128)(2,1)S(1)} collective-permute-done((bf16[128,1024]{1,0:T(8,128)(2,1)}, bf16[128,1024]{1,0:T(8,128)(2,1)S(1)}, u32[]{:S(2)}, u32[]{:S(2)}) %collective-permute-start.2) | collective-permute-done | bytes 262176 | tf_op jit(solution)/shard_map/ppermute | solution.py:221
  17.0 1.0 broadcast_select_fusion.2
  18.0 1.6 %collective-permute-start.3 = (bf16[128,1024]{1,0:T(8,128)(2,1)S(1)}, bf16[128,1024]{1,0:T(8,128)(2,1)S(1)}, u32[]{:S(2)}, u32[]{:S(2)}) collective-permute-start(bf16[128,1024]{1,0:T(8,128)(2,1)S(1)} %broadcast_select_fusion.2), channel_id=1, source_target_pairs={{0,4},{4,0},{8,12},{12,8},{16,20},{20,16},{24,28},{28,24},{1,5},{5... | collective-permute-start | bytes 786440 | tf_op jit(solution)/shard_map/ppermute | solution.py:224
  19.6 1.5 %collective-permute-start.12 = (bf16[128,1024]{1,0:T(8,128)(2,1)}, bf16[128,1024]{1,0:T(8,128)(2,1)}, u32[]{:S(2)}, u32[]{:S(2)}) collective-permute-start(bf16[128,1024]{1,0:T(8,128)(2,1)} %bitcast.29), channel_id=1, source_target_pairs={{0,2},{1,3},{2,0},{3,1},{4,6},{5,7},{6,4},{7,5},{8,10},{9,11},{10,... | collective-permute-start | bytes 786440 | tf_op jit(solution)/shard_map/ppermute | solution.py:246
  21.5 1.3 %collective-permute-start.4 = (bf16[128,1024]{1,0:T(8,128)(2,1)}, bf16[128,1024]{1,0:T(8,128)(2,1)}, u32[]{:S(2)}, u32[]{:S(2)}) collective-permute-start(bf16[128,1024]{1,0:T(8,128)(2,1)} %bitcast.15), channel_id=1, source_target_pairs={{8,0},{12,4},{16,8},{20,12},{24,16},{28,20},{9,1},{13,5},{17,9},{2... | collective-permute-start | bytes 786440 | tf_op jit(solution)/shard_map/ppermute | solution.py:221
  22.8 1.6 %copy-done = bf16[1024,1024]{1,0:T(8,128)(2,1)S(1)} copy-done((bf16[1024,1024]{1,0:T(8,128)(2,1)S(1)}, bf16[1024,1024]{1,0:T(8,128)(2,1)}, u32[]{:S(2)}) %copy-start) | copy-done | bytes 2097176
  24.4 0.9 copy-done.2
  25.4 0.9 copy-done.4
  26.3 0.9 copy-done.6
  27.3 0.9 copy-done.10
  28.2 0.7 copy-done.19
  28.9 2.5 %shard_map.118 = (f32[128,1024]{1,0:T(8,128)S(1)}, f32[128,1024]{1,0:T(8,128)S(1)}) custom-call(s32[1,4]{1,0:T(1,128)S(1)} %copy-done.19, s32[2]{0:T(128)S(1)} %pad_add_fusion.place_ref, bf16[128,1024]{1,0:T(8,128)(2,1)S(1)} %bitcast.16, bf16[128,1024]{1,0:T(8,128)(2,1)S(1)} %bitcast.21, bf16[128,1024]{1,0:T(8,128)(2,1)S(1)} %bitcast.25, ...), custom_call_target="tpu_custom_call" | custom-call | flops 335544320 | bytes 4194304 | tf_op jit(solution)/shard_map/pallas_call | solution.py:70
  31.5 3.8 %shard_map.119 = (bf16[128,1024]{1,0:T(8,128)(2,1)S(1)}, bf16[128,1024]{1,0:T(8,128)(2,1)}, bf16[128,1024]{1,0:T(8,128)(2,1)S(1)}, bf16[128,256]{1,0:T(8,128)(2,...) custom-call(s32[1,4]{1,0:T(1,128)S(1)} %copy-done.19, ...), custom_call_target="tpu_custom_call" | custom-call | flops 134217728 | bytes 3670016 | tf_op jit(solution)/shard_map/pallas_call | solution.py:70
  35.2 0.7 copy-done.8
  35.9 0.7 copy-done.14
  36.6 0.7 copy-done.17
  37.6 1.5 %collective-permute-start.9 = (bf16[128,256]{1,0:T(8,128)(2,1)}, bf16[128,256]{1,0:T(8,128)(2,1)}, u32[]{:S(2)}, u32[]{:S(2)}) collective-permute-start(bf16[128,256]{1,0:T(8,128)(2,1)} %get-tuple-element.38), channel_id=1, source_target_pairs={{0,2},{1,3},{2,0},{3,1},{4,6},{5,7},{6,4},{7,5},{8,10},{9,11},{10,... | collective-permute-start | bytes 196616 | tf_op jit(solution)/shard_map/ppermute | solution.py:262
  39.2 1.4 %collective-permute-start.6 = (bf16[128,1024]{1,0:T(8,128)(2,1)}, bf16[128,1024]{1,0:T(8,128)(2,1)S(1)}, u32[]{:S(2)}, u32[]{:S(2)}) collective-permute-start(bf16[128,1024]{1,0:T(8,128)(2,1)} %copy-done.8), channel_id=1, source_target_pairs={{8,0},{12,4},{16,8},{20,12},{24,16},{28,20},{9,1},{13,5},{17,9},{2... | collective-permute-start | bytes 786440 | tf_op jit(solution)/shard_map/ppermute | solution.py:221
  40.6 1.6 %collective-permute-done.9.refs_2_ = bf16[128,256]{1,0:T(8,128)(2,1)} collective-permute-done((bf16[128,256]{1,0:T(8,128)(2,1)}, bf16[128,256]{1,0:T(8,128)(2,1)}, u32[]{:S(2)}, u32[]{:S(2)}) %collective-permute-start.9) | collective-permute-done | bytes 65568 | tf_op jit(solution)/shard_map/ppermute | solution.py:262
  42.2 1.5 %collective-permute-done.10.refs_3_ = bf16[128,256]{1,0:T(8,128)(2,1)} collective-permute-done((bf16[128,256]{1,0:T(8,128)(2,1)}, bf16[128,256]{1,0:T(8,128)(2,1)}, u32[]{:S(2)}, u32[]{:S(2)}) %collective-permute-start.10) | collective-permute-done | bytes 65568 | tf_op jit(solution)/shard_map/ppermute | solution.py:262
  43.7 0.9 copy-done.11
  44.7 2.0 %shard_map.122 = (f32[32,1024]{1,0:T(8,128)S(1)}, bf16[32,1024]{1,0:T(8,128)(2,1)S(1)}, bf16[32,1024]{1,0:T(8,128)(2,1)S(1)}, bf16[32,1024]{1,0:T(8,128)(2,1)S(1...) custom-call(s32[2]{0:T(128)S(1)} %pad_add_fusion.place_ref, ...), custom_call_target="tpu_custom_call" | custom-call | flops 268435456 | bytes 1900544 | tf_op jit(solution)/shard_map/pallas_call | solution.py:70
  46.7 0.6 collective-permute-start.14
  47.3 3.0 %collective-permute-start.15 = (bf16[32,1024]{1,0:T(8,128)(2,1)S(1)}, bf16[32,1024]{1,0:T(8,128)(2,1)S(1)}, u32[]{:S(2)}, u32[]{:S(2)}) collective-permute-start(bf16[32,1024]{1,0:T(8,128)(2,1)S(1)} %get-tuple-element.42), channel_id=1, source_target_pairs={{0,8},{4,12},{8,0},{12,4},{16,24},{20,28},{24,16},{28,20},{1,9},{5... | collective-permute-start | bytes 196616 | tf_op jit(solution)/shard_map/ppermute | solution.py:280
  50.3 1.0 broadcast_select_fusion.1
  51.4 3.4 %collective-permute-start.17 = (bf16[32,1024]{1,0:T(8,128)(2,1)S(1)}, bf16[32,1024]{1,0:T(8,128)(2,1)S(1)}, u32[]{:S(2)}, u32[]{:S(2)}) collective-permute-start(bf16[32,1024]{1,0:T(8,128)(2,1)S(1)} %get-tuple-element.44), channel_id=1, source_target_pairs={{0,16},{4,20},{8,24},{12,28},{16,0},{20,4},{24,8},{28,12},{1,17},{... | collective-permute-start | bytes 196616 | tf_op jit(solution)/shard_map/ppermute | solution.py:280
  54.8 0.8 collective-permute-start.18
  55.6 4.4 %collective-permute-start.19 = (bf16[32,1024]{1,0:T(8,128)(2,1)S(1)}, bf16[32,1024]{1,0:T(8,128)(2,1)S(1)}, u32[]{:S(2)}, u32[]{:S(2)}) collective-permute-start(bf16[32,1024]{1,0:T(8,128)(2,1)S(1)} %get-tuple-element.46), channel_id=1, source_target_pairs={{0,24},{4,28},{8,16},{12,20},{16,8},{20,12},{24,0},{28,4},{1,25},{... | collective-permute-start | bytes 196616 | tf_op jit(solution)/shard_map/ppermute | solution.py:280
  60.1 2.5 %collective-permute-start.5 = (bf16[128,1024]{1,0:T(8,128)(2,1)S(1)}, bf16[128,1024]{1,0:T(8,128)(2,1)S(1)}, u32[]{:S(2)}, u32[]{:S(2)}) collective-permute-start(bf16[128,1024]{1,0:T(8,128)(2,1)S(1)} %broadcast_select_fusion.1), channel_id=1, source_target_pairs={{0,4},{4,0},{8,12},{12,8},{16,20},{20,16},{24,28},{28,24},{1,5},{5... | collective-permute-start | bytes 786440 | tf_op jit(solution)/shard_map/ppermute | solution.py:224
  62.7 2.4 %collective-permute-done.18.refs_4_ = bf16[32,1024]{1,0:T(8,128)(2,1)S(1)} collective-permute-done((bf16[32,1024]{1,0:T(8,128)(2,1)S(1)}, bf16[32,1024]{1,0:T(8,128)(2,1)S(1)}, u32[]{:S(2)}, u32[]{:S(2)}) %collective-permute-start.18) | collective-permute-done | bytes 65568 | tf_op jit(solution)/shard_map/ppermute | solution.py:280
  65.1 2.0 %collective-permute-done.20.refs_6_ = bf16[32,1024]{1,0:T(8,128)(2,1)S(1)} collective-permute-done((bf16[32,1024]{1,0:T(8,128)(2,1)S(1)}, bf16[32,1024]{1,0:T(8,128)(2,1)S(1)}, u32[]{:S(2)}, u32[]{:S(2)}) %collective-permute-start.20) | collective-permute-done | bytes 65568 | tf_op jit(solution)/shard_map/ppermute | solution.py:280
  67.2 0.6 collective-permute-start.21
  67.8 2.0 %collective-permute-start.22 = (bf16[32,1024]{1,0:T(8,128)(2,1)S(1)}, bf16[32,1024]{1,0:T(8,128)(2,1)S(1)}, u32[]{:S(2)}, u32[]{:S(2)}) collective-permute-start(bf16[32,1024]{1,0:T(8,128)(2,1)S(1)} %shard_map.123.refs_0_), channel_id=1, source_target_pairs={{0,8},{4,12},{8,0},{12,4},{16,24},{20,28},{24,16},{28,20},{1,9},{5... | collective-permute-start | bytes 196616 | tf_op jit(solution)/shard_map/ppermute | solution.py:282
  69.8 0.9 collective-permute-start.23
  70.7 7.3 %collective-permute-done.21.refs_1_ = bf16[32,1024]{1,0:T(8,128)(2,1)S(1)} collective-permute-done((bf16[32,1024]{1,0:T(8,128)(2,1)S(1)}, bf16[32,1024]{1,0:T(8,128)(2,1)S(1)}, u32[]{:S(2)}, u32[]{:S(2)}) %collective-permute-start.21) | collective-permute-done | bytes 65568 | tf_op jit(solution)/shard_map/ppermute | solution.py:282
  78.1 3.8 %collective-permute-start.25 = (bf16[32,1024]{1,0:T(8,128)(2,1)S(1)}, bf16[32,1024]{1,0:T(8,128)(2,1)S(1)}, u32[]{:S(2)}, u32[]{:S(2)}) collective-permute-start(bf16[32,1024]{1,0:T(8,128)(2,1)S(1)} %shard_map.123.refs_0_), channel_id=1, source_target_pairs={{0,20},{4,16},{8,28},{12,24},{16,4},{20,0},{24,12},{28,8},{1,21},{... | collective-permute-start | bytes 196616 | tf_op jit(solution)/shard_map/ppermute | solution.py:282
  81.9 2.7 %collective-permute-start.26 = (bf16[32,1024]{1,0:T(8,128)(2,1)S(1)}, bf16[32,1024]{1,0:T(8,128)(2,1)S(1)}, u32[]{:S(2)}, u32[]{:S(2)}) collective-permute-start(bf16[32,1024]{1,0:T(8,128)(2,1)S(1)} %shard_map.123.refs_0_), channel_id=1, source_target_pairs={{0,24},{4,28},{8,16},{12,20},{16,8},{20,12},{24,0},{28,4},{1,25},{... | collective-permute-start | bytes 196616 | tf_op jit(solution)/shard_map/ppermute | solution.py:282
  84.6 1.1 %collective-permute-done.24.refs_4_ = bf16[32,1024]{1,0:T(8,128)(2,1)S(1)} collective-permute-done((bf16[32,1024]{1,0:T(8,128)(2,1)S(1)}, bf16[32,1024]{1,0:T(8,128)(2,1)S(1)}, u32[]{:S(2)}, u32[]{:S(2)}) %collective-permute-start.24) | collective-permute-done | bytes 65568 | tf_op jit(solution)/shard_map/ppermute | solution.py:282
  85.7 2.5 %collective-permute-start.27 = (bf16[32,1024]{1,0:T(8,128)(2,1)S(1)}, bf16[32,1024]{1,0:T(8,128)(2,1)S(1)}, u32[]{:S(2)}, u32[]{:S(2)}) collective-permute-start(bf16[32,1024]{1,0:T(8,128)(2,1)S(1)} %shard_map.123.refs_0_), channel_id=1, source_target_pairs={{0,28},{4,24},{8,20},{12,16},{16,12},{20,8},{24,4},{28,0},{1,29},{... | collective-permute-start | bytes 196616 | tf_op jit(solution)/shard_map/ppermute | solution.py:282
  88.3 0.9 copy-done.18
  89.2 4.7 %shard_map.120 = (bf16[128,1024]{1,0:T(8,128)(2,1)}, bf16[128,1024]{1,0:T(8,128)(2,1)}) custom-call(s32[1,4]{1,0:T(1,128)S(1)} %copy-done.20, s32[2]{0:T(128)S(1)} %pad_add_fusion.place_ref, bf16[128,1024]{1,0:T(8,128)(2,1)S(1)} %bitcast.18, bf16[128,1024]{1,0:T(8,128)(2,1)S(1)} %bitcast.22, bf16[128,1024]{1,0:T(8,128)(2,1)S(1)} %copy-done.13, ...), custom_call_target="tpu_custom_call" | custom-call | flops 570425344 | bytes 4980736 | tf_op jit(solution)/shard_map/pallas_call | solution.py:70
  93.9 1.6 %shard_map.124 = f32[256,1024]{1,0:T(8,128)} custom-call(s32[2]{0:T(128)S(1)} %pad_add_fusion.place_ref, bf16[32,1024]{1,0:T(8,128)(2,1)S(1)} %shard_map.123.refs_0_, bf16[32,1024]{1,0:T(8,128)(2,1)S(1)} %collective-permute-done.21.refs_1_, bf16[32,1024]{1,0:T(8,128)(2,1)S(1)} %collective-permute-done.22.refs_2_, ...), custom_call_target="tpu_custom_call" | custom-call | flops 262144 | bytes 1572864 | tf_op jit(solution)/shard_map/pallas_call | solution.py:70
  95.5 5.4 %shard_map.121 = (bf16[128,1024]{1,0:T(8,128)(2,1)}, bf16[128,1024]{1,0:T(8,128)(2,1)}) custom-call(s32[1,4]{1,0:T(1,128)S(1)} %copy-done.20, s32[2]{0:T(128)S(1)} %pad_add_fusion.place_ref, bf16[128,1024]{1,0:T(8,128)(2,1)S(1)} %bitcast.23, bf16[128,1024]{1,0:T(8,128)(2,1)S(1)} %bitcast.27, bf16[128,1024]{1,0:T(8,128)(2,1)S(1)} %bitcast.19, ...), custom_call_target="tpu_custom_call" | custom-call | flops 402653184 | bytes 2621440 | tf_op jit(solution)/shard_map/pallas_call | solution.py:70
  (62 shorter events, 1.2 us)
Async XLA Ops:
  0.6 11.9 %collective-permute-start = (bf16[128,1024]{1,0:T(8,128)(2,1)}, bf16[128,1024]{1,0:T(8,128)(2,1)S(1)}, u32[]{:S(2)}, u32[]{:S(2)}) collective-permute-start(bf16[128,1024]{1,0:T(8,128)(2,1)} %bitcast.20), channel_id=1, source_target_pairs={{0,8},{4,12},{8,16},{12,20},{16,24},{20,28},{1,9},{5,13},{9,17},{1... | collective-permute-start | bytes 786440 | tf_op jit(solution)/shard_map/ppermute | solution.py:221
  5.6 11.5 %collective-permute-start.2 = (bf16[128,1024]{1,0:T(8,128)(2,1)}, bf16[128,1024]{1,0:T(8,128)(2,1)S(1)}, u32[]{:S(2)}, u32[]{:S(2)}) collective-permute-start(bf16[128,1024]{1,0:T(8,128)(2,1)} %bitcast.24), channel_id=1, source_target_pairs={{0,8},{4,12},{8,16},{12,20},{16,24},{20,28},{1,9},{5,13},{9,17},{1... | collective-permute-start | bytes 786440 | tf_op jit(solution)/shard_map/ppermute | solution.py:221
  13.6 17.9 %copy-start.16 = (bf16[1,128,1024]{2,1,0:T(8,128)(2,1)S(1)}, bf16[1,128,1024]{2,1,0:T(8,128)(2,1)}, u32[]{:S(2)}) copy-start(bf16[1,128,1024]{2,1,0:T(8,128)(2,1)} %param.10) | copy-start | bytes 786436
  13.6 7.9 %collective-permute-start.1 = (bf16[128,1024]{1,0:T(8,128)(2,1)S(1)}, bf16[128,1024]{1,0:T(8,128)(2,1)S(1)}, u32[]{:S(2)}, u32[]{:S(2)}) collective-permute-start(bf16[128,1024]{1,0:T(8,128)(2,1)S(1)} %broadcast_select_fusion.3), channel_id=1, source_target_pairs={{0,4},{4,0},{8,12},{12,8},{16,20},{20,16},{24,28},{28,24},{1,5},{5... | collective-permute-start | bytes 786440 | tf_op jit(solution)/shard_map/ppermute | solution.py:224
  18.0 13.4 %collective-permute-start.3 = (bf16[128,1024]{1,0:T(8,128)(2,1)S(1)}, bf16[128,1024]{1,0:T(8,128)(2,1)S(1)}, u32[]{:S(2)}, u32[]{:S(2)}) collective-permute-start(bf16[128,1024]{1,0:T(8,128)(2,1)S(1)} %broadcast_select_fusion.2), channel_id=1, source_target_pairs={{0,4},{4,0},{8,12},{12,8},{16,20},{20,16},{24,28},{28,24},{1,5},{5... | collective-permute-start | bytes 786440 | tf_op jit(solution)/shard_map/ppermute | solution.py:224
  19.6 18.0 %collective-permute-start.11 = (bf16[128,1024]{1,0:T(8,128)(2,1)}, bf16[128,1024]{1,0:T(8,128)(2,1)}, u32[]{:S(2)}, u32[]{:S(2)}) collective-permute-start(bf16[128,1024]{1,0:T(8,128)(2,1)} %bitcast.28), channel_id=1, source_target_pairs={{0,1},{1,0},{2,3},{3,2},{4,5},{5,4},{6,7},{7,6},{8,9},{9,8},{10,11... | collective-permute-start | bytes 786440 | tf_op jit(solution)/shard_map/ppermute | solution.py:246
  19.6 19.6 %collective-permute-start.12 = (bf16[128,1024]{1,0:T(8,128)(2,1)}, bf16[128,1024]{1,0:T(8,128)(2,1)}, u32[]{:S(2)}, u32[]{:S(2)}) collective-permute-start(bf16[128,1024]{1,0:T(8,128)(2,1)} %bitcast.29), channel_id=1, source_target_pairs={{0,2},{1,3},{2,0},{3,1},{4,6},{5,7},{6,4},{7,5},{8,10},{9,11},{10,... | collective-permute-start | bytes 786440 | tf_op jit(solution)/shard_map/ppermute | solution.py:246
  21.1 18.1 %collective-permute-start.13 = (bf16[128,1024]{1,0:T(8,128)(2,1)}, bf16[128,1024]{1,0:T(8,128)(2,1)}, u32[]{:S(2)}, u32[]{:S(2)}) collective-permute-start(bf16[128,1024]{1,0:T(8,128)(2,1)} %bitcast.30), channel_id=1, source_target_pairs={{0,3},{1,2},{2,1},{3,0},{4,7},{5,6},{6,5},{7,4},{8,11},{9,10},{10,... | collective-permute-start | bytes 786440 | tf_op jit(solution)/shard_map/ppermute | solution.py:246
  21.5 10.0 %copy-start.12 = (bf16[128,1024]{1,0:T(8,128)(2,1)}, bf16[128,1024]{1,0:T(8,128)(2,1)S(1)}, u32[]{:S(2)}) copy-start(bf16[128,1024]{1,0:T(8,128)(2,1)S(1)} %collective-permute-done.1.k1) | copy-start | bytes 786436
  21.5 28.9 %collective-permute-start.4 = (bf16[128,1024]{1,0:T(8,128)(2,1)}, bf16[128,1024]{1,0:T(8,128)(2,1)}, u32[]{:S(2)}, u32[]{:S(2)}) collective-permute-start(bf16[128,1024]{1,0:T(8,128)(2,1)} %bitcast.15), channel_id=1, source_target_pairs={{8,0},{12,4},{16,8},{20,12},{24,16},{28,20},{9,1},{13,5},{17,9},{2... | collective-permute-start | bytes 786440 | tf_op jit(solution)/shard_map/ppermute | solution.py:221
  22.8 1.6 %copy-start = (bf16[1024,1024]{1,0:T(8,128)(2,1)S(1)}, bf16[1024,1024]{1,0:T(8,128)(2,1)}, u32[]{:S(2)}) copy-start(bf16[1024,1024]{1,0:T(8,128)(2,1)} %w.3) | copy-start | bytes 6291460
  24.4 0.9 copy-start.2
  25.4 0.9 copy-start.4
  26.3 0.9 copy-start.6
  27.3 0.9 copy-start.10
  31.4 18.9 %copy-start.3 = (bf16[1,128,1024]{2,1,0:T(8,128)(2,1)S(1)}, bf16[1,128,1024]{2,1,0:T(8,128)(2,1)}, u32[]{:S(2)}) copy-start(bf16[1,128,1024]{2,1,0:T(8,128)(2,1)} %param.7) | copy-start | bytes 786436
  31.4 56.8 %copy-start.20 = (s32[1,4]{1,0:T(1,128)S(1)}, s32[1,4]{1,0:T(1,128)}, u32[]{:S(2)}) copy-start(s32[1,4]{1,0:T(1,128)} %len_ref.7) | copy-start | bytes 52
  35.2 0.7 copy-start.8
  35.9 0.7 copy-start.14
  36.6 0.7 copy-start.17
  37.3 50.9 %copy-start.1 = (bf16[1024,1024]{1,0:T(8,128)(2,1)S(1)}, bf16[1024,1024]{1,0:T(8,128)(2,1)}, u32[]{:S(2)}) copy-start(bf16[1024,1024]{1,0:T(8,128)(2,1)} %w.3) | copy-start | bytes 6291460
  37.3 50.9 %copy-start.5 = (bf16[1,128,1024]{2,1,0:T(8,128)(2,1)S(1)}, bf16[1,128,1024]{2,1,0:T(8,128)(2,1)}, u32[]{:S(2)}) copy-start(bf16[1,128,1024]{2,1,0:T(8,128)(2,1)} %param.8) | copy-start | bytes 786436
  37.3 50.9 %copy-start.7 = (bf16[1,128,1024]{2,1,0:T(8,128)(2,1)S(1)}, bf16[1,128,1024]{2,1,0:T(8,128)(2,1)}, u32[]{:S(2)}) copy-start(bf16[1,128,1024]{2,1,0:T(8,128)(2,1)} %param.9) | copy-start | bytes 786436
  37.3 3.3 %collective-permute-start.8 = (bf16[128,256]{1,0:T(8,128)(2,1)}, bf16[128,256]{1,0:T(8,128)(2,1)S(1)}, u32[]{:S(2)}, u32[]{:S(2)}) collective-permute-start(bf16[128,256]{1,0:T(8,128)(2,1)} %get-tuple-element.37), channel_id=1, source_target_pairs={{0,1},{1,0},{2,3},{3,2},{4,5},{5,4},{6,7},{7,6},{8,9},{9,8},{10,11... | collective-permute-start | bytes 196616 | tf_op jit(solution)/shard_map/ppermute | solution.py:262
  37.6 4.6 %collective-permute-start.9 = (bf16[128,256]{1,0:T(8,128)(2,1)}, bf16[128,256]{1,0:T(8,128)(2,1)}, u32[]{:S(2)}, u32[]{:S(2)}) collective-permute-start(bf16[128,256]{1,0:T(8,128)(2,1)} %get-tuple-element.38), channel_id=1, source_target_pairs={{0,2},{1,3},{2,0},{3,1},{4,6},{5,7},{6,4},{7,5},{8,10},{9,11},{10,... | collective-permute-start | bytes 196616 | tf_op jit(solution)/shard_map/ppermute | solution.py:262
  39.1 4.6 %collective-permute-start.10 = (bf16[128,256]{1,0:T(8,128)(2,1)}, bf16[128,256]{1,0:T(8,128)(2,1)}, u32[]{:S(2)}, u32[]{:S(2)}) collective-permute-start(bf16[128,256]{1,0:T(8,128)(2,1)} %get-tuple-element.39), channel_id=1, source_target_pairs={{0,3},{1,2},{2,1},{3,0},{4,7},{5,6},{6,5},{7,4},{8,11},{9,10},{10,... | collective-permute-start | bytes 196616 | tf_op jit(solution)/shard_map/ppermute | solution.py:262
  39.2 49.0 %copy-start.9 = (bf16[128,1024]{1,0:T(8,128)(2,1)S(1)}, bf16[128,1024]{1,0:T(8,128)(2,1)}, u32[]{:S(2)}) copy-start(bf16[128,1024]{1,0:T(8,128)(2,1)} %copy-done.8) | copy-start | bytes 786436
  39.2 20.8 %collective-permute-start.6 = (bf16[128,1024]{1,0:T(8,128)(2,1)}, bf16[128,1024]{1,0:T(8,128)(2,1)S(1)}, u32[]{:S(2)}, u32[]{:S(2)}) collective-permute-start(bf16[128,1024]{1,0:T(8,128)(2,1)} %copy-done.8), channel_id=1, source_target_pairs={{8,0},{12,4},{16,8},{20,12},{24,16},{28,20},{9,1},{13,5},{17,9},{2... | collective-permute-start | bytes 786440 | tf_op jit(solution)/shard_map/ppermute | solution.py:221
  43.7 1.0 copy-start.11
  44.7 43.6 %copy-start.13 = (bf16[128,1024]{1,0:T(8,128)(2,1)S(1)}, bf16[128,1024]{1,0:T(8,128)(2,1)}, u32[]{:S(2)}) copy-start(bf16[128,1024]{1,0:T(8,128)(2,1)} %copy-done.12) | copy-start | bytes 786436
  44.7 43.6 %copy-start.15 = (bf16[128,1024]{1,0:T(8,128)(2,1)S(1)}, bf16[128,1024]{1,0:T(8,128)(2,1)}, u32[]{:S(2)}) copy-start(bf16[128,1024]{1,0:T(8,128)(2,1)} %copy-done.14) | copy-start | bytes 786436
  46.7 8.0 %collective-permute-start.14 = (bf16[32,1024]{1,0:T(8,128)(2,1)S(1)}, bf16[32,1024]{1,0:T(8,128)(2,1)S(1)}, u32[]{:S(2)}, u32[]{:S(2)}) collective-permute-start(bf16[32,1024]{1,0:T(8,128)(2,1)S(1)} %get-tuple-element.41), channel_id=1, source_target_pairs={{0,4},{4,0},{8,12},{12,8},{16,20},{20,16},{24,28},{28,24},{1,5},{5... | collective-permute-start | bytes 196616 | tf_op jit(solution)/shard_map/ppermute | solution.py:280
  47.3 8.3 %collective-permute-start.15 = (bf16[32,1024]{1,0:T(8,128)(2,1)S(1)}, bf16[32,1024]{1,0:T(8,128)(2,1)S(1)}, u32[]{:S(2)}, u32[]{:S(2)}) collective-permute-start(bf16[32,1024]{1,0:T(8,128)(2,1)S(1)} %get-tuple-element.42), channel_id=1, source_target_pairs={{0,8},{4,12},{8,0},{12,4},{16,24},{20,28},{24,16},{28,20},{1,9},{5... | collective-permute-start | bytes 196616 | tf_op jit(solution)/shard_map/ppermute | solution.py:280
  51.3 8.8 %collective-permute-start.16 = (bf16[32,1024]{1,0:T(8,128)(2,1)S(1)}, bf16[32,1024]{1,0:T(8,128)(2,1)S(1)}, u32[]{:S(2)}, u32[]{:S(2)}) collective-permute-start(bf16[32,1024]{1,0:T(8,128)(2,1)S(1)} %get-tuple-element.43), channel_id=1, source_target_pairs={{0,12},{4,8},{8,4},{12,0},{16,28},{20,24},{24,20},{28,16},{1,13},{... | collective-permute-start | bytes 196616 | tf_op jit(solution)/shard_map/ppermute | solution.py:280
  51.4 11.2 %collective-permute-start.17 = (bf16[32,1024]{1,0:T(8,128)(2,1)S(1)}, bf16[32,1024]{1,0:T(8,128)(2,1)S(1)}, u32[]{:S(2)}, u32[]{:S(2)}) collective-permute-start(bf16[32,1024]{1,0:T(8,128)(2,1)S(1)} %get-tuple-element.44), channel_id=1, source_target_pairs={{0,16},{4,20},{8,24},{12,28},{16,0},{20,4},{24,8},{28,12},{1,17},{... | collective-permute-start | bytes 196616 | tf_op jit(solution)/shard_map/ppermute | solution.py:280
  54.8 10.3 %collective-permute-start.18 = (bf16[32,1024]{1,0:T(8,128)(2,1)S(1)}, bf16[32,1024]{1,0:T(8,128)(2,1)S(1)}, u32[]{:S(2)}, u32[]{:S(2)}) collective-permute-start(bf16[32,1024]{1,0:T(8,128)(2,1)S(1)} %get-tuple-element.45), channel_id=1, source_target_pairs={{0,20},{4,16},{8,28},{12,24},{16,4},{20,0},{24,12},{28,8},{1,21},{... | collective-permute-start | bytes 196616 | tf_op jit(solution)/shard_map/ppermute | solution.py:280
  55.6 9.5 %collective-permute-start.19 = (bf16[32,1024]{1,0:T(8,128)(2,1)S(1)}, bf16[32,1024]{1,0:T(8,128)(2,1)S(1)}, u32[]{:S(2)}, u32[]{:S(2)}) collective-permute-start(bf16[32,1024]{1,0:T(8,128)(2,1)S(1)} %get-tuple-element.46), channel_id=1, source_target_pairs={{0,24},{4,28},{8,16},{12,20},{16,8},{20,12},{24,0},{28,4},{1,25},{... | collective-permute-start | bytes 196616 | tf_op jit(solution)/shard_map/ppermute | solution.py:280
  60.0 7.1 %collective-permute-start.20 = (bf16[32,1024]{1,0:T(8,128)(2,1)S(1)}, bf16[32,1024]{1,0:T(8,128)(2,1)S(1)}, u32[]{:S(2)}, u32[]{:S(2)}) collective-permute-start(bf16[32,1024]{1,0:T(8,128)(2,1)S(1)} %get-tuple-element.47), channel_id=1, source_target_pairs={{0,28},{4,24},{8,20},{12,16},{16,12},{20,8},{24,4},{28,0},{1,29},{... | collective-permute-start | bytes 196616 | tf_op jit(solution)/shard_map/ppermute | solution.py:280
  60.1 35.4 %collective-permute-start.5 = (bf16[128,1024]{1,0:T(8,128)(2,1)S(1)}, bf16[128,1024]{1,0:T(8,128)(2,1)S(1)}, u32[]{:S(2)}, u32[]{:S(2)}) collective-permute-start(bf16[128,1024]{1,0:T(8,128)(2,1)S(1)} %broadcast_select_fusion.1), channel_id=1, source_target_pairs={{0,4},{4,0},{8,12},{12,8},{16,20},{20,16},{24,28},{28,24},{1,5},{5... | collective-permute-start | bytes 786440 | tf_op jit(solution)/shard_map/ppermute | solution.py:224
  62.6 32.9 %collective-permute-start.7 = (bf16[128,1024]{1,0:T(8,128)(2,1)S(1)}, bf16[128,1024]{1,0:T(8,128)(2,1)S(1)}, u32[]{:S(2)}, u32[]{:S(2)}) collective-permute-start(bf16[128,1024]{1,0:T(8,128)(2,1)S(1)} %broadcast_select_fusion), channel_id=1, source_target_pairs={{0,4},{4,0},{8,12},{12,8},{16,20},{20,16},{24,28},{28,24},{1,5},{5... | collective-permute-start | bytes 786440 | tf_op jit(solution)/shard_map/ppermute | solution.py:224
  67.2 10.9 %collective-permute-start.21 = (bf16[32,1024]{1,0:T(8,128)(2,1)S(1)}, bf16[32,1024]{1,0:T(8,128)(2,1)S(1)}, u32[]{:S(2)}, u32[]{:S(2)}) collective-permute-start(bf16[32,1024]{1,0:T(8,128)(2,1)S(1)} %shard_map.123.refs_0_), channel_id=1, source_target_pairs={{0,4},{4,0},{8,12},{12,8},{16,20},{20,16},{24,28},{28,24},{1,5},{5... | collective-permute-start | bytes 196616 | tf_op jit(solution)/shard_map/ppermute | solution.py:282
  67.8 10.3 %collective-permute-start.22 = (bf16[32,1024]{1,0:T(8,128)(2,1)S(1)}, bf16[32,1024]{1,0:T(8,128)(2,1)S(1)}, u32[]{:S(2)}, u32[]{:S(2)}) collective-permute-start(bf16[32,1024]{1,0:T(8,128)(2,1)S(1)} %shard_map.123.refs_0_), channel_id=1, source_target_pairs={{0,8},{4,12},{8,0},{12,4},{16,24},{20,28},{24,16},{28,20},{1,9},{5... | collective-permute-start | bytes 196616 | tf_op jit(solution)/shard_map/ppermute | solution.py:282
  69.8 12.1 %collective-permute-start.23 = (bf16[32,1024]{1,0:T(8,128)(2,1)S(1)}, bf16[32,1024]{1,0:T(8,128)(2,1)S(1)}, u32[]{:S(2)}, u32[]{:S(2)}) collective-permute-start(bf16[32,1024]{1,0:T(8,128)(2,1)S(1)} %shard_map.123.refs_0_), channel_id=1, source_target_pairs={{0,12},{4,8},{8,4},{12,0},{16,28},{20,24},{24,20},{28,16},{1,13},{... | collective-permute-start | bytes 196616 | tf_op jit(solution)/shard_map/ppermute | solution.py:282
  78.1 7.6 %collective-permute-start.24 = (bf16[32,1024]{1,0:T(8,128)(2,1)S(1)}, bf16[32,1024]{1,0:T(8,128)(2,1)S(1)}, u32[]{:S(2)}, u32[]{:S(2)}) collective-permute-start(bf16[32,1024]{1,0:T(8,128)(2,1)S(1)} %shard_map.123.refs_0_), channel_id=1, source_target_pairs={{0,16},{4,20},{8,24},{12,28},{16,0},{20,4},{24,8},{28,12},{1,17},{... | collective-permute-start | bytes 196616 | tf_op jit(solution)/shard_map/ppermute | solution.py:282
  78.1 15.8 %collective-permute-start.25 = (bf16[32,1024]{1,0:T(8,128)(2,1)S(1)}, bf16[32,1024]{1,0:T(8,128)(2,1)S(1)}, u32[]{:S(2)}, u32[]{:S(2)}) collective-permute-start(bf16[32,1024]{1,0:T(8,128)(2,1)S(1)} %shard_map.123.refs_0_), channel_id=1, source_target_pairs={{0,20},{4,16},{8,28},{12,24},{16,4},{20,0},{24,12},{28,8},{1,21},{... | collective-permute-start | bytes 196616 | tf_op jit(solution)/shard_map/ppermute | solution.py:282
  81.9 12.0 %collective-permute-start.26 = (bf16[32,1024]{1,0:T(8,128)(2,1)S(1)}, bf16[32,1024]{1,0:T(8,128)(2,1)S(1)}, u32[]{:S(2)}, u32[]{:S(2)}) collective-permute-start(bf16[32,1024]{1,0:T(8,128)(2,1)S(1)} %shard_map.123.refs_0_), channel_id=1, source_target_pairs={{0,24},{4,28},{8,16},{12,20},{16,8},{20,12},{24,0},{28,4},{1,25},{... | collective-permute-start | bytes 196616 | tf_op jit(solution)/shard_map/ppermute | solution.py:282
  85.7 8.2 %collective-permute-start.27 = (bf16[32,1024]{1,0:T(8,128)(2,1)S(1)}, bf16[32,1024]{1,0:T(8,128)(2,1)S(1)}, u32[]{:S(2)}, u32[]{:S(2)}) collective-permute-start(bf16[32,1024]{1,0:T(8,128)(2,1)S(1)} %shard_map.123.refs_0_), channel_id=1, source_target_pairs={{0,28},{4,24},{8,20},{12,16},{16,12},{20,8},{24,4},{28,0},{1,29},{... | collective-permute-start | bytes 196616 | tf_op jit(solution)/shard_map/ppermute | solution.py:282
  88.3 1.0 copy-start.18
  (1 other events, 0.7 us)

commit v2 on v1

--- a/solution.py
+++ b/solution.py
@@ -96,8 +96,7 @@
     groups, len_ref, place_ref, q, k1, k2, v1, v2, mixed_own, grad_hidden, gates, *rest
 ):
     hidden, grad_gates, grad_mix = rest[:3]
-    slices = rest[3 : 3 + groups]
-    mixed = rest[3 + groups]
+    slices, mixed = rest[3:]
     rows, width = q.shape
     size = width // HEADS
     scale = size ** (-0.5)
@@ -129,9 +128,8 @@
         * inv_std
     ).astype(BF16)
     part = width // groups
-    for d, ref in enumerate(slices):
-        at = pl.multiple_of((place_ref[1] ^ d) * part, 128)
-        ref[...] = hidden[:, pl.ds(at, part)]
+    for d in range(groups):
+        slices[d * rows : (d + 1) * rows, :] = hidden[:, d * part : (d + 1) * part]
 
 
 def query_kernel(len_ref, place_ref, q, k0, k1, k2, v0, v1, v2, grad_mix, hidden, w, output, grad_queries):
@@ -176,39 +174,28 @@
         grad_values[:, cols] = values_total.astype(BF16)
 
 
-def weight_kernel(groups, place_ref, *refs):
-    hidden = refs[:groups]
-    grads = refs[groups : 2 * groups]
-    own = refs[2 * groups]
-    sends = refs[2 * groups + 1 : -1]
-    total = refs[-1]
-    acc = dot_tn(hidden[0][...], grads[0][...])
-    for a, b in zip(hidden[1:], grads[1:]):
-        acc = acc + dot_tn(a[...], b[...])
-    total[...] = acc
-    rows = own.shape[0]
-    if not sends:
-        own[...] = acc
-        return
-    own[...] = total[pl.ds(pl.multiple_of(place_ref[0] * rows, rows), rows), :]
-    for e, ref in enumerate(sends):
-        at = pl.multiple_of((place_ref[0] ^ (e + 1)) * rows, rows)
-        ref[...] = total[pl.ds(at, rows), :].astype(BF16)
-
-
-def sum_kernel(scale, own, *refs):
-    total = own[...]
-    for ref in refs[:-1]:
-        total = total + ref[...].astype(F32)
-    refs[-1][...] = (total * scale).astype(BF16)
-
-
-def place_kernel(place_ref, *refs):
-    out = refs[-1]
-    rows = refs[0].shape[0]
-    for e, ref in enumerate(refs[:-1]):
-        at = pl.multiple_of((place_ref[0] ^ e) * rows, rows)
-        out[pl.ds(at, rows), :] = ref[...].astype(F32)
+def weight_kernel(place_ref, hidden, *refs):
+    grads, total = refs[:-1], refs[-1]
+    rows = grads[0].shape[0]
+    acc = jnp.zeros(total.shape, F32)
+    for d, grad in enumerate(grads):
+        at = pl.multiple_of((place_ref[1] ^ d) * rows, rows)
+        acc = acc + dot_tn(hidden[pl.ds(at, rows), :], grad[...])
+    total[...] = acc.astype(total.dtype)
+
+
+def sum_kernel(count, scale, parts, out):
+    rows = parts.shape[0] // count
+    total = parts[:rows, :].astype(F32)
+    for e in range(1, parts.shape[0] // rows):
+        total = total + parts[e * rows : (e + 1) * rows, :].astype(F32)
+    piece = (total * scale).astype(BF16)
+    for e in range(parts.shape[0] // rows):
+        out[e * rows : (e + 1) * rows, :] = piece
+
+
+def widen_kernel(parts, out):
+    out[...] = parts[...].astype(F32)
 
 
 def xor_route(size, mask):
@@ -249,46 +236,29 @@
         own_kernel, [wide, wide], scalars, (q, k, v, grad, w_out), proj_flops + 2 * block_flops
     )
     part = width // batch
-    piece = jax.ShapeDtypeStruct((rows, part), BF16)
-    hidden, grad_gates, grad_mix, *slices = call(
+    hidden, grad_gates, grad_mix, slices = call(
         functools.partial(forward_kernel, batch),
-        [full, full, full] + [piece] * batch,
+        [full, full, full, jax.ShapeDtypeStruct((batch * rows, part), BF16)],
         scalars,
         (q, k1, k2, v1, v2, mixed_own, grad_hidden, gate),
         4 * block_flops,
         [pltpu.VMEM((rows, width), F32)],
     )
-    hiddens = [slices[0]] + [
-        lax.ppermute(slices[d], "batch", xor_route(batch, d)) for d in range(1, batch)
-    ]
+    gathered = lax.all_to_all(slices, "batch", 0, 0, tiled=True)
     g1, g2 = halo(grad_mix, -2, even)
 
-    direct = seq == 8
-    rows_w = part // seq if direct else part
-    own_shape = jax.ShapeDtypeStruct((rows_w, width), F32)
-    send_shape = jax.ShapeDtypeStruct((rows_w, width), BF16)
+    direct = part % (16 * seq) == 0
     scale = (rows * seq * batch) ** (-0.5)
-    own, *sends = call(
-        functools.partial(weight_kernel, batch),
-        [own_shape] + ([send_shape] * (seq - 1) if direct else []),
-        (place,),
-        (*hiddens, *grads),
-        proj_flops,
-        [pltpu.VMEM((part, width), F32)],
-    )
+    narrow = jax.ShapeDtypeStruct((part, width), BF16)
+    result = jax.ShapeDtypeStruct((part, width), F32)
+    (total,) = call(weight_kernel, [narrow if direct else result], (place,), (gathered, *grads), proj_flops)
     if direct:
-        got = [lax.ppermute(s, "seq", xor_route(seq, e + 1)) for e, s in enumerate(sends)]
-        (mine,) = call(functools.partial(sum_kernel, scale), [send_shape], (), (own, *got), own.size * 8)
-        shares = [mine] + [lax.ppermute(mine, "seq", xor_route(seq, e)) for e in range(1, seq)]
-        (grad_weight,) = call(
-            place_kernel,
-            [jax.ShapeDtypeStruct((part, width), F32)],
-            (place,),
-            tuple(shares),
-            part * width,
-        )
+        parts = lax.all_to_all(total, "seq", 0, 0, tiled=True)
+        (mine,) = call(functools.partial(sum_kernel, seq, scale), [narrow], (), (parts,), part * width)
+        shares = lax.all_to_all(mine, "seq", 0, 0, tiled=True)
+        (grad_weight,) = call(widen_kernel, [result], (), (shares,), part * width)
     else:
-        grad_weight = lax.psum(own, "seq") * scale
+        grad_weight = lax.psum(total, "seq") * scale
 
     output, grad_queries = call(
         query_kernel,

time: 101 us -> 111 us (1.099)
  the two profiles are of different devices: /device:TPU:0 before, /device:TPU:8 now
where the time goes in v2:
time: 111 us; the launch traced here: 110 us
  waiting for transfers between devices  36.1 us (33%)
  starting transfers between devices  34.3 us (31%)
  Pallas kernels  21.6 us (19%)
  local copies, waits for them, and re-layouts  12.8 us (12%)
  other arithmetic  4 us (4%)
    pallas_call x7, Pallas kernels, call(): pl.pallas_call(kernel, out_shape=outs, in_specs=[SMEM] * len(scalars) + [...  21.6 us
    ppermute x4, waiting for transfers between devices, halo(): far = lax.ppermute(block, 'seq', route)  19 us
    unnamed x46, local copies, waits for them, and re-layouts  12.8 us
    all_to_all x1, waiting for transfers between devices, on_device(): parts = lax.all_to_all(total, 'seq', 0, 0, tiled=True)  11.2 us
    ppermute x4, starting transfers between devices, halo(): far = lax.ppermute(block, 'seq', route)  11.1 us
    all_to_all x1, starting transfers between devices, on_device(): shares = lax.all_to_all(mine, 'seq', 0, 0, tiled=True)  6.82 us
    all_to_all x1, waiting for transfers between devices, on_device(): gathered = lax.all_to_all(slices, 'batch', 0, 0, tiled=True)  5.97 us
    ppermute x4, starting transfers between devices, halo(): near = lax.ppermute(passed, 'seq', xor_route(count, 1))  5.64 us
  transfers between devices with their start and end apart: 14, of which 5 were waited for; matrix products, arithmetic and copies ran while one was open for 4% of the time, Pallas kernels for 16%

profile of v2, /device:TPU:8, one launch (start us, length us, event | category | flops | bytes accessed | tf_op | source)
XLA Modules:
  0.0 109.6 jit_solution(582692993407220662)
XLA Ops:
  0.6 3.5 %collective-permute-start = (bf16[128,1024]{1,0:T(8,128)(2,1)}, bf16[128,1024]{1,0:T(8,128)(2,1)S(1)}, u32[]{:S(2)}, u32[]{:S(2)}) collective-permute-start(bf16[128,1024]{1,0:T(8,128)(2,1)} %bitcast.26), channel_id=1, source_target_pairs={{0,8},{4,12},{8,16},{12,20},{16,24},{20,28},{1,9},{5,13},{9,17},{1... | collective-permute-start | bytes 786440 | tf_op jit(solution)/shard_map/ppermute | solution.py:208
  4.1 3.5 %collective-permute-start.2 = (bf16[128,1024]{1,0:T(8,128)(2,1)}, bf16[128,1024]{1,0:T(8,128)(2,1)S(1)}, u32[]{:S(2)}, u32[]{:S(2)}) collective-permute-start(bf16[128,1024]{1,0:T(8,128)(2,1)} %bitcast.30), channel_id=1, source_target_pairs={{0,8},{4,12},{8,16},{12,20},{16,24},{20,28},{1,9},{5,13},{9,17},{1... | collective-permute-start | bytes 786440 | tf_op jit(solution)/shard_map/ppermute | solution.py:208
  7.6 4.3 %collective-permute-done.k2 = bf16[128,1024]{1,0:T(8,128)(2,1)S(1)} collective-permute-done((bf16[128,1024]{1,0:T(8,128)(2,1)}, bf16[128,1024]{1,0:T(8,128)(2,1)S(1)}, u32[]{:S(2)}, u32[]{:S(2)}) %collective-permute-start) | collective-permute-done | bytes 262176 | tf_op jit(solution)/shard_map/ppermute | solution.py:208
  11.9 1.0 broadcast_select_fusion.3
  12.9 0.0 copy-start.18
  12.9 1.6 %collective-permute-start.1 = (bf16[128,1024]{1,0:T(8,128)(2,1)S(1)}, bf16[128,1024]{1,0:T(8,128)(2,1)S(1)}, u32[]{:S(2)}, u32[]{:S(2)}) collective-permute-start(bf16[128,1024]{1,0:T(8,128)(2,1)S(1)} %broadcast_select_fusion.3), channel_id=1, source_target_pairs={{0,4},{4,0},{8,12},{12,8},{16,20},{20,16},{24,28},{28,24},{1,5},{5... | collective-permute-start | bytes 786440 | tf_op jit(solution)/shard_map/ppermute | solution.py:211
  14.5 1.9 %collective-permute-done.2.v2 = bf16[128,1024]{1,0:T(8,128)(2,1)S(1)} collective-permute-done((bf16[128,1024]{1,0:T(8,128)(2,1)}, bf16[128,1024]{1,0:T(8,128)(2,1)S(1)}, u32[]{:S(2)}, u32[]{:S(2)}) %collective-permute-start.2) | collective-permute-done | bytes 262176 | tf_op jit(solution)/shard_map/ppermute | solution.py:208
  16.4 1.0 broadcast_select_fusion.2
  17.4 1.6 %collective-permute-start.3 = (bf16[128,1024]{1,0:T(8,128)(2,1)S(1)}, bf16[128,1024]{1,0:T(8,128)(2,1)S(1)}, u32[]{:S(2)}, u32[]{:S(2)}) collective-permute-start(bf16[128,1024]{1,0:T(8,128)(2,1)S(1)} %broadcast_select_fusion.2), channel_id=1, source_target_pairs={{0,4},{4,0},{8,12},{12,8},{16,20},{20,16},{24,28},{28,24},{1,5},{5... | collective-permute-start | bytes 786440 | tf_op jit(solution)/shard_map/ppermute | solution.py:211
  18.9 1.5 %collective-permute-start.9 = (bf16[128,1024]{1,0:T(8,128)(2,1)}, bf16[128,1024]{1,0:T(8,128)(2,1)S(1)}, u32[]{:S(2)}, u32[]{:S(2)}) collective-permute-start(bf16[128,1024]{1,0:T(8,128)(2,1)} %bitcast.36), channel_id=1, source_target_pairs={{0,2},{1,3},{2,0},{3,1},{4,6},{5,7},{6,4},{7,5},{8,10},{9,11},{10,... | collective-permute-start | bytes 786440 | tf_op jit(solution)/shard_map/ppermute | solution.py:233
  20.5 0.3 collective-permute-start.10
  20.8 0.1 pad_add_fusion.place_ref
  20.9 1.6 %copy-done = bf16[1024,1024]{1,0:T(8,128)(2,1)S(1)} copy-done((bf16[1024,1024]{1,0:T(8,128)(2,1)S(1)}, bf16[1024,1024]{1,0:T(8,128)(2,1)}, u32[]{:S(2)}) %copy-start) | copy-done | bytes 2097176
  22.5 0.9 copy-done.2
  23.4 0.9 copy-done.4
  24.4 0.9 copy-done.6
  25.3 0.9 copy-done.16
  26.3 0.7 copy-done.21
  26.9 2.5 %shard_map.118 = (f32[128,1024]{1,0:T(8,128)S(1)}, f32[128,1024]{1,0:T(8,128)S(1)}) custom-call(s32[1,4]{1,0:T(1,128)S(1)} %copy-done.21, s32[2]{0:T(128)S(1)} %pad_add_fusion.place_ref, bf16[128,1024]{1,0:T(8,128)(2,1)S(1)} %bitcast.21, bf16[128,1024]{1,0:T(8,128)(2,1)S(1)} %bitcast.27, bf16[128,1024]{1,0:T(8,128)(2,1)S(1)} %bitcast.31, ...), custom_call_target="tpu_custom_call" | custom-call | flops 335544320 | bytes 4194304 | tf_op jit(solution)/shard_map/pallas_call | solution.py:70
  29.5 0.0 copy-start.17
  29.5 3.8 %shard_map.119 = (bf16[128,1024]{1,0:T(8,128)(2,1)S(1)}, bf16[128,1024]{1,0:T(8,128)(2,1)}, bf16[128,1024]{1,0:T(8,128)(2,1)S(1)}, bf16[512,256]{1,0:T(8,128)(2,1)}) custom-call(s32[1,4]{1,0:T(1,128)S(1)} %copy-done.21, s32[2]{0:T(128)S(1)} %pad_add_fusion.place_ref, bf16[128,1024]{1,0:T(8,128)(2,1)S(1)} %bitcast.22, ...), custom_call_target="tpu_custom_call" | custom-call | flops 134217728 | bytes 3670016 | tf_op jit(solution)/shard_map/pallas_call | solution.py:70
  33.3 0.7 copy-done.8
  34.0 0.7 copy-done.12
  34.7 0.7 copy-done.19
  35.4 3.5 %all-to-all-start = ((bf16[4,128,256]{2,1,0:T(8,128)(2,1)}), bf16[4,128,256]{2,1,0:T(8,128)(2,1)S(1)}, u32[]{:S(2)}, u32[]{:S(2)}) async-start(bf16[4,128,256]{2,1,0:T(8,128)(2,1)} %bitcast.12), calls=%async_computation | async-start | bytes 524288 | tf_op jit(solution)/shard_map/all_to_all | solution.py:247
  39.0 6.0 %all-to-all-done = bf16[4,128,256]{2,1,0:T(8,128)(2,1)S(1)} async-done(((bf16[4,128,256]{2,1,0:T(8,128)(2,1)}), bf16[4,128,256]{2,1,0:T(8,128)(2,1)S(1)}, u32[]{:S(2)}, u32[]{:S(2)}) %all-to-all-start) | async-done | bytes 262176 | tf_op jit(solution)/shard_map/all_to_all | solution.py:247
  44.9 2.1 %shard_map.122 = bf16[256,1024]{1,0:T(8,128)(2,1)} custom-call(s32[2]{0:T(128)S(1)} %pad_add_fusion.place_ref, bf16[512,256]{1,0:T(8,128)(2,1)S(1)} %bitcast.40, bf16[128,1024]{1,0:T(8,128)(2,1)S(1)} %bitcast.39, bf16[128,1024]{1,0:T(8,128)(2,1)S(1)} %collective-permute-done.8.refs_1_, bf16[128,1024]{1,0:T(8,128)(2,1)S(1)} %collective-permute-done.9.refs_2_, ...), custom_call_target="tpu_custom_call" | custom-call | flops 268435456 | bytes 1835008 | tf_op jit(solution)/shard_map/pallas_call | solution.py:70
  47.0 5.3 %all-to-all-start.1 = ((bf16[8,32,1024]{2,1,0:T(8,128)(2,1)}), bf16[8,32,1024]{2,1,0:T(8,128)(2,1)}, u32[]{:S(2)}, u32[]{:S(2)}) async-start(bf16[8,32,1024]{2,1,0:T(8,128)(2,1)} %bitcast.14), calls=%async_computation.1 | async-start | bytes 1048576 | tf_op jit(solution)/shard_map/all_to_all | solution.py:256
  52.3 0.0 copy-start.22
  52.4 2.1 %collective-permute-start.4 = (bf16[128,1024]{1,0:T(8,128)(2,1)S(1)}, bf16[128,1024]{1,0:T(8,128)(2,1)}, u32[]{:S(2)}, u32[]{:S(2)}) collective-permute-start(bf16[128,1024]{1,0:T(8,128)(2,1)S(1)} %bitcast.23), channel_id=1, source_target_pairs={{8,0},{12,4},{16,8},{20,12},{24,16},{28,20},{9,1},{13,5},{17,9},{2... | collective-permute-start | bytes 786440 | tf_op jit(solution)/shard_map/ppermute | solution.py:208
  54.4 11.2 %all-to-all-done.1 = bf16[8,32,1024]{2,1,0:T(8,128)(2,1)} async-done(((bf16[8,32,1024]{2,1,0:T(8,128)(2,1)}), bf16[8,32,1024]{2,1,0:T(8,128)(2,1)}, u32[]{:S(2)}, u32[]{:S(2)}) %all-to-all-start.1) | async-done | bytes 524320 | tf_op jit(solution)/shard_map/all_to_all | solution.py:256
  65.6 1.1 %shard_map.123 = bf16[256,1024]{1,0:T(8,128)(2,1)S(1)} custom-call(bf16[256,1024]{1,0:T(8,128)(2,1)} %bitcast.15.parts), custom_call_target="tpu_custom_call" | custom-call | flops 262144 | bytes 1048576 | tf_op jit(solution)/shard_map/pallas_call | solution.py:70
  66.7 0.0 copy-start.11
  66.7 0.8 copy-done.11
  67.5 6.8 %all-to-all-start.2 = ((bf16[8,32,1024]{2,1,0:T(8,128)(2,1)}), bf16[8,32,1024]{2,1,0:T(8,128)(2,1)}, u32[]{:S(2)}, u32[]{:S(2)}) async-start(bf16[8,32,1024]{2,1,0:T(8,128)(2,1)} %bitcast.34), calls=%async_computation.2 | async-start | bytes 1048576 | tf_op jit(solution)/shard_map/all_to_all | solution.py:258
  74.3 2.0 %collective-permute-start.6 = (bf16[128,1024]{1,0:T(8,128)(2,1)}, bf16[128,1024]{1,0:T(8,128)(2,1)}, u32[]{:S(2)}, u32[]{:S(2)}) collective-permute-start(bf16[128,1024]{1,0:T(8,128)(2,1)} %copy-done.8), channel_id=1, source_target_pairs={{8,0},{12,4},{16,8},{20,12},{24,16},{28,20},{9,1},{13,5},{17,9},{2... | collective-permute-start | bytes 786440 | tf_op jit(solution)/shard_map/ppermute | solution.py:208
  76.4 1.0 broadcast_select_fusion.1
  77.4 1.0 collective-permute-start.5
  78.4 12.7 %collective-permute-done.6.g2 = bf16[128,1024]{1,0:T(8,128)(2,1)} collective-permute-done((bf16[128,1024]{1,0:T(8,128)(2,1)}, bf16[128,1024]{1,0:T(8,128)(2,1)}, u32[]{:S(2)}, u32[]{:S(2)}) %collective-permute-start.6) | collective-permute-done | bytes 262176 | tf_op jit(solution)/shard_map/ppermute | solution.py:208
  91.1 1.0 broadcast_select_fusion
  92.1 1.5 %collective-permute-start.7 = (bf16[128,1024]{1,0:T(8,128)(2,1)S(1)}, bf16[128,1024]{1,0:T(8,128)(2,1)S(1)}, u32[]{:S(2)}, u32[]{:S(2)}) collective-permute-start(bf16[128,1024]{1,0:T(8,128)(2,1)S(1)} %broadcast_select_fusion), channel_id=1, source_target_pairs={{0,4},{4,0},{8,12},{12,8},{16,20},{20,16},{24,28},{28,24},{1,5},{5... | collective-permute-start | bytes 786440 | tf_op jit(solution)/shard_map/ppermute | solution.py:211
  93.7 0.9 copy-done.9
  94.6 0.9 copy-done.13
  95.6 0.9 copy-done.15
  96.5 0.9 copy-done.20
  97.5 4.6 %shard_map.120 = (bf16[128,1024]{1,0:T(8,128)(2,1)}, bf16[128,1024]{1,0:T(8,128)(2,1)}) custom-call(s32[1,4]{1,0:T(1,128)S(1)} %copy-done.22, s32[2]{0:T(128)S(1)} %pad_add_fusion.place_ref, bf16[128,1024]{1,0:T(8,128)(2,1)S(1)} %bitcast.24, bf16[128,1024]{1,0:T(8,128)(2,1)S(1)} %bitcast.28, bf16[128,1024]{1,0:T(8,128)(2,1)S(1)} %copy-done.13, ...), custom_call_target="tpu_custom_call" | custom-call | flops 570425344 | bytes 4980736 | tf_op jit(solution)/shard_map/pallas_call | solution.py:70
  102.1 5.4 %shard_map.121 = (bf16[128,1024]{1,0:T(8,128)(2,1)}, bf16[128,1024]{1,0:T(8,128)(2,1)}) custom-call(s32[1,4]{1,0:T(1,128)S(1)} %copy-done.22, s32[2]{0:T(128)S(1)} %pad_add_fusion.place_ref, bf16[128,1024]{1,0:T(8,128)(2,1)S(1)} %bitcast.29, bf16[128,1024]{1,0:T(8,128)(2,1)S(1)} %bitcast.33, bf16[128,1024]{1,0:T(8,128)(2,1)S(1)} %bitcast.25, ...), custom_call_target="tpu_custom_call" | custom-call | flops 402653184 | bytes 2621440 | tf_op jit(solution)/shard_map/pallas_call | solution.py:70
  107.6 2.1 %shard_map.124 = f32[256,1024]{1,0:T(8,128)} custom-call(bf16[256,1024]{1,0:T(8,128)(2,1)} %bitcast.17.parts), custom_call_target="tpu_custom_call" | custom-call | flops 262144 | bytes 1572864 | tf_op jit(solution)/shard_map/pallas_call | solution.py:70
  (38 shorter events, 0.1 us)
Async XLA Ops:
  0.6 11.3 %collective-permute-start = (bf16[128,1024]{1,0:T(8,128)(2,1)}, bf16[128,1024]{1,0:T(8,128)(2,1)S(1)}, u32[]{:S(2)}, u32[]{:S(2)}) collective-permute-start(bf16[128,1024]{1,0:T(8,128)(2,1)} %bitcast.26), channel_id=1, source_target_pairs={{0,8},{4,12},{8,16},{12,20},{16,24},{20,28},{1,9},{5,13},{9,17},{1... | collective-permute-start | bytes 786440 | tf_op jit(solution)/shard_map/ppermute | solution.py:208
  4.1 12.3 %collective-permute-start.2 = (bf16[128,1024]{1,0:T(8,128)(2,1)}, bf16[128,1024]{1,0:T(8,128)(2,1)S(1)}, u32[]{:S(2)}, u32[]{:S(2)}) collective-permute-start(bf16[128,1024]{1,0:T(8,128)(2,1)} %bitcast.30), channel_id=1, source_target_pairs={{0,8},{4,12},{8,16},{12,20},{16,24},{20,28},{1,9},{5,13},{9,17},{1... | collective-permute-start | bytes 786440 | tf_op jit(solution)/shard_map/ppermute | solution.py:208
  12.9 16.6 %copy-start.18 = (bf16[1,128,1024]{2,1,0:T(8,128)(2,1)S(1)}, bf16[1,128,1024]{2,1,0:T(8,128)(2,1)}, u32[]{:S(2)}) copy-start(bf16[1,128,1024]{2,1,0:T(8,128)(2,1)} %param.10) | copy-start | bytes 786436
  12.9 16.6 %collective-permute-start.1 = (bf16[128,1024]{1,0:T(8,128)(2,1)S(1)}, bf16[128,1024]{1,0:T(8,128)(2,1)S(1)}, u32[]{:S(2)}, u32[]{:S(2)}) collective-permute-start(bf16[128,1024]{1,0:T(8,128)(2,1)S(1)} %broadcast_select_fusion.3), channel_id=1, source_target_pairs={{0,4},{4,0},{8,12},{12,8},{16,20},{20,16},{24,28},{28,24},{1,5},{5... | collective-permute-start | bytes 786440 | tf_op jit(solution)/shard_map/ppermute | solution.py:211
  17.4 12.1 %collective-permute-start.3 = (bf16[128,1024]{1,0:T(8,128)(2,1)S(1)}, bf16[128,1024]{1,0:T(8,128)(2,1)S(1)}, u32[]{:S(2)}, u32[]{:S(2)}) collective-permute-start(bf16[128,1024]{1,0:T(8,128)(2,1)S(1)} %broadcast_select_fusion.2), channel_id=1, source_target_pairs={{0,4},{4,0},{8,12},{12,8},{16,20},{20,16},{24,28},{28,24},{1,5},{5... | collective-permute-start | bytes 786440 | tf_op jit(solution)/shard_map/ppermute | solution.py:211
  18.9 20.0 %collective-permute-start.8 = (bf16[128,1024]{1,0:T(8,128)(2,1)}, bf16[128,1024]{1,0:T(8,128)(2,1)S(1)}, u32[]{:S(2)}, u32[]{:S(2)}) collective-permute-start(bf16[128,1024]{1,0:T(8,128)(2,1)} %bitcast.35), channel_id=1, source_target_pairs={{0,1},{1,0},{2,3},{3,2},{4,5},{5,4},{6,7},{7,6},{8,9},{9,8},{10,11... | collective-permute-start | bytes 786440 | tf_op jit(solution)/shard_map/ppermute | solution.py:233
  18.9 20.0 %collective-permute-start.9 = (bf16[128,1024]{1,0:T(8,128)(2,1)}, bf16[128,1024]{1,0:T(8,128)(2,1)S(1)}, u32[]{:S(2)}, u32[]{:S(2)}) collective-permute-start(bf16[128,1024]{1,0:T(8,128)(2,1)} %bitcast.36), channel_id=1, source_target_pairs={{0,2},{1,3},{2,0},{3,1},{4,6},{5,7},{6,4},{7,5},{8,10},{9,11},{10,... | collective-permute-start | bytes 786440 | tf_op jit(solution)/shard_map/ppermute | solution.py:233
  20.5 18.5 %collective-permute-start.10 = (bf16[128,1024]{1,0:T(8,128)(2,1)}, bf16[128,1024]{1,0:T(8,128)(2,1)S(1)}, u32[]{:S(2)}, u32[]{:S(2)}) collective-permute-start(bf16[128,1024]{1,0:T(8,128)(2,1)} %bitcast.37), channel_id=1, source_target_pairs={{0,3},{1,2},{2,1},{3,0},{4,7},{5,6},{6,5},{7,4},{8,11},{9,10},{10,... | collective-permute-start | bytes 786440 | tf_op jit(solution)/shard_map/ppermute | solution.py:233
  20.9 1.6 %copy-start = (bf16[1024,1024]{1,0:T(8,128)(2,1)S(1)}, bf16[1024,1024]{1,0:T(8,128)(2,1)}, u32[]{:S(2)}) copy-start(bf16[1024,1024]{1,0:T(8,128)(2,1)} %w.3) | copy-start | bytes 6291460
  22.5 0.9 copy-start.2
  23.4 0.9 copy-start.4
  24.4 0.9 copy-start.6
  25.3 0.9 copy-start.16
  26.3 0.7 copy-start.21
  29.5 15.5 %copy-start.17 = (bf16[1,128,1024]{2,1,0:T(8,128)(2,1)S(1)}, bf16[1,128,1024]{2,1,0:T(8,128)(2,1)}, u32[]{:S(2)}) copy-start(bf16[1,128,1024]{2,1,0:T(8,128)(2,1)} %param.11) | copy-start | bytes 786436
  29.5 17.5 %copy-start.14 = (bf16[128,1024]{1,0:T(8,128)(2,1)}, bf16[128,1024]{1,0:T(8,128)(2,1)S(1)}, u32[]{:S(2)}) copy-start(bf16[128,1024]{1,0:T(8,128)(2,1)S(1)} %collective-permute-done.3.v1) | copy-start | bytes 786436
  33.3 0.7 copy-start.8
  34.0 0.7 copy-start.12
  34.7 0.7 copy-start.19
  35.4 16.9 %copy-start.3 = (bf16[1,128,1024]{2,1,0:T(8,128)(2,1)S(1)}, bf16[1,128,1024]{2,1,0:T(8,128)(2,1)}, u32[]{:S(2)}) copy-start(bf16[1,128,1024]{2,1,0:T(8,128)(2,1)} %param.7) | copy-start | bytes 786436
  35.4 9.5 %all-to-all-start = ((bf16[4,128,256]{2,1,0:T(8,128)(2,1)}), bf16[4,128,256]{2,1,0:T(8,128)(2,1)S(1)}, u32[]{:S(2)}, u32[]{:S(2)}) async-start(bf16[4,128,256]{2,1,0:T(8,128)(2,1)} %bitcast.12), calls=%async_computation | async-start | bytes 524288 | tf_op jit(solution)/shard_map/all_to_all | solution.py:247
  47.0 18.6 %all-to-all-start.1 = ((bf16[8,32,1024]{2,1,0:T(8,128)(2,1)}), bf16[8,32,1024]{2,1,0:T(8,128)(2,1)}, u32[]{:S(2)}, u32[]{:S(2)}) async-start(bf16[8,32,1024]{2,1,0:T(8,128)(2,1)} %bitcast.14), calls=%async_computation.1 | async-start | bytes 1048576 | tf_op jit(solution)/shard_map/all_to_all | solution.py:256
  52.3 41.3 %copy-start.1 = (bf16[1024,1024]{1,0:T(8,128)(2,1)S(1)}, bf16[1024,1024]{1,0:T(8,128)(2,1)}, u32[]{:S(2)}) copy-start(bf16[1024,1024]{1,0:T(8,128)(2,1)} %w.3) | copy-start | bytes 6291460
  52.3 41.3 %copy-start.5 = (bf16[1,128,1024]{2,1,0:T(8,128)(2,1)S(1)}, bf16[1,128,1024]{2,1,0:T(8,128)(2,1)}, u32[]{:S(2)}) copy-start(bf16[1,128,1024]{2,1,0:T(8,128)(2,1)} %param.8) | copy-start | bytes 786436
  52.3 41.3 %copy-start.7 = (bf16[1,128,1024]{2,1,0:T(8,128)(2,1)S(1)}, bf16[1,128,1024]{2,1,0:T(8,128)(2,1)}, u32[]{:S(2)}) copy-start(bf16[1,128,1024]{2,1,0:T(8,128)(2,1)} %param.9) | copy-start | bytes 786436
  52.3 41.3 %copy-start.22 = (s32[1,4]{1,0:T(1,128)S(1)}, s32[1,4]{1,0:T(1,128)}, u32[]{:S(2)}) copy-start(s32[1,4]{1,0:T(1,128)} %len_ref.7) | copy-start | bytes 52
  52.4 24.0 %collective-permute-start.4 = (bf16[128,1024]{1,0:T(8,128)(2,1)S(1)}, bf16[128,1024]{1,0:T(8,128)(2,1)}, u32[]{:S(2)}, u32[]{:S(2)}) collective-permute-start(bf16[128,1024]{1,0:T(8,128)(2,1)S(1)} %bitcast.23), channel_id=1, source_target_pairs={{8,0},{12,4},{16,8},{20,12},{24,16},{28,20},{9,1},{13,5},{17,9},{2... | collective-permute-start | bytes 786440 | tf_op jit(solution)/shard_map/ppermute | solution.py:208
  66.7 0.8 copy-start.11
  67.5 40.0 %all-to-all-start.2 = ((bf16[8,32,1024]{2,1,0:T(8,128)(2,1)}), bf16[8,32,1024]{2,1,0:T(8,128)(2,1)}, u32[]{:S(2)}, u32[]{:S(2)}) async-start(bf16[8,32,1024]{2,1,0:T(8,128)(2,1)} %bitcast.34), calls=%async_computation.2 | async-start | bytes 1048576 | tf_op jit(solution)/shard_map/all_to_all | solution.py:258
  74.3 16.8 %collective-permute-start.6 = (bf16[128,1024]{1,0:T(8,128)(2,1)}, bf16[128,1024]{1,0:T(8,128)(2,1)}, u32[]{:S(2)}, u32[]{:S(2)}) collective-permute-start(bf16[128,1024]{1,0:T(8,128)(2,1)} %copy-done.8), channel_id=1, source_target_pairs={{8,0},{12,4},{16,8},{20,12},{24,16},{28,20},{9,1},{13,5},{17,9},{2... | collective-permute-start | bytes 786440 | tf_op jit(solution)/shard_map/ppermute | solution.py:208
  77.4 24.7 %collective-permute-start.5 = (bf16[128,1024]{1,0:T(8,128)(2,1)S(1)}, bf16[128,1024]{1,0:T(8,128)(2,1)S(1)}, u32[]{:S(2)}, u32[]{:S(2)}) collective-permute-start(bf16[128,1024]{1,0:T(8,128)(2,1)S(1)} %broadcast_select_fusion.1), channel_id=1, source_target_pairs={{0,4},{4,0},{8,12},{12,8},{16,20},{20,16},{24,28},{28,24},{1,5},{5... | collective-permute-start | bytes 786440 | tf_op jit(solution)/shard_map/ppermute | solution.py:211
  92.1 10.0 %collective-permute-start.7 = (bf16[128,1024]{1,0:T(8,128)(2,1)S(1)}, bf16[128,1024]{1,0:T(8,128)(2,1)S(1)}, u32[]{:S(2)}, u32[]{:S(2)}) collective-permute-start(bf16[128,1024]{1,0:T(8,128)(2,1)S(1)} %broadcast_select_fusion), channel_id=1, source_target_pairs={{0,4},{4,0},{8,12},{12,8},{16,20},{20,16},{24,28},{28,24},{1,5},{5... | collective-permute-start | bytes 786440 | tf_op jit(solution)/shard_map/ppermute | solution.py:211
  93.7 1.0 copy-start.9
  94.6 0.9 copy-start.13
  95.6 0.9 copy-start.15
  96.5 0.9 copy-start.20
  97.5 4.7 %copy-start.10 = (bf16[128,1024]{1,0:T(8,128)(2,1)S(1)}, bf16[128,1024]{1,0:T(8,128)(2,1)}, u32[]{:S(2)}) copy-start(bf16[128,1024]{1,0:T(8,128)(2,1)} %copy-done.8) | copy-start | bytes 786436

commit v3 on v1

v3 whole, which is shorter than its diff:
```python
import functools

import jax
import jax.numpy as jnp
from jax import lax
from jax.experimental import pallas as pl
from jax.experimental.pallas import tpu as pltpu
from jax.sharding import PartitionSpec as P

HEADS = 8
WINDOW = 256
REACH = 2

VMEM = pl.BlockSpec(memory_space=pltpu.VMEM)
SMEM = pl.BlockSpec(memory_space=pltpu.SMEM)
F32 = jnp.float32
BF16 = jnp.bfloat16
NT = (((1,), (1,)), ((), ()))
TN = (((0,), (0,)), ((), ()))


def dot(a, b):
    return jnp.dot(a, b, preferred_element_type=F32)


def dot_nt(a, b):
    return lax.dot_general(a, b, NT, preferred_element_type=F32)


def dot_tn(a, b):
    return lax.dot_general(a, b, TN, preferred_element_type=F32)


def logistic(scores):
    return 0.5 * jnp.tanh(0.5 * scores) + 0.5


def silu_slope(scores, gate):
    return gate * (1.0 + scores * (1.0 - gate))


def start_of(positions, len_ref):
    total = jnp.zeros_like(positions)
    end = jnp.int32(0)
    for k in range(len_ref.shape[1]):
        length = len_ref[0, k]
        end = end + length
        total = total + jnp.where(positions >= end, length, 0)
    return total


def allowed_block(rows, first_query, first_key, len_ref, query_dim):
    shape = (rows, rows)
    query_pos = first_query + lax.broadcasted_iota(jnp.int32, shape, query_dim)
    key_pos = first_key + lax.broadcasted_iota(jnp.int32, shape, 1 - query_dim)
    start = start_of(query_pos, len_ref)
    return (key_pos >= start) & (key_pos <= query_pos) & (key_pos > query_pos - WINDOW)


def head_slice(h, width):
    return slice(h * width, (h + 1) * width)


def cost(flops, arrays):
    total = sum(a.size * a.dtype.itemsize for a in arrays)
    return pl.CostEstimate(flops=flops, bytes_accessed=total, transcendentals=0)


def call(kernel, outs, scalars, arrays, flops, scratch=(), spaces=None):
    spaces = spaces or [VMEM] * len(arrays)
    return pl.pallas_call(
        kernel,
        out_shape=outs,
        in_specs=[SMEM] * len(scalars) + spaces,
        out_specs=[VMEM] * len(outs),
        scratch_shapes=list(scratch),
        cost_estimate=cost(flops, list(arrays) + list(outs)),
        compiler_params=pltpu.CompilerParams(vmem_limit_bytes=40 * 1024 * 1024),
    )(*scalars, *arrays)


def own_kernel(
    len_ref, place_ref, q_in, k_in, v_in, grad_in, w_in, q, k, v, grad, w, mixed, grad_hidden, slope, sems
):
    moves = [
        pltpu.make_async_copy(src, dst, sems.at[i])
        for i, (src, dst) in enumerate(
            ((q_in, q), (k_in, k), (v_in, v), (grad_in, grad), (w_in, w))
        )
    ]
    for move in moves:
        move.start()
    rows, width = q.shape
    size = width // HEADS
    scale = size ** (-0.5)
    first = place_ref[0] * rows
    allowed = allowed_block(rows, first, first, len_ref, 0)
    for move in moves[:3]:
        move.wait()
    for h in range(HEADS):
        cols = head_slice(h, size)
        scores = dot_nt(q[:, cols], k[:, cols]) * scale
        gate = logistic(scores)
        attention = jnp.where(allowed, scores * gate, 0.0).astype(BF16)
        slope[:, cols] = jnp.where(allowed, silu_slope(scores, gate) * scale, 0.0)
        mixed[:, cols] = dot(attention, v[:, cols])
    for move in moves[3:]:
        move.wait()
    grad_hidden[...] = dot_nt(grad[...], w[...])


def far_kernel(len_ref, place_ref, q, k1, k2, attention1, attention2, slope1, slope2):
    rows, width = q.shape
    size = width // HEADS
    scale = size ** (-0.5)
    first = place_ref[0] * rows
    parts = ((k1, attention1, slope1), (k2, attention2, slope2))
    for d, (keys, attention, slope) in enumerate(parts):
        allowed = allowed_block(rows, first, first - (d + 1) * rows, len_ref, 0)
        for h in range(HEADS):
            cols = head_slice(h, size)
            scores = dot_nt(q[:, cols], keys[:, cols]) * scale
            gate = logistic(scores)
            attention[:, cols] = jnp.where(allowed, scores * gate, 0.0).astype(BF16)
            slope[:, cols] = jnp.where(allowed, silu_slope(scores, gate) * scale, 0.0)


def forward_kernel(
    groups, place_ref, attention1, attention2, v1, v2, mixed_own, grad_hidden, gates, *rest
):
    hidden, grad_gates, grad_mix = rest[:3]
    slices = rest[3 : 3 + groups]
    mixed = rest[3 + groups]
    rows, width = v1.shape
    size = width // HEADS
    for h in range(HEADS):
        cols = head_slice(h, size)
        mixed[:, cols] = (
            mixed_own[:, cols]
            + dot(attention1[:, cols], v1[:, cols])
            + dot(attention2[:, cols], v2[:, cols])
        )
    values = mixed[...]
    centered = values - jnp.mean(values, axis=1, keepdims=True)
    inv_std = lax.rsqrt(jnp.mean(centered * centered, axis=1, keepdims=True) + 1e-05)
    normed = centered * inv_std
    gate = gates[...].astype(F32)
    hidden[...] = (normed * gate).astype(BF16)
    part = width // groups
    for d, ref in enumerate(slices):
        at = pl.multiple_of((place_ref[1] ^ d) * part, 128)
        ref[...] = hidden[:, pl.ds(at, part)]
    gh = grad_hidden[...]
    grad_gates[...] = (gh * normed).astype(BF16)
    grad_norm = gh * gate
    grad_mix[...] = (
        (
            grad_norm
            - jnp.mean(grad_norm, axis=1, keepdims=True)
            - normed * jnp.mean(grad_norm * normed, axis=1, keepdims=True)
        )
        * inv_std
    ).astype(BF16)


def query_kernel(k0, k1, k2, v0, v1, v2, slope0, slope1, slope2, grad_mix, hidden, w, output, grad_queries):
    rows, width = k0.shape
    size = width // HEADS
    output[...] = dot(hidden[...], w[...]).astype(BF16)
    parts = ((k0, v0, slope0), (k1, v1, slope1), (k2, v2, slope2))
    for h in range(HEADS):
        cols = head_slice(h, size)
        total = jnp.zeros((rows, size), F32)
        for keys, vals, slope in parts:
            grad_attention = dot_nt(grad_mix[:, cols], vals[:, cols])
            grad_scores = (grad_attention * slope[:, cols]).astype(BF16)
            total = total + dot(grad_scores, keys[:, cols])
        grad_queries[:, cols] = total.astype(BF16)


def key_kernel(len_ref, place_ref, k, v, q0, q1, q2, g0, g1, g2, grad_keys, grad_values):
    rows, width = k.shape
    size = width // HEADS
    scale = size ** (-0.5)
    first = place_ref[0] * rows
    masks = [allowed_block(rows, first + d * rows, first, len_ref, 1) for d in range(REACH + 1)]
    for h in range(HEADS):
        cols = head_slice(h, size)
        keys_total = jnp.zeros((rows, size), F32)
        values_total = jnp.zeros((rows, size), F32)
        for mask, qd, gd in zip(masks, (q0, q1, q2), (g0, g1, g2)):
            scores = dot_nt(k[:, cols], qd[:, cols]) * scale
            gate = logistic(scores)
            attention = jnp.where(mask, scores * gate, 0.0).astype(BF16)
            grad_attention = dot_nt(v[:, cols], gd[:, cols])
            slope = jnp.where(mask, silu_slope(scores, gate) * scale, 0.0)
            grad_scores = (grad_attention * slope).astype(BF16)
            keys_total = keys_total + dot(grad_scores, qd[:, cols])
            values_total = values_total + dot(attention, gd[:, cols])
        grad_keys[:, cols] = keys_total.astype(BF16)
        grad_values[:, cols] = values_total.astype(BF16)


def weight_kernel(groups, place_ref, *refs):
    hidden = jnp.concatenate([ref[...] for ref in refs[:groups]], axis=0)
    grads = jnp.concatenate([ref[...] for ref in refs[groups : 2 * groups]], axis=0)
    own = refs[2 * groups]
    sends = refs[2 * groups + 1 : -1]
    total = refs[-1]
    total[...] = dot_tn(hidden, grads)
    if not sends:
        own[...] = total[...]
        return
    rows = own.shape[0]
    corner = place_ref[0] & len(sends)
    own[...] = total[pl.ds(pl.multiple_of(corner * rows, rows), rows), :]
    for e, ref in enumerate(sends):
        at = pl.multiple_of((corner ^ (e + 1)) * rows, rows)
        ref[...] = total[pl.ds(at, rows), :].astype(BF16)


def corner_kernel(corners, place_ref, own, *refs):
    got, (keep, send, total) = refs[:-3], refs[-3:]
    acc = own[...]
    for ref in got:
        acc = acc + ref[...].astype(F32)
    total[...] = acc
    rows = keep.shape[0]
    side = place_ref[0] // corners
    keep[...] = total[pl.ds(pl.multiple_of(side * rows, rows), rows), :]
    send[...] = total[pl.ds(pl.multiple_of((1 - side) * rows, rows), rows), :].astype(BF16)


def piece_kernel(scale, keep, got, piece):
    piece[...] = ((keep[...] + got[...].astype(F32)) * scale).astype(BF16)


def pair_kernel(corners, place_ref, mine, other, both):
    rows = mine.shape[0]
    side = place_ref[0] // corners
    both[pl.ds(pl.multiple_of(side * rows, rows), rows), :] = mine[...]
    both[pl.ds(pl.multiple_of((1 - side) * rows, rows), rows), :] = other[...]


def place_kernel(corners, place_ref, *refs):
    out = refs[-1]
    rows = refs[0].shape[0]
    corner = place_ref[0] & (corners - 1)
    for e, ref in enumerate(refs[:-1]):
        at = pl.multiple_of((corner ^ e) * rows, rows)
        out[pl.ds(at, rows), :] = ref[...].astype(F32)


def xor_route(size, mask):
    return [(i, i ^ mask) for i in range(size)]


def shifted(block, distance):
    count = lax.axis_size("seq")
    route = [(i, i + distance) for i in range(count) if 0 <= i + distance < count]
    return lax.ppermute(block, "seq", route)


def swapped(block, axis, mask):
    return lax.ppermute(block, axis, xor_route(lax.axis_size(axis), mask))


def after(value, *others):
    return lax.optimization_barrier((value, *others))[0]


def on_device(queries, keys, values, gates, out_grad, w_out, hist_lengths):
    rows, width = queries.shape[1:]
    seq = lax.axis_size("seq")
    batch = lax.axis_size("batch")
    seq_at = lax.axis_index("seq")
    place = jnp.stack([seq_at, lax.axis_index("batch")]).astype(jnp.int32)
    scalars = (hist_lengths, place)
    even = (seq_at & 1) == 0
    full = jax.ShapeDtypeStruct((rows, width), BF16)
    wide = jax.ShapeDtypeStruct((rows, width), F32)
    block_flops = 2 * rows * rows * width
    proj_flops = 2 * rows * width * width

    k2 = shifted(keys[0], 2)
    v2 = shifted(values[0], 2)
    v1 = shifted(values[0], 1)
    q, k, v, grad, w, mixed_own, grad_hidden, slope0 = call(
        own_kernel,
        [full, full, full, full, jax.ShapeDtypeStruct(w_out.shape, BF16), wide, wide, wide],
        scalars,
        (queries[0], keys[0], values[0], out_grad[0], w_out),
        proj_flops + 2 * block_flops,
        [pltpu.SemaphoreType.DMA((5,))],
        [pl.BlockSpec(memory_space=pltpu.HBM)] * 5,
    )
    k1 = swapped(jnp.where(even, k, k2), "seq", 1)
    grads = [grad] + [swapped(grad, "batch", d) for d in range(1, batch)]
    q2 = shifted(q, -2)
    attention1, attention2, slope1, slope2 = call(
        far_kernel, [full, full, wide, wide], scalars, (q, k1, k2), 2 * block_flops
    )
    q1 = swapped(jnp.where(even, q2, q), "seq", 1)
    part = width // batch
    piece = jax.ShapeDtypeStruct((rows, part), BF16)
    hidden, grad_gates, grad_mix, *slices = call(
        functools.partial(forward_kernel, batch),
        [full, full, full] + [piece] * batch,
        (place,),
        (attention1, attention2, v1, v2, mixed_own, grad_hidden, gates[0]),
        2 * block_flops,
        [pltpu.VMEM((rows, width), F32)],
    )
    hiddens = [slices[0]] + [swapped(slices[d], "batch", d) for d in range(1, batch)]
    g2 = shifted(grad_mix, -2)
    g1 = swapped(jnp.where(even, g2, grad_mix), "seq", 1)

    corners = 4
    direct = seq == 2 * corners
    rows_w = part // corners if direct else part
    scale = (rows * seq * batch) ** (-0.5)
    own, *sends = call(
        functools.partial(weight_kernel, batch),
        [jax.ShapeDtypeStruct((rows_w, width), F32)]
        + ([jax.ShapeDtypeStruct((rows_w, width), BF16)] * (corners - 1) if direct else []),
        (place,),
        (*hiddens, *grads),
        proj_flops,
        [pltpu.VMEM((part, width), F32)],
    )
    output, grad_queries = call(
        query_kernel,
        [full, full],
        (),
        (k, k1, k2, v, v1, v2, slope0, slope1, slope2, grad_mix, after(hidden, own), w),
        proj_flops + 6 * block_flops,
    )
    if direct:
        half = jax.ShapeDtypeStruct((rows_w // 2, width), BF16)
        half_wide = jax.ShapeDtypeStruct((rows_w // 2, width), F32)
        got = [swapped(s, "seq", e + 1) for e, s in enumerate(sends)]
        keep, send = call(
            functools.partial(corner_kernel, corners),
            [half_wide, half],
            (place,),
            (own, *got),
            own.size * 4,
            [pltpu.VMEM((rows_w, width), F32)],
        )
        (mine,) = call(
            functools.partial(piece_kernel, scale),
            [half],
            (),
            (keep, swapped(send, "seq", corners)),
            own.size,
        )
        (both,) = call(
            functools.partial(pair_kernel, corners),
            [jax.ShapeDtypeStruct((rows_w, width), BF16)],
            (place,),
            (mine, swapped(mine, "seq", corners)),
            own.size,
        )
        shares = [both] + [swapped(both, "seq", e) for e in range(1, corners)]
        (grad_weight,) = call(
            functools.partial(place_kernel, corners),
            [jax.ShapeDtypeStruct((part, width), F32)],
            (place,),
            tuple(shares),
            part * width,
        )
        v_late = after(v, mine)
    else:
        grad_weight = lax.psum(own, "seq") * scale
        v_late = v
    grad_keys, grad_values = call(
        key_kernel, [full, full], scalars, (k, v_late, q, q1, q2, grad_mix, g1, g2), 12 * block_flops
    )
    return (
        output[None],
        grad_queries[None],
        grad_keys[None],
        grad_values[None],
        grad_gates[None],
        grad_weight,
    )


def solution(mesh):
    token = P("batch", "seq", None)
    return jax.shard_map(
        on_device,
        mesh=mesh,
        in_specs=(token, token, token, token, token, P(), P("batch", None)),
        out_specs=(token, token, token, token, token, P("batch", None)),
        check_vma=False,
    )
```

time: 101 us -> 81.6 us (0.81)
  starting transfers between devices: 45.4 us -> 30 us
  waiting for transfers between devices: 21.4 us -> 26.3 us
  local copies, waits for them, and re-layouts: 10.1 us -> 6.05 us
  other arithmetic: 3.06 us -> 0.17 us
  Pallas kernels: 20 us -> 17.9 us
    ppermute x28 -> x22, starting transfers between devices: 45.4 us -> 30 us  [the longest x17 15.6 us: swapped(): return lax.ppermute(block, axis, xor_route(lax.axis_size(axis), mask))]
    ppermute x28 -> x22, waiting for transfers between devices: 21.4 us -> 26.3 us  [the longest x17 26.3 us: swapped(): return lax.ppermute(block, axis, xor_route(lax.axis_size(axis), mask))]
    unnamed x42 -> x14, local copies, waits for them, and re-layouts: 10.1 us -> 6.05 us
    select_n x4 -> x3, other arithmetic: 2.98 us -> 0.1 us  [the longest x1 0.04 us: on_device(): k1 = swapped(jnp.where(even, k, k2), 'seq', 1)]
    pallas_call x7 -> x10, Pallas kernels: 20 us -> 17.9 us  [call(): pl.pallas_call(kernel, out_shape=outs, in_specs=[SMEM] * len(scalars) + s...]
  transfers between devices with their start and end apart: 28 -> 22, of which waited for: 8 -> 12; matrix products, arithmetic and copies ran while one was open for 3% -> 0% of each run, Pallas kernels for 14% -> 16%
where the time goes in v3:
time: 81.6 us; the launch traced here: 81.3 us
  starting transfers between devices  30 us (37%)
  waiting for transfers between devices  26.3 us (32%)
  Pallas kernels  17.9 us (22%)
  local copies, waits for them, and re-layouts  6.05 us (7%)
    ppermute x17, waiting for transfers between devices, swapped(): return lax.ppermute(block, axis, xor_route(lax.axis_size(axis), mask))  26.3 us
    pallas_call x10, Pallas kernels, call(): pl.pallas_call(kernel, out_shape=outs, in_specs=[SMEM] * len(scalars) + s...  17.9 us
    ppermute x17, starting transfers between devices, swapped(): return lax.ppermute(block, axis, xor_route(lax.axis_size(axis), mask))  15.6 us
    ppermute x5, starting transfers between devices, shifted(): return lax.ppermute(block, 'seq', route)  14.4 us
    unnamed x14, local copies, waits for them, and re-layouts  6.05 us
  transfers between devices with their start and end apart: 22, of which 12 were waited for; matrix products, arithmetic and copies ran while one was open for 0% of the time, Pallas kernels for 16%

profile of v3, /device:TPU:0, one launch (start us, length us, event | category | flops | bytes accessed | tf_op | source)
XLA Modules:
  0.0 81.3 jit_solution(11216006557260052150)
XLA Ops:
  0.6 4.9 %collective-permute-start = (bf16[128,1024]{1,0:T(8,128)(2,1)}, bf16[128,1024]{1,0:T(8,128)(2,1)S(1)}, u32[]{:S(2)}, u32[]{:S(2)}) collective-permute-start(bf16[128,1024]{1,0:T(8,128)(2,1)} %bitcast.14), channel_id=1, source_target_pairs={{0,8},{4,12},{8,16},{12,20},{16,24},{20,28},{1,9},{5,13},{9,17},{1... | collective-permute-start | bytes 786440 | tf_op jit(solution)/shard_map/ppermute | solution.py:261
  5.6 3.4 %collective-permute-start.2 = (bf16[128,1024]{1,0:T(8,128)(2,1)}, bf16[128,1024]{1,0:T(8,128)(2,1)S(1)}, u32[]{:S(2)}, u32[]{:S(2)}) collective-permute-start(bf16[128,1024]{1,0:T(8,128)(2,1)} %bitcast.16), channel_id=1, source_target_pairs={{0,4},{4,8},{8,12},{12,16},{16,20},{20,24},{24,28},{1,5},{5,9},{9,... | collective-permute-start | bytes 786440 | tf_op jit(solution)/shard_map/ppermute | solution.py:261
  9.0 0.1 pad_add_fusion.place_ref
  9.1 1.6 %copy-done = bf16[1024,1024]{1,0:T(8,128)(2,1)S(1)} copy-done((bf16[1024,1024]{1,0:T(8,128)(2,1)S(1)}, bf16[1024,1024]{1,0:T(8,128)(2,1)}, u32[]{:S(2)}) %copy-start) | copy-done | bytes 2097176
  10.7 0.9 %copy-done.1 = bf16[1,128,1024]{2,1,0:T(8,128)(2,1)S(1)} copy-done((bf16[1,128,1024]{2,1,0:T(8,128)(2,1)S(1)}, bf16[1,128,1024]{2,1,0:T(8,128)(2,1)}, u32[]{:S(2)}) %copy-start.1) | copy-done | bytes 262168
  11.6 0.9 %copy-done.2 = bf16[1,128,1024]{2,1,0:T(8,128)(2,1)S(1)} copy-done((bf16[1,128,1024]{2,1,0:T(8,128)(2,1)S(1)}, bf16[1,128,1024]{2,1,0:T(8,128)(2,1)}, u32[]{:S(2)}) %copy-start.2) | copy-done | bytes 262168
  12.6 0.9 %copy-done.3 = bf16[1,128,1024]{2,1,0:T(8,128)(2,1)S(1)} copy-done((bf16[1,128,1024]{2,1,0:T(8,128)(2,1)S(1)}, bf16[1,128,1024]{2,1,0:T(8,128)(2,1)}, u32[]{:S(2)}) %copy-start.3) | copy-done | bytes 262168
  13.5 0.9 %copy-done.4 = bf16[1,128,1024]{2,1,0:T(8,128)(2,1)S(1)} copy-done((bf16[1,128,1024]{2,1,0:T(8,128)(2,1)S(1)}, bf16[1,128,1024]{2,1,0:T(8,128)(2,1)}, u32[]{:S(2)}) %copy-start.4) | copy-done | bytes 262168
  14.5 0.7 copy-done.6
  15.1 3.1 %shard_map.118 = (bf16[128,1024]{1,0:T(8,128)(2,1)S(1)}, bf16[128,1024]{1,0:T(8,128)(2,1)S(1)}, bf16[128,1024]{1,0:T(8,128)(2,1)S(1)}, bf16[128,1024]{1,0:T(8,12...) custom-call(s32[1,4]{1,0:T(1,128)S(1)} %copy-done.6, ...), custom_call_target="tpu_custom_call" | custom-call | flops 335544320 | bytes 7864320 | tf_op jit(solution)/shard_map/pallas_call | solution.py:71
  18.3 1.6 %collective-permute-start.1 = (bf16[128,1024]{1,0:T(8,128)(2,1)S(1)}, bf16[128,1024]{1,0:T(8,128)(2,1)S(1)}, u32[]{:S(2)}, u32[]{:S(2)}) collective-permute-start(bf16[128,1024]{1,0:T(8,128)(2,1)S(1)} %broadcast_select_fusion.2), channel_id=1, source_target_pairs={{0,4},{4,0},{8,12},{12,8},{16,20},{20,16},{24,28},{28,24},{1,5},{5... | collective-permute-start | bytes 786440 | tf_op jit(solution)/shard_map/ppermute | solution.py:265
  19.9 3.5 %collective-permute-start.3 = (bf16[128,1024]{1,0:T(8,128)(2,1)S(1)}, bf16[128,1024]{1,0:T(8,128)(2,1)S(1)}, u32[]{:S(2)}, u32[]{:S(2)}) collective-permute-start(bf16[128,1024]{1,0:T(8,128)(2,1)S(1)} %bitcast.18), channel_id=1, source_target_pairs={{0,8},{4,12},{8,16},{12,20},{16,24},{20,28},{1,9},{5,13},{9,17},{1... | collective-permute-start | bytes 786440 | tf_op jit(solution)/shard_map/ppermute | solution.py:261
  23.4 0.1 collective-permute-start.7
  23.5 1.6 %collective-permute-start.8 = (bf16[128,1024]{1,0:T(8,128)(2,1)S(1)}, bf16[128,1024]{1,0:T(8,128)(2,1)S(1)}, u32[]{:S(2)}, u32[]{:S(2)}) collective-permute-start(bf16[128,1024]{1,0:T(8,128)(2,1)S(1)} %get-tuple-element.53.refs_4_), channel_id=1, source_target_pairs={{0,2},{1,3},{2,0},{3,1},{4,6},{5,7},{6,4},{7,5},{8,10},{9,11},{10,... | collective-permute-start | bytes 786440 | tf_op jit(solution)/shard_map/ppermute | solution.py:265
  25.1 0.3 collective-permute-start.9
  25.3 0.5 collective-permute-done.1.k1
  25.9 1.3 %collective-permute-start.14 = (bf16[128,1024]{1,0:T(8,128)(2,1)S(1)}, bf16[128,1024]{1,0:T(8,128)(2,1)S(1)}, u32[]{:S(2)}, u32[]{:S(2)}) collective-permute-start(bf16[128,1024]{1,0:T(8,128)(2,1)S(1)} %get-tuple-element.40.q.q0), channel_id=1, source_target_pairs={{8,0},{12,4},{16,8},{20,12},{24,16},{28,20},{9,1},{13,5},{17,9},{2... | collective-permute-start | bytes 786440 | tf_op jit(solution)/shard_map/ppermute | solution.py:261
  27.2 1.4 %shard_map.119 = (bf16[128,1024]{1,0:T(8,128)(2,1)S(1)}, bf16[128,1024]{1,0:T(8,128)(2,1)S(1)}, f32[128,1024]{1,0:T(8,128)S(1)}, f32[128,1024]{1,0:T(8,128)S(1)}) custom-call(s32[1,4]{1,0:T(1,128)S(1)} %copy-done.6, s32[2]{0:T(128)S(1)} %pad_add_fusion.place_ref, bf16[128,1024]{1,0:T(8,128)(2,1)S(1)} %get-tuple-element.40.q.q0, ...), custom_call_target="tpu_custom_call" | custom-call | flops 67108864 | bytes 2359296 | tf_op jit(solution)/shard_map/pallas_call | solution.py:71
  28.6 1.9 %shard_map.120 = (bf16[128,1024]{1,0:T(8,128)(2,1)S(1)}, bf16[128,1024]{1,0:T(8,128)(2,1)}, bf16[128,1024]{1,0:T(8,128)(2,1)S(1)}, bf16[128,256]{1,0:T(8,128)(2,...) custom-call(s32[2]{0:T(128)S(1)} %pad_add_fusion.place_ref, ...), custom_call_target="tpu_custom_call" | custom-call | flops 67108864 | bytes 3407872 | tf_op jit(solution)/shard_map/pallas_call | solution.py:71
  30.5 1.5 %collective-permute-start.5 = (bf16[128,256]{1,0:T(8,128)(2,1)S(1)}, bf16[128,256]{1,0:T(8,128)(2,1)S(1)}, u32[]{:S(2)}, u32[]{:S(2)}) collective-permute-start(bf16[128,256]{1,0:T(8,128)(2,1)S(1)} %get-tuple-element.51), channel_id=1, source_target_pairs={{0,2},{1,3},{2,0},{3,1},{4,6},{5,7},{6,4},{7,5},{8,10},{9,11},{10,... | collective-permute-start | bytes 196616 | tf_op jit(solution)/shard_map/ppermute | solution.py:265
  32.0 0.6 collective-permute-done.8.refs_6_
  32.7 0.3 collective-permute-start.6
  33.0 4.4 %collective-permute-done.9.refs_7_ = bf16[128,1024]{1,0:T(8,128)(2,1)S(1)} collective-permute-done((bf16[128,1024]{1,0:T(8,128)(2,1)S(1)}, bf16[128,1024]{1,0:T(8,128)(2,1)S(1)}, u32[]{:S(2)}, u32[]{:S(2)}) %collective-permute-start.9) | collective-permute-done | bytes 262176 | tf_op jit(solution)/shard_map/ppermute | solution.py:265
  37.4 1.3 %collective-permute-start.16 = (bf16[128,1024]{1,0:T(8,128)(2,1)S(1)}, bf16[128,1024]{1,0:T(8,128)(2,1)S(1)}, u32[]{:S(2)}, u32[]{:S(2)}) collective-permute-start(bf16[128,1024]{1,0:T(8,128)(2,1)S(1)} %get-tuple-element.47.grad_mix.g0), channel_id=1, source_target_pairs={{8,0},{12,4},{16,8},{20,12},{24,16},{28,20},{9,1},{13,5},{17,9},{2... | collective-permute-start | bytes 786440 | tf_op jit(solution)/shard_map/ppermute | solution.py:261
  38.7 1.0 %collective-permute-done.5.refs_2_ = bf16[128,256]{1,0:T(8,128)(2,1)S(1)} collective-permute-done((bf16[128,256]{1,0:T(8,128)(2,1)S(1)}, bf16[128,256]{1,0:T(8,128)(2,1)S(1)}, u32[]{:S(2)}, u32[]{:S(2)}) %collective-permute-start.5) | collective-permute-done | bytes 65568 | tf_op jit(solution)/shard_map/ppermute | solution.py:265
  39.7 0.5 collective-permute-done.6.refs_3_
  40.2 1.1 %shard_map.121 = (f32[64,1024]{1,0:T(8,128)S(1)}, bf16[64,1024]{1,0:T(8,128)(2,1)S(1)}, bf16[64,1024]{1,0:T(8,128)(2,1)S(1)}, bf16[64,1024]{1,0:T(8,128)(2,1)S(1)}) custom-call(s32[2]{0:T(128)S(1)} %pad_add_fusion.place_ref, bf16[128,256]{1,0:T(8,128)(2,1)S(1)} %get-tuple-element.49.refs_0_, bf16[128,256]{1,0:T(8,128)(2,1)S(1)} %collective-permute-done.4.refs_1_, ...), custom_call_target="tpu_custom_call" | custom-call | flops 268435456 | bytes 1966080 | tf_op jit(solution)/shard_map/pallas_call | solution.py:71
  41.2 0.5 collective-permute-start.10
  41.8 1.6 %collective-permute-start.11 = (bf16[64,1024]{1,0:T(8,128)(2,1)S(1)}, bf16[64,1024]{1,0:T(8,128)(2,1)S(1)}, u32[]{:S(2)}, u32[]{:S(2)}) collective-permute-start(bf16[64,1024]{1,0:T(8,128)(2,1)S(1)} %get-tuple-element.60), channel_id=1, source_target_pairs={{0,8},{4,12},{8,0},{12,4},{16,24},{20,28},{24,16},{28,20},{1,9},{5... | collective-permute-start | bytes 393224 | tf_op jit(solution)/shard_map/ppermute | solution.py:265
  43.4 1.4 %collective-permute-start.12 = (bf16[64,1024]{1,0:T(8,128)(2,1)S(1)}, bf16[64,1024]{1,0:T(8,128)(2,1)S(1)}, u32[]{:S(2)}, u32[]{:S(2)}) collective-permute-start(bf16[64,1024]{1,0:T(8,128)(2,1)S(1)} %get-tuple-element.61), channel_id=1, source_target_pairs={{0,12},{4,8},{8,4},{12,0},{16,28},{20,24},{24,20},{28,16},{1,13},{... | collective-permute-start | bytes 393224 | tf_op jit(solution)/shard_map/ppermute | solution.py:265
  44.8 0.5 collective-permute-start.15
  45.4 1.6 %collective-permute-done.10.refs_0_ = bf16[64,1024]{1,0:T(8,128)(2,1)S(1)} collective-permute-done((bf16[64,1024]{1,0:T(8,128)(2,1)S(1)}, bf16[64,1024]{1,0:T(8,128)(2,1)S(1)}, u32[]{:S(2)}, u32[]{:S(2)}) %collective-permute-start.10) | collective-permute-done | bytes 131104 | tf_op jit(solution)/shard_map/ppermute | solution.py:265
  47.0 4.3 %collective-permute-done.11.refs_1_ = bf16[64,1024]{1,0:T(8,128)(2,1)S(1)} collective-permute-done((bf16[64,1024]{1,0:T(8,128)(2,1)S(1)}, bf16[64,1024]{1,0:T(8,128)(2,1)S(1)}, u32[]{:S(2)}, u32[]{:S(2)}) %collective-permute-start.11) | collective-permute-done | bytes 131104 | tf_op jit(solution)/shard_map/ppermute | solution.py:265
  51.2 2.6 %collective-permute-done.12.refs_2_ = bf16[64,1024]{1,0:T(8,128)(2,1)S(1)} collective-permute-done((bf16[64,1024]{1,0:T(8,128)(2,1)S(1)}, bf16[64,1024]{1,0:T(8,128)(2,1)S(1)}, u32[]{:S(2)}, u32[]{:S(2)}) %collective-permute-start.12) | collective-permute-done | bytes 131104 | tf_op jit(solution)/shard_map/ppermute | solution.py:265
  53.8 0.6 shard_map.123
  54.5 1.1 %collective-permute-start.13 = (bf16[32,1024]{1,0:T(8,128)(2,1)S(1)}, bf16[32,1024]{1,0:T(8,128)(2,1)S(1)}, u32[]{:S(2)}, u32[]{:S(2)}) collective-permute-start(bf16[32,1024]{1,0:T(8,128)(2,1)S(1)} %get-tuple-element.63), channel_id=1, source_target_pairs={{0,16},{4,20},{8,24},{12,28},{16,0},{20,4},{24,8},{28,12},{1,17},{... | collective-permute-start | bytes 196616 | tf_op jit(solution)/shard_map/ppermute | solution.py:265
  55.6 0.6 collective-permute-start.17
  56.2 3.7 %collective-permute-done.13.got = bf16[32,1024]{1,0:T(8,128)(2,1)S(1)} collective-permute-done((bf16[32,1024]{1,0:T(8,128)(2,1)S(1)}, bf16[32,1024]{1,0:T(8,128)(2,1)S(1)}, u32[]{:S(2)}, u32[]{:S(2)}) %collective-permute-start.13) | collective-permute-done | bytes 65568 | tf_op jit(solution)/shard_map/ppermute | solution.py:265
  59.9 0.9 %collective-permute-start.18 = (bf16[32,1024]{1,0:T(8,128)(2,1)S(1)}, bf16[32,1024]{1,0:T(8,128)(2,1)S(1)}, u32[]{:S(2)}, u32[]{:S(2)}) collective-permute-start(bf16[32,1024]{1,0:T(8,128)(2,1)S(1)} %shard_map.124.mine), channel_id=1, source_target_pairs={{0,16},{4,20},{8,24},{12,28},{16,0},{20,4},{24,8},{28,12},{1,17},{... | collective-permute-start | bytes 196616 | tf_op jit(solution)/shard_map/ppermute | solution.py:265
  60.8 4.4 %collective-permute-done.18.other = bf16[32,1024]{1,0:T(8,128)(2,1)S(1)} collective-permute-done((bf16[32,1024]{1,0:T(8,128)(2,1)S(1)}, bf16[32,1024]{1,0:T(8,128)(2,1)S(1)}, u32[]{:S(2)}, u32[]{:S(2)}) %collective-permute-start.18) | collective-permute-done | bytes 65568 | tf_op jit(solution)/shard_map/ppermute | solution.py:265
  65.2 0.6 shard_map.126.refs_0_
  65.8 1.3 %collective-permute-start.19 = (bf16[64,1024]{1,0:T(8,128)(2,1)S(1)}, bf16[64,1024]{1,0:T(8,128)(2,1)S(1)}, u32[]{:S(2)}, u32[]{:S(2)}) collective-permute-start(bf16[64,1024]{1,0:T(8,128)(2,1)S(1)} %shard_map.126.refs_0_), channel_id=1, source_target_pairs={{0,4},{4,0},{8,12},{12,8},{16,20},{20,16},{24,28},{28,24},{1,5},{5... | collective-permute-start | bytes 393224 | tf_op jit(solution)/shard_map/ppermute | solution.py:265
  67.1 2.2 %collective-permute-start.21 = (bf16[64,1024]{1,0:T(8,128)(2,1)S(1)}, bf16[64,1024]{1,0:T(8,128)(2,1)S(1)}, u32[]{:S(2)}, u32[]{:S(2)}) collective-permute-start(bf16[64,1024]{1,0:T(8,128)(2,1)S(1)} %shard_map.126.refs_0_), channel_id=1, source_target_pairs={{0,12},{4,8},{8,4},{12,0},{16,28},{20,24},{24,20},{28,16},{1,13},{... | collective-permute-start | bytes 393224 | tf_op jit(solution)/shard_map/ppermute | solution.py:265
  69.4 2.7 %shard_map.122 = (bf16[128,1024]{1,0:T(8,128)(2,1)}, bf16[128,1024]{1,0:T(8,128)(2,1)}) custom-call(bf16[128,1024]{1,0:T(8,128)(2,1)S(1)} %get-tuple-element.37.k0.k, bf16[128,1024]{1,0:T(8,128)(2,1)S(1)} %collective-permute-done.1.k1, bf16[128,1024]{1,0:T(8,128)(2,1)S(1)} %collective-permute-done.k2, bf16[128,1024]{1,0:T(8,128)(2,1)S(1)} %get-tuple-element.64.v0.v, ...), custom_call_target="tpu_custom_call" | custom-call | flops 469762048 | bytes 6291456 | tf_op jit(solution)/shard_map/pallas_call | solution.py:71
  72.1 0.2 collective-permute-done.20.refs_2_
  72.2 2.5 %collective-permute-done.21.refs_3_ = bf16[64,1024]{1,0:T(8,128)(2,1)S(1)} collective-permute-done((bf16[64,1024]{1,0:T(8,128)(2,1)S(1)}, bf16[64,1024]{1,0:T(8,128)(2,1)S(1)}, u32[]{:S(2)}, u32[]{:S(2)}) %collective-permute-start.21) | collective-permute-done | bytes 131104 | tf_op jit(solution)/shard_map/ppermute | solution.py:265
  74.7 1.6 %shard_map.127 = f32[256,1024]{1,0:T(8,128)} custom-call(s32[2]{0:T(128)S(1)} %pad_add_fusion.place_ref, bf16[64,1024]{1,0:T(8,128)(2,1)S(1)} %shard_map.126.refs_0_, bf16[64,1024]{1,0:T(8,128)(2,1)S(1)} %collective-permute-done.19.refs_1_, bf16[64,1024]{1,0:T(8,128)(2,1)S(1)} %collective-permute-done.20.refs_2_, ...), custom_call_target="tpu_custom_call" | custom-call | flops 262144 | bytes 1572864 | tf_op jit(solution)/shard_map/pallas_call | solution.py:71
  76.3 5.0 %shard_map.125 = (bf16[128,1024]{1,0:T(8,128)(2,1)}, bf16[128,1024]{1,0:T(8,128)(2,1)}) custom-call(s32[1,4]{1,0:T(1,128)S(1)} %copy-done.6, s32[2]{0:T(128)S(1)} %pad_add_fusion.place_ref, bf16[128,1024]{1,0:T(8,128)(2,1)S(1)} %get-tuple-element.37.k0.k, bf16[128,1024]{1,0:T(8,128)(2,1)S(1)} %get-tuple-element.64.v0.v, ...), custom_call_target="tpu_custom_call" | custom-call | flops 402653184 | bytes 2621440 | tf_op jit(solution)/shard_map/pallas_call | solution.py:71
  (24 shorter events, 0.2 us)
Async XLA Ops:
  0.6 17.6 %collective-permute-start = (bf16[128,1024]{1,0:T(8,128)(2,1)}, bf16[128,1024]{1,0:T(8,128)(2,1)S(1)}, u32[]{:S(2)}, u32[]{:S(2)}) collective-permute-start(bf16[128,1024]{1,0:T(8,128)(2,1)} %bitcast.14), channel_id=1, source_target_pairs={{0,8},{4,12},{8,16},{12,20},{16,24},{20,28},{1,9},{5,13},{9,17},{1... | collective-permute-start | bytes 786440 | tf_op jit(solution)/shard_map/ppermute | solution.py:261
  5.6 19.5 %collective-permute-start.2 = (bf16[128,1024]{1,0:T(8,128)(2,1)}, bf16[128,1024]{1,0:T(8,128)(2,1)S(1)}, u32[]{:S(2)}, u32[]{:S(2)}) collective-permute-start(bf16[128,1024]{1,0:T(8,128)(2,1)} %bitcast.16), channel_id=1, source_target_pairs={{0,4},{4,8},{8,12},{12,16},{16,20},{20,24},{24,28},{1,5},{5,9},{9,... | collective-permute-start | bytes 786440 | tf_op jit(solution)/shard_map/ppermute | solution.py:261
  9.1 1.6 %copy-start = (bf16[1024,1024]{1,0:T(8,128)(2,1)S(1)}, bf16[1024,1024]{1,0:T(8,128)(2,1)}, u32[]{:S(2)}) copy-start(bf16[1024,1024]{1,0:T(8,128)(2,1)} %w_in.1) | copy-start | bytes 6291460
  10.7 0.9 %copy-start.1 = (bf16[1,128,1024]{2,1,0:T(8,128)(2,1)S(1)}, bf16[1,128,1024]{2,1,0:T(8,128)(2,1)}, u32[]{:S(2)}) copy-start(bf16[1,128,1024]{2,1,0:T(8,128)(2,1)} %param.7) | copy-start | bytes 786436
  11.6 0.9 %copy-start.2 = (bf16[1,128,1024]{2,1,0:T(8,128)(2,1)S(1)}, bf16[1,128,1024]{2,1,0:T(8,128)(2,1)}, u32[]{:S(2)}) copy-start(bf16[1,128,1024]{2,1,0:T(8,128)(2,1)} %param.11) | copy-start | bytes 786436
  12.6 0.9 %copy-start.3 = (bf16[1,128,1024]{2,1,0:T(8,128)(2,1)S(1)}, bf16[1,128,1024]{2,1,0:T(8,128)(2,1)}, u32[]{:S(2)}) copy-start(bf16[1,128,1024]{2,1,0:T(8,128)(2,1)} %param.8) | copy-start | bytes 786436
  13.5 0.9 %copy-start.4 = (bf16[1,128,1024]{2,1,0:T(8,128)(2,1)S(1)}, bf16[1,128,1024]{2,1,0:T(8,128)(2,1)}, u32[]{:S(2)}) copy-start(bf16[1,128,1024]{2,1,0:T(8,128)(2,1)} %param.9) | copy-start | bytes 786436
  14.5 0.7 copy-start.6
  15.1 13.4 %copy-start.5 = (bf16[1,128,1024]{2,1,0:T(8,128)(2,1)S(1)}, bf16[1,128,1024]{2,1,0:T(8,128)(2,1)}, u32[]{:S(2)}) copy-start(bf16[1,128,1024]{2,1,0:T(8,128)(2,1)} %param.10) | copy-start | bytes 786436
  18.3 7.5 %collective-permute-start.1 = (bf16[128,1024]{1,0:T(8,128)(2,1)S(1)}, bf16[128,1024]{1,0:T(8,128)(2,1)S(1)}, u32[]{:S(2)}, u32[]{:S(2)}) collective-permute-start(bf16[128,1024]{1,0:T(8,128)(2,1)S(1)} %broadcast_select_fusion.2), channel_id=1, source_target_pairs={{0,4},{4,0},{8,12},{12,8},{16,20},{20,16},{24,28},{28,24},{1,5},{5... | collective-permute-start | bytes 786440 | tf_op jit(solution)/shard_map/ppermute | solution.py:265
  19.9 8.7 %collective-permute-start.3 = (bf16[128,1024]{1,0:T(8,128)(2,1)S(1)}, bf16[128,1024]{1,0:T(8,128)(2,1)S(1)}, u32[]{:S(2)}, u32[]{:S(2)}) collective-permute-start(bf16[128,1024]{1,0:T(8,128)(2,1)S(1)} %bitcast.18), channel_id=1, source_target_pairs={{0,8},{4,12},{8,16},{12,20},{16,24},{20,28},{1,9},{5,13},{9,17},{1... | collective-permute-start | bytes 786440 | tf_op jit(solution)/shard_map/ppermute | solution.py:261
  23.4 7.1 %collective-permute-start.7 = (bf16[128,1024]{1,0:T(8,128)(2,1)S(1)}, bf16[128,1024]{1,0:T(8,128)(2,1)S(1)}, u32[]{:S(2)}, u32[]{:S(2)}) collective-permute-start(bf16[128,1024]{1,0:T(8,128)(2,1)S(1)} %get-tuple-element.53.refs_4_), channel_id=1, source_target_pairs={{0,1},{1,0},{2,3},{3,2},{4,5},{5,4},{6,7},{7,6},{8,9},{9,8},{10,11... | collective-permute-start | bytes 786440 | tf_op jit(solution)/shard_map/ppermute | solution.py:265
  23.5 9.2 %collective-permute-start.8 = (bf16[128,1024]{1,0:T(8,128)(2,1)S(1)}, bf16[128,1024]{1,0:T(8,128)(2,1)S(1)}, u32[]{:S(2)}, u32[]{:S(2)}) collective-permute-start(bf16[128,1024]{1,0:T(8,128)(2,1)S(1)} %get-tuple-element.53.refs_4_), channel_id=1, source_target_pairs={{0,2},{1,3},{2,0},{3,1},{4,6},{5,7},{6,4},{7,5},{8,10},{9,11},{10,... | collective-permute-start | bytes 786440 | tf_op jit(solution)/shard_map/ppermute | solution.py:265
  25.1 12.3 %collective-permute-start.9 = (bf16[128,1024]{1,0:T(8,128)(2,1)S(1)}, bf16[128,1024]{1,0:T(8,128)(2,1)S(1)}, u32[]{:S(2)}, u32[]{:S(2)}) collective-permute-start(bf16[128,1024]{1,0:T(8,128)(2,1)S(1)} %get-tuple-element.53.refs_4_), channel_id=1, source_target_pairs={{0,3},{1,2},{2,1},{3,0},{4,7},{5,6},{6,5},{7,4},{8,11},{9,10},{10,... | collective-permute-start | bytes 786440 | tf_op jit(solution)/shard_map/ppermute | solution.py:265
  25.9 18.9 %collective-permute-start.14 = (bf16[128,1024]{1,0:T(8,128)(2,1)S(1)}, bf16[128,1024]{1,0:T(8,128)(2,1)S(1)}, u32[]{:S(2)}, u32[]{:S(2)}) collective-permute-start(bf16[128,1024]{1,0:T(8,128)(2,1)S(1)} %get-tuple-element.40.q.q0), channel_id=1, source_target_pairs={{8,0},{12,4},{16,8},{20,12},{24,16},{28,20},{9,1},{13,5},{17,9},{2... | collective-permute-start | bytes 786440 | tf_op jit(solution)/shard_map/ppermute | solution.py:261
  30.5 8.2 %collective-permute-start.4 = (bf16[128,256]{1,0:T(8,128)(2,1)S(1)}, bf16[128,256]{1,0:T(8,128)(2,1)S(1)}, u32[]{:S(2)}, u32[]{:S(2)}) collective-permute-start(bf16[128,256]{1,0:T(8,128)(2,1)S(1)} %get-tuple-element.50), channel_id=1, source_target_pairs={{0,1},{1,0},{2,3},{3,2},{4,5},{5,4},{6,7},{7,6},{8,9},{9,8},{10,11... | collective-permute-start | bytes 196616 | tf_op jit(solution)/shard_map/ppermute | solution.py:265
  30.5 9.2 %collective-permute-start.5 = (bf16[128,256]{1,0:T(8,128)(2,1)S(1)}, bf16[128,256]{1,0:T(8,128)(2,1)S(1)}, u32[]{:S(2)}, u32[]{:S(2)}) collective-permute-start(bf16[128,256]{1,0:T(8,128)(2,1)S(1)} %get-tuple-element.51), channel_id=1, source_target_pairs={{0,2},{1,3},{2,0},{3,1},{4,6},{5,7},{6,4},{7,5},{8,10},{9,11},{10,... | collective-permute-start | bytes 196616 | tf_op jit(solution)/shard_map/ppermute | solution.py:265
  32.7 7.5 %collective-permute-start.6 = (bf16[128,256]{1,0:T(8,128)(2,1)S(1)}, bf16[128,256]{1,0:T(8,128)(2,1)S(1)}, u32[]{:S(2)}, u32[]{:S(2)}) collective-permute-start(bf16[128,256]{1,0:T(8,128)(2,1)S(1)} %get-tuple-element.52), channel_id=1, source_target_pairs={{0,3},{1,2},{2,1},{3,0},{4,7},{5,6},{6,5},{7,4},{8,11},{9,10},{10,... | collective-permute-start | bytes 196616 | tf_op jit(solution)/shard_map/ppermute | solution.py:265
  37.4 18.2 %collective-permute-start.16 = (bf16[128,1024]{1,0:T(8,128)(2,1)S(1)}, bf16[128,1024]{1,0:T(8,128)(2,1)S(1)}, u32[]{:S(2)}, u32[]{:S(2)}) collective-permute-start(bf16[128,1024]{1,0:T(8,128)(2,1)S(1)} %get-tuple-element.47.grad_mix.g0), channel_id=1, source_target_pairs={{8,0},{12,4},{16,8},{20,12},{24,16},{28,20},{9,1},{13,5},{17,9},{2... | collective-permute-start | bytes 786440 | tf_op jit(solution)/shard_map/ppermute | solution.py:261
  41.2 5.7 %collective-permute-start.10 = (bf16[64,1024]{1,0:T(8,128)(2,1)S(1)}, bf16[64,1024]{1,0:T(8,128)(2,1)S(1)}, u32[]{:S(2)}, u32[]{:S(2)}) collective-permute-start(bf16[64,1024]{1,0:T(8,128)(2,1)S(1)} %get-tuple-element.59), channel_id=1, source_target_pairs={{0,4},{4,0},{8,12},{12,8},{16,20},{20,16},{24,28},{28,24},{1,5},{5... | collective-permute-start | bytes 393224 | tf_op jit(solution)/shard_map/ppermute | solution.py:265
  41.8 9.5 %collective-permute-start.11 = (bf16[64,1024]{1,0:T(8,128)(2,1)S(1)}, bf16[64,1024]{1,0:T(8,128)(2,1)S(1)}, u32[]{:S(2)}, u32[]{:S(2)}) collective-permute-start(bf16[64,1024]{1,0:T(8,128)(2,1)S(1)} %get-tuple-element.60), channel_id=1, source_target_pairs={{0,8},{4,12},{8,0},{12,4},{16,24},{20,28},{24,16},{28,20},{1,9},{5... | collective-permute-start | bytes 393224 | tf_op jit(solution)/shard_map/ppermute | solution.py:265
  43.4 10.5 %collective-permute-start.12 = (bf16[64,1024]{1,0:T(8,128)(2,1)S(1)}, bf16[64,1024]{1,0:T(8,128)(2,1)S(1)}, u32[]{:S(2)}, u32[]{:S(2)}) collective-permute-start(bf16[64,1024]{1,0:T(8,128)(2,1)S(1)} %get-tuple-element.61), channel_id=1, source_target_pairs={{0,12},{4,8},{8,4},{12,0},{16,28},{20,24},{24,20},{28,16},{1,13},{... | collective-permute-start | bytes 393224 | tf_op jit(solution)/shard_map/ppermute | solution.py:265
  44.8 31.5 %collective-permute-start.15 = (bf16[128,1024]{1,0:T(8,128)(2,1)S(1)}, bf16[128,1024]{1,0:T(8,128)(2,1)S(1)}, u32[]{:S(2)}, u32[]{:S(2)}) collective-permute-start(bf16[128,1024]{1,0:T(8,128)(2,1)S(1)} %broadcast_select_fusion.1), channel_id=1, source_target_pairs={{0,4},{4,0},{8,12},{12,8},{16,20},{20,16},{24,28},{28,24},{1,5},{5... | collective-permute-start | bytes 786440 | tf_op jit(solution)/shard_map/ppermute | solution.py:265
  54.5 5.5 %collective-permute-start.13 = (bf16[32,1024]{1,0:T(8,128)(2,1)S(1)}, bf16[32,1024]{1,0:T(8,128)(2,1)S(1)}, u32[]{:S(2)}, u32[]{:S(2)}) collective-permute-start(bf16[32,1024]{1,0:T(8,128)(2,1)S(1)} %get-tuple-element.63), channel_id=1, source_target_pairs={{0,16},{4,20},{8,24},{12,28},{16,0},{20,4},{24,8},{28,12},{1,17},{... | collective-permute-start | bytes 196616 | tf_op jit(solution)/shard_map/ppermute | solution.py:265
  55.6 20.7 %collective-permute-start.17 = (bf16[128,1024]{1,0:T(8,128)(2,1)S(1)}, bf16[128,1024]{1,0:T(8,128)(2,1)S(1)}, u32[]{:S(2)}, u32[]{:S(2)}) collective-permute-start(bf16[128,1024]{1,0:T(8,128)(2,1)S(1)} %broadcast_select_fusion), channel_id=1, source_target_pairs={{0,4},{4,0},{8,12},{12,8},{16,20},{20,16},{24,28},{28,24},{1,5},{5... | collective-permute-start | bytes 786440 | tf_op jit(solution)/shard_map/ppermute | solution.py:265
  59.9 5.3 %collective-permute-start.18 = (bf16[32,1024]{1,0:T(8,128)(2,1)S(1)}, bf16[32,1024]{1,0:T(8,128)(2,1)S(1)}, u32[]{:S(2)}, u32[]{:S(2)}) collective-permute-start(bf16[32,1024]{1,0:T(8,128)(2,1)S(1)} %shard_map.124.mine), channel_id=1, source_target_pairs={{0,16},{4,20},{8,24},{12,28},{16,0},{20,4},{24,8},{28,12},{1,17},{... | collective-permute-start | bytes 196616 | tf_op jit(solution)/shard_map/ppermute | solution.py:265
  65.8 6.3 %collective-permute-start.19 = (bf16[64,1024]{1,0:T(8,128)(2,1)S(1)}, bf16[64,1024]{1,0:T(8,128)(2,1)S(1)}, u32[]{:S(2)}, u32[]{:S(2)}) collective-permute-start(bf16[64,1024]{1,0:T(8,128)(2,1)S(1)} %shard_map.126.refs_0_), channel_id=1, source_target_pairs={{0,4},{4,0},{8,12},{12,8},{16,20},{20,16},{24,28},{28,24},{1,5},{5... | collective-permute-start | bytes 393224 | tf_op jit(solution)/shard_map/ppermute | solution.py:265
  67.1 5.1 %collective-permute-start.20 = (bf16[64,1024]{1,0:T(8,128)(2,1)S(1)}, bf16[64,1024]{1,0:T(8,128)(2,1)S(1)}, u32[]{:S(2)}, u32[]{:S(2)}) collective-permute-start(bf16[64,1024]{1,0:T(8,128)(2,1)S(1)} %shard_map.126.refs_0_), channel_id=1, source_target_pairs={{0,8},{4,12},{8,0},{12,4},{16,24},{20,28},{24,16},{28,20},{1,9},{5... | collective-permute-start | bytes 393224 | tf_op jit(solution)/shard_map/ppermute | solution.py:265
  67.1 7.6 %collective-permute-start.21 = (bf16[64,1024]{1,0:T(8,128)(2,1)S(1)}, bf16[64,1024]{1,0:T(8,128)(2,1)S(1)}, u32[]{:S(2)}, u32[]{:S(2)}) collective-permute-start(bf16[64,1024]{1,0:T(8,128)(2,1)S(1)} %shard_map.126.refs_0_), channel_id=1, source_target_pairs={{0,12},{4,8},{8,4},{12,0},{16,28},{20,24},{24,20},{28,16},{1,13},{... | collective-permute-start | bytes 393224 | tf_op jit(solution)/shard_map/ppermute | solution.py:265

commit v4 on v3

--- a/solution.py
+++ b/solution.py
@@ -66,13 +66,13 @@
     return pl.CostEstimate(flops=flops, bytes_accessed=total, transcendentals=0)
 
 
-def call(kernel, outs, scalars, arrays, flops, scratch=(), spaces=None):
+def call(kernel, outs, scalars, arrays, flops, scratch=(), spaces=None, out_space=VMEM):
     spaces = spaces or [VMEM] * len(arrays)
     return pl.pallas_call(
         kernel,
         out_shape=outs,
         in_specs=[SMEM] * len(scalars) + spaces,
-        out_specs=[VMEM] * len(outs),
+        out_specs=[out_space] * len(outs),
         scratch_shapes=list(scratch),
         cost_estimate=cost(flops, list(arrays) + list(outs)),
         compiler_params=pltpu.CompilerParams(vmem_limit_bytes=40 * 1024 * 1024),
@@ -80,12 +80,12 @@
 
 
 def own_kernel(
-    len_ref, place_ref, q_in, k_in, v_in, grad_in, w_in, q, k, v, grad, w, mixed, grad_hidden, slope, sems
+    len_ref, place_ref, q_in, k_in, v_in, grad_in, w_in, gate_in, q, k, v, grad, w, gates, mixed, grad_hidden, slope, sems
 ):
     moves = [
         pltpu.make_async_copy(src, dst, sems.at[i])
         for i, (src, dst) in enumerate(
-            ((q_in, q), (k_in, k), (v_in, v), (grad_in, grad), (w_in, w))
+            ((q_in, q), (k_in, k), (v_in, v), (grad_in, grad), (w_in, w), (gate_in, gates))
         )
     ]
     for move in moves:
@@ -109,57 +109,67 @@
     grad_hidden[...] = dot_nt(grad[...], w[...])
 
 
-def far_kernel(len_ref, place_ref, q, k1, k2, attention1, attention2, slope1, slope2):
+def far_scores(h, allowed, q, keys, slope):
+    size = q.shape[1] // HEADS
+    scale = size ** (-0.5)
+    cols = head_slice(h, size)
+    scores = dot_nt(q[:, cols], keys[:, cols]) * scale
+    gate = logistic(scores)
+    slope[:, cols] = jnp.where(allowed, silu_slope(scores, gate) * scale, 0.0)
+    return jnp.where(allowed, scores * gate, 0.0).astype(BF16)
+
+
+def second_kernel(len_ref, place_ref, q, keys, vals, mixed_own, mixed, slope):
     rows, width = q.shape
     size = width // HEADS
-    scale = size ** (-0.5)
     first = place_ref[0] * rows
-    parts = ((k1, attention1, slope1), (k2, attention2, slope2))
-    for d, (keys, attention, slope) in enumerate(parts):
-        allowed = allowed_block(rows, first, first - (d + 1) * rows, len_ref, 0)
-        for h in range(HEADS):
-            cols = head_slice(h, size)
-            scores = dot_nt(q[:, cols], keys[:, cols]) * scale
-            gate = logistic(scores)
-            attention[:, cols] = jnp.where(allowed, scores * gate, 0.0).astype(BF16)
-            slope[:, cols] = jnp.where(allowed, silu_slope(scores, gate) * scale, 0.0)
-
-
-def forward_kernel(
-    groups, place_ref, attention1, attention2, v1, v2, mixed_own, grad_hidden, gates, *rest
-):
-    hidden, grad_gates, grad_mix = rest[:3]
-    slices = rest[3 : 3 + groups]
-    mixed = rest[3 + groups]
-    rows, width = v1.shape
-    size = width // HEADS
-    for h in range(HEADS):
-        cols = head_slice(h, size)
-        mixed[:, cols] = (
-            mixed_own[:, cols]
-            + dot(attention1[:, cols], v1[:, cols])
-            + dot(attention2[:, cols], v2[:, cols])
-        )
+    allowed = allowed_block(rows, first, first - 2 * rows, len_ref, 0)
+    for h in range(HEADS):
+        cols = head_slice(h, size)
+        attention = far_scores(h, allowed, q, keys, slope)
+        mixed[:, cols] = mixed_own[:, cols] + dot(attention, vals[:, cols])
+
+
+def first_kernel(len_ref, place_ref, q, keys, attention, slope):
+    rows, width = q.shape
+    size = width // HEADS
+    first = place_ref[0] * rows
+    allowed = allowed_block(rows, first, first - rows, len_ref, 0)
+    for h in range(HEADS):
+        attention[:, head_slice(h, size)] = far_scores(h, allowed, q, keys, slope)
+
+
+def forward_kernel(groups, place_ref, attention, vals, mixed_far, gates, hidden, normed, inv_std, *rest):
+    slices, mixed = rest[:-1], rest[-1]
+    rows, width = vals.shape
+    size = width // HEADS
+    for h in range(HEADS):
+        cols = head_slice(h, size)
+        mixed[:, cols] = mixed_far[:, cols] + dot(attention[:, cols], vals[:, cols])
     values = mixed[...]
     centered = values - jnp.mean(values, axis=1, keepdims=True)
-    inv_std = lax.rsqrt(jnp.mean(centered * centered, axis=1, keepdims=True) + 1e-05)
-    normed = centered * inv_std
-    gate = gates[...].astype(F32)
-    hidden[...] = (normed * gate).astype(BF16)
+    inverse = lax.rsqrt(jnp.mean(centered * centered, axis=1, keepdims=True) + 1e-05)
+    inv_std[...] = jnp.broadcast_to(inverse, inv_std.shape)
+    normed[...] = centered * inverse
+    hidden[...] = (normed[...] * gates[...].astype(F32)).astype(BF16)
     part = width // groups
     for d, ref in enumerate(slices):
         at = pl.multiple_of((place_ref[1] ^ d) * part, 128)
         ref[...] = hidden[:, pl.ds(at, part)]
+
+
+def mix_kernel(grad_hidden, gates, normed, inv_std, grad_gates, grad_mix):
     gh = grad_hidden[...]
-    grad_gates[...] = (gh * normed).astype(BF16)
-    grad_norm = gh * gate
+    norm = normed[...]
+    grad_gates[...] = (gh * norm).astype(BF16)
+    grad_norm = gh * gates[...].astype(F32)
     grad_mix[...] = (
         (
             grad_norm
             - jnp.mean(grad_norm, axis=1, keepdims=True)
-            - normed * jnp.mean(grad_norm * normed, axis=1, keepdims=True)
+            - norm * jnp.mean(grad_norm * norm, axis=1, keepdims=True)
         )
-        * inv_std
+        * inv_std[:, :1]
     ).astype(BF16)
 
 
@@ -219,36 +229,30 @@
         ref[...] = total[pl.ds(at, rows), :].astype(BF16)
 
 
-def corner_kernel(corners, place_ref, own, *refs):
-    got, (keep, send, total) = refs[:-3], refs[-3:]
+def corner_kernel(own, *refs):
+    got, narrow = refs[:-1], refs[-1]
     acc = own[...]
     for ref in got:
         acc = acc + ref[...].astype(F32)
-    total[...] = acc
-    rows = keep.shape[0]
-    side = place_ref[0] // corners
-    keep[...] = total[pl.ds(pl.multiple_of(side * rows, rows), rows), :]
-    send[...] = total[pl.ds(pl.multiple_of((1 - side) * rows, rows), rows), :].astype(BF16)
-
-
-def piece_kernel(scale, keep, got, piece):
-    piece[...] = ((keep[...] + got[...].astype(F32)) * scale).astype(BF16)
-
-
-def pair_kernel(corners, place_ref, mine, other, both):
-    rows = mine.shape[0]
-    side = place_ref[0] // corners
-    both[pl.ds(pl.multiple_of(side * rows, rows), rows), :] = mine[...]
-    both[pl.ds(pl.multiple_of((1 - side) * rows, rows), rows), :] = other[...]
+    narrow[...] = acc.astype(BF16)
+
+
+def pair_kernel(scale, mine, other, both):
+    both[...] = ((mine[...].astype(F32) + other[...].astype(F32)) * scale).astype(BF16)
 
 
 def place_kernel(corners, place_ref, *refs):
-    out = refs[-1]
-    rows = refs[0].shape[0]
+    shares, (out, wide, sems) = refs[:corners], refs[corners:]
+    rows = shares[0].shape[0]
     corner = place_ref[0] & (corners - 1)
-    for e, ref in enumerate(refs[:-1]):
+    moves = []
+    for e, ref in enumerate(shares):
+        wide[e] = ref[...].astype(F32)
         at = pl.multiple_of((corner ^ e) * rows, rows)
-        out[pl.ds(at, rows), :] = ref[...].astype(F32)
+        moves.append(pltpu.make_async_copy(wide.at[e], out.at[pl.ds(at, rows), :], sems.at[e]))
+        moves[-1].start()
+    for move in moves:
+        move.wait()
 
 
 def xor_route(size, mask):
@@ -285,44 +289,55 @@
     k2 = shifted(keys[0], 2)
     v2 = shifted(values[0], 2)
     v1 = shifted(values[0], 1)
-    q, k, v, grad, w, mixed_own, grad_hidden, slope0 = call(
+    grads = [out_grad[0]]
+    for d in range(1, batch):
+        low = d & -d
+        grads.append(swapped(grads[d ^ low], "batch", low))
+    q, k, v, grad, w, gate, mixed_own, grad_hidden, slope0 = call(
         own_kernel,
-        [full, full, full, full, jax.ShapeDtypeStruct(w_out.shape, BF16), wide, wide, wide],
+        [full, full, full, full, jax.ShapeDtypeStruct(w_out.shape, BF16), full, wide, wide, wide],
         scalars,
-        (queries[0], keys[0], values[0], out_grad[0], w_out),
+        tuple(
+            pltpu.with_memory_space_constraint(a, pltpu.HBM)
+            for a in (queries[0], keys[0], values[0], out_grad[0], w_out, gates[0])
+        ),
         proj_flops + 2 * block_flops,
-        [pltpu.SemaphoreType.DMA((5,))],
-        [pl.BlockSpec(memory_space=pltpu.HBM)] * 5,
-    )
+        [pltpu.SemaphoreType.DMA((6,))],
+        [pl.BlockSpec(memory_space=pltpu.HBM)] * 6,
+    )
+    grads[0] = grad
     k1 = swapped(jnp.where(even, k, k2), "seq", 1)
-    grads = [grad] + [swapped(grad, "batch", d) for d in range(1, batch)]
     q2 = shifted(q, -2)
-    attention1, attention2, slope1, slope2 = call(
-        far_kernel, [full, full, wide, wide], scalars, (q, k1, k2), 2 * block_flops
+    mixed_far, slope2 = call(
+        second_kernel, [wide, wide], scalars, (q, k2, v2, mixed_own), 2 * block_flops
     )
     q1 = swapped(jnp.where(even, q2, q), "seq", 1)
+    attention1, slope1 = call(first_kernel, [full, wide], scalars, (q, k1), block_flops)
     part = width // batch
     piece = jax.ShapeDtypeStruct((rows, part), BF16)
-    hidden, grad_gates, grad_mix, *slices = call(
+    hidden, normed, inv_std, *slices = call(
         functools.partial(forward_kernel, batch),
-        [full, full, full] + [piece] * batch,
+        [full, wide, jax.ShapeDtypeStruct((rows, 128), F32)] + [piece] * batch,
         (place,),
-        (attention1, attention2, v1, v2, mixed_own, grad_hidden, gates[0]),
-        2 * block_flops,
+        (attention1, v1, mixed_far, gate),
+        block_flops,
         [pltpu.VMEM((rows, width), F32)],
     )
     hiddens = [slices[0]] + [swapped(slices[d], "batch", d) for d in range(1, batch)]
+    grad_gates, grad_mix = call(
+        mix_kernel, [full, full], (), (grad_hidden, gate, normed, inv_std), block_flops // 4
+    )
     g2 = shifted(grad_mix, -2)
     g1 = swapped(jnp.where(even, g2, grad_mix), "seq", 1)
 
     corners = 4
     direct = seq == 2 * corners
     rows_w = part // corners if direct else part
+    share = jax.ShapeDtypeStruct((rows_w, width), BF16)
     scale = (rows * seq * batch) ** (-0.5)
     own, *sends = call(
         functools.partial(weight_kernel, batch),
-        [jax.ShapeDtypeStruct((rows_w, width), F32)]
-        + ([jax.ShapeDtypeStruct((rows_w, width), BF16)] * (corners - 1) if direct else []),
+        [jax.ShapeDtypeStruct((rows_w, width), F32)] + [share] * (corners - 1 if direct else 0),
         (place,),
         (*hiddens, *grads),
         proj_flops,
@@ -336,46 +351,31 @@
         proj_flops + 6 * block_flops,
     )
     if direct:
-        half = jax.ShapeDtypeStruct((rows_w // 2, width), BF16)
-        half_wide = jax.ShapeDtypeStruct((rows_w // 2, width), F32)
         got = [swapped(s, "seq", e + 1) for e, s in enumerate(sends)]
-        keep, send = call(
-            functools.partial(corner_kernel, corners),
-            [half_wide, half],
-            (place,),
-            (own, *got),
-            own.size * 4,
-            [pltpu.VMEM((rows_w, width), F32)],
+        (mine,) = call(corner_kernel, [share], (), (after(own, output), *got), own.size * 4)
+        other = swapped(mine, "seq", corners)
+        (both,) = call(
+            functools.partial(pair_kernel, scale), [share], (), (mine, other), own.size * 2
         )
-        (mine,) = call(
-            functools.partial(piece_kernel, scale),
-            [half],
-            (),
-            (keep, swapped(send, "seq", corners)),
-            own.size,
-        )
-        (both,) = call(
-            functools.partial(pair_kernel, corners),
-            [jax.ShapeDtypeStruct((rows_w, width), BF16)],
-            (place,),
-            (mine, swapped(mine, "seq", corners)),
-            own.size,
-        )
-        shares = [both] + [swapped(both, "seq", e) for e in range(1, corners)]
+        last = after(v, both)
+    else:
+        last = v
+    grad_keys, grad_values = call(
+        key_kernel, [full, full], scalars, (k, last, q, q1, q2, grad_mix, g1, g2), 12 * block_flops
+    )
+    if direct:
+        shares = [swapped(both, "seq", e) for e in range(1, corners)]
         (grad_weight,) = call(
             functools.partial(place_kernel, corners),
             [jax.ShapeDtypeStruct((part, width), F32)],
             (place,),
-            tuple(shares),
+            (after(both, grad_keys), *shares),
             part * width,
+            [pltpu.VMEM((corners, rows_w, width), F32), pltpu.SemaphoreType.DMA((corners,))],
+            out_space=pl.BlockSpec(memory_space=pltpu.HBM),
         )
-        v_late = after(v, mine)
     else:
         grad_weight = lax.psum(own, "seq") * scale
-        v_late = v
-    grad_keys, grad_values = call(
-        key_kernel, [full, full], scalars, (k, v_late, q, q1, q2, grad_mix, g1, g2), 12 * block_flops
-    )
     return (
         output[None],
         grad_queries[None],

time: 81.6 us -> 73 us (0.89)
  waiting for transfers between devices: 26.3 us -> 12.4 us
  starting transfers between devices: 30 us -> 34.1 us
  Pallas kernels: 17.9 us -> 19.7 us
    ppermute x17 -> x16, waiting for transfers between devices: 26.3 us -> 7.39 us  [swapped(): return lax.ppermute(block, axis, xor_route(lax.axis_size(axis), mask))]
    ppermute x5, waiting for transfers between devices: 0.01 us -> 5.04 us  [shifted(): return lax.ppermute(block, 'seq', route)]
    ppermute x17 -> x16, starting transfers between devices: 15.6 us -> 20.6 us  [swapped(): return lax.ppermute(block, axis, xor_route(lax.axis_size(axis), mask))]
    pallas_call x10 -> x11, Pallas kernels: 17.9 us -> 19.7 us  [call(): pl.pallas_call(kernel, out_shape=outs, in_specs=[SMEM] * len(scalars) + s...]
    ppermute x5, starting transfers between devices: 14.4 us -> 13.5 us  [shifted(): return lax.ppermute(block, 'seq', route)]
    unnamed x14 -> x24, local copies, waits for them, and re-layouts: 6.05 us -> 5.51 us
  transfers between devices with their start and end apart: 22 -> 21, of which waited for: 12 -> 5; matrix products, arithmetic and copies ran while one was open for 0% -> 0% of each run, Pallas kernels for 16% -> 25%
where the time goes in v4:
time: 73 us; the launch traced here: 72.7 us
  starting transfers between devices  34.1 us (47%)
  Pallas kernels  19.7 us (27%)
  waiting for transfers between devices  12.4 us (17%)
  local copies, waits for them, and re-layouts  5.51 us (8%)
  between operations  0.83 us (1%)
    ppermute x16, starting transfers between devices, swapped(): return lax.ppermute(block, axis, xor_route(lax.axis_size(axis), mask))  20.6 us
    pallas_call x11, Pallas kernels, call(): pl.pallas_call(kernel, out_shape=outs, in_specs=[SMEM] * len(scalars) + s...  19.7 us
    ppermute x5, starting transfers between devices, shifted(): return lax.ppermute(block, 'seq', route)  13.5 us
    ppermute x16, waiting for transfers between devices, swapped(): return lax.ppermute(block, axis, xor_route(lax.axis_size(axis), mask))  7.39 us
    unnamed x24, local copies, waits for them, and re-layouts  5.51 us
    ppermute x5, waiting for transfers between devices, shifted(): return lax.ppermute(block, 'seq', route)  5.04 us
  transfers between devices with their start and end apart: 21, of which 5 were waited for; matrix products, arithmetic and copies ran while one was open for 0% of the time, Pallas kernels for 25%

profile of v4, /device:TPU:0, one launch (start us, length us, event | category | flops | bytes accessed | tf_op | source)
XLA Modules:
  0.0 72.7 jit_solution(11570723560414794445)
XLA Ops:
  0.6 4.9 %collective-permute-start = (bf16[128,1024]{1,0:T(8,128)(2,1)}, bf16[128,1024]{1,0:T(8,128)(2,1)S(1)}, u32[]{:S(2)}, u32[]{:S(2)}) collective-permute-start(bf16[128,1024]{1,0:T(8,128)(2,1)} %bitcast.14), channel_id=1, source_target_pairs={{0,8},{4,12},{8,16},{12,20},{16,24},{20,28},{1,9},{5,13},{9,17},{1... | collective-permute-start | bytes 786440 | tf_op jit(solution)/shard_map/ppermute | solution.py:265
  5.6 3.5 %collective-permute-start.3 = (bf16[128,1024]{1,0:T(8,128)(2,1)}, bf16[128,1024]{1,0:T(8,128)(2,1)S(1)}, u32[]{:S(2)}, u32[]{:S(2)}) collective-permute-start(bf16[128,1024]{1,0:T(8,128)(2,1)} %bitcast.16), channel_id=1, source_target_pairs={{0,8},{4,12},{8,16},{12,20},{16,24},{20,28},{1,9},{5,13},{9,17},{1... | collective-permute-start | bytes 786440 | tf_op jit(solution)/shard_map/ppermute | solution.py:265
  9.1 1.6 %collective-permute-start.8 = (bf16[128,1024]{1,0:T(8,128)(2,1)}, bf16[128,1024]{1,0:T(8,128)(2,1)}, u32[]{:S(2)}, u32[]{:S(2)}) collective-permute-start(bf16[128,1024]{1,0:T(8,128)(2,1)} %bitcast.19), channel_id=1, source_target_pairs={{0,2},{1,3},{2,0},{3,1},{4,6},{5,7},{6,4},{7,5},{8,10},{9,11},{10,... | collective-permute-start | bytes 786440 | tf_op jit(solution)/shard_map/ppermute | solution.py:269
  10.7 0.1 pad_add_fusion.place_ref
  10.7 0.7 copy-done.10
  11.4 4.0 %shard_map.118 = (bf16[128,1024]{1,0:T(8,128)(2,1)S(1)}, bf16[128,1024]{1,0:T(8,128)(2,1)S(1)}, bf16[128,1024]{1,0:T(8,128)(2,1)S(1)}, bf16[128,1024]{1,0:T(8,12...) custom-call(s32[1,4]{1,0:T(1,128)S(1)} %copy-done.10, ...), custom_call_target="tpu_custom_call" | custom-call | flops 335544320 | bytes 8388608 | tf_op jit(solution)/shard_map/pallas_call | solution.py:71
  15.4 0.0 copy-start
  15.4 0.7 copy-done
  16.1 0.8 %copy-done.2 = f32[128,1024]{1,0:T(8,128)} copy-done((f32[128,1024]{1,0:T(8,128)}, f32[128,1024]{1,0:T(8,128)S(1)}, u32[]{:S(2)}) %copy-start.2) | copy-done | bytes 524312
  16.9 0.8 %copy-done.4 = f32[128,1024]{1,0:T(8,128)} copy-done((f32[128,1024]{1,0:T(8,128)}, f32[128,1024]{1,0:T(8,128)S(1)}, u32[]{:S(2)}) %copy-start.4) | copy-done | bytes 524312
  17.7 0.8 %copy-done.6 = f32[128,1024]{1,0:T(8,128)} copy-done((f32[128,1024]{1,0:T(8,128)}, f32[128,1024]{1,0:T(8,128)S(1)}, u32[]{:S(2)}) %copy-start.6) | copy-done | bytes 524312
  18.5 0.7 copy-done.8
  19.2 1.6 %collective-permute-start.1 = (bf16[128,1024]{1,0:T(8,128)(2,1)S(1)}, bf16[128,1024]{1,0:T(8,128)(2,1)S(1)}, u32[]{:S(2)}, u32[]{:S(2)}) collective-permute-start(bf16[128,1024]{1,0:T(8,128)(2,1)S(1)} %broadcast_select_fusion.2), channel_id=1, source_target_pairs={{0,4},{4,0},{8,12},{12,8},{16,20},{20,16},{24,28},{28,24},{1,5},{5... | collective-permute-start | bytes 786440 | tf_op jit(solution)/shard_map/ppermute | solution.py:269
  20.8 2.4 %collective-permute-start.2 = (bf16[128,1024]{1,0:T(8,128)(2,1)}, bf16[128,1024]{1,0:T(8,128)(2,1)S(1)}, u32[]{:S(2)}, u32[]{:S(2)}) collective-permute-start(bf16[128,1024]{1,0:T(8,128)(2,1)} %bitcast.18), channel_id=1, source_target_pairs={{0,4},{4,8},{8,12},{12,16},{16,20},{20,24},{24,28},{1,5},{5,9},{9,... | collective-permute-start | bytes 786440 | tf_op jit(solution)/shard_map/ppermute | solution.py:265
  23.2 0.1 collective-permute-start.7
  23.3 1.3 %collective-permute-start.14 = (bf16[128,1024]{1,0:T(8,128)(2,1)S(1)}, bf16[128,1024]{1,0:T(8,128)(2,1)S(1)}, u32[]{:S(2)}, u32[]{:S(2)}) collective-permute-start(bf16[128,1024]{1,0:T(8,128)(2,1)S(1)} %get-tuple-element.43.q.q0), channel_id=1, source_target_pairs={{8,0},{12,4},{16,8},{20,12},{24,16},{28,20},{9,1},{13,5},{17,9},{2... | collective-permute-start | bytes 786440 | tf_op jit(solution)/shard_map/ppermute | solution.py:265
  24.6 0.0 collective-permute-done.8.refs_6_
  24.6 0.5 collective-permute-start.9
  25.2 1.0 %copy-done.5 = f32[128,1024]{1,0:T(8,128)S(1)} copy-done((f32[128,1024]{1,0:T(8,128)S(1)}, f32[128,1024]{1,0:T(8,128)}, u32[]{:S(2)}) %copy-start.5) | copy-done | bytes 524312
  26.2 2.0 %shard_map.120 = (f32[128,1024]{1,0:T(8,128)S(1)}, f32[128,1024]{1,0:T(8,128)S(1)}) custom-call(s32[1,4]{1,0:T(1,128)S(1)} %copy-done.11, s32[2]{0:T(128)S(1)} %pad_add_fusion.place_ref, bf16[128,1024]{1,0:T(8,128)(2,1)S(1)} %get-tuple-element.43.q.q0, bf16[128,1024]{1,0:T(8,128)(2,1)S(1)} %collective-permute-done.keys.k2, ...), custom_call_target="tpu_custom_call" | custom-call | flops 67108864 | bytes 2359296 | tf_op jit(solution)/shard_map/pallas_call | solution.py:71
  28.2 0.0 copy-start.9
  28.2 0.0 collective-permute-done.1.keys.k1
  28.2 1.0 %shard_map.119 = (bf16[128,1024]{1,0:T(8,128)(2,1)S(1)}, f32[128,1024]{1,0:T(8,128)S(1)}) custom-call(s32[1,4]{1,0:T(1,128)S(1)} %copy-done.11, s32[2]{0:T(128)S(1)} %pad_add_fusion.place_ref, bf16[128,1024]{1,0:T(8,128)(2,1)S(1)} %get-tuple-element.43.q.q0, bf16[128,1024]{1,0:T(8,128)(2,1)S(1)} %collective-permute-done.1.keys.k1), custom_call_target="tpu_custom_call" | custom-call | flops 33554432 | bytes 1310720 | tf_op jit(solution)/shard_map/pallas_call | solution.py:71
  29.3 2.0 %collective-permute-done.2.vals.v1 = bf16[128,1024]{1,0:T(8,128)(2,1)S(1)} collective-permute-done((bf16[128,1024]{1,0:T(8,128)(2,1)}, bf16[128,1024]{1,0:T(8,128)(2,1)S(1)}, u32[]{:S(2)}, u32[]{:S(2)}) %collective-permute-start.2) | collective-permute-done | bytes 262176 | tf_op jit(solution)/shard_map/ppermute | solution.py:265
  31.2 1.0 %shard_map.121 = (bf16[128,1024]{1,0:T(8,128)(2,1)S(1)}, f32[128,1024]{1,0:T(8,128)S(1)}, f32[128,128]{1,0:T(8,128)S(1)}, bf16[128,256]{1,0:T(8,128)(2,1)S(1)}, ...) custom-call(s32[2]{0:T(128)S(1)} %pad_add_fusion.place_ref, ...), custom_call_target="tpu_custom_call" | custom-call | flops 33554432 | bytes 2424832 | tf_op jit(solution)/shard_map/pallas_call | solution.py:71
  32.3 0.1 collective-permute-start.4
  32.3 0.6 collective-permute-start.5
  32.9 0.9 %shard_map.122 = (bf16[128,1024]{1,0:T(8,128)(2,1)}, bf16[128,1024]{1,0:T(8,128)(2,1)S(1)}) custom-call(f32[128,1024]{1,0:T(8,128)S(1)} %copy-done.3, bf16[128,1024]{1,0:T(8,128)(2,1)S(1)} %get-tuple-element.48.gates, f32[128,1024]{1,0:T(8,128)S(1)} %get-tuple-element.51.normed, f32[128,128]{1,0:T(8,128)S(1)} %get-tuple-element.52.inv_std), custom_call_target="tpu_custom_call" | custom-call | flops 8388608 | bytes 1900544 | tf_op jit(solution)/shard_map/pallas_call | solution.py:71
  33.8 0.0 collective-permute-done.7.refs_5_
  33.8 1.3 %collective-permute-start.6 = (bf16[128,256]{1,0:T(8,128)(2,1)S(1)}, bf16[128,256]{1,0:T(8,128)(2,1)S(1)}, u32[]{:S(2)}, u32[]{:S(2)}) collective-permute-start(bf16[128,256]{1,0:T(8,128)(2,1)S(1)} %get-tuple-element.58), channel_id=1, source_target_pairs={{0,3},{1,2},{2,1},{3,0},{4,7},{5,6},{6,5},{7,4},{8,11},{9,10},{10,... | collective-permute-start | bytes 196616 | tf_op jit(solution)/shard_map/ppermute | solution.py:269
  35.1 1.3 %collective-permute-start.16 = (bf16[128,1024]{1,0:T(8,128)(2,1)S(1)}, bf16[128,1024]{1,0:T(8,128)(2,1)S(1)}, u32[]{:S(2)}, u32[]{:S(2)}) collective-permute-start(bf16[128,1024]{1,0:T(8,128)(2,1)S(1)} %get-tuple-element.53.grad_mix.g0), channel_id=1, source_target_pairs={{8,0},{12,4},{16,8},{20,12},{24,16},{28,20},{9,1},{13,5},{17,9},{2... | collective-permute-start | bytes 786440 | tf_op jit(solution)/shard_map/ppermute | solution.py:265
  36.4 2.4 %collective-permute-start.15 = (bf16[128,1024]{1,0:T(8,128)(2,1)S(1)}, bf16[128,1024]{1,0:T(8,128)(2,1)S(1)}, u32[]{:S(2)}, u32[]{:S(2)}) collective-permute-start(bf16[128,1024]{1,0:T(8,128)(2,1)S(1)} %broadcast_select_fusion.1), channel_id=1, source_target_pairs={{0,4},{4,0},{8,12},{12,8},{16,20},{20,16},{24,28},{28,24},{1,5},{5... | collective-permute-start | bytes 786440 | tf_op jit(solution)/shard_map/ppermute | solution.py:269
  38.9 1.5 %shard_map.123 = (f32[64,1024]{1,0:T(8,128)S(1)}, bf16[64,1024]{1,0:T(8,128)(2,1)S(1)}, bf16[64,1024]{1,0:T(8,128)(2,1)S(1)}, bf16[64,1024]{1,0:T(8,128)(2,1)S(1)}) custom-call(s32[2]{0:T(128)S(1)} %pad_add_fusion.place_ref, bf16[128,256]{1,0:T(8,128)(2,1)S(1)} %get-tuple-element.55.refs_0_, bf16[128,256]{1,0:T(8,128)(2,1)S(1)} %collective-permute-done.4.refs_1_, ...), custom_call_target="tpu_custom_call" | custom-call | flops 268435456 | bytes 1966080 | tf_op jit(solution)/shard_map/pallas_call | solution.py:71
  40.4 1.5 %collective-permute-start.10 = (bf16[64,1024]{1,0:T(8,128)(2,1)S(1)}, bf16[64,1024]{1,0:T(8,128)(2,1)S(1)}, u32[]{:S(2)}, u32[]{:S(2)}) collective-permute-start(bf16[64,1024]{1,0:T(8,128)(2,1)S(1)} %get-tuple-element.66), channel_id=1, source_target_pairs={{0,4},{4,0},{8,12},{12,8},{16,20},{20,16},{24,28},{28,24},{1,5},{5... | collective-permute-start | bytes 393224 | tf_op jit(solution)/shard_map/ppermute | solution.py:269
  41.9 2.3 %collective-permute-start.11 = (bf16[64,1024]{1,0:T(8,128)(2,1)S(1)}, bf16[64,1024]{1,0:T(8,128)(2,1)S(1)}, u32[]{:S(2)}, u32[]{:S(2)}) collective-permute-start(bf16[64,1024]{1,0:T(8,128)(2,1)S(1)} %get-tuple-element.67), channel_id=1, source_target_pairs={{0,8},{4,12},{8,0},{12,4},{16,24},{20,28},{24,16},{28,20},{1,9},{5... | collective-permute-start | bytes 393224 | tf_op jit(solution)/shard_map/ppermute | solution.py:269
  44.2 0.3 collective-permute-start.12
  44.5 3.1 %collective-permute-done.16.g2 = bf16[128,1024]{1,0:T(8,128)(2,1)S(1)} collective-permute-done((bf16[128,1024]{1,0:T(8,128)(2,1)S(1)}, bf16[128,1024]{1,0:T(8,128)(2,1)S(1)}, u32[]{:S(2)}, u32[]{:S(2)}) %collective-permute-start.16) | collective-permute-done | bytes 262176 | tf_op jit(solution)/shard_map/ppermute | solution.py:265
  47.6 0.9 %collective-permute-start.17 = (bf16[128,1024]{1,0:T(8,128)(2,1)S(1)}, bf16[128,1024]{1,0:T(8,128)(2,1)S(1)}, u32[]{:S(2)}, u32[]{:S(2)}) collective-permute-start(bf16[128,1024]{1,0:T(8,128)(2,1)S(1)} %broadcast_select_fusion), channel_id=1, source_target_pairs={{0,4},{4,0},{8,12},{12,8},{16,20},{20,16},{24,28},{28,24},{1,5},{5... | collective-permute-start | bytes 786440 | tf_op jit(solution)/shard_map/ppermute | solution.py:269
  48.6 2.7 %shard_map.124 = (bf16[128,1024]{1,0:T(8,128)(2,1)}, bf16[128,1024]{1,0:T(8,128)(2,1)}) custom-call(bf16[128,1024]{1,0:T(8,128)(2,1)S(1)} %get-tuple-element.40.k0.k, bf16[128,1024]{1,0:T(8,128)(2,1)S(1)} %collective-permute-done.1.keys.k1, bf16[128,1024]{1,0:T(8,128)(2,1)S(1)} %collective-permute-done.keys.k2, bf16[128,1024]{1,0:T(8,128)(2,1)S(1)} %copy-done.1, ...), custom_call_target="tpu_custom_call" | custom-call | flops 469762048 | bytes 6291456 | tf_op jit(solution)/shard_map/pallas_call | solution.py:71
  51.3 1.8 %collective-permute-done.12.refs_2_ = bf16[64,1024]{1,0:T(8,128)(2,1)S(1)} collective-permute-done((bf16[64,1024]{1,0:T(8,128)(2,1)S(1)}, bf16[64,1024]{1,0:T(8,128)(2,1)S(1)}, u32[]{:S(2)}, u32[]{:S(2)}) %collective-permute-start.12) | collective-permute-done | bytes 131104 | tf_op jit(solution)/shard_map/ppermute | solution.py:269
  53.0 0.1 shard_map.125.mine
  53.1 3.9 %collective-permute-start.13 = (bf16[64,1024]{1,0:T(8,128)(2,1)S(1)}, bf16[64,1024]{1,0:T(8,128)(2,1)S(1)}, u32[]{:S(2)}, u32[]{:S(2)}) collective-permute-start(bf16[64,1024]{1,0:T(8,128)(2,1)S(1)} %shard_map.125.mine), channel_id=1, source_target_pairs={{0,16},{4,20},{8,24},{12,28},{16,0},{20,4},{24,8},{28,12},{1,17},{... | collective-permute-start | bytes 393224 | tf_op jit(solution)/shard_map/ppermute | solution.py:269
  57.0 4.8 %collective-permute-done.13.other = bf16[64,1024]{1,0:T(8,128)(2,1)S(1)} collective-permute-done((bf16[64,1024]{1,0:T(8,128)(2,1)S(1)}, bf16[64,1024]{1,0:T(8,128)(2,1)S(1)}, u32[]{:S(2)}, u32[]{:S(2)}) %collective-permute-start.13) | collective-permute-done | bytes 131104 | tf_op jit(solution)/shard_map/ppermute | solution.py:269
  61.8 1.6 %collective-permute-start.18 = (bf16[64,1024]{1,0:T(8,128)(2,1)S(1)}, bf16[64,1024]{1,0:T(8,128)(2,1)S(1)}, u32[]{:S(2)}, u32[]{:S(2)}) collective-permute-start(bf16[64,1024]{1,0:T(8,128)(2,1)S(1)} %shard_map.126.refs_0_), channel_id=1, source_target_pairs={{0,4},{4,0},{8,12},{12,8},{16,20},{20,16},{24,28},{28,24},{1,5},{5... | collective-permute-start | bytes 393224 | tf_op jit(solution)/shard_map/ppermute | solution.py:269
  63.4 2.0 %collective-permute-start.20 = (bf16[64,1024]{1,0:T(8,128)(2,1)S(1)}, bf16[64,1024]{1,0:T(8,128)(2,1)S(1)}, u32[]{:S(2)}, u32[]{:S(2)}) collective-permute-start(bf16[64,1024]{1,0:T(8,128)(2,1)S(1)} %shard_map.126.refs_0_), channel_id=1, source_target_pairs={{0,12},{4,8},{8,4},{12,0},{16,28},{20,24},{24,20},{28,16},{1,13},{... | collective-permute-start | bytes 393224 | tf_op jit(solution)/shard_map/ppermute | solution.py:269
  65.4 5.0 %shard_map.127 = (bf16[128,1024]{1,0:T(8,128)(2,1)}, bf16[128,1024]{1,0:T(8,128)(2,1)}) custom-call(s32[1,4]{1,0:T(1,128)S(1)} %copy-done.11, s32[2]{0:T(128)S(1)} %pad_add_fusion.place_ref, bf16[128,1024]{1,0:T(8,128)(2,1)S(1)} %get-tuple-element.40.k0.k, bf16[128,1024]{1,0:T(8,128)(2,1)S(1)} %copy-done.1, bf16[128,1024]{1,0:T(8,128)(2,1)S(1)} %get-tuple-element.43.q.q0, ...), custom_call_target="tpu_custom_call" | custom-call | flops 402653184 | bytes 2621440 | tf_op jit(solution)/shard_map/pallas_call | solution.py:71
  70.4 0.8 %collective-permute-done.20.refs_3_ = bf16[64,1024]{1,0:T(8,128)(2,1)S(1)} collective-permute-done((bf16[64,1024]{1,0:T(8,128)(2,1)S(1)}, bf16[64,1024]{1,0:T(8,128)(2,1)S(1)}, u32[]{:S(2)}, u32[]{:S(2)}) %collective-permute-start.20) | collective-permute-done | bytes 131104 | tf_op jit(solution)/shard_map/ppermute | solution.py:269
  71.2 1.6 %shard_map.128 = f32[256,1024]{1,0:T(8,128)} custom-call(s32[2]{0:T(128)S(1)} %pad_add_fusion.place_ref, bf16[64,1024]{1,0:T(8,128)(2,1)S(1)} %shard_map.126.refs_0_, bf16[64,1024]{1,0:T(8,128)(2,1)S(1)} %collective-permute-done.18.refs_1_, bf16[64,1024]{1,0:T(8,128)(2,1)S(1)} %collective-permute-done.19.refs_2_, ...), custom_call_target="tpu_custom_call" | custom-call | flops 262144 | bytes 1572864 | tf_op jit(solution)/shard_map/pallas_call | solution.py:71
  (33 shorter events, 0.2 us)
Async XLA Ops:
  0.6 18.6 %collective-permute-start = (bf16[128,1024]{1,0:T(8,128)(2,1)}, bf16[128,1024]{1,0:T(8,128)(2,1)S(1)}, u32[]{:S(2)}, u32[]{:S(2)}) collective-permute-start(bf16[128,1024]{1,0:T(8,128)(2,1)} %bitcast.14), channel_id=1, source_target_pairs={{0,8},{4,12},{8,16},{12,20},{16,24},{20,28},{1,9},{5,13},{9,17},{1... | collective-permute-start | bytes 786440 | tf_op jit(solution)/shard_map/ppermute | solution.py:265
  5.6 17.7 %collective-permute-start.3 = (bf16[128,1024]{1,0:T(8,128)(2,1)}, bf16[128,1024]{1,0:T(8,128)(2,1)S(1)}, u32[]{:S(2)}, u32[]{:S(2)}) collective-permute-start(bf16[128,1024]{1,0:T(8,128)(2,1)} %bitcast.16), channel_id=1, source_target_pairs={{0,8},{4,12},{8,16},{12,20},{16,24},{20,28},{1,9},{5,13},{9,17},{1... | collective-permute-start | bytes 786440 | tf_op jit(solution)/shard_map/ppermute | solution.py:265
  9.1 15.5 %collective-permute-start.8 = (bf16[128,1024]{1,0:T(8,128)(2,1)}, bf16[128,1024]{1,0:T(8,128)(2,1)}, u32[]{:S(2)}, u32[]{:S(2)}) collective-permute-start(bf16[128,1024]{1,0:T(8,128)(2,1)} %bitcast.19), channel_id=1, source_target_pairs={{0,2},{1,3},{2,0},{3,1},{4,6},{5,7},{6,4},{7,5},{8,10},{9,11},{10,... | collective-permute-start | bytes 786440 | tf_op jit(solution)/shard_map/ppermute | solution.py:269
  10.7 0.7 copy-start.10
  11.4 13.8 %copy-start.11 = (s32[1,4]{1,0:T(1,128)S(1)}, s32[1,4]{1,0:T(1,128)}, u32[]{:S(2)}) copy-start(s32[1,4]{1,0:T(1,128)} %len_ref.7) | copy-start | bytes 52
  15.4 0.7 copy-start
  16.1 0.8 %copy-start.2 = (f32[128,1024]{1,0:T(8,128)}, f32[128,1024]{1,0:T(8,128)S(1)}, u32[]{:S(2)}) copy-start(f32[128,1024]{1,0:T(8,128)S(1)} %get-tuple-element.47.grad_hidden) | copy-start | bytes 1572868
  16.9 0.8 %copy-start.4 = (f32[128,1024]{1,0:T(8,128)}, f32[128,1024]{1,0:T(8,128)S(1)}, u32[]{:S(2)}) copy-start(f32[128,1024]{1,0:T(8,128)S(1)} %get-tuple-element.45.mixed_own) | copy-start | bytes 1572868
  17.7 0.8 %copy-start.6 = (f32[128,1024]{1,0:T(8,128)}, f32[128,1024]{1,0:T(8,128)S(1)}, u32[]{:S(2)}) copy-start(f32[128,1024]{1,0:T(8,128)S(1)} %get-tuple-element.42.slope0) | copy-start | bytes 1572868
  18.5 0.7 copy-start.8
  19.2 13.7 %copy-start.3 = (f32[128,1024]{1,0:T(8,128)S(1)}, f32[128,1024]{1,0:T(8,128)}, u32[]{:S(2)}) copy-start(f32[128,1024]{1,0:T(8,128)} %copy-done.2) | copy-start | bytes 1572868
  19.2 9.0 %collective-permute-start.1 = (bf16[128,1024]{1,0:T(8,128)(2,1)S(1)}, bf16[128,1024]{1,0:T(8,128)(2,1)S(1)}, u32[]{:S(2)}, u32[]{:S(2)}) collective-permute-start(bf16[128,1024]{1,0:T(8,128)(2,1)S(1)} %broadcast_select_fusion.2), channel_id=1, source_target_pairs={{0,4},{4,0},{8,12},{12,8},{16,20},{20,16},{24,28},{28,24},{1,5},{5... | collective-permute-start | bytes 786440 | tf_op jit(solution)/shard_map/ppermute | solution.py:269
  20.8 10.4 %collective-permute-start.2 = (bf16[128,1024]{1,0:T(8,128)(2,1)}, bf16[128,1024]{1,0:T(8,128)(2,1)S(1)}, u32[]{:S(2)}, u32[]{:S(2)}) collective-permute-start(bf16[128,1024]{1,0:T(8,128)(2,1)} %bitcast.18), channel_id=1, source_target_pairs={{0,4},{4,8},{8,12},{12,16},{16,20},{20,24},{24,28},{1,5},{5,9},{9,... | collective-permute-start | bytes 786440 | tf_op jit(solution)/shard_map/ppermute | solution.py:265
  23.2 10.6 %collective-permute-start.7 = (bf16[128,1024]{1,0:T(8,128)(2,1)}, bf16[128,1024]{1,0:T(8,128)(2,1)S(1)}, u32[]{:S(2)}, u32[]{:S(2)}) collective-permute-start(bf16[128,1024]{1,0:T(8,128)(2,1)} %bitcast.21), channel_id=1, source_target_pairs={{0,1},{1,0},{2,3},{3,2},{4,5},{5,4},{6,7},{7,6},{8,9},{9,8},{10,11... | collective-permute-start | bytes 786440 | tf_op jit(solution)/shard_map/ppermute | solution.py:269
  23.3 11.8 %collective-permute-start.14 = (bf16[128,1024]{1,0:T(8,128)(2,1)S(1)}, bf16[128,1024]{1,0:T(8,128)(2,1)S(1)}, u32[]{:S(2)}, u32[]{:S(2)}) collective-permute-start(bf16[128,1024]{1,0:T(8,128)(2,1)S(1)} %get-tuple-element.43.q.q0), channel_id=1, source_target_pairs={{8,0},{12,4},{16,8},{20,12},{24,16},{28,20},{9,1},{13,5},{17,9},{2... | collective-permute-start | bytes 786440 | tf_op jit(solution)/shard_map/ppermute | solution.py:265
  24.6 11.8 %collective-permute-start.9 = (bf16[128,1024]{1,0:T(8,128)(2,1)}, bf16[128,1024]{1,0:T(8,128)(2,1)S(1)}, u32[]{:S(2)}, u32[]{:S(2)}) collective-permute-start(bf16[128,1024]{1,0:T(8,128)(2,1)} %collective-permute-done.8.refs_6_), channel_id=1, source_target_pairs={{0,1},{1,0},{2,3},{3,2},{4,5},{5,4},{6,7},{7,6},{8,9},{9,8},{10,11... | collective-permute-start | bytes 786440 | tf_op jit(solution)/shard_map/ppermute | solution.py:269
  25.2 1.0 %copy-start.5 = (f32[128,1024]{1,0:T(8,128)S(1)}, f32[128,1024]{1,0:T(8,128)}, u32[]{:S(2)}) copy-start(f32[128,1024]{1,0:T(8,128)} %copy-done.4) | copy-start | bytes 1572868
  28.2 10.6 %copy-start.9 = (bf16[128,1024]{1,0:T(8,128)(2,1)S(1)}, bf16[128,1024]{1,0:T(8,128)(2,1)}, u32[]{:S(2)}) copy-start(bf16[128,1024]{1,0:T(8,128)(2,1)} %copy-done.8) | copy-start | bytes 786436
  32.3 6.6 %collective-permute-start.4 = (bf16[128,256]{1,0:T(8,128)(2,1)S(1)}, bf16[128,256]{1,0:T(8,128)(2,1)S(1)}, u32[]{:S(2)}, u32[]{:S(2)}) collective-permute-start(bf16[128,256]{1,0:T(8,128)(2,1)S(1)} %get-tuple-element.56), channel_id=1, source_target_pairs={{0,1},{1,0},{2,3},{3,2},{4,5},{5,4},{6,7},{7,6},{8,9},{9,8},{10,11... | collective-permute-start | bytes 196616 | tf_op jit(solution)/shard_map/ppermute | solution.py:269
  32.3 6.5 %collective-permute-start.5 = (bf16[128,256]{1,0:T(8,128)(2,1)S(1)}, bf16[128,256]{1,0:T(8,128)(2,1)S(1)}, u32[]{:S(2)}, u32[]{:S(2)}) collective-permute-start(bf16[128,256]{1,0:T(8,128)(2,1)S(1)} %get-tuple-element.57), channel_id=1, source_target_pairs={{0,2},{1,3},{2,0},{3,1},{4,6},{5,7},{6,4},{7,5},{8,10},{9,11},{10,... | collective-permute-start | bytes 196616 | tf_op jit(solution)/shard_map/ppermute | solution.py:269
  32.9 15.6 %copy-start.1 = (bf16[128,1024]{1,0:T(8,128)(2,1)S(1)}, bf16[128,1024]{1,0:T(8,128)(2,1)}, u32[]{:S(2)}) copy-start(bf16[128,1024]{1,0:T(8,128)(2,1)} %copy-done) | copy-start | bytes 786436
  32.9 15.6 %copy-start.7 = (f32[128,1024]{1,0:T(8,128)S(1)}, f32[128,1024]{1,0:T(8,128)}, u32[]{:S(2)}) copy-start(f32[128,1024]{1,0:T(8,128)} %copy-done.6) | copy-start | bytes 1572868
  33.8 5.1 %collective-permute-start.6 = (bf16[128,256]{1,0:T(8,128)(2,1)S(1)}, bf16[128,256]{1,0:T(8,128)(2,1)S(1)}, u32[]{:S(2)}, u32[]{:S(2)}) collective-permute-start(bf16[128,256]{1,0:T(8,128)(2,1)S(1)} %get-tuple-element.58), channel_id=1, source_target_pairs={{0,3},{1,2},{2,1},{3,0},{4,7},{5,6},{6,5},{7,4},{8,11},{9,10},{10,... | collective-permute-start | bytes 196616 | tf_op jit(solution)/shard_map/ppermute | solution.py:269
  35.1 12.5 %collective-permute-start.16 = (bf16[128,1024]{1,0:T(8,128)(2,1)S(1)}, bf16[128,1024]{1,0:T(8,128)(2,1)S(1)}, u32[]{:S(2)}, u32[]{:S(2)}) collective-permute-start(bf16[128,1024]{1,0:T(8,128)(2,1)S(1)} %get-tuple-element.53.grad_mix.g0), channel_id=1, source_target_pairs={{8,0},{12,4},{16,8},{20,12},{24,16},{28,20},{9,1},{13,5},{17,9},{2... | collective-permute-start | bytes 786440 | tf_op jit(solution)/shard_map/ppermute | solution.py:265
  36.4 29.0 %collective-permute-start.15 = (bf16[128,1024]{1,0:T(8,128)(2,1)S(1)}, bf16[128,1024]{1,0:T(8,128)(2,1)S(1)}, u32[]{:S(2)}, u32[]{:S(2)}) collective-permute-start(bf16[128,1024]{1,0:T(8,128)(2,1)S(1)} %broadcast_select_fusion.1), channel_id=1, source_target_pairs={{0,4},{4,0},{8,12},{12,8},{16,20},{20,16},{24,28},{28,24},{1,5},{5... | collective-permute-start | bytes 786440 | tf_op jit(solution)/shard_map/ppermute | solution.py:269
  40.4 10.9 %collective-permute-start.10 = (bf16[64,1024]{1,0:T(8,128)(2,1)S(1)}, bf16[64,1024]{1,0:T(8,128)(2,1)S(1)}, u32[]{:S(2)}, u32[]{:S(2)}) collective-permute-start(bf16[64,1024]{1,0:T(8,128)(2,1)S(1)} %get-tuple-element.66), channel_id=1, source_target_pairs={{0,4},{4,0},{8,12},{12,8},{16,20},{20,16},{24,28},{28,24},{1,5},{5... | collective-permute-start | bytes 393224 | tf_op jit(solution)/shard_map/ppermute | solution.py:269
  41.9 9.4 %collective-permute-start.11 = (bf16[64,1024]{1,0:T(8,128)(2,1)S(1)}, bf16[64,1024]{1,0:T(8,128)(2,1)S(1)}, u32[]{:S(2)}, u32[]{:S(2)}) collective-permute-start(bf16[64,1024]{1,0:T(8,128)(2,1)S(1)} %get-tuple-element.67), channel_id=1, source_target_pairs={{0,8},{4,12},{8,0},{12,4},{16,24},{20,28},{24,16},{28,20},{1,9},{5... | collective-permute-start | bytes 393224 | tf_op jit(solution)/shard_map/ppermute | solution.py:269
  44.2 8.8 %collective-permute-start.12 = (bf16[64,1024]{1,0:T(8,128)(2,1)S(1)}, bf16[64,1024]{1,0:T(8,128)(2,1)S(1)}, u32[]{:S(2)}, u32[]{:S(2)}) collective-permute-start(bf16[64,1024]{1,0:T(8,128)(2,1)S(1)} %get-tuple-element.68), channel_id=1, source_target_pairs={{0,12},{4,8},{8,4},{12,0},{16,28},{20,24},{24,20},{28,16},{1,13},{... | collective-permute-start | bytes 393224 | tf_op jit(solution)/shard_map/ppermute | solution.py:269
  47.6 17.7 %collective-permute-start.17 = (bf16[128,1024]{1,0:T(8,128)(2,1)S(1)}, bf16[128,1024]{1,0:T(8,128)(2,1)S(1)}, u32[]{:S(2)}, u32[]{:S(2)}) collective-permute-start(bf16[128,1024]{1,0:T(8,128)(2,1)S(1)} %broadcast_select_fusion), channel_id=1, source_target_pairs={{0,4},{4,0},{8,12},{12,8},{16,20},{20,16},{24,28},{28,24},{1,5},{5... | collective-permute-start | bytes 786440 | tf_op jit(solution)/shard_map/ppermute | solution.py:269
  53.1 8.7 %collective-permute-start.13 = (bf16[64,1024]{1,0:T(8,128)(2,1)S(1)}, bf16[64,1024]{1,0:T(8,128)(2,1)S(1)}, u32[]{:S(2)}, u32[]{:S(2)}) collective-permute-start(bf16[64,1024]{1,0:T(8,128)(2,1)S(1)} %shard_map.125.mine), channel_id=1, source_target_pairs={{0,16},{4,20},{8,24},{12,28},{16,0},{20,4},{24,8},{28,12},{1,17},{... | collective-permute-start | bytes 393224 | tf_op jit(solution)/shard_map/ppermute | solution.py:269
  61.8 8.5 %collective-permute-start.18 = (bf16[64,1024]{1,0:T(8,128)(2,1)S(1)}, bf16[64,1024]{1,0:T(8,128)(2,1)S(1)}, u32[]{:S(2)}, u32[]{:S(2)}) collective-permute-start(bf16[64,1024]{1,0:T(8,128)(2,1)S(1)} %shard_map.126.refs_0_), channel_id=1, source_target_pairs={{0,4},{4,0},{8,12},{12,8},{16,20},{20,16},{24,28},{28,24},{1,5},{5... | collective-permute-start | bytes 393224 | tf_op jit(solution)/shard_map/ppermute | solution.py:269
  63.4 6.9 %collective-permute-start.19 = (bf16[64,1024]{1,0:T(8,128)(2,1)S(1)}, bf16[64,1024]{1,0:T(8,128)(2,1)S(1)}, u32[]{:S(2)}, u32[]{:S(2)}) collective-permute-start(bf16[64,1024]{1,0:T(8,128)(2,1)S(1)} %shard_map.126.refs_0_), channel_id=1, source_target_pairs={{0,8},{4,12},{8,0},{12,4},{16,24},{20,28},{24,16},{28,20},{1,9},{5... | collective-permute-start | bytes 393224 | tf_op jit(solution)/shard_map/ppermute | solution.py:269
  63.4 7.7 %collective-permute-start.20 = (bf16[64,1024]{1,0:T(8,128)(2,1)S(1)}, bf16[64,1024]{1,0:T(8,128)(2,1)S(1)}, u32[]{:S(2)}, u32[]{:S(2)}) collective-permute-start(bf16[64,1024]{1,0:T(8,128)(2,1)S(1)} %shard_map.126.refs_0_), channel_id=1, source_target_pairs={{0,12},{4,8},{8,4},{12,0},{16,28},{20,24},{24,20},{28,16},{1,13},{... | collective-permute-start | bytes 393224 | tf_op jit(solution)/shard_map/ppermute | solution.py:269

commit v5 on v4

v5 whole, which is shorter than its diff:
```python
import functools
import math

import jax
import jax.numpy as jnp
from jax import lax
from jax.experimental import pallas as pl
from jax.experimental.pallas import tpu as pltpu
from jax.sharding import PartitionSpec as P

HEADS = 8
WINDOW = 256
REACH = 2
CHUNKS = 4

VMEM = pl.BlockSpec(memory_space=pltpu.VMEM)
SMEM = pl.BlockSpec(memory_space=pltpu.SMEM)
F32 = jnp.float32
BF16 = jnp.bfloat16
NT = (((1,), (1,)), ((), ()))
TN = (((0,), (0,)), ((), ()))


def dot(a, b):
    return jnp.dot(a, b, preferred_element_type=F32)


def dot_nt(a, b):
    return lax.dot_general(a, b, NT, preferred_element_type=F32)


def dot_tn(a, b):
    return lax.dot_general(a, b, TN, preferred_element_type=F32)


def logistic(scores):
    return 0.5 * jnp.tanh(0.5 * scores) + 0.5


def silu_slope(scores, gate):
    return gate * (1.0 + scores * (1.0 - gate))


def start_of(positions, len_ref):
    total = jnp.zeros_like(positions)
    end = jnp.int32(0)
    for k in range(len_ref.shape[1]):
        length = len_ref[0, k]
        end = end + length
        total = total + jnp.where(positions >= end, length, 0)
    return total


def allowed_block(rows, first_query, first_key, len_ref, query_dim):
    shape = (rows, rows)
    query_pos = first_query + lax.broadcasted_iota(jnp.int32, shape, query_dim)
    key_pos = first_key + lax.broadcasted_iota(jnp.int32, shape, 1 - query_dim)
    start = start_of(query_pos, len_ref)
    return (key_pos >= start) & (key_pos <= query_pos) & (key_pos > query_pos - WINDOW)


def head_slice(h, width):
    return slice(h * width, (h + 1) * width)


def kept(shape, dtype):
    return pltpu.VMEM(shape, dtype)


def in_hbm(array):
    return pltpu.with_memory_space_constraint(array, pltpu.HBM)


def nbytes(arrays):
    return sum(math.prod(a.shape) * jnp.dtype(a.dtype).itemsize for a in arrays)


def call(kernel, outs, scalars, arrays, flops, scratch=(), spaces=None, out_space=VMEM, aliases={}):
    return pl.pallas_call(
        kernel,
        out_shape=outs,
        in_specs=[SMEM] * len(scalars) + (spaces or [VMEM] * len(arrays)),
        out_specs=[out_space] * len(outs),
        scratch_shapes=list(scratch),
        input_output_aliases=aliases,
        cost_estimate=pl.CostEstimate(
            flops=flops, bytes_accessed=nbytes([*arrays, *outs]), transcendentals=0
        ),
        compiler_params=pltpu.CompilerParams(vmem_limit_bytes=32 * 1024 * 1024),
    )(*scalars, *arrays)


def own_kernel(len_ref, place_ref, q_in, k_in, v_in, q, k, v, mixed, slope, sems):
    moves = [
        pltpu.make_async_copy(src, dst, sems.at[i])
        for i, (src, dst) in enumerate(((q_in, q), (k_in, k), (v_in, v)))
    ]
    for move in moves:
        move.start()
    rows, width = q.shape
    size = width // HEADS
    first = place_ref[0] * rows
    allowed = allowed_block(rows, first, first, len_ref, 0)
    for move in moves:
        move.wait()
    for h in range(HEADS):
        cols = head_slice(h, size)
        attention = block_scores(h, allowed, q, k, slope)
        mixed[:, cols] = dot(attention, v[:, cols])


def project_kernel(grad_in, w_in, gate_in, grad, w, gates, grad_hidden, sems):
    width = w.shape[0]
    part = width // CHUNKS
    moves = [pltpu.make_async_copy(grad_in, grad, sems.at[0])]
    for c in range(CHUNKS):
        here = pl.ds(c * part, part)
        moves.append(pltpu.make_async_copy(w_in.at[here, :], w.at[here, :], sems.at[c + 1]))
    moves.append(pltpu.make_async_copy(gate_in, gates, sems.at[CHUNKS + 1]))
    for move in moves:
        move.start()
    moves[0].wait()
    for c in range(CHUNKS):
        moves[c + 1].wait()
        here = slice(c * part, (c + 1) * part)
        grad_hidden[:, here] = dot_nt(grad[...], w[here, :])
    moves[-1].wait()


def block_scores(h, allowed, q, keys, slope):
    size = q.shape[1] // HEADS
    scale = size ** (-0.5)
    cols = head_slice(h, size)
    scores = dot_nt(q[:, cols], keys[:, cols]) * scale
    gate = logistic(scores)
    slope[:, cols] = jnp.where(allowed, silu_slope(scores, gate) * scale, 0.0)
    return jnp.where(allowed, scores * gate, 0.0).astype(BF16)


def second_kernel(len_ref, place_ref, q, keys, vals, mixed_own, mixed, slope):
    rows, width = q.shape
    size = width // HEADS
    first = place_ref[0] * rows
    allowed = allowed_block(rows, first, first - 2 * rows, len_ref, 0)
    for h in range(HEADS):
        cols = head_slice(h, size)
        attention = block_scores(h, allowed, q, keys, slope)
        mixed[:, cols] = mixed_own[:, cols] + dot(attention, vals[:, cols])


def first_kernel(len_ref, place_ref, q, keys, attention, slope):
    rows, width = q.shape
    size = width // HEADS
    first = place_ref[0] * rows
    allowed = allowed_block(rows, first, first - rows, len_ref, 0)
    for h in range(HEADS):
        attention[:, head_slice(h, size)] = block_scores(h, allowed, q, keys, slope)


def forward_kernel(groups, place_ref, attention, vals, mixed_far, gates, hidden, normed, inv_std, *rest):
    slices, mixed = rest[:-1], rest[-1]
    rows, width = vals.shape
    size = width // HEADS
    for h in range(HEADS):
        cols = head_slice(h, size)
        mixed[:, cols] = mixed_far[:, cols] + dot(attention[:, cols], vals[:, cols])
    values = mixed[...]
    centered = values - jnp.mean(values, axis=1, keepdims=True)
    inverse = lax.rsqrt(jnp.mean(centered * centered, axis=1, keepdims=True) + 1e-05)
    inv_std[...] = jnp.broadcast_to(inverse, inv_std.shape)
    normed[...] = centered * inverse
    hidden[...] = (normed[...] * gates[...].astype(F32)).astype(BF16)
    part = width // groups
    for d, ref in enumerate(slices):
        at = pl.multiple_of((place_ref[1] ^ d) * part, 128)
        ref[...] = hidden[:, pl.ds(at, part)]


def mix_kernel(grad_hidden, gates, normed, inv_std, grad_gates, grad_mix):
    gh = grad_hidden[...]
    norm = normed[...]
    grad_gates[...] = (gh * norm).astype(BF16)
    grad_norm = gh * gates[...].astype(F32)
    grad_mix[...] = (
        (
            grad_norm
            - jnp.mean(grad_norm, axis=1, keepdims=True)
            - norm * jnp.mean(grad_norm * norm, axis=1, keepdims=True)
        )
        * inv_std[:, :1]
    ).astype(BF16)


def query_kernel(k0, k1, k2, v0, v1, v2, slope0, slope1, slope2, grad_mix, hidden, w, output, grad_queries):
    rows, width = k0.shape
    size = width // HEADS
    output[...] = dot(hidden[...], w[...]).astype(BF16)
    parts = ((k0, v0, slope0), (k1, v1, slope1), (k2, v2, slope2))
    for h in range(HEADS):
        cols = head_slice(h, size)
        total = jnp.zeros((rows, size), F32)
        for keys, vals, slope in parts:
            grad_attention = dot_nt(grad_mix[:, cols], vals[:, cols])
            grad_scores = (grad_attention * slope[:, cols]).astype(BF16)
            total = total + dot(grad_scores, keys[:, cols])
        grad_queries[:, cols] = total.astype(BF16)


def key_terms(h, mask, k, v, qd, gd):
    size = k.shape[1] // HEADS
    scale = size ** (-0.5)
    cols = head_slice(h, size)
    scores = dot_nt(k[:, cols], qd[:, cols]) * scale
    gate = logistic(scores)
    attention = jnp.where(mask, scores * gate, 0.0).astype(BF16)
    grad_attention = dot_nt(v[:, cols], gd[:, cols])
    slope = jnp.where(mask, silu_slope(scores, gate) * scale, 0.0)
    grad_scores = (grad_attention * slope).astype(BF16)
    return dot(grad_scores, qd[:, cols]), dot(attention, gd[:, cols])


def key_kernel(len_ref, place_ref, k, v, q0, q2, g0, g2, keys_total, values_total):
    rows, width = k.shape
    first = place_ref[0] * rows
    masks = [allowed_block(rows, first + d * rows, first, len_ref, 1) for d in (0, 2)]
    for h in range(HEADS):
        cols = head_slice(h, width // HEADS)
        own = key_terms(h, masks[0], k, v, q0, g0)
        far = key_terms(h, masks[1], k, v, q2, g2)
        keys_total[:, cols] = own[0] + far[0]
        values_total[:, cols] = own[1] + far[1]


def key_end_kernel(len_ref, place_ref, k, v, q1, g1, keys_part, values_part, grad_keys, grad_values):
    rows, width = k.shape
    first = place_ref[0] * rows
    mask = allowed_block(rows, first + rows, first, len_ref, 1)
    for h in range(HEADS):
        cols = head_slice(h, width // HEADS)
        near = key_terms(h, mask, k, v, q1, g1)
        grad_keys[:, cols] = (keys_part[:, cols] + near[0]).astype(BF16)
        grad_values[:, cols] = (values_part[:, cols] + near[1]).astype(BF16)


def weight_kernel(groups, place_ref, *refs):
    hidden = jnp.concatenate([ref[...] for ref in refs[:groups]], axis=0)
    grads = jnp.concatenate([ref[...] for ref in refs[groups : 2 * groups]], axis=0)
    own = refs[2 * groups]
    sends = refs[2 * groups + 1 : -1]
    total = refs[-1]
    total[...] = dot_tn(hidden, grads)
    if not sends:
        own[...] = total[...]
        return
    rows = own.shape[0]
    corner = place_ref[0] & len(sends)
    own[...] = total[pl.ds(pl.multiple_of(corner * rows, rows), rows), :]
    for e, ref in enumerate(sends):
        at = pl.multiple_of((corner ^ (e + 1)) * rows, rows)
        ref[...] = total[pl.ds(at, rows), :].astype(BF16)


def corner_kernel(own, *refs):
    got, narrow = refs[:-1], refs[-1]
    acc = own[...]
    for ref in got:
        acc = acc + ref[...].astype(F32)
    narrow[...] = acc.astype(BF16)


def pair_kernel(scale, mine, other, both):
    both[...] = ((mine[...].astype(F32) + other[...].astype(F32)) * scale).astype(BF16)


def place_kernel(corners, partner, place_ref, share, *refs):
    out, wide, sem = refs[-3:]
    rows = share.shape[0]
    corner = (place_ref[0] & (corners - 1)) ^ partner
    wide[...] = share[...].astype(F32)
    at = pl.multiple_of(corner * rows, rows)
    move = pltpu.make_async_copy(wide, out.at[pl.ds(at, rows), :], sem)
    move.start()
    move.wait()


def xor_route(size, mask):
    return [(i, i ^ mask) for i in range(size)]


def shifted(block, distance):
    count = lax.axis_size("seq")
    route = [(i, i + distance) for i in range(count) if 0 <= i + distance < count]
    return lax.ppermute(block, "seq", route)


def swapped(block, axis, mask):
    return lax.ppermute(block, axis, xor_route(lax.axis_size(axis), mask))


def after(value, *others):
    return lax.optimization_barrier((value, *others))[0]


def on_device(queries, keys, values, gates, out_grad, w_out, hist_lengths):
    rows, width = queries.shape[1:]
    seq = lax.axis_size("seq")
    batch = lax.axis_size("batch")
    seq_at = lax.axis_index("seq")
    place = jnp.stack([seq_at, lax.axis_index("batch")]).astype(jnp.int32)
    scalars = (hist_lengths, place)
    even = (seq_at & 1) == 0
    full = jax.ShapeDtypeStruct((rows, width), BF16)
    near = kept((rows, width), BF16)
    wide = kept((rows, width), F32)
    block_flops = 2 * rows * rows * width
    proj_flops = 2 * rows * width * width
    part = width // batch
    hbm = pl.BlockSpec(memory_space=pltpu.HBM)

    k2 = shifted(keys[0], 2)
    v2 = shifted(values[0], 2)
    q, k, v, mixed_own, slope0 = call(
        own_kernel,
        [near, near, near, wide, wide],
        scalars,
        (in_hbm(queries[0]), in_hbm(keys[0]), in_hbm(values[0])),
        2 * block_flops,
        [pltpu.SemaphoreType.DMA((3,))],
        [hbm] * 3,
    )
    passed = jnp.where(even, k, k2)
    k1 = swapped(passed, "seq", 1)
    v1 = shifted(v, 1)
    grad, w, gate, grad_hidden = call(
        project_kernel,
        [near, kept(w_out.shape, BF16), near, wide],
        (),
        (in_hbm(after(out_grad[0], passed)), in_hbm(w_out), in_hbm(gates[0])),
        proj_flops,
        [pltpu.SemaphoreType.DMA((CHUNKS + 2,))],
        [hbm] * 3,
    )
    grads = [grad]
    for d in range(1, batch):
        low = d & -d
        source = out_grad[0] if d == low else grads[d ^ low]
        grads.append(swapped(after(source, v2) if d == 1 else source, "batch", low))
    q2 = shifted(q, -2)
    mixed_far, slope2 = call(
        second_kernel, [wide, wide], scalars, (after(q, grads[-2]), k2, v2, mixed_own), 2 * block_flops
    )
    passed_q = jnp.where(even, q2, q)
    q1 = swapped(passed_q, "seq", 1)
    attention1, slope1 = call(first_kernel, [near, wide], scalars, (after(q, passed_q, grads[1], grads[-1]), k1), block_flops)
    hidden, normed, inv_std, *slices = call(
        functools.partial(forward_kernel, batch),
        [near, wide, kept((rows, 128), F32)] + [kept((rows, part), BF16)] * batch,
        (place,),
        (attention1, v1, mixed_far, gate),
        block_flops,
        [pltpu.VMEM((rows, width), F32)],
    )
    hiddens = [slices[0]] + [swapped(slices[d], "batch", d) for d in range(1, batch)]
    grad_gates, grad_mix = call(
        mix_kernel, [full, near], (), (grad_hidden, gate, normed, inv_std), block_flops // 4
    )
    g2 = shifted(grad_mix, -2)
    passed_g = jnp.where(even, g2, grad_mix)

    corners = 4
    direct = seq == 2 * corners
    rows_w = part // corners if direct else part
    share = kept((rows_w, width), BF16)
    scale = (rows * seq * batch) ** (-0.5)
    own, *sends = call(
        functools.partial(weight_kernel, batch),
        [kept((rows_w, width), F32)] + [share] * (corners - 1 if direct else 0),
        (place,),
        (*hiddens, *grads),
        proj_flops,
        [pltpu.VMEM((part, width), F32)],
    )
    keys_part, values_part = call(
        key_kernel,
        [wide, wide],
        scalars,
        (k, after(v, own), q, q2, grad_mix, g2),
        8 * block_flops,
    )
    hidden_late = hidden
    if direct:
        got = [swapped(s, "seq", e + 1) for e, s in enumerate(sends)]
        (mine,) = call(corner_kernel, [share], (), (after(own, keys_part), *got), own.size * 4)
        other = swapped(mine, "seq", corners)
        passed_g = after(passed_g, got[0])
        hidden_late = after(hidden, mine)
    output, grad_queries = call(
        query_kernel,
        [full, full],
        (),
        (k, k1, k2, v, v1, v2, slope0, slope1, slope2, grad_mix, hidden_late, w),
        proj_flops + 6 * block_flops,
    )
    g1 = swapped(passed_g, "seq", 1)
    last = v
    if direct:
        (both,) = call(
            functools.partial(pair_kernel, scale),
            [share],
            (),
            (after(mine, output), other),
            own.size * 2,
        )
        last = after(v, both)
    grad_keys, grad_values = call(
        key_end_kernel,
        [full, full],
        scalars,
        (k, last, q1, g1, keys_part, values_part),
        4 * block_flops,
    )
    if direct:
        result = jax.ShapeDtypeStruct((part, width), F32)
        shares = [after(both, grad_keys)] + [swapped(both, "seq", e) for e in range(1, corners)]
        grad_weight = None
        for e, piece in enumerate(shares):
            (grad_weight,) = call(
                functools.partial(place_kernel, corners, e),
                [result],
                (place,),
                (piece,) if e == 0 else (piece, grad_weight),
                piece.size,
                [pltpu.VMEM((rows_w, width), F32), pltpu.SemaphoreType.DMA(())],
                spaces=[VMEM] if e == 0 else [VMEM, hbm],
                out_space=hbm,
                aliases={} if e == 0 else {2: 0},
            )
    else:
        grad_weight = lax.psum(own, "seq") * scale
    return (
        output[None],
        grad_queries[None],
        grad_keys[None],
        grad_values[None],
        grad_gates[None],
        grad_weight,
    )


def solution(mesh):
    token = P("batch", "seq", None)
    return jax.shard_map(
        on_device,
        mesh=mesh,
        in_specs=(token, token, token, token, token, P(), P("batch", None)),
        out_specs=(token, token, token, token, token, P("batch", None)),
        check_vma=False,
    )
```

time: 73 us -> 72.5 us (level)
  Pallas kernels: 19.7 us -> 25.5 us
  local copies, waits for them, and re-layouts: 5.51 us -> 0.66 us
  waiting for transfers between devices: 12.4 us -> 8.24 us
  starting transfers between devices: 34.1 us -> 36.8 us
    pallas_call x11 -> x16, Pallas kernels: 19.7 us -> 25.5 us  [call(): pl.pallas_call(kernel, out_shape=outs, in_specs=[SMEM] * len(scalars) + (...]
    unnamed x24 -> x4, local copies, waits for them, and re-layouts: 5.51 us -> 0.66 us
    ppermute x5, waiting for transfers between devices: 5.04 us -> 0.47 us  [shifted(): return lax.ppermute(block, 'seq', route)]
    ppermute x16, starting transfers between devices: 20.6 us -> 22.4 us  [swapped(): return lax.ppermute(block, axis, xor_route(lax.axis_size(axis), mask))]
    ppermute x5, starting transfers between devices: 13.5 us -> 14.4 us  [shifted(): return lax.ppermute(block, 'seq', route)]
  transfers between devices with their start and end apart: 21 -> 21, of which waited for: 5 -> 7; matrix products, arithmetic and copies ran while one was open for 0% -> 0% of each run, Pallas kernels for 25% -> 31%
where the time goes in v5:
time: 72.5 us; the launch traced here: 72.2 us
  starting transfers between devices  36.8 us (51%)
  Pallas kernels  25.5 us (35%)
  waiting for transfers between devices  8.24 us (11%)
  between operations  0.87 us (1%)
    pallas_call x16, Pallas kernels, call(): pl.pallas_call(kernel, out_shape=outs, in_specs=[SMEM] * len(scalars) + (...  25.5 us
    ppermute x16, starting transfers between devices, swapped(): return lax.ppermute(block, axis, xor_route(lax.axis_size(axis), mask))  22.4 us
    ppermute x5, starting transfers between devices, shifted(): return lax.ppermute(block, 'seq', route)  14.4 us
    ppermute x16, waiting for transfers between devices, swapped(): return lax.ppermute(block, axis, xor_route(lax.axis_size(axis), mask))  7.77 us
  transfers between devices with their start and end apart: 21, of which 7 were waited for; matrix products, arithmetic and copies ran while one was open for 0% of the time, Pallas kernels for 31%

profile of v5, /device:TPU:0, one launch (start us, length us, event | category | flops | bytes accessed | tf_op | source)
XLA Modules:
  0.0 72.2 jit_solution(1718895913049994295)
XLA Ops:
  0.6 4.9 %collective-permute-start = (bf16[128,1024]{1,0:T(8,128)(2,1)}, bf16[128,1024]{1,0:T(8,128)(2,1)S(1)}, u32[]{:S(2)}, u32[]{:S(2)}) collective-permute-start(bf16[128,1024]{1,0:T(8,128)(2,1)} %bitcast.17), channel_id=1, source_target_pairs={{0,8},{4,12},{8,16},{12,20},{16,24},{20,28},{1,9},{5,13},{9,17},{1... | collective-permute-start | bytes 786440 | tf_op jit(solution)/shard_map/ppermute | solution.py:293
  5.6 3.5 %collective-permute-start.3 = (bf16[128,1024]{1,0:T(8,128)(2,1)}, bf16[128,1024]{1,0:T(8,128)(2,1)S(1)}, u32[]{:S(2)}, u32[]{:S(2)}) collective-permute-start(bf16[128,1024]{1,0:T(8,128)(2,1)} %bitcast.19), channel_id=1, source_target_pairs={{0,8},{4,12},{8,16},{12,20},{16,24},{20,28},{1,9},{5,13},{9,17},{1... | collective-permute-start | bytes 786440 | tf_op jit(solution)/shard_map/ppermute | solution.py:293
  9.1 1.6 %collective-permute-start.6 = (bf16[128,1024]{1,0:T(8,128)(2,1)}, bf16[128,1024]{1,0:T(8,128)(2,1)S(1)}, u32[]{:S(2)}, u32[]{:S(2)}) collective-permute-start(bf16[128,1024]{1,0:T(8,128)(2,1)} %bitcast.13), channel_id=1, source_target_pairs={{0,2},{1,3},{2,0},{3,1},{4,6},{5,7},{6,4},{7,5},{8,10},{9,11},{10,... | collective-permute-start | bytes 786440 | tf_op jit(solution)/shard_map/ppermute | solution.py:297
  10.7 0.1 pad_add_fusion.place_ref
  10.7 0.7 copy-done
  11.4 3.1 %shard_map.118 = (bf16[128,1024]{1,0:T(8,128)(2,1)S(1)}, bf16[128,1024]{1,0:T(8,128)(2,1)S(1)}, bf16[128,1024]{1,0:T(8,128)(2,1)S(1)}, f32[128,1024]{1,0:T(8,128)S(1)}, f32[128,1024]{1,0:T(8,128)S(1)}) custom-call(s32[1,4]{1,0:T(1,128)S(1)} %copy-done, s32[2]{0:T(128)S(1)} %pad_add_fusion.place_ref, bf16[128,1024]{1,0:T(8,128)(2,1)} %bitcast.16, ...), custom_call_target="tpu_custom_call" | custom-call | flops 67108864 | bytes 2621440 | tf_op jit(solution)/shard_map/pallas_call | solution.py:79
  14.5 3.4 %collective-permute-start.2 = (bf16[128,1024]{1,0:T(8,128)(2,1)S(1)}, bf16[128,1024]{1,0:T(8,128)(2,1)S(1)}, u32[]{:S(2)}, u32[]{:S(2)}) collective-permute-start(bf16[128,1024]{1,0:T(8,128)(2,1)S(1)} %get-tuple-element.85.v.v0), channel_id=1, source_target_pairs={{0,4},{4,8},{8,12},{12,16},{16,20},{20,24},{24,28},{1,5},{5,9},{9,... | collective-permute-start | bytes 786440 | tf_op jit(solution)/shard_map/ppermute | solution.py:293
  17.9 1.3 %collective-permute-start.4 = (bf16[128,1024]{1,0:T(8,128)(2,1)S(1)}, bf16[128,1024]{1,0:T(8,128)(2,1)S(1)}, u32[]{:S(2)}, u32[]{:S(2)}) collective-permute-start(bf16[128,1024]{1,0:T(8,128)(2,1)S(1)} %get-tuple-element.56.q.q0), channel_id=1, source_target_pairs={{8,0},{12,4},{16,8},{20,12},{24,16},{28,20},{9,1},{13,5},{17,9},{2... | collective-permute-start | bytes 786440 | tf_op jit(solution)/shard_map/ppermute | solution.py:293
  19.2 0.0 collective-permute-done.keys.k2
  19.3 1.6 %collective-permute-start.1 = (bf16[128,1024]{1,0:T(8,128)(2,1)S(1)}, bf16[128,1024]{1,0:T(8,128)(2,1)S(1)}, u32[]{:S(2)}, u32[]{:S(2)}) collective-permute-start(bf16[128,1024]{1,0:T(8,128)(2,1)S(1)} %broadcast_select_fusion.2), channel_id=1, source_target_pairs={{0,4},{4,0},{8,12},{12,8},{16,20},{20,16},{24,28},{28,24},{1,5},{5... | collective-permute-start | bytes 786440 | tf_op jit(solution)/shard_map/ppermute | solution.py:297
  20.9 0.5 collective-permute-start.7
  21.4 2.9 %shard_map.121 = (bf16[128,1024]{1,0:T(8,128)(2,1)S(1)}, bf16[1024,1024]{1,0:T(8,128)(2,1)S(1)}, bf16[128,1024]{1,0:T(8,128)(2,1)S(1)}, f32[128,1024]{1,0:T(8,128)S(1)}) custom-call(bf16[128,1024]{1,0:T(8,128)(2,1)} %bitcast.15, bf16[1024,1024]{1,0:T(8,128)(2,1)} %w_in.1, bf16[128,1024]{1,0:T(8,128)(2,1)} %bitcast.12), custom_call_target="tpu_custom_call" | custom-call | flops 268435456 | bytes 5767168 | tf_op jit(solution)/shard_map/pallas_call | solution.py:79
  24.3 2.0 %shard_map.120 = (f32[128,1024]{1,0:T(8,128)S(1)}, f32[128,1024]{1,0:T(8,128)S(1)}) custom-call(s32[1,4]{1,0:T(1,128)S(1)} %copy-done.1, s32[2]{0:T(128)S(1)} %pad_add_fusion.place_ref, bf16[128,1024]{1,0:T(8,128)(2,1)S(1)} %get-tuple-element.56.q.q0, bf16[128,1024]{1,0:T(8,128)(2,1)S(1)} %collective-permute-done.keys.k2, ...), custom_call_target="tpu_custom_call" | custom-call | flops 67108864 | bytes 2359296 | tf_op jit(solution)/shard_map/pallas_call | solution.py:79
  26.3 0.5 collective-permute-done.4.q2
  26.8 0.0 collective-permute-done.5.refs_5_
  26.8 0.0 collective-permute-done.7.refs_7_
  26.8 1.4 %collective-permute-done.1.keys.k1 = bf16[128,1024]{1,0:T(8,128)(2,1)S(1)} collective-permute-done((bf16[128,1024]{1,0:T(8,128)(2,1)S(1)}, bf16[128,1024]{1,0:T(8,128)(2,1)S(1)}, u32[]{:S(2)}, u32[]{:S(2)}) %collective-permute-start.1) | collective-permute-done | bytes 262176 | tf_op jit(solution)/shard_map/ppermute | solution.py:297
  28.3 1.0 %shard_map.119 = (bf16[128,1024]{1,0:T(8,128)(2,1)S(1)}, f32[128,1024]{1,0:T(8,128)S(1)}) custom-call(s32[1,4]{1,0:T(1,128)S(1)} %copy-done.1, s32[2]{0:T(128)S(1)} %pad_add_fusion.place_ref, bf16[128,1024]{1,0:T(8,128)(2,1)S(1)} %get-tuple-element.56.q.q0, bf16[128,1024]{1,0:T(8,128)(2,1)S(1)} %collective-permute-done.1.keys.k1), custom_call_target="tpu_custom_call" | custom-call | flops 33554432 | bytes 1310720 | tf_op jit(solution)/shard_map/pallas_call | solution.py:79
  29.3 0.0 collective-permute-done.2.vals.v1
  29.3 1.0 %shard_map.122 = (bf16[128,1024]{1,0:T(8,128)(2,1)S(1)}, f32[128,1024]{1,0:T(8,128)S(1)}, f32[128,128]{1,0:T(8,128)S(1)}, bf16[128,256]{1,0:T(8,128)(2,1)S(1)}, ...) custom-call(s32[2]{0:T(128)S(1)} %pad_add_fusion.place_ref, ...), custom_call_target="tpu_custom_call" | custom-call | flops 33554432 | bytes 2424832 | tf_op jit(solution)/shard_map/pallas_call | solution.py:79
  30.3 0.9 %shard_map.123 = (bf16[128,1024]{1,0:T(8,128)(2,1)}, bf16[128,1024]{1,0:T(8,128)(2,1)S(1)}) custom-call(f32[128,1024]{1,0:T(8,128)S(1)} %get-tuple-element.60.grad_hidden, bf16[128,1024]{1,0:T(8,128)(2,1)S(1)} %get-tuple-element.61.gates, f32[128,1024]{1,0:T(8,128)S(1)} %get-tuple-element.64.normed, f32[128,128]{1,0:T(8,128)S(1)} %get-tuple-element.65.inv_std), custom_call_target="tpu_custom_call" | custom-call | flops 8388608 | bytes 1900544 | tf_op jit(solution)/shard_map/pallas_call | solution.py:79
  31.2 1.3 %collective-permute-start.11 = (bf16[128,1024]{1,0:T(8,128)(2,1)S(1)}, bf16[128,1024]{1,0:T(8,128)(2,1)S(1)}, u32[]{:S(2)}, u32[]{:S(2)}) collective-permute-start(bf16[128,1024]{1,0:T(8,128)(2,1)S(1)} %get-tuple-element.66.g0.grad_mix), channel_id=1, source_target_pairs={{8,0},{12,4},{16,8},{20,12},{24,16},{28,20},{9,1},{13,5},{17,9},{2... | collective-permute-start | bytes 786440 | tf_op jit(solution)/shard_map/ppermute | solution.py:293
  32.5 0.1 collective-permute-start.8
  32.6 0.6 collective-permute-start.9
  33.1 1.3 %collective-permute-start.10 = (bf16[128,256]{1,0:T(8,128)(2,1)S(1)}, bf16[128,256]{1,0:T(8,128)(2,1)S(1)}, u32[]{:S(2)}, u32[]{:S(2)}) collective-permute-start(bf16[128,256]{1,0:T(8,128)(2,1)S(1)} %get-tuple-element.71), channel_id=1, source_target_pairs={{0,3},{1,2},{2,1},{3,0},{4,7},{5,6},{6,5},{7,4},{8,11},{9,10},{10,... | collective-permute-start | bytes 196616 | tf_op jit(solution)/shard_map/ppermute | solution.py:297
  34.4 2.5 %collective-permute-start.16 = (bf16[128,1024]{1,0:T(8,128)(2,1)S(1)}, bf16[128,1024]{1,0:T(8,128)(2,1)S(1)}, u32[]{:S(2)}, u32[]{:S(2)}) collective-permute-start(bf16[128,1024]{1,0:T(8,128)(2,1)S(1)} %broadcast_select_fusion.1), channel_id=1, source_target_pairs={{0,4},{4,0},{8,12},{12,8},{16,20},{20,16},{24,28},{28,24},{1,5},{5... | collective-permute-start | bytes 786440 | tf_op jit(solution)/shard_map/ppermute | solution.py:297
  36.9 0.6 collective-permute-done.9.refs_2_
  37.5 0.5 collective-permute-done.10.refs_3_
  38.0 1.1 %shard_map.124 = (f32[64,1024]{1,0:T(8,128)S(1)}, bf16[64,1024]{1,0:T(8,128)(2,1)S(1)}, bf16[64,1024]{1,0:T(8,128)(2,1)S(1)}, bf16[64,1024]{1,0:T(8,128)(2,1)S(1)}) custom-call(s32[2]{0:T(128)S(1)} %pad_add_fusion.place_ref, bf16[128,256]{1,0:T(8,128)(2,1)S(1)} %get-tuple-element.68.refs_0_, bf16[128,256]{1,0:T(8,128)(2,1)S(1)} %collective-permute-done.8.refs_1_, ...), custom_call_target="tpu_custom_call" | custom-call | flops 268435456 | bytes 1966080 | tf_op jit(solution)/shard_map/pallas_call | solution.py:79
  39.1 2.5 %collective-permute-start.12 = (bf16[64,1024]{1,0:T(8,128)(2,1)S(1)}, bf16[64,1024]{1,0:T(8,128)(2,1)S(1)}, u32[]{:S(2)}, u32[]{:S(2)}) collective-permute-start(bf16[64,1024]{1,0:T(8,128)(2,1)S(1)} %get-tuple-element.77), channel_id=1, source_target_pairs={{0,4},{4,0},{8,12},{12,8},{16,20},{20,16},{24,28},{28,24},{1,5},{5... | collective-permute-start | bytes 393224 | tf_op jit(solution)/shard_map/ppermute | solution.py:297
  41.6 2.6 %collective-permute-start.13 = (bf16[64,1024]{1,0:T(8,128)(2,1)S(1)}, bf16[64,1024]{1,0:T(8,128)(2,1)S(1)}, u32[]{:S(2)}, u32[]{:S(2)}) collective-permute-start(bf16[64,1024]{1,0:T(8,128)(2,1)S(1)} %get-tuple-element.78), channel_id=1, source_target_pairs={{0,8},{4,12},{8,0},{12,4},{16,24},{20,28},{24,16},{28,20},{1,9},{5... | collective-permute-start | bytes 393224 | tf_op jit(solution)/shard_map/ppermute | solution.py:297
  44.3 0.6 collective-permute-start.14
  44.9 1.6 %collective-permute-done.12.refs_0_ = bf16[64,1024]{1,0:T(8,128)(2,1)S(1)} collective-permute-done((bf16[64,1024]{1,0:T(8,128)(2,1)S(1)}, bf16[64,1024]{1,0:T(8,128)(2,1)S(1)}, u32[]{:S(2)}, u32[]{:S(2)}) %collective-permute-start.12) | collective-permute-done | bytes 131104 | tf_op jit(solution)/shard_map/ppermute | solution.py:297
  46.5 1.7 %collective-permute-start.17 = (bf16[128,1024]{1,0:T(8,128)(2,1)S(1)}, bf16[128,1024]{1,0:T(8,128)(2,1)S(1)}, u32[]{:S(2)}, u32[]{:S(2)}) collective-permute-start(bf16[128,1024]{1,0:T(8,128)(2,1)S(1)} %broadcast_select_fusion), channel_id=1, source_target_pairs={{0,4},{4,0},{8,12},{12,8},{16,20},{20,16},{24,28},{28,24},{1,5},{5... | collective-permute-start | bytes 786440 | tf_op jit(solution)/shard_map/ppermute | solution.py:297
  48.3 2.7 %shard_map.125 = (f32[128,1024]{1,0:T(8,128)S(1)}, f32[128,1024]{1,0:T(8,128)S(1)}) custom-call(s32[1,4]{1,0:T(1,128)S(1)} %copy-done.1, s32[2]{0:T(128)S(1)} %pad_add_fusion.place_ref, bf16[128,1024]{1,0:T(8,128)(2,1)S(1)} %get-tuple-element.49.k.k0, bf16[128,1024]{1,0:T(8,128)(2,1)S(1)} %get-tuple-element.85.v.v0, ...), custom_call_target="tpu_custom_call" | custom-call | flops 268435456 | bytes 2621440 | tf_op jit(solution)/shard_map/pallas_call | solution.py:79
  51.0 0.6 collective-permute-done.14.refs_2_
  51.6 0.1 shard_map.126.mine
  51.6 3.3 %collective-permute-start.15 = (bf16[64,1024]{1,0:T(8,128)(2,1)S(1)}, bf16[64,1024]{1,0:T(8,128)(2,1)S(1)}, u32[]{:S(2)}, u32[]{:S(2)}) collective-permute-start(bf16[64,1024]{1,0:T(8,128)(2,1)S(1)} %shard_map.126.mine), channel_id=1, source_target_pairs={{0,16},{4,20},{8,24},{12,28},{16,0},{20,4},{24,8},{28,12},{1,17},{... | collective-permute-start | bytes 393224 | tf_op jit(solution)/shard_map/ppermute | solution.py:297
  54.9 2.7 %shard_map.127 = (bf16[128,1024]{1,0:T(8,128)(2,1)}, bf16[128,1024]{1,0:T(8,128)(2,1)}) custom-call(bf16[128,1024]{1,0:T(8,128)(2,1)S(1)} %get-tuple-element.49.k.k0, bf16[128,1024]{1,0:T(8,128)(2,1)S(1)} %collective-permute-done.1.keys.k1, bf16[128,1024]{1,0:T(8,128)(2,1)S(1)} %collective-permute-done.keys.k2, ...), custom_call_target="tpu_custom_call" | custom-call | flops 469762048 | bytes 6291456 | tf_op jit(solution)/shard_map/pallas_call | solution.py:79
  57.6 3.0 %collective-permute-done.15.other = bf16[64,1024]{1,0:T(8,128)(2,1)S(1)} collective-permute-done((bf16[64,1024]{1,0:T(8,128)(2,1)S(1)}, bf16[64,1024]{1,0:T(8,128)(2,1)S(1)}, u32[]{:S(2)}, u32[]{:S(2)}) %collective-permute-start.15) | collective-permute-done | bytes 131104 | tf_op jit(solution)/shard_map/ppermute | solution.py:297
  60.6 1.4 %collective-permute-start.20 = (bf16[64,1024]{1,0:T(8,128)(2,1)S(1)}, bf16[64,1024]{1,0:T(8,128)(2,1)S(1)}, u32[]{:S(2)}, u32[]{:S(2)}) collective-permute-start(bf16[64,1024]{1,0:T(8,128)(2,1)S(1)} %shard_map.128.share), channel_id=1, source_target_pairs={{0,4},{4,0},{8,12},{12,8},{16,20},{20,16},{24,28},{28,24},{1,5},{5... | collective-permute-start | bytes 393224 | tf_op jit(solution)/shard_map/ppermute | solution.py:297
  62.1 0.7 collective-permute-start.19
  62.8 1.4 %collective-permute-start.18 = (bf16[64,1024]{1,0:T(8,128)(2,1)S(1)}, bf16[64,1024]{1,0:T(8,128)(2,1)S(1)}, u32[]{:S(2)}, u32[]{:S(2)}) collective-permute-start(bf16[64,1024]{1,0:T(8,128)(2,1)S(1)} %shard_map.128.share), channel_id=1, source_target_pairs={{0,12},{4,8},{8,4},{12,0},{16,28},{20,24},{24,20},{28,16},{1,13},{... | collective-permute-start | bytes 393224 | tf_op jit(solution)/shard_map/ppermute | solution.py:297
  64.2 2.9 %shard_map.129 = (bf16[128,1024]{1,0:T(8,128)(2,1)}, bf16[128,1024]{1,0:T(8,128)(2,1)}) custom-call(s32[1,4]{1,0:T(1,128)S(1)} %copy-done.1, s32[2]{0:T(128)S(1)} %pad_add_fusion.place_ref, bf16[128,1024]{1,0:T(8,128)(2,1)S(1)} %get-tuple-element.49.k.k0, bf16[128,1024]{1,0:T(8,128)(2,1)S(1)} %get-tuple-element.85.v.v0, ...), custom_call_target="tpu_custom_call" | custom-call | flops 134217728 | bytes 2621440 | tf_op jit(solution)/shard_map/pallas_call | solution.py:79
  67.1 1.3 %shard_map.130.refs_0_ = f32[256,1024]{1,0:T(8,128)} custom-call(s32[2]{0:T(128)S(1)} %pad_add_fusion.place_ref, bf16[64,1024]{1,0:T(8,128)(2,1)S(1)} %shard_map.128.share), custom_call_target="tpu_custom_call" | custom-call | flops 65536 | bytes 1179648 | tf_op jit(solution)/shard_map/pallas_call | solution.py:79
  68.4 1.3 %shard_map.131.refs_0_ = f32[256,1024]{1,0:T(8,128)} custom-call(s32[2]{0:T(128)S(1)} %pad_add_fusion.place_ref, bf16[64,1024]{1,0:T(8,128)(2,1)S(1)} %collective-permute-done.20.share, f32[256,1024]{1,0:T(8,128)} %shard_map.130.refs_0_), custom_call_target="tpu_custom_call", output_to_operand_aliasing={{}: (2, {})} | custom-call | flops 65536 | bytes 2228224 | tf_op jit(solution)/shard_map/pallas_call | solution.py:79
  69.7 1.3 %shard_map.132.refs_0_ = f32[256,1024]{1,0:T(8,128)} custom-call(s32[2]{0:T(128)S(1)} %pad_add_fusion.place_ref, bf16[64,1024]{1,0:T(8,128)(2,1)S(1)} %collective-permute-done.19.share, f32[256,1024]{1,0:T(8,128)} %shard_map.131.refs_0_), custom_call_target="tpu_custom_call", output_to_operand_aliasing={{}: (2, {})} | custom-call | flops 65536 | bytes 2228224 | tf_op jit(solution)/shard_map/pallas_call | solution.py:79
  71.0 1.3 %shard_map.133 = f32[256,1024]{1,0:T(8,128)} custom-call(s32[2]{0:T(128)S(1)} %pad_add_fusion.place_ref, bf16[64,1024]{1,0:T(8,128)(2,1)S(1)} %collective-permute-done.18.share, f32[256,1024]{1,0:T(8,128)} %shard_map.132.refs_0_), custom_call_target="tpu_custom_call", output_to_operand_aliasing={{}: (2, {})} | custom-call | flops 65536 | bytes 2228224 | tf_op jit(solution)/shard_map/pallas_call | solution.py:79
  (18 shorter events, 0.2 us)
Async XLA Ops:
  0.6 18.6 %collective-permute-start = (bf16[128,1024]{1,0:T(8,128)(2,1)}, bf16[128,1024]{1,0:T(8,128)(2,1)S(1)}, u32[]{:S(2)}, u32[]{:S(2)}) collective-permute-start(bf16[128,1024]{1,0:T(8,128)(2,1)} %bitcast.17), channel_id=1, source_target_pairs={{0,8},{4,12},{8,16},{12,20},{16,24},{20,28},{1,9},{5,13},{9,17},{1... | collective-permute-start | bytes 786440 | tf_op jit(solution)/shard_map/ppermute | solution.py:293
  5.6 15.3 %collective-permute-start.3 = (bf16[128,1024]{1,0:T(8,128)(2,1)}, bf16[128,1024]{1,0:T(8,128)(2,1)S(1)}, u32[]{:S(2)}, u32[]{:S(2)}) collective-permute-start(bf16[128,1024]{1,0:T(8,128)(2,1)} %bitcast.19), channel_id=1, source_target_pairs={{0,8},{4,12},{8,16},{12,20},{16,24},{20,28},{1,9},{5,13},{9,17},{1... | collective-permute-start | bytes 786440 | tf_op jit(solution)/shard_map/ppermute | solution.py:293
  9.1 11.8 %collective-permute-start.6 = (bf16[128,1024]{1,0:T(8,128)(2,1)}, bf16[128,1024]{1,0:T(8,128)(2,1)S(1)}, u32[]{:S(2)}, u32[]{:S(2)}) collective-permute-start(bf16[128,1024]{1,0:T(8,128)(2,1)} %bitcast.13), channel_id=1, source_target_pairs={{0,2},{1,3},{2,0},{3,1},{4,6},{5,7},{6,4},{7,5},{8,10},{9,11},{10,... | collective-permute-start | bytes 786440 | tf_op jit(solution)/shard_map/ppermute | solution.py:297
  10.7 0.7 copy-start
  11.4 12.9 %copy-start.1 = (s32[1,4]{1,0:T(1,128)S(1)}, s32[1,4]{1,0:T(1,128)}, u32[]{:S(2)}) copy-start(s32[1,4]{1,0:T(1,128)} %len_ref.9) | copy-start | bytes 52
  14.5 14.8 %collective-permute-start.2 = (bf16[128,1024]{1,0:T(8,128)(2,1)S(1)}, bf16[128,1024]{1,0:T(8,128)(2,1)S(1)}, u32[]{:S(2)}, u32[]{:S(2)}) collective-permute-start(bf16[128,1024]{1,0:T(8,128)(2,1)S(1)} %get-tuple-element.85.v.v0), channel_id=1, source_target_pairs={{0,4},{4,8},{8,12},{12,16},{16,20},{20,24},{24,28},{1,5},{5,9},{9,... | collective-permute-start | bytes 786440 | tf_op jit(solution)/shard_map/ppermute | solution.py:293
  17.9 8.8 %collective-permute-start.4 = (bf16[128,1024]{1,0:T(8,128)(2,1)S(1)}, bf16[128,1024]{1,0:T(8,128)(2,1)S(1)}, u32[]{:S(2)}, u32[]{:S(2)}) collective-permute-start(bf16[128,1024]{1,0:T(8,128)(2,1)S(1)} %get-tuple-element.56.q.q0), channel_id=1, source_target_pairs={{8,0},{12,4},{16,8},{20,12},{24,16},{28,20},{9,1},{13,5},{17,9},{2... | collective-permute-start | bytes 786440 | tf_op jit(solution)/shard_map/ppermute | solution.py:293
  19.3 9.0 %collective-permute-start.1 = (bf16[128,1024]{1,0:T(8,128)(2,1)S(1)}, bf16[128,1024]{1,0:T(8,128)(2,1)S(1)}, u32[]{:S(2)}, u32[]{:S(2)}) collective-permute-start(bf16[128,1024]{1,0:T(8,128)(2,1)S(1)} %broadcast_select_fusion.2), channel_id=1, source_target_pairs={{0,4},{4,0},{8,12},{12,8},{16,20},{20,16},{24,28},{28,24},{1,5},{5... | collective-permute-start | bytes 786440 | tf_op jit(solution)/shard_map/ppermute | solution.py:297
  20.9 5.9 %collective-permute-start.5 = (bf16[128,1024]{1,0:T(8,128)(2,1)}, bf16[128,1024]{1,0:T(8,128)(2,1)S(1)}, u32[]{:S(2)}, u32[]{:S(2)}) collective-permute-start(bf16[128,1024]{1,0:T(8,128)(2,1)} %bitcast.14), channel_id=1, source_target_pairs={{0,1},{1,0},{2,3},{3,2},{4,5},{5,4},{6,7},{7,6},{8,9},{9,8},{10,11... | collective-permute-start | bytes 786440 | tf_op jit(solution)/shard_map/ppermute | solution.py:297
  20.9 5.9 %collective-permute-start.7 = (bf16[128,1024]{1,0:T(8,128)(2,1)S(1)}, bf16[128,1024]{1,0:T(8,128)(2,1)S(1)}, u32[]{:S(2)}, u32[]{:S(2)}) collective-permute-start(bf16[128,1024]{1,0:T(8,128)(2,1)S(1)} %collective-permute-done.6.refs_6_), channel_id=1, source_target_pairs={{0,1},{1,0},{2,3},{3,2},{4,5},{5,4},{6,7},{7,6},{8,9},{9,8},{10,11... | collective-permute-start | bytes 786440 | tf_op jit(solution)/shard_map/ppermute | solution.py:297
  31.2 13.7 %collective-permute-start.11 = (bf16[128,1024]{1,0:T(8,128)(2,1)S(1)}, bf16[128,1024]{1,0:T(8,128)(2,1)S(1)}, u32[]{:S(2)}, u32[]{:S(2)}) collective-permute-start(bf16[128,1024]{1,0:T(8,128)(2,1)S(1)} %get-tuple-element.66.g0.grad_mix), channel_id=1, source_target_pairs={{8,0},{12,4},{16,8},{20,12},{24,16},{28,20},{9,1},{13,5},{17,9},{2... | collective-permute-start | bytes 786440 | tf_op jit(solution)/shard_map/ppermute | solution.py:293
  32.5 4.4 %collective-permute-start.8 = (bf16[128,256]{1,0:T(8,128)(2,1)S(1)}, bf16[128,256]{1,0:T(8,128)(2,1)S(1)}, u32[]{:S(2)}, u32[]{:S(2)}) collective-permute-start(bf16[128,256]{1,0:T(8,128)(2,1)S(1)} %get-tuple-element.69), channel_id=1, source_target_pairs={{0,1},{1,0},{2,3},{3,2},{4,5},{5,4},{6,7},{7,6},{8,9},{9,8},{10,11... | collective-permute-start | bytes 196616 | tf_op jit(solution)/shard_map/ppermute | solution.py:297
  32.6 5.0 %collective-permute-start.9 = (bf16[128,256]{1,0:T(8,128)(2,1)S(1)}, bf16[128,256]{1,0:T(8,128)(2,1)S(1)}, u32[]{:S(2)}, u32[]{:S(2)}) collective-permute-start(bf16[128,256]{1,0:T(8,128)(2,1)S(1)} %get-tuple-element.70), channel_id=1, source_target_pairs={{0,2},{1,3},{2,0},{3,1},{4,6},{5,7},{6,4},{7,5},{8,10},{9,11},{10,... | collective-permute-start | bytes 196616 | tf_op jit(solution)/shard_map/ppermute | solution.py:297
  33.1 4.9 %collective-permute-start.10 = (bf16[128,256]{1,0:T(8,128)(2,1)S(1)}, bf16[128,256]{1,0:T(8,128)(2,1)S(1)}, u32[]{:S(2)}, u32[]{:S(2)}) collective-permute-start(bf16[128,256]{1,0:T(8,128)(2,1)S(1)} %get-tuple-element.71), channel_id=1, source_target_pairs={{0,3},{1,2},{2,1},{3,0},{4,7},{5,6},{6,5},{7,4},{8,11},{9,10},{10,... | collective-permute-start | bytes 196616 | tf_op jit(solution)/shard_map/ppermute | solution.py:297
  34.4 29.8 %collective-permute-start.16 = (bf16[128,1024]{1,0:T(8,128)(2,1)S(1)}, bf16[128,1024]{1,0:T(8,128)(2,1)S(1)}, u32[]{:S(2)}, u32[]{:S(2)}) collective-permute-start(bf16[128,1024]{1,0:T(8,128)(2,1)S(1)} %broadcast_select_fusion.1), channel_id=1, source_target_pairs={{0,4},{4,0},{8,12},{12,8},{16,20},{20,16},{24,28},{28,24},{1,5},{5... | collective-permute-start | bytes 786440 | tf_op jit(solution)/shard_map/ppermute | solution.py:297
  39.1 7.4 %collective-permute-start.12 = (bf16[64,1024]{1,0:T(8,128)(2,1)S(1)}, bf16[64,1024]{1,0:T(8,128)(2,1)S(1)}, u32[]{:S(2)}, u32[]{:S(2)}) collective-permute-start(bf16[64,1024]{1,0:T(8,128)(2,1)S(1)} %get-tuple-element.77), channel_id=1, source_target_pairs={{0,4},{4,0},{8,12},{12,8},{16,20},{20,16},{24,28},{28,24},{1,5},{5... | collective-permute-start | bytes 393224 | tf_op jit(solution)/shard_map/ppermute | solution.py:297
  41.6 9.4 %collective-permute-start.13 = (bf16[64,1024]{1,0:T(8,128)(2,1)S(1)}, bf16[64,1024]{1,0:T(8,128)(2,1)S(1)}, u32[]{:S(2)}, u32[]{:S(2)}) collective-permute-start(bf16[64,1024]{1,0:T(8,128)(2,1)S(1)} %get-tuple-element.78), channel_id=1, source_target_pairs={{0,8},{4,12},{8,0},{12,4},{16,24},{20,28},{24,16},{28,20},{1,9},{5... | collective-permute-start | bytes 393224 | tf_op jit(solution)/shard_map/ppermute | solution.py:297
  44.3 7.3 %collective-permute-start.14 = (bf16[64,1024]{1,0:T(8,128)(2,1)S(1)}, bf16[64,1024]{1,0:T(8,128)(2,1)S(1)}, u32[]{:S(2)}, u32[]{:S(2)}) collective-permute-start(bf16[64,1024]{1,0:T(8,128)(2,1)S(1)} %get-tuple-element.79), channel_id=1, source_target_pairs={{0,12},{4,8},{8,4},{12,0},{16,28},{20,24},{24,20},{28,16},{1,13},{... | collective-permute-start | bytes 393224 | tf_op jit(solution)/shard_map/ppermute | solution.py:297
  46.5 17.7 %collective-permute-start.17 = (bf16[128,1024]{1,0:T(8,128)(2,1)S(1)}, bf16[128,1024]{1,0:T(8,128)(2,1)S(1)}, u32[]{:S(2)}, u32[]{:S(2)}) collective-permute-start(bf16[128,1024]{1,0:T(8,128)(2,1)S(1)} %broadcast_select_fusion), channel_id=1, source_target_pairs={{0,4},{4,0},{8,12},{12,8},{16,20},{20,16},{24,28},{28,24},{1,5},{5... | collective-permute-start | bytes 786440 | tf_op jit(solution)/shard_map/ppermute | solution.py:297
  51.6 8.9 %collective-permute-start.15 = (bf16[64,1024]{1,0:T(8,128)(2,1)S(1)}, bf16[64,1024]{1,0:T(8,128)(2,1)S(1)}, u32[]{:S(2)}, u32[]{:S(2)}) collective-permute-start(bf16[64,1024]{1,0:T(8,128)(2,1)S(1)} %shard_map.126.mine), channel_id=1, source_target_pairs={{0,16},{4,20},{8,24},{12,28},{16,0},{20,4},{24,8},{28,12},{1,17},{... | collective-permute-start | bytes 393224 | tf_op jit(solution)/shard_map/ppermute | solution.py:297
  60.6 7.7 %collective-permute-start.20 = (bf16[64,1024]{1,0:T(8,128)(2,1)S(1)}, bf16[64,1024]{1,0:T(8,128)(2,1)S(1)}, u32[]{:S(2)}, u32[]{:S(2)}) collective-permute-start(bf16[64,1024]{1,0:T(8,128)(2,1)S(1)} %shard_map.128.share), channel_id=1, source_target_pairs={{0,4},{4,0},{8,12},{12,8},{16,20},{20,16},{24,28},{28,24},{1,5},{5... | collective-permute-start | bytes 393224 | tf_op jit(solution)/shard_map/ppermute | solution.py:297
  62.1 7.6 %collective-permute-start.19 = (bf16[64,1024]{1,0:T(8,128)(2,1)S(1)}, bf16[64,1024]{1,0:T(8,128)(2,1)S(1)}, u32[]{:S(2)}, u32[]{:S(2)}) collective-permute-start(bf16[64,1024]{1,0:T(8,128)(2,1)S(1)} %shard_map.128.share), channel_id=1, source_target_pairs={{0,8},{4,12},{8,0},{12,4},{16,24},{20,28},{24,16},{28,20},{1,9},{5... | collective-permute-start | bytes 393224 | tf_op jit(solution)/shard_map/ppermute | solution.py:297
  62.8 8.2 %collective-permute-start.18 = (bf16[64,1024]{1,0:T(8,128)(2,1)S(1)}, bf16[64,1024]{1,0:T(8,128)(2,1)S(1)}, u32[]{:S(2)}, u32[]{:S(2)}) collective-permute-start(bf16[64,1024]{1,0:T(8,128)(2,1)S(1)} %shard_map.128.share), channel_id=1, source_target_pairs={{0,12},{4,8},{8,4},{12,0},{16,28},{20,24},{24,20},{28,16},{1,13},{... | collective-permute-start | bytes 393224 | tf_op jit(solution)/shard_map/ppermute | solution.py:297

commit v6 on v5

--- a/solution.py
+++ b/solution.py
@@ -272,15 +272,18 @@
     both[...] = ((mine[...].astype(F32) + other[...].astype(F32)) * scale).astype(BF16)
 
 
-def place_kernel(corners, partner, place_ref, share, *refs):
-    out, wide, sem = refs[-3:]
-    rows = share.shape[0]
-    corner = (place_ref[0] & (corners - 1)) ^ partner
-    wide[...] = share[...].astype(F32)
-    at = pl.multiple_of(corner * rows, rows)
-    move = pltpu.make_async_copy(wide, out.at[pl.ds(at, rows), :], sem)
-    move.start()
-    move.wait()
+def place_kernel(corners, place_ref, *refs):
+    shares, (out, wide, sems) = refs[:corners], refs[corners:]
+    rows = shares[0].shape[0]
+    corner = place_ref[0] & (corners - 1)
+    moves = []
+    for e, ref in enumerate(shares):
+        wide[e] = ref[...].astype(F32)
+        at = pl.multiple_of((corner ^ e) * rows, rows)
+        moves.append(pltpu.make_async_copy(wide.at[e], out.at[pl.ds(at, rows), :], sems.at[e]))
+        moves[-1].start()
+    for move in moves:
+        move.wait()
 
 
 def xor_route(size, mask):
@@ -330,7 +333,7 @@
     )
     passed = jnp.where(even, k, k2)
     k1 = swapped(passed, "seq", 1)
-    v1 = shifted(v, 1)
+    v1 = shifted(after(v, passed), 1)
     grad, w, gate, grad_hidden = call(
         project_kernel,
         [near, kept(w_out.shape, BF16), near, wide],
@@ -343,15 +346,15 @@
     grads = [grad]
     for d in range(1, batch):
         low = d & -d
-        source = out_grad[0] if d == low else grads[d ^ low]
-        grads.append(swapped(after(source, v2) if d == 1 else source, "batch", low))
-    q2 = shifted(q, -2)
+        source = after(out_grad[0], passed) if d == 1 else out_grad[0] if d == low else grads[d ^ low]
+        grads.append(swapped(source, "batch", low))
     mixed_far, slope2 = call(
-        second_kernel, [wide, wide], scalars, (after(q, grads[-2]), k2, v2, mixed_own), 2 * block_flops
-    )
+        second_kernel, [wide, wide], scalars, (q, k2, v2, mixed_own), 2 * block_flops
+    )
+    q2 = shifted(after(q, mixed_far), -2)
     passed_q = jnp.where(even, q2, q)
     q1 = swapped(passed_q, "seq", 1)
-    attention1, slope1 = call(first_kernel, [near, wide], scalars, (after(q, passed_q, grads[1], grads[-1]), k1), block_flops)
+    attention1, slope1 = call(first_kernel, [near, wide], scalars, (after(q, grads[1]), k1), block_flops)
     hidden, normed, inv_std, *slices = call(
         functools.partial(forward_kernel, batch),
         [near, wide, kept((rows, 128), F32)] + [kept((rows, part), BF16)] * batch,
@@ -372,11 +375,18 @@
     rows_w = part // corners if direct else part
     share = kept((rows_w, width), BF16)
     scale = (rows * seq * batch) ** (-0.5)
+    output, grad_queries = call(
+        query_kernel,
+        [full, full],
+        (),
+        (k, k1, k2, v, v1, v2, slope0, slope1, slope2, grad_mix, hidden, w),
+        proj_flops + 6 * block_flops,
+    )
     own, *sends = call(
         functools.partial(weight_kernel, batch),
         [kept((rows_w, width), F32)] + [share] * (corners - 1 if direct else 0),
         (place,),
-        (*hiddens, *grads),
+        (after(hiddens[0], output), *hiddens[1:], *grads),
         proj_flops,
         [pltpu.VMEM((part, width), F32)],
     )
@@ -387,54 +397,37 @@
         (k, after(v, own), q, q2, grad_mix, g2),
         8 * block_flops,
     )
-    hidden_late = hidden
     if direct:
         got = [swapped(s, "seq", e + 1) for e, s in enumerate(sends)]
         (mine,) = call(corner_kernel, [share], (), (after(own, keys_part), *got), own.size * 4)
         other = swapped(mine, "seq", corners)
-        passed_g = after(passed_g, got[0])
-        hidden_late = after(hidden, mine)
-    output, grad_queries = call(
-        query_kernel,
+        passed_g = after(passed_g, mine)
+    g1 = swapped(passed_g, "seq", 1)
+    grad_keys, grad_values = call(
+        key_end_kernel,
         [full, full],
-        (),
-        (k, k1, k2, v, v1, v2, slope0, slope1, slope2, grad_mix, hidden_late, w),
-        proj_flops + 6 * block_flops,
-    )
-    g1 = swapped(passed_g, "seq", 1)
-    last = v
+        scalars,
+        (k, after(v, mine) if direct else v, q1, g1, keys_part, values_part),
+        4 * block_flops,
+    )
     if direct:
         (both,) = call(
             functools.partial(pair_kernel, scale),
             [share],
             (),
-            (after(mine, output), other),
+            (after(mine, grad_keys), other),
             own.size * 2,
         )
-        last = after(v, both)
-    grad_keys, grad_values = call(
-        key_end_kernel,
-        [full, full],
-        scalars,
-        (k, last, q1, g1, keys_part, values_part),
-        4 * block_flops,
-    )
-    if direct:
-        result = jax.ShapeDtypeStruct((part, width), F32)
-        shares = [after(both, grad_keys)] + [swapped(both, "seq", e) for e in range(1, corners)]
-        grad_weight = None
-        for e, piece in enumerate(shares):
-            (grad_weight,) = call(
-                functools.partial(place_kernel, corners, e),
-                [result],
-                (place,),
-                (piece,) if e == 0 else (piece, grad_weight),
-                piece.size,
-                [pltpu.VMEM((rows_w, width), F32), pltpu.SemaphoreType.DMA(())],
-                spaces=[VMEM] if e == 0 else [VMEM, hbm],
-                out_space=hbm,
-                aliases={} if e == 0 else {2: 0},
-            )
+        shares = [both] + [swapped(both, "seq", e) for e in range(1, corners)]
+        (grad_weight,) = call(
+            functools.partial(place_kernel, corners),
+            [jax.ShapeDtypeStruct((part, width), F32)],
+            (place,),
+            shares,
+            part * width,
+            [pltpu.VMEM((corners, rows_w, width), F32), pltpu.SemaphoreType.DMA((corners,))],
+            out_space=hbm,
+        )
     else:
         grad_weight = lax.psum(own, "seq") * scale
     return (

time: 72.5 us -> 73.3 us (1.011)
  waiting for transfers between devices: 8.24 us -> 14.2 us
  Pallas kernels: 25.5 us -> 21.9 us
  starting transfers between devices: 36.8 us -> 35.2 us
    ppermute x16, waiting for transfers between devices: 7.77 us -> 11.5 us  [swapped(): return lax.ppermute(block, axis, xor_route(lax.axis_size(axis), mask))]
    pallas_call x16 -> x13, Pallas kernels: 25.5 us -> 21.9 us  [call(): pl.pallas_call(kernel, out_shape=outs, in_specs=[SMEM] * len(scalars) + (...]
    ppermute x5, waiting for transfers between devices: 0.47 us -> 2.68 us  [shifted(): return lax.ppermute(block, 'seq', route)]
    ppermute x5, starting transfers between devices: 14.4 us -> 13.4 us  [shifted(): return lax.ppermute(block, 'seq', route)]
  transfers between devices with their start and end apart: 21 -> 21, of which waited for: 7 -> 7; matrix products, arithmetic and copies ran while one was open for 0% -> 0% of each run, Pallas kernels for 31% -> 28%
where the time goes in v6:
time: 73.3 us; the launch traced here: 73 us
  starting transfers between devices  35.2 us (48%)
  Pallas kernels  21.9 us (30%)
  waiting for transfers between devices  14.2 us (19%)
  between operations  0.84 us (1%)
    pallas_call x13, Pallas kernels, call(): pl.pallas_call(kernel, out_shape=outs, in_specs=[SMEM] * len(scalars) + (...  21.9 us
    ppermute x16, starting transfers between devices, swapped(): return lax.ppermute(block, axis, xor_route(lax.axis_size(axis), mask))  21.7 us
    ppermute x5, starting transfers between devices, shifted(): return lax.ppermute(block, 'seq', route)  13.4 us
    ppermute x16, waiting for transfers between devices, swapped(): return lax.ppermute(block, axis, xor_route(lax.axis_size(axis), mask))  11.5 us
    ppermute x5, waiting for transfers between devices, shifted(): return lax.ppermute(block, 'seq', route)  2.68 us
  transfers between devices with their start and end apart: 21, of which 7 were waited for; matrix products, arithmetic and copies ran while one was open for 0% of the time, Pallas kernels for 28%

profile of v6, /device:TPU:0, one launch (start us, length us, event | category | flops | bytes accessed | tf_op | source)
XLA Modules:
  0.0 73.0 jit_solution(9182026479211356738)
XLA Ops:
  0.6 4.9 %collective-permute-start = (bf16[128,1024]{1,0:T(8,128)(2,1)}, bf16[128,1024]{1,0:T(8,128)(2,1)S(1)}, u32[]{:S(2)}, u32[]{:S(2)}) collective-permute-start(bf16[128,1024]{1,0:T(8,128)(2,1)} %bitcast.17), channel_id=1, source_target_pairs={{0,8},{4,12},{8,16},{12,20},{16,24},{20,28},{1,9},{5,13},{9,17},{1... | collective-permute-start | bytes 786440 | tf_op jit(solution)/shard_map/ppermute | solution.py:296
  5.6 3.5 %collective-permute-start.3 = (bf16[128,1024]{1,0:T(8,128)(2,1)}, bf16[128,1024]{1,0:T(8,128)(2,1)S(1)}, u32[]{:S(2)}, u32[]{:S(2)}) collective-permute-start(bf16[128,1024]{1,0:T(8,128)(2,1)} %bitcast.19), channel_id=1, source_target_pairs={{0,8},{4,12},{8,16},{12,20},{16,24},{20,28},{1,9},{5,13},{9,17},{1... | collective-permute-start | bytes 786440 | tf_op jit(solution)/shard_map/ppermute | solution.py:296
  9.1 1.6 %collective-permute-start.8 = (bf16[128,1024]{1,0:T(8,128)(2,1)}, bf16[128,1024]{1,0:T(8,128)(2,1)S(1)}, u32[]{:S(2)}, u32[]{:S(2)}) collective-permute-start(bf16[128,1024]{1,0:T(8,128)(2,1)} %bitcast.13), channel_id=1, source_target_pairs={{0,2},{1,3},{2,0},{3,1},{4,6},{5,7},{6,4},{7,5},{8,10},{9,11},{10,... | collective-permute-start | bytes 786440 | tf_op jit(solution)/shard_map/ppermute | solution.py:300
  10.7 0.1 pad_add_fusion.place_ref
  10.7 0.7 copy-done
  11.4 3.1 %shard_map.118 = (bf16[128,1024]{1,0:T(8,128)(2,1)S(1)}, bf16[128,1024]{1,0:T(8,128)(2,1)S(1)}, bf16[128,1024]{1,0:T(8,128)(2,1)S(1)}, f32[128,1024]{1,0:T(8,128)S(1)}, f32[128,1024]{1,0:T(8,128)S(1)}) custom-call(s32[1,4]{1,0:T(1,128)S(1)} %copy-done, s32[2]{0:T(128)S(1)} %pad_add_fusion.place_ref, bf16[128,1024]{1,0:T(8,128)(2,1)} %bitcast.16, ...), custom_call_target="tpu_custom_call" | custom-call | flops 67108864 | bytes 2621440 | tf_op jit(solution)/shard_map/pallas_call | solution.py:79
  14.5 0.0 collective-permute-done.keys.k2
  14.6 0.1 collective-permute-start.4
  14.7 1.6 %collective-permute-start.1 = (bf16[128,1024]{1,0:T(8,128)(2,1)S(1)}, bf16[128,1024]{1,0:T(8,128)(2,1)S(1)}, u32[]{:S(2)}, u32[]{:S(2)}) collective-permute-start(bf16[128,1024]{1,0:T(8,128)(2,1)S(1)} %broadcast_select_fusion.2), channel_id=1, source_target_pairs={{0,4},{4,0},{8,12},{12,8},{16,20},{20,16},{24,28},{28,24},{1,5},{5... | collective-permute-start | bytes 786440 | tf_op jit(solution)/shard_map/ppermute | solution.py:300
  16.2 2.4 %collective-permute-start.2 = (bf16[128,1024]{1,0:T(8,128)(2,1)S(1)}, bf16[128,1024]{1,0:T(8,128)(2,1)S(1)}, u32[]{:S(2)}, u32[]{:S(2)}) collective-permute-start(bf16[128,1024]{1,0:T(8,128)(2,1)S(1)} %get-tuple-element.83.v0.v), channel_id=1, source_target_pairs={{0,4},{4,8},{8,12},{12,16},{16,20},{20,24},{24,28},{1,5},{5,9},{9,... | collective-permute-start | bytes 786440 | tf_op jit(solution)/shard_map/ppermute | solution.py:296
  18.7 2.0 %shard_map.120 = (f32[128,1024]{1,0:T(8,128)S(1)}, f32[128,1024]{1,0:T(8,128)S(1)}) custom-call(s32[1,4]{1,0:T(1,128)S(1)} %copy-done, s32[2]{0:T(128)S(1)} %pad_add_fusion.place_ref, bf16[128,1024]{1,0:T(8,128)(2,1)S(1)} %get-tuple-element.77.q.q0, bf16[128,1024]{1,0:T(8,128)(2,1)S(1)} %collective-permute-done.keys.k2, ...), custom_call_target="tpu_custom_call" | custom-call | flops 67108864 | bytes 2359296 | tf_op jit(solution)/shard_map/pallas_call | solution.py:79
  20.7 1.3 %collective-permute-start.10 = (bf16[128,1024]{1,0:T(8,128)(2,1)S(1)}, bf16[128,1024]{1,0:T(8,128)(2,1)S(1)}, u32[]{:S(2)}, u32[]{:S(2)}) collective-permute-start(bf16[128,1024]{1,0:T(8,128)(2,1)S(1)} %get-tuple-element.77.q.q0), channel_id=1, source_target_pairs={{8,0},{12,4},{16,8},{20,12},{24,16},{28,20},{9,1},{13,5},{17,9},{2... | collective-permute-start | bytes 786440 | tf_op jit(solution)/shard_map/ppermute | solution.py:296
  22.0 0.1 collective-permute-start.9
  22.1 2.9 %shard_map.121 = (bf16[128,1024]{1,0:T(8,128)(2,1)S(1)}, bf16[1024,1024]{1,0:T(8,128)(2,1)S(1)}, bf16[128,1024]{1,0:T(8,128)(2,1)S(1)}, f32[128,1024]{1,0:T(8,128)S(1)}) custom-call(bf16[128,1024]{1,0:T(8,128)(2,1)} %bitcast.15, bf16[1024,1024]{1,0:T(8,128)(2,1)} %w_in.1, bf16[128,1024]{1,0:T(8,128)(2,1)} %bitcast.12), custom_call_target="tpu_custom_call" | custom-call | flops 268435456 | bytes 5767168 | tf_op jit(solution)/shard_map/pallas_call | solution.py:79
  25.0 0.0 collective-permute-done.4.refs_5_
  25.0 0.0 collective-permute-done.1.keys.k1
  25.0 1.0 %shard_map.119 = (bf16[128,1024]{1,0:T(8,128)(2,1)S(1)}, f32[128,1024]{1,0:T(8,128)S(1)}) custom-call(s32[1,4]{1,0:T(1,128)S(1)} %copy-done, s32[2]{0:T(128)S(1)} %pad_add_fusion.place_ref, bf16[128,1024]{1,0:T(8,128)(2,1)S(1)} %get-tuple-element.77.q.q0, bf16[128,1024]{1,0:T(8,128)(2,1)S(1)} %collective-permute-done.1.keys.k1), custom_call_target="tpu_custom_call" | custom-call | flops 33554432 | bytes 1310720 | tf_op jit(solution)/shard_map/pallas_call | solution.py:79
  26.0 2.0 %collective-permute-done.2.vals.v1 = bf16[128,1024]{1,0:T(8,128)(2,1)S(1)} collective-permute-done((bf16[128,1024]{1,0:T(8,128)(2,1)S(1)}, bf16[128,1024]{1,0:T(8,128)(2,1)S(1)}, u32[]{:S(2)}, u32[]{:S(2)}) %collective-permute-start.2) | collective-permute-done | bytes 262176 | tf_op jit(solution)/shard_map/ppermute | solution.py:296
  28.0 1.0 %shard_map.122 = (bf16[128,1024]{1,0:T(8,128)(2,1)S(1)}, f32[128,1024]{1,0:T(8,128)S(1)}, f32[128,128]{1,0:T(8,128)S(1)}, bf16[128,256]{1,0:T(8,128)(2,1)S(1)}, ...) custom-call(s32[2]{0:T(128)S(1)} %pad_add_fusion.place_ref, ...), custom_call_target="tpu_custom_call" | custom-call | flops 33554432 | bytes 2424832 | tf_op jit(solution)/shard_map/pallas_call | solution.py:79
  29.0 0.1 collective-permute-start.5
  29.1 0.6 collective-permute-start.6
  29.7 1.3 %collective-permute-start.7 = (bf16[128,256]{1,0:T(8,128)(2,1)S(1)}, bf16[128,256]{1,0:T(8,128)(2,1)S(1)}, u32[]{:S(2)}, u32[]{:S(2)}) collective-permute-start(bf16[128,256]{1,0:T(8,128)(2,1)S(1)} %get-tuple-element.73), channel_id=1, source_target_pairs={{0,3},{1,2},{2,1},{3,0},{4,7},{5,6},{6,5},{7,4},{8,11},{9,10},{10,... | collective-permute-start | bytes 196616 | tf_op jit(solution)/shard_map/ppermute | solution.py:300
  31.0 0.9 %shard_map.123 = (bf16[128,1024]{1,0:T(8,128)(2,1)}, bf16[128,1024]{1,0:T(8,128)(2,1)S(1)}) custom-call(f32[128,1024]{1,0:T(8,128)S(1)} %get-tuple-element.58.grad_hidden, bf16[128,1024]{1,0:T(8,128)(2,1)S(1)} %get-tuple-element.59.gates, f32[128,1024]{1,0:T(8,128)S(1)} %get-tuple-element.62.normed, f32[128,128]{1,0:T(8,128)S(1)} %get-tuple-element.63.inv_std), custom_call_target="tpu_custom_call" | custom-call | flops 8388608 | bytes 1900544 | tf_op jit(solution)/shard_map/pallas_call | solution.py:79
  31.8 0.0 collective-permute-done.10.q2
  31.8 1.3 %collective-permute-start.11 = (bf16[128,1024]{1,0:T(8,128)(2,1)S(1)}, bf16[128,1024]{1,0:T(8,128)(2,1)S(1)}, u32[]{:S(2)}, u32[]{:S(2)}) collective-permute-start(bf16[128,1024]{1,0:T(8,128)(2,1)S(1)} %get-tuple-element.64.grad_mix.g0), channel_id=1, source_target_pairs={{8,0},{12,4},{16,8},{20,12},{24,16},{28,20},{9,1},{13,5},{17,9},{2... | collective-permute-start | bytes 786440 | tf_op jit(solution)/shard_map/ppermute | solution.py:296
  33.2 0.0 copy-start.1
  33.2 2.7 %shard_map.124 = (bf16[128,1024]{1,0:T(8,128)(2,1)}, bf16[128,1024]{1,0:T(8,128)(2,1)}) custom-call(bf16[128,1024]{1,0:T(8,128)(2,1)S(1)} %get-tuple-element.48.k0.k, bf16[128,1024]{1,0:T(8,128)(2,1)S(1)} %collective-permute-done.1.keys.k1, bf16[128,1024]{1,0:T(8,128)(2,1)S(1)} %collective-permute-done.keys.k2, ...), custom_call_target="tpu_custom_call" | custom-call | flops 469762048 | bytes 6291456 | tf_op jit(solution)/shard_map/pallas_call | solution.py:79
  35.9 0.0 collective-permute-done.9.refs_7_
  35.9 2.5 %collective-permute-start.15 = (bf16[128,1024]{1,0:T(8,128)(2,1)S(1)}, bf16[128,1024]{1,0:T(8,128)(2,1)S(1)}, u32[]{:S(2)}, u32[]{:S(2)}) collective-permute-start(bf16[128,1024]{1,0:T(8,128)(2,1)S(1)} %broadcast_select_fusion.1), channel_id=1, source_target_pairs={{0,4},{4,0},{8,12},{12,8},{16,20},{20,16},{24,28},{28,24},{1,5},{5... | collective-permute-start | bytes 786440 | tf_op jit(solution)/shard_map/ppermute | solution.py:300
  38.4 1.1 %shard_map.125 = (f32[64,1024]{1,0:T(8,128)S(1)}, bf16[64,1024]{1,0:T(8,128)(2,1)S(1)}, bf16[64,1024]{1,0:T(8,128)(2,1)S(1)}, bf16[64,1024]{1,0:T(8,128)(2,1)S(1)}) custom-call(s32[2]{0:T(128)S(1)} %pad_add_fusion.place_ref, bf16[128,256]{1,0:T(8,128)(2,1)S(1)} %get-tuple-element.70.refs_0_, bf16[128,256]{1,0:T(8,128)(2,1)S(1)} %collective-permute-done.5.refs_1_, ...), custom_call_target="tpu_custom_call" | custom-call | flops 268435456 | bytes 1966080 | tf_op jit(solution)/shard_map/pallas_call | solution.py:79
  39.4 0.1 collective-permute-start.12
  39.5 3.8 %collective-permute-start.13 = (bf16[64,1024]{1,0:T(8,128)(2,1)S(1)}, bf16[64,1024]{1,0:T(8,128)(2,1)S(1)}, u32[]{:S(2)}, u32[]{:S(2)}) collective-permute-start(bf16[64,1024]{1,0:T(8,128)(2,1)S(1)} %get-tuple-element.81), channel_id=1, source_target_pairs={{0,8},{4,12},{8,0},{12,4},{16,24},{20,28},{24,16},{28,20},{1,9},{5... | collective-permute-start | bytes 393224 | tf_op jit(solution)/shard_map/ppermute | solution.py:300
  43.3 0.3 collective-permute-start.14
  43.6 0.7 collective-permute-done.11.g2
  44.3 2.7 %shard_map.126 = (f32[128,1024]{1,0:T(8,128)S(1)}, f32[128,1024]{1,0:T(8,128)S(1)}) custom-call(s32[1,4]{1,0:T(1,128)S(1)} %copy-done.1, s32[2]{0:T(128)S(1)} %pad_add_fusion.place_ref, bf16[128,1024]{1,0:T(8,128)(2,1)S(1)} %get-tuple-element.48.k0.k, bf16[128,1024]{1,0:T(8,128)(2,1)S(1)} %get-tuple-element.83.v0.v, ...), custom_call_target="tpu_custom_call" | custom-call | flops 268435456 | bytes 2621440 | tf_op jit(solution)/shard_map/pallas_call | solution.py:79
  47.0 3.8 %collective-permute-done.12.refs_0_ = bf16[64,1024]{1,0:T(8,128)(2,1)S(1)} collective-permute-done((bf16[64,1024]{1,0:T(8,128)(2,1)S(1)}, bf16[64,1024]{1,0:T(8,128)(2,1)S(1)}, u32[]{:S(2)}, u32[]{:S(2)}) %collective-permute-start.12) | collective-permute-done | bytes 131104 | tf_op jit(solution)/shard_map/ppermute | solution.py:300
  50.8 0.1 shard_map.127.mine
  50.9 1.8 %collective-permute-start.16 = (bf16[128,1024]{1,0:T(8,128)(2,1)S(1)}, bf16[128,1024]{1,0:T(8,128)(2,1)S(1)}, u32[]{:S(2)}, u32[]{:S(2)}) collective-permute-start(bf16[128,1024]{1,0:T(8,128)(2,1)S(1)} %broadcast_select_fusion), channel_id=1, source_target_pairs={{0,4},{4,0},{8,12},{12,8},{16,20},{20,16},{24,28},{28,24},{1,5},{5... | collective-permute-start | bytes 786440 | tf_op jit(solution)/shard_map/ppermute | solution.py:300
  52.7 3.4 %collective-permute-start.17 = (bf16[64,1024]{1,0:T(8,128)(2,1)S(1)}, bf16[64,1024]{1,0:T(8,128)(2,1)S(1)}, u32[]{:S(2)}, u32[]{:S(2)}) collective-permute-start(bf16[64,1024]{1,0:T(8,128)(2,1)S(1)} %shard_map.127.mine), channel_id=1, source_target_pairs={{0,16},{4,20},{8,24},{12,28},{16,0},{20,4},{24,8},{28,12},{1,17},{... | collective-permute-start | bytes 393224 | tf_op jit(solution)/shard_map/ppermute | solution.py:300
  56.0 3.0 %collective-permute-done.16.g1 = bf16[128,1024]{1,0:T(8,128)(2,1)S(1)} collective-permute-done((bf16[128,1024]{1,0:T(8,128)(2,1)S(1)}, bf16[128,1024]{1,0:T(8,128)(2,1)S(1)}, u32[]{:S(2)}, u32[]{:S(2)}) %collective-permute-start.16) | collective-permute-done | bytes 262176 | tf_op jit(solution)/shard_map/ppermute | solution.py:300
  59.0 2.9 %shard_map.128 = (bf16[128,1024]{1,0:T(8,128)(2,1)}, bf16[128,1024]{1,0:T(8,128)(2,1)}) custom-call(s32[1,4]{1,0:T(1,128)S(1)} %copy-done.1, s32[2]{0:T(128)S(1)} %pad_add_fusion.place_ref, bf16[128,1024]{1,0:T(8,128)(2,1)S(1)} %get-tuple-element.48.k0.k, bf16[128,1024]{1,0:T(8,128)(2,1)S(1)} %get-tuple-element.83.v0.v, ...), custom_call_target="tpu_custom_call" | custom-call | flops 134217728 | bytes 2621440 | tf_op jit(solution)/shard_map/pallas_call | solution.py:79
  62.0 1.5 %collective-permute-start.18 = (bf16[64,1024]{1,0:T(8,128)(2,1)S(1)}, bf16[64,1024]{1,0:T(8,128)(2,1)S(1)}, u32[]{:S(2)}, u32[]{:S(2)}) collective-permute-start(bf16[64,1024]{1,0:T(8,128)(2,1)S(1)} %shard_map.129.refs_0_), channel_id=1, source_target_pairs={{0,4},{4,0},{8,12},{12,8},{16,20},{20,16},{24,28},{28,24},{1,5},{5... | collective-permute-start | bytes 393224 | tf_op jit(solution)/shard_map/ppermute | solution.py:300
  63.5 2.0 %collective-permute-start.19 = (bf16[64,1024]{1,0:T(8,128)(2,1)S(1)}, bf16[64,1024]{1,0:T(8,128)(2,1)S(1)}, u32[]{:S(2)}, u32[]{:S(2)}) collective-permute-start(bf16[64,1024]{1,0:T(8,128)(2,1)S(1)} %shard_map.129.refs_0_), channel_id=1, source_target_pairs={{0,8},{4,12},{8,0},{12,4},{16,24},{20,28},{24,16},{28,20},{1,9},{5... | collective-permute-start | bytes 393224 | tf_op jit(solution)/shard_map/ppermute | solution.py:300
  65.5 1.2 %collective-permute-start.20 = (bf16[64,1024]{1,0:T(8,128)(2,1)S(1)}, bf16[64,1024]{1,0:T(8,128)(2,1)S(1)}, u32[]{:S(2)}, u32[]{:S(2)}) collective-permute-start(bf16[64,1024]{1,0:T(8,128)(2,1)S(1)} %shard_map.129.refs_0_), channel_id=1, source_target_pairs={{0,12},{4,8},{8,4},{12,0},{16,28},{20,24},{24,20},{28,16},{1,13},{... | collective-permute-start | bytes 393224 | tf_op jit(solution)/shard_map/ppermute | solution.py:300
  66.7 0.3 collective-permute-done.18.refs_1_
  67.0 2.6 %collective-permute-done.19.refs_2_ = bf16[64,1024]{1,0:T(8,128)(2,1)S(1)} collective-permute-done((bf16[64,1024]{1,0:T(8,128)(2,1)S(1)}, bf16[64,1024]{1,0:T(8,128)(2,1)S(1)}, u32[]{:S(2)}, u32[]{:S(2)}) %collective-permute-start.19) | collective-permute-done | bytes 131104 | tf_op jit(solution)/shard_map/ppermute | solution.py:300
  69.6 1.9 %collective-permute-done.20.refs_3_ = bf16[64,1024]{1,0:T(8,128)(2,1)S(1)} collective-permute-done((bf16[64,1024]{1,0:T(8,128)(2,1)S(1)}, bf16[64,1024]{1,0:T(8,128)(2,1)S(1)}, u32[]{:S(2)}, u32[]{:S(2)}) %collective-permute-start.20) | collective-permute-done | bytes 131104 | tf_op jit(solution)/shard_map/ppermute | solution.py:300
  71.5 1.6 %shard_map.130 = f32[256,1024]{1,0:T(8,128)} custom-call(s32[2]{0:T(128)S(1)} %pad_add_fusion.place_ref, bf16[64,1024]{1,0:T(8,128)(2,1)S(1)} %shard_map.129.refs_0_, bf16[64,1024]{1,0:T(8,128)(2,1)S(1)} %collective-permute-done.18.refs_1_, bf16[64,1024]{1,0:T(8,128)(2,1)S(1)} %collective-permute-done.19.refs_2_, ...), custom_call_target="tpu_custom_call" | custom-call | flops 262144 | bytes 1572864 | tf_op jit(solution)/shard_map/pallas_call | solution.py:79
  (15 shorter events, 0.2 us)
Async XLA Ops:
  0.6 13.9 %collective-permute-start = (bf16[128,1024]{1,0:T(8,128)(2,1)}, bf16[128,1024]{1,0:T(8,128)(2,1)S(1)}, u32[]{:S(2)}, u32[]{:S(2)}) collective-permute-start(bf16[128,1024]{1,0:T(8,128)(2,1)} %bitcast.17), channel_id=1, source_target_pairs={{0,8},{4,12},{8,16},{12,20},{16,24},{20,28},{1,9},{5,13},{9,17},{1... | collective-permute-start | bytes 786440 | tf_op jit(solution)/shard_map/ppermute | solution.py:296
  5.6 13.1 %collective-permute-start.3 = (bf16[128,1024]{1,0:T(8,128)(2,1)}, bf16[128,1024]{1,0:T(8,128)(2,1)S(1)}, u32[]{:S(2)}, u32[]{:S(2)}) collective-permute-start(bf16[128,1024]{1,0:T(8,128)(2,1)} %bitcast.19), channel_id=1, source_target_pairs={{0,8},{4,12},{8,16},{12,20},{16,24},{20,28},{1,9},{5,13},{9,17},{1... | collective-permute-start | bytes 786440 | tf_op jit(solution)/shard_map/ppermute | solution.py:296
  9.1 12.9 %collective-permute-start.8 = (bf16[128,1024]{1,0:T(8,128)(2,1)}, bf16[128,1024]{1,0:T(8,128)(2,1)S(1)}, u32[]{:S(2)}, u32[]{:S(2)}) collective-permute-start(bf16[128,1024]{1,0:T(8,128)(2,1)} %bitcast.13), channel_id=1, source_target_pairs={{0,2},{1,3},{2,0},{3,1},{4,6},{5,7},{6,4},{7,5},{8,10},{9,11},{10,... | collective-permute-start | bytes 786440 | tf_op jit(solution)/shard_map/ppermute | solution.py:300
  10.7 0.7 copy-start
  14.6 10.4 %collective-permute-start.4 = (bf16[128,1024]{1,0:T(8,128)(2,1)}, bf16[128,1024]{1,0:T(8,128)(2,1)S(1)}, u32[]{:S(2)}, u32[]{:S(2)}) collective-permute-start(bf16[128,1024]{1,0:T(8,128)(2,1)} %bitcast.14), channel_id=1, source_target_pairs={{0,1},{1,0},{2,3},{3,2},{4,5},{5,4},{6,7},{7,6},{8,9},{9,8},{10,11... | collective-permute-start | bytes 786440 | tf_op jit(solution)/shard_map/ppermute | solution.py:300
  14.7 10.3 %collective-permute-start.1 = (bf16[128,1024]{1,0:T(8,128)(2,1)S(1)}, bf16[128,1024]{1,0:T(8,128)(2,1)S(1)}, u32[]{:S(2)}, u32[]{:S(2)}) collective-permute-start(bf16[128,1024]{1,0:T(8,128)(2,1)S(1)} %broadcast_select_fusion.2), channel_id=1, source_target_pairs={{0,4},{4,0},{8,12},{12,8},{16,20},{20,16},{24,28},{28,24},{1,5},{5... | collective-permute-start | bytes 786440 | tf_op jit(solution)/shard_map/ppermute | solution.py:300
  16.2 11.8 %collective-permute-start.2 = (bf16[128,1024]{1,0:T(8,128)(2,1)S(1)}, bf16[128,1024]{1,0:T(8,128)(2,1)S(1)}, u32[]{:S(2)}, u32[]{:S(2)}) collective-permute-start(bf16[128,1024]{1,0:T(8,128)(2,1)S(1)} %get-tuple-element.83.v0.v), channel_id=1, source_target_pairs={{0,4},{4,8},{8,12},{12,16},{16,20},{20,24},{24,28},{1,5},{5,9},{9,... | collective-permute-start | bytes 786440 | tf_op jit(solution)/shard_map/ppermute | solution.py:296
  20.7 11.2 %collective-permute-start.10 = (bf16[128,1024]{1,0:T(8,128)(2,1)S(1)}, bf16[128,1024]{1,0:T(8,128)(2,1)S(1)}, u32[]{:S(2)}, u32[]{:S(2)}) collective-permute-start(bf16[128,1024]{1,0:T(8,128)(2,1)S(1)} %get-tuple-element.77.q.q0), channel_id=1, source_target_pairs={{8,0},{12,4},{16,8},{20,12},{24,16},{28,20},{9,1},{13,5},{17,9},{2... | collective-permute-start | bytes 786440 | tf_op jit(solution)/shard_map/ppermute | solution.py:296
  22.0 13.9 %collective-permute-start.9 = (bf16[128,1024]{1,0:T(8,128)(2,1)S(1)}, bf16[128,1024]{1,0:T(8,128)(2,1)S(1)}, u32[]{:S(2)}, u32[]{:S(2)}) collective-permute-start(bf16[128,1024]{1,0:T(8,128)(2,1)S(1)} %collective-permute-done.8.refs_6_), channel_id=1, source_target_pairs={{0,1},{1,0},{2,3},{3,2},{4,5},{5,4},{6,7},{7,6},{8,9},{9,8},{10,11... | collective-permute-start | bytes 786440 | tf_op jit(solution)/shard_map/ppermute | solution.py:300
  29.0 9.3 %collective-permute-start.5 = (bf16[128,256]{1,0:T(8,128)(2,1)S(1)}, bf16[128,256]{1,0:T(8,128)(2,1)S(1)}, u32[]{:S(2)}, u32[]{:S(2)}) collective-permute-start(bf16[128,256]{1,0:T(8,128)(2,1)S(1)} %get-tuple-element.71), channel_id=1, source_target_pairs={{0,1},{1,0},{2,3},{3,2},{4,5},{5,4},{6,7},{7,6},{8,9},{9,8},{10,11... | collective-permute-start | bytes 196616 | tf_op jit(solution)/shard_map/ppermute | solution.py:300
  29.1 9.3 %collective-permute-start.6 = (bf16[128,256]{1,0:T(8,128)(2,1)S(1)}, bf16[128,256]{1,0:T(8,128)(2,1)S(1)}, u32[]{:S(2)}, u32[]{:S(2)}) collective-permute-start(bf16[128,256]{1,0:T(8,128)(2,1)S(1)} %get-tuple-element.72), channel_id=1, source_target_pairs={{0,2},{1,3},{2,0},{3,1},{4,6},{5,7},{6,4},{7,5},{8,10},{9,11},{10,... | collective-permute-start | bytes 196616 | tf_op jit(solution)/shard_map/ppermute | solution.py:300
  29.7 8.7 %collective-permute-start.7 = (bf16[128,256]{1,0:T(8,128)(2,1)S(1)}, bf16[128,256]{1,0:T(8,128)(2,1)S(1)}, u32[]{:S(2)}, u32[]{:S(2)}) collective-permute-start(bf16[128,256]{1,0:T(8,128)(2,1)S(1)} %get-tuple-element.73), channel_id=1, source_target_pairs={{0,3},{1,2},{2,1},{3,0},{4,7},{5,6},{6,5},{7,4},{8,11},{9,10},{10,... | collective-permute-start | bytes 196616 | tf_op jit(solution)/shard_map/ppermute | solution.py:300
  31.8 12.4 %collective-permute-start.11 = (bf16[128,1024]{1,0:T(8,128)(2,1)S(1)}, bf16[128,1024]{1,0:T(8,128)(2,1)S(1)}, u32[]{:S(2)}, u32[]{:S(2)}) collective-permute-start(bf16[128,1024]{1,0:T(8,128)(2,1)S(1)} %get-tuple-element.64.grad_mix.g0), channel_id=1, source_target_pairs={{8,0},{12,4},{16,8},{20,12},{24,16},{28,20},{9,1},{13,5},{17,9},{2... | collective-permute-start | bytes 786440 | tf_op jit(solution)/shard_map/ppermute | solution.py:296
  33.2 11.1 %copy-start.1 = (s32[1,4]{1,0:T(1,128)S(1)}, s32[1,4]{1,0:T(1,128)}, u32[]{:S(2)}) copy-start(s32[1,4]{1,0:T(1,128)} %len_ref.9) | copy-start | bytes 52
  35.9 20.2 %collective-permute-start.15 = (bf16[128,1024]{1,0:T(8,128)(2,1)S(1)}, bf16[128,1024]{1,0:T(8,128)(2,1)S(1)}, u32[]{:S(2)}, u32[]{:S(2)}) collective-permute-start(bf16[128,1024]{1,0:T(8,128)(2,1)S(1)} %broadcast_select_fusion.1), channel_id=1, source_target_pairs={{0,4},{4,0},{8,12},{12,8},{16,20},{20,16},{24,28},{28,24},{1,5},{5... | collective-permute-start | bytes 786440 | tf_op jit(solution)/shard_map/ppermute | solution.py:300
  39.4 11.3 %collective-permute-start.12 = (bf16[64,1024]{1,0:T(8,128)(2,1)S(1)}, bf16[64,1024]{1,0:T(8,128)(2,1)S(1)}, u32[]{:S(2)}, u32[]{:S(2)}) collective-permute-start(bf16[64,1024]{1,0:T(8,128)(2,1)S(1)} %get-tuple-element.80), channel_id=1, source_target_pairs={{0,4},{4,0},{8,12},{12,8},{16,20},{20,16},{24,28},{28,24},{1,5},{5... | collective-permute-start | bytes 393224 | tf_op jit(solution)/shard_map/ppermute | solution.py:300
  39.5 11.3 %collective-permute-start.13 = (bf16[64,1024]{1,0:T(8,128)(2,1)S(1)}, bf16[64,1024]{1,0:T(8,128)(2,1)S(1)}, u32[]{:S(2)}, u32[]{:S(2)}) collective-permute-start(bf16[64,1024]{1,0:T(8,128)(2,1)S(1)} %get-tuple-element.81), channel_id=1, source_target_pairs={{0,8},{4,12},{8,0},{12,4},{16,24},{20,28},{24,16},{28,20},{1,9},{5... | collective-permute-start | bytes 393224 | tf_op jit(solution)/shard_map/ppermute | solution.py:300
  43.3 7.5 %collective-permute-start.14 = (bf16[64,1024]{1,0:T(8,128)(2,1)S(1)}, bf16[64,1024]{1,0:T(8,128)(2,1)S(1)}, u32[]{:S(2)}, u32[]{:S(2)}) collective-permute-start(bf16[64,1024]{1,0:T(8,128)(2,1)S(1)} %get-tuple-element.82), channel_id=1, source_target_pairs={{0,12},{4,8},{8,4},{12,0},{16,28},{20,24},{24,20},{28,16},{1,13},{... | collective-permute-start | bytes 393224 | tf_op jit(solution)/shard_map/ppermute | solution.py:300
  50.9 8.1 %collective-permute-start.16 = (bf16[128,1024]{1,0:T(8,128)(2,1)S(1)}, bf16[128,1024]{1,0:T(8,128)(2,1)S(1)}, u32[]{:S(2)}, u32[]{:S(2)}) collective-permute-start(bf16[128,1024]{1,0:T(8,128)(2,1)S(1)} %broadcast_select_fusion), channel_id=1, source_target_pairs={{0,4},{4,0},{8,12},{12,8},{16,20},{20,16},{24,28},{28,24},{1,5},{5... | collective-permute-start | bytes 786440 | tf_op jit(solution)/shard_map/ppermute | solution.py:300
  52.7 9.2 %collective-permute-start.17 = (bf16[64,1024]{1,0:T(8,128)(2,1)S(1)}, bf16[64,1024]{1,0:T(8,128)(2,1)S(1)}, u32[]{:S(2)}, u32[]{:S(2)}) collective-permute-start(bf16[64,1024]{1,0:T(8,128)(2,1)S(1)} %shard_map.127.mine), channel_id=1, source_target_pairs={{0,16},{4,20},{8,24},{12,28},{16,0},{20,4},{24,8},{28,12},{1,17},{... | collective-permute-start | bytes 393224 | tf_op jit(solution)/shard_map/ppermute | solution.py:300
  62.0 5.0 %collective-permute-start.18 = (bf16[64,1024]{1,0:T(8,128)(2,1)S(1)}, bf16[64,1024]{1,0:T(8,128)(2,1)S(1)}, u32[]{:S(2)}, u32[]{:S(2)}) collective-permute-start(bf16[64,1024]{1,0:T(8,128)(2,1)S(1)} %shard_map.129.refs_0_), channel_id=1, source_target_pairs={{0,4},{4,0},{8,12},{12,8},{16,20},{20,16},{24,28},{28,24},{1,5},{5... | collective-permute-start | bytes 393224 | tf_op jit(solution)/shard_map/ppermute | solution.py:300
  63.5 6.1 %collective-permute-start.19 = (bf16[64,1024]{1,0:T(8,128)(2,1)S(1)}, bf16[64,1024]{1,0:T(8,128)(2,1)S(1)}, u32[]{:S(2)}, u32[]{:S(2)}) collective-permute-start(bf16[64,1024]{1,0:T(8,128)(2,1)S(1)} %shard_map.129.refs_0_), channel_id=1, source_target_pairs={{0,8},{4,12},{8,0},{12,4},{16,24},{20,28},{24,16},{28,20},{1,9},{5... | collective-permute-start | bytes 393224 | tf_op jit(solution)/shard_map/ppermute | solution.py:300
  65.5 6.0 %collective-permute-start.20 = (bf16[64,1024]{1,0:T(8,128)(2,1)S(1)}, bf16[64,1024]{1,0:T(8,128)(2,1)S(1)}, u32[]{:S(2)}, u32[]{:S(2)}) collective-permute-start(bf16[64,1024]{1,0:T(8,128)(2,1)S(1)} %shard_map.129.refs_0_), channel_id=1, source_target_pairs={{0,12},{4,8},{8,4},{12,0},{16,28},{20,24},{24,20},{28,16},{1,13},{... | collective-permute-start | bytes 393224 | tf_op jit(solution)/shard_map/ppermute | solution.py:300

commit v7 on v6

--- a/solution.py
+++ b/solution.py
@@ -333,7 +333,7 @@
     )
     passed = jnp.where(even, k, k2)
     k1 = swapped(passed, "seq", 1)
-    v1 = shifted(after(v, passed), 1)
+    v1 = shifted(values[0], 1)
     grad, w, gate, grad_hidden = call(
         project_kernel,
         [near, kept(w_out.shape, BF16), near, wide],
@@ -349,17 +349,17 @@
         source = after(out_grad[0], passed) if d == 1 else out_grad[0] if d == low else grads[d ^ low]
         grads.append(swapped(source, "batch", low))
     mixed_far, slope2 = call(
-        second_kernel, [wide, wide], scalars, (q, k2, v2, mixed_own), 2 * block_flops
-    )
-    q2 = shifted(after(q, mixed_far), -2)
+        second_kernel, [wide, wide], scalars, (after(q, v1, grad_hidden), k2, v2, mixed_own), 2 * block_flops
+    )
+    q2 = shifted(after(q, grads[2]), -2)
     passed_q = jnp.where(even, q2, q)
     q1 = swapped(passed_q, "seq", 1)
-    attention1, slope1 = call(first_kernel, [near, wide], scalars, (after(q, grads[1]), k1), block_flops)
+    attention1, slope1 = call(first_kernel, [near, wide], scalars, (after(q, v1), k1), block_flops)
     hidden, normed, inv_std, *slices = call(
         functools.partial(forward_kernel, batch),
         [near, wide, kept((rows, 128), F32)] + [kept((rows, part), BF16)] * batch,
         (place,),
-        (attention1, v1, mixed_far, gate),
+        (attention1, v1, after(mixed_far, grads[1]), gate),
         block_flops,
         [pltpu.VMEM((rows, width), F32)],
     )
@@ -368,25 +368,18 @@
         mix_kernel, [full, near], (), (grad_hidden, gate, normed, inv_std), block_flops // 4
     )
     g2 = shifted(grad_mix, -2)
-    passed_g = jnp.where(even, g2, grad_mix)
+    g2_late = g2
 
     corners = 4
     direct = seq == 2 * corners
     rows_w = part // corners if direct else part
     share = kept((rows_w, width), BF16)
     scale = (rows * seq * batch) ** (-0.5)
-    output, grad_queries = call(
-        query_kernel,
-        [full, full],
-        (),
-        (k, k1, k2, v, v1, v2, slope0, slope1, slope2, grad_mix, hidden, w),
-        proj_flops + 6 * block_flops,
-    )
     own, *sends = call(
         functools.partial(weight_kernel, batch),
         [kept((rows_w, width), F32)] + [share] * (corners - 1 if direct else 0),
         (place,),
-        (after(hiddens[0], output), *hiddens[1:], *grads),
+        (*hiddens, *grads),
         proj_flops,
         [pltpu.VMEM((part, width), F32)],
     )
@@ -401,24 +394,36 @@
         got = [swapped(s, "seq", e + 1) for e, s in enumerate(sends)]
         (mine,) = call(corner_kernel, [share], (), (after(own, keys_part), *got), own.size * 4)
         other = swapped(mine, "seq", corners)
-        passed_g = after(passed_g, mine)
-    g1 = swapped(passed_g, "seq", 1)
-    grad_keys, grad_values = call(
-        key_end_kernel,
+        g2_late = after(g2, mine)
+    else:
+        mine = own
+    output, grad_queries = call(
+        query_kernel,
         [full, full],
-        scalars,
-        (k, after(v, mine) if direct else v, q1, g1, keys_part, values_part),
-        4 * block_flops,
-    )
+        (),
+        (k, k1, k2, v, v1, v2, slope0, slope1, slope2, grad_mix, after(hidden, mine), w),
+        proj_flops + 6 * block_flops,
+    )
+    g1 = swapped(jnp.where(even, g2_late, grad_mix), "seq", 1)
     if direct:
         (both,) = call(
             functools.partial(pair_kernel, scale),
             [share],
             (),
-            (after(mine, grad_keys), other),
+            (after(mine, output), other),
             own.size * 2,
         )
-        shares = [both] + [swapped(both, "seq", e) for e in range(1, corners)]
+    else:
+        both = own
+    grad_keys, grad_values = call(
+        key_end_kernel,
+        [full, full],
+        scalars,
+        (k, after(v, both), q1, g1, keys_part, values_part),
+        4 * block_flops,
+    )
+    if direct:
+        shares = [after(both, grad_keys)] + [swapped(both, "seq", e) for e in range(1, corners)]
         (grad_weight,) = call(
             functools.partial(place_kernel, corners),
             [jax.ShapeDtypeStruct((part, width), F32)],

time: 73.3 us -> 69 us (0.941)
  starting transfers between devices: 35.2 us -> 31.8 us
  waiting for transfers between devices: 14.2 us -> 13.4 us
    ppermute x16, starting transfers between devices: 21.7 us -> 17.4 us  [swapped(): return lax.ppermute(block, axis, xor_route(lax.axis_size(axis), mask))]
    ppermute x5, waiting for transfers between devices: 2.68 us -> 1.58 us  [shifted(): return lax.ppermute(block, 'seq', route)]
    ppermute x5, starting transfers between devices: 13.4 us -> 14.4 us  [shifted(): return lax.ppermute(block, 'seq', route)]
  transfers between devices with their start and end apart: 21 -> 21, of which waited for: 7 -> 10; matrix products, arithmetic and copies ran while one was open for 0% -> 0% of each run, Pallas kernels for 28% -> 30%
where the time goes in v7:
time: 69 us; the launch traced here: 68.8 us
  starting transfers between devices  31.8 us (46%)
  Pallas kernels  21.9 us (32%)
  waiting for transfers between devices  13.4 us (19%)
  between operations  0.83 us (1%)
    pallas_call x13, Pallas kernels, call(): pl.pallas_call(kernel, out_shape=outs, in_specs=[SMEM] * len(scalars) + (...  21.9 us
    ppermute x16, starting transfers between devices, swapped(): return lax.ppermute(block, axis, xor_route(lax.axis_size(axis), mask))  17.4 us
    ppermute x5, starting transfers between devices, shifted(): return lax.ppermute(block, 'seq', route)  14.4 us
    ppermute x16, waiting for transfers between devices, swapped(): return lax.ppermute(block, axis, xor_route(lax.axis_size(axis), mask))  11.8 us
    ppermute x5, waiting for transfers between devices, shifted(): return lax.ppermute(block, 'seq', route)  1.58 us
  transfers between devices with their start and end apart: 21, of which 10 were waited for; matrix products, arithmetic and copies ran while one was open for 0% of the time, Pallas kernels for 30%

profile of v7, /device:TPU:0, one launch (start us, length us, event | category | flops | bytes accessed | tf_op | source)
XLA Modules:
  0.0 68.8 jit_solution(17025875665471650076)
XLA Ops:
  0.6 4.9 %collective-permute-start = (bf16[128,1024]{1,0:T(8,128)(2,1)}, bf16[128,1024]{1,0:T(8,128)(2,1)S(1)}, u32[]{:S(2)}, u32[]{:S(2)}) collective-permute-start(bf16[128,1024]{1,0:T(8,128)(2,1)} %bitcast.17), channel_id=1, source_target_pairs={{0,8},{4,12},{8,16},{12,20},{16,24},{20,28},{1,9},{5,13},{9,17},{1... | collective-permute-start | bytes 786440 | tf_op jit(solution)/shard_map/ppermute | solution.py:296
  5.6 3.4 %collective-permute-start.2 = (bf16[128,1024]{1,0:T(8,128)(2,1)}, bf16[128,1024]{1,0:T(8,128)(2,1)S(1)}, u32[]{:S(2)}, u32[]{:S(2)}) collective-permute-start(bf16[128,1024]{1,0:T(8,128)(2,1)} %bitcast.19), channel_id=1, source_target_pairs={{0,4},{4,8},{8,12},{12,16},{16,20},{20,24},{24,28},{1,5},{5,9},{9,... | collective-permute-start | bytes 786440 | tf_op jit(solution)/shard_map/ppermute | solution.py:296
  9.0 3.5 %collective-permute-start.3 = (bf16[128,1024]{1,0:T(8,128)(2,1)}, bf16[128,1024]{1,0:T(8,128)(2,1)S(1)}, u32[]{:S(2)}, u32[]{:S(2)}) collective-permute-start(bf16[128,1024]{1,0:T(8,128)(2,1)} %bitcast.20), channel_id=1, source_target_pairs={{0,8},{4,12},{8,16},{12,20},{16,24},{20,28},{1,9},{5,13},{9,17},{1... | collective-permute-start | bytes 786440 | tf_op jit(solution)/shard_map/ppermute | solution.py:296
  12.5 1.6 %collective-permute-start.8 = (bf16[128,1024]{1,0:T(8,128)(2,1)}, bf16[128,1024]{1,0:T(8,128)(2,1)S(1)}, u32[]{:S(2)}, u32[]{:S(2)}) collective-permute-start(bf16[128,1024]{1,0:T(8,128)(2,1)} %bitcast.13), channel_id=1, source_target_pairs={{0,2},{1,3},{2,0},{3,1},{4,6},{5,7},{6,4},{7,5},{8,10},{9,11},{10,... | collective-permute-start | bytes 786440 | tf_op jit(solution)/shard_map/ppermute | solution.py:300
  14.1 0.1 pad_add_fusion.place_ref
  14.2 0.7 copy-done
  14.8 3.1 %shard_map.118 = (bf16[128,1024]{1,0:T(8,128)(2,1)S(1)}, bf16[128,1024]{1,0:T(8,128)(2,1)S(1)}, bf16[128,1024]{1,0:T(8,128)(2,1)S(1)}, f32[128,1024]{1,0:T(8,128)S(1)}, f32[128,1024]{1,0:T(8,128)S(1)}) custom-call(s32[1,4]{1,0:T(1,128)S(1)} %copy-done, s32[2]{0:T(128)S(1)} %pad_add_fusion.place_ref, bf16[128,1024]{1,0:T(8,128)(2,1)} %bitcast.16, ...), custom_call_target="tpu_custom_call" | custom-call | flops 67108864 | bytes 2621440 | tf_op jit(solution)/shard_map/pallas_call | solution.py:79
  17.9 0.0 collective-permute-done.keys.k2
  18.0 0.1 collective-permute-start.4
  18.1 1.6 %collective-permute-start.1 = (bf16[128,1024]{1,0:T(8,128)(2,1)S(1)}, bf16[128,1024]{1,0:T(8,128)(2,1)S(1)}, u32[]{:S(2)}, u32[]{:S(2)}) collective-permute-start(bf16[128,1024]{1,0:T(8,128)(2,1)S(1)} %broadcast_select_fusion.2), channel_id=1, source_target_pairs={{0,4},{4,0},{8,12},{12,8},{16,20},{20,16},{24,28},{28,24},{1,5},{5... | collective-permute-start | bytes 786440 | tf_op jit(solution)/shard_map/ppermute | solution.py:300
  19.7 0.3 collective-permute-done.8.refs_6_
  20.0 0.0 collective-permute-start.9
  20.0 0.0 collective-permute-done.2.vals.v1
  20.0 1.3 %collective-permute-start.10 = (bf16[128,1024]{1,0:T(8,128)(2,1)S(1)}, bf16[128,1024]{1,0:T(8,128)(2,1)S(1)}, u32[]{:S(2)}, u32[]{:S(2)}) collective-permute-start(bf16[128,1024]{1,0:T(8,128)(2,1)S(1)} %get-tuple-element.76.q.q0), channel_id=1, source_target_pairs={{8,0},{12,4},{16,8},{20,12},{24,16},{28,20},{9,1},{13,5},{17,9},{2... | collective-permute-start | bytes 786440 | tf_op jit(solution)/shard_map/ppermute | solution.py:296
  21.3 2.9 %shard_map.120 = (bf16[128,1024]{1,0:T(8,128)(2,1)S(1)}, bf16[1024,1024]{1,0:T(8,128)(2,1)S(1)}, bf16[128,1024]{1,0:T(8,128)(2,1)S(1)}, f32[128,1024]{1,0:T(8,128)S(1)}) custom-call(bf16[128,1024]{1,0:T(8,128)(2,1)} %bitcast.15, bf16[1024,1024]{1,0:T(8,128)(2,1)} %w_in.1, bf16[128,1024]{1,0:T(8,128)(2,1)} %bitcast.12), custom_call_target="tpu_custom_call" | custom-call | flops 268435456 | bytes 5767168 | tf_op jit(solution)/shard_map/pallas_call | solution.py:79
  24.2 0.0 collective-permute-done.3.vals.v2
  24.2 2.0 %shard_map.121 = (f32[128,1024]{1,0:T(8,128)S(1)}, f32[128,1024]{1,0:T(8,128)S(1)}) custom-call(s32[1,4]{1,0:T(1,128)S(1)} %copy-done, s32[2]{0:T(128)S(1)} %pad_add_fusion.place_ref, bf16[128,1024]{1,0:T(8,128)(2,1)S(1)} %get-tuple-element.76.q.q0, bf16[128,1024]{1,0:T(8,128)(2,1)S(1)} %collective-permute-done.keys.k2, ...), custom_call_target="tpu_custom_call" | custom-call | flops 67108864 | bytes 2359296 | tf_op jit(solution)/shard_map/pallas_call | solution.py:79
  26.2 0.0 collective-permute-done.4.refs_5_
  26.2 0.6 collective-permute-done.1.keys.k1
  26.8 1.0 %shard_map.119 = (bf16[128,1024]{1,0:T(8,128)(2,1)S(1)}, f32[128,1024]{1,0:T(8,128)S(1)}) custom-call(s32[1,4]{1,0:T(1,128)S(1)} %copy-done, s32[2]{0:T(128)S(1)} %pad_add_fusion.place_ref, bf16[128,1024]{1,0:T(8,128)(2,1)S(1)} %get-tuple-element.76.q.q0, bf16[128,1024]{1,0:T(8,128)(2,1)S(1)} %collective-permute-done.1.keys.k1), custom_call_target="tpu_custom_call" | custom-call | flops 33554432 | bytes 1310720 | tf_op jit(solution)/shard_map/pallas_call | solution.py:79
  27.8 0.0 copy-start.1
  27.8 1.0 %shard_map.122 = (bf16[128,1024]{1,0:T(8,128)(2,1)S(1)}, f32[128,1024]{1,0:T(8,128)S(1)}, f32[128,128]{1,0:T(8,128)S(1)}, bf16[128,256]{1,0:T(8,128)(2,1)S(1)}, ...) custom-call(s32[2]{0:T(128)S(1)} %pad_add_fusion.place_ref, ...), custom_call_target="tpu_custom_call" | custom-call | flops 33554432 | bytes 2424832 | tf_op jit(solution)/shard_map/pallas_call | solution.py:79
  28.9 0.1 collective-permute-start.5
  28.9 1.4 %collective-permute-start.6 = (bf16[128,256]{1,0:T(8,128)(2,1)S(1)}, bf16[128,256]{1,0:T(8,128)(2,1)S(1)}, u32[]{:S(2)}, u32[]{:S(2)}) collective-permute-start(bf16[128,256]{1,0:T(8,128)(2,1)S(1)} %get-tuple-element.71), channel_id=1, source_target_pairs={{0,2},{1,3},{2,0},{3,1},{4,6},{5,7},{6,4},{7,5},{8,10},{9,11},{10,... | collective-permute-start | bytes 196616 | tf_op jit(solution)/shard_map/ppermute | solution.py:300
  30.4 0.4 collective-permute-start.7
  30.8 0.9 %shard_map.123 = (bf16[128,1024]{1,0:T(8,128)(2,1)}, bf16[128,1024]{1,0:T(8,128)(2,1)S(1)}) custom-call(f32[128,1024]{1,0:T(8,128)S(1)} %get-tuple-element.57.grad_hidden, bf16[128,1024]{1,0:T(8,128)(2,1)S(1)} %get-tuple-element.61.gates, f32[128,1024]{1,0:T(8,128)S(1)} %get-tuple-element.65.normed, f32[128,128]{1,0:T(8,128)S(1)} %get-tuple-element.66.inv_std), custom_call_target="tpu_custom_call" | custom-call | flops 8388608 | bytes 1900544 | tf_op jit(solution)/shard_map/pallas_call | solution.py:79
  31.7 1.3 %collective-permute-start.11 = (bf16[128,1024]{1,0:T(8,128)(2,1)S(1)}, bf16[128,1024]{1,0:T(8,128)(2,1)S(1)}, u32[]{:S(2)}, u32[]{:S(2)}) collective-permute-start(bf16[128,1024]{1,0:T(8,128)(2,1)S(1)} %get-tuple-element.67.g0.grad_mix), channel_id=1, source_target_pairs={{8,0},{12,4},{16,8},{20,12},{24,16},{28,20},{9,1},{13,5},{17,9},{2... | collective-permute-start | bytes 786440 | tf_op jit(solution)/shard_map/ppermute | solution.py:296
  33.0 0.6 collective-permute-done.6.refs_2_
  33.6 1.2 %collective-permute-done.7.refs_3_ = bf16[128,256]{1,0:T(8,128)(2,1)S(1)} collective-permute-done((bf16[128,256]{1,0:T(8,128)(2,1)S(1)}, bf16[128,256]{1,0:T(8,128)(2,1)S(1)}, u32[]{:S(2)}, u32[]{:S(2)}) %collective-permute-start.7) | collective-permute-done | bytes 65568 | tf_op jit(solution)/shard_map/ppermute | solution.py:300
  34.7 1.1 %shard_map.124 = (f32[64,1024]{1,0:T(8,128)S(1)}, bf16[64,1024]{1,0:T(8,128)(2,1)S(1)}, bf16[64,1024]{1,0:T(8,128)(2,1)S(1)}, bf16[64,1024]{1,0:T(8,128)(2,1)S(1)}) custom-call(s32[2]{0:T(128)S(1)} %pad_add_fusion.place_ref, bf16[128,256]{1,0:T(8,128)(2,1)S(1)} %get-tuple-element.69.refs_0_, bf16[128,256]{1,0:T(8,128)(2,1)S(1)} %collective-permute-done.5.refs_1_, ...), custom_call_target="tpu_custom_call" | custom-call | flops 268435456 | bytes 1966080 | tf_op jit(solution)/shard_map/pallas_call | solution.py:79
  35.8 1.6 %collective-permute-start.12 = (bf16[64,1024]{1,0:T(8,128)(2,1)S(1)}, bf16[64,1024]{1,0:T(8,128)(2,1)S(1)}, u32[]{:S(2)}, u32[]{:S(2)}) collective-permute-start(bf16[64,1024]{1,0:T(8,128)(2,1)S(1)} %get-tuple-element.79), channel_id=1, source_target_pairs={{0,4},{4,0},{8,12},{12,8},{16,20},{20,16},{24,28},{28,24},{1,5},{5... | collective-permute-start | bytes 393224 | tf_op jit(solution)/shard_map/ppermute | solution.py:300
  37.4 2.2 %collective-permute-start.13 = (bf16[64,1024]{1,0:T(8,128)(2,1)S(1)}, bf16[64,1024]{1,0:T(8,128)(2,1)S(1)}, u32[]{:S(2)}, u32[]{:S(2)}) collective-permute-start(bf16[64,1024]{1,0:T(8,128)(2,1)S(1)} %get-tuple-element.80), channel_id=1, source_target_pairs={{0,8},{4,12},{8,0},{12,4},{16,24},{20,28},{24,16},{28,20},{1,9},{5... | collective-permute-start | bytes 393224 | tf_op jit(solution)/shard_map/ppermute | solution.py:300
  39.7 1.5 %collective-permute-start.16 = (bf16[128,1024]{1,0:T(8,128)(2,1)S(1)}, bf16[128,1024]{1,0:T(8,128)(2,1)S(1)}, u32[]{:S(2)}, u32[]{:S(2)}) collective-permute-start(bf16[128,1024]{1,0:T(8,128)(2,1)S(1)} %broadcast_select_fusion.1), channel_id=1, source_target_pairs={{0,4},{4,0},{8,12},{12,8},{16,20},{20,16},{24,28},{28,24},{1,5},{5... | collective-permute-start | bytes 786440 | tf_op jit(solution)/shard_map/ppermute | solution.py:300
  41.2 1.6 %collective-permute-done.11.g2 = bf16[128,1024]{1,0:T(8,128)(2,1)S(1)} collective-permute-done((bf16[128,1024]{1,0:T(8,128)(2,1)S(1)}, bf16[128,1024]{1,0:T(8,128)(2,1)S(1)}, u32[]{:S(2)}, u32[]{:S(2)}) %collective-permute-start.11) | collective-permute-done | bytes 262176 | tf_op jit(solution)/shard_map/ppermute | solution.py:296
  42.8 2.7 %shard_map.125 = (f32[128,1024]{1,0:T(8,128)S(1)}, f32[128,1024]{1,0:T(8,128)S(1)}) custom-call(s32[1,4]{1,0:T(1,128)S(1)} %copy-done.1, s32[2]{0:T(128)S(1)} %pad_add_fusion.place_ref, bf16[128,1024]{1,0:T(8,128)(2,1)S(1)} %get-tuple-element.50.k.k0, bf16[128,1024]{1,0:T(8,128)(2,1)S(1)} %get-tuple-element.87.v.v0, ...), custom_call_target="tpu_custom_call" | custom-call | flops 268435456 | bytes 2621440 | tf_op jit(solution)/shard_map/pallas_call | solution.py:79
  45.5 0.1 collective-permute-done.13.refs_1_
  45.6 3.7 %collective-permute-done.14.refs_2_ = bf16[64,1024]{1,0:T(8,128)(2,1)S(1)} collective-permute-done((bf16[64,1024]{1,0:T(8,128)(2,1)S(1)}, bf16[64,1024]{1,0:T(8,128)(2,1)S(1)}, u32[]{:S(2)}, u32[]{:S(2)}) %collective-permute-start.14) | collective-permute-done | bytes 131104 | tf_op jit(solution)/shard_map/ppermute | solution.py:300
  49.3 0.1 shard_map.126.mine
  49.4 0.5 collective-permute-start.17
  49.9 2.7 %collective-permute-start.15 = (bf16[64,1024]{1,0:T(8,128)(2,1)S(1)}, bf16[64,1024]{1,0:T(8,128)(2,1)S(1)}, u32[]{:S(2)}, u32[]{:S(2)}) collective-permute-start(bf16[64,1024]{1,0:T(8,128)(2,1)S(1)} %shard_map.126.mine), channel_id=1, source_target_pairs={{0,16},{4,20},{8,24},{12,28},{16,0},{20,4},{24,8},{28,12},{1,17},{... | collective-permute-start | bytes 393224 | tf_op jit(solution)/shard_map/ppermute | solution.py:300
  52.7 2.7 %shard_map.127 = (bf16[128,1024]{1,0:T(8,128)(2,1)}, bf16[128,1024]{1,0:T(8,128)(2,1)}) custom-call(bf16[128,1024]{1,0:T(8,128)(2,1)S(1)} %get-tuple-element.50.k.k0, bf16[128,1024]{1,0:T(8,128)(2,1)S(1)} %collective-permute-done.1.keys.k1, bf16[128,1024]{1,0:T(8,128)(2,1)S(1)} %collective-permute-done.keys.k2, ...), custom_call_target="tpu_custom_call" | custom-call | flops 469762048 | bytes 6291456 | tf_op jit(solution)/shard_map/pallas_call | solution.py:79
  55.4 2.3 %collective-permute-done.15.other = bf16[64,1024]{1,0:T(8,128)(2,1)S(1)} collective-permute-done((bf16[64,1024]{1,0:T(8,128)(2,1)S(1)}, bf16[64,1024]{1,0:T(8,128)(2,1)S(1)}, u32[]{:S(2)}, u32[]{:S(2)}) %collective-permute-start.15) | collective-permute-done | bytes 131104 | tf_op jit(solution)/shard_map/ppermute | solution.py:300
  57.7 0.5 collective-permute-start.18
  58.3 3.0 %collective-permute-start.20 = (bf16[64,1024]{1,0:T(8,128)(2,1)S(1)}, bf16[64,1024]{1,0:T(8,128)(2,1)S(1)}, u32[]{:S(2)}, u32[]{:S(2)}) collective-permute-start(bf16[64,1024]{1,0:T(8,128)(2,1)S(1)} %shard_map.128.refs_0_), channel_id=1, source_target_pairs={{0,12},{4,8},{8,4},{12,0},{16,28},{20,24},{24,20},{28,16},{1,13},{... | collective-permute-start | bytes 393224 | tf_op jit(solution)/shard_map/ppermute | solution.py:300
  61.3 2.9 %shard_map.129 = (bf16[128,1024]{1,0:T(8,128)(2,1)}, bf16[128,1024]{1,0:T(8,128)(2,1)}) custom-call(s32[1,4]{1,0:T(1,128)S(1)} %copy-done.1, s32[2]{0:T(128)S(1)} %pad_add_fusion.place_ref, bf16[128,1024]{1,0:T(8,128)(2,1)S(1)} %get-tuple-element.50.k.k0, bf16[128,1024]{1,0:T(8,128)(2,1)S(1)} %get-tuple-element.87.v.v0, ...), custom_call_target="tpu_custom_call" | custom-call | flops 134217728 | bytes 2621440 | tf_op jit(solution)/shard_map/pallas_call | solution.py:79
  64.2 0.5 collective-permute-done.19.refs_2_
  64.7 2.5 %collective-permute-done.20.refs_3_ = bf16[64,1024]{1,0:T(8,128)(2,1)S(1)} collective-permute-done((bf16[64,1024]{1,0:T(8,128)(2,1)S(1)}, bf16[64,1024]{1,0:T(8,128)(2,1)S(1)}, u32[]{:S(2)}, u32[]{:S(2)}) %collective-permute-start.20) | collective-permute-done | bytes 131104 | tf_op jit(solution)/shard_map/ppermute | solution.py:300
  67.2 1.6 %shard_map.130 = f32[256,1024]{1,0:T(8,128)} custom-call(s32[2]{0:T(128)S(1)} %pad_add_fusion.place_ref, bf16[64,1024]{1,0:T(8,128)(2,1)S(1)} %shard_map.128.refs_0_, bf16[64,1024]{1,0:T(8,128)(2,1)S(1)} %collective-permute-done.18.refs_1_, bf16[64,1024]{1,0:T(8,128)(2,1)S(1)} %collective-permute-done.19.refs_2_, ...), custom_call_target="tpu_custom_call" | custom-call | flops 262144 | bytes 1572864 | tf_op jit(solution)/shard_map/pallas_call | solution.py:79
  (15 shorter events, 0.2 us)
Async XLA Ops:
  0.6 17.3 %collective-permute-start = (bf16[128,1024]{1,0:T(8,128)(2,1)}, bf16[128,1024]{1,0:T(8,128)(2,1)S(1)}, u32[]{:S(2)}, u32[]{:S(2)}) collective-permute-start(bf16[128,1024]{1,0:T(8,128)(2,1)} %bitcast.17), channel_id=1, source_target_pairs={{0,8},{4,12},{8,16},{12,20},{16,24},{20,28},{1,9},{5,13},{9,17},{1... | collective-permute-start | bytes 786440 | tf_op jit(solution)/shard_map/ppermute | solution.py:296
  5.6 14.4 %collective-permute-start.2 = (bf16[128,1024]{1,0:T(8,128)(2,1)}, bf16[128,1024]{1,0:T(8,128)(2,1)S(1)}, u32[]{:S(2)}, u32[]{:S(2)}) collective-permute-start(bf16[128,1024]{1,0:T(8,128)(2,1)} %bitcast.19), channel_id=1, source_target_pairs={{0,4},{4,8},{8,12},{12,16},{16,20},{20,24},{24,28},{1,5},{5,9},{9,... | collective-permute-start | bytes 786440 | tf_op jit(solution)/shard_map/ppermute | solution.py:296
  9.0 15.2 %collective-permute-start.3 = (bf16[128,1024]{1,0:T(8,128)(2,1)}, bf16[128,1024]{1,0:T(8,128)(2,1)S(1)}, u32[]{:S(2)}, u32[]{:S(2)}) collective-permute-start(bf16[128,1024]{1,0:T(8,128)(2,1)} %bitcast.20), channel_id=1, source_target_pairs={{0,8},{4,12},{8,16},{12,20},{16,24},{20,28},{1,9},{5,13},{9,17},{1... | collective-permute-start | bytes 786440 | tf_op jit(solution)/shard_map/ppermute | solution.py:296
  12.5 7.5 %collective-permute-start.8 = (bf16[128,1024]{1,0:T(8,128)(2,1)}, bf16[128,1024]{1,0:T(8,128)(2,1)S(1)}, u32[]{:S(2)}, u32[]{:S(2)}) collective-permute-start(bf16[128,1024]{1,0:T(8,128)(2,1)} %bitcast.13), channel_id=1, source_target_pairs={{0,2},{1,3},{2,0},{3,1},{4,6},{5,7},{6,4},{7,5},{8,10},{9,11},{10,... | collective-permute-start | bytes 786440 | tf_op jit(solution)/shard_map/ppermute | solution.py:300
  14.1 0.7 copy-start
  18.0 8.2 %collective-permute-start.4 = (bf16[128,1024]{1,0:T(8,128)(2,1)}, bf16[128,1024]{1,0:T(8,128)(2,1)S(1)}, u32[]{:S(2)}, u32[]{:S(2)}) collective-permute-start(bf16[128,1024]{1,0:T(8,128)(2,1)} %bitcast.14), channel_id=1, source_target_pairs={{0,1},{1,0},{2,3},{3,2},{4,5},{5,4},{6,7},{7,6},{8,9},{9,8},{10,11... | collective-permute-start | bytes 786440 | tf_op jit(solution)/shard_map/ppermute | solution.py:300
  18.1 8.7 %collective-permute-start.1 = (bf16[128,1024]{1,0:T(8,128)(2,1)S(1)}, bf16[128,1024]{1,0:T(8,128)(2,1)S(1)}, u32[]{:S(2)}, u32[]{:S(2)}) collective-permute-start(bf16[128,1024]{1,0:T(8,128)(2,1)S(1)} %broadcast_select_fusion.2), channel_id=1, source_target_pairs={{0,4},{4,0},{8,12},{12,8},{16,20},{20,16},{24,28},{28,24},{1,5},{5... | collective-permute-start | bytes 786440 | tf_op jit(solution)/shard_map/ppermute | solution.py:300
  20.0 11.7 %collective-permute-start.9 = (bf16[128,1024]{1,0:T(8,128)(2,1)S(1)}, bf16[128,1024]{1,0:T(8,128)(2,1)S(1)}, u32[]{:S(2)}, u32[]{:S(2)}) collective-permute-start(bf16[128,1024]{1,0:T(8,128)(2,1)S(1)} %collective-permute-done.8.refs_6_), channel_id=1, source_target_pairs={{0,1},{1,0},{2,3},{3,2},{4,5},{5,4},{6,7},{7,6},{8,9},{9,8},{10,11... | collective-permute-start | bytes 786440 | tf_op jit(solution)/shard_map/ppermute | solution.py:300
  20.0 19.6 %collective-permute-start.10 = (bf16[128,1024]{1,0:T(8,128)(2,1)S(1)}, bf16[128,1024]{1,0:T(8,128)(2,1)S(1)}, u32[]{:S(2)}, u32[]{:S(2)}) collective-permute-start(bf16[128,1024]{1,0:T(8,128)(2,1)S(1)} %get-tuple-element.76.q.q0), channel_id=1, source_target_pairs={{8,0},{12,4},{16,8},{20,12},{24,16},{28,20},{9,1},{13,5},{17,9},{2... | collective-permute-start | bytes 786440 | tf_op jit(solution)/shard_map/ppermute | solution.py:296
  27.8 15.0 %copy-start.1 = (s32[1,4]{1,0:T(1,128)S(1)}, s32[1,4]{1,0:T(1,128)}, u32[]{:S(2)}) copy-start(s32[1,4]{1,0:T(1,128)} %len_ref.9) | copy-start | bytes 52
  28.9 4.1 %collective-permute-start.5 = (bf16[128,256]{1,0:T(8,128)(2,1)S(1)}, bf16[128,256]{1,0:T(8,128)(2,1)S(1)}, u32[]{:S(2)}, u32[]{:S(2)}) collective-permute-start(bf16[128,256]{1,0:T(8,128)(2,1)S(1)} %get-tuple-element.70), channel_id=1, source_target_pairs={{0,1},{1,0},{2,3},{3,2},{4,5},{5,4},{6,7},{7,6},{8,9},{9,8},{10,11... | collective-permute-start | bytes 196616 | tf_op jit(solution)/shard_map/ppermute | solution.py:300
  28.9 4.6 %collective-permute-start.6 = (bf16[128,256]{1,0:T(8,128)(2,1)S(1)}, bf16[128,256]{1,0:T(8,128)(2,1)S(1)}, u32[]{:S(2)}, u32[]{:S(2)}) collective-permute-start(bf16[128,256]{1,0:T(8,128)(2,1)S(1)} %get-tuple-element.71), channel_id=1, source_target_pairs={{0,2},{1,3},{2,0},{3,1},{4,6},{5,7},{6,4},{7,5},{8,10},{9,11},{10,... | collective-permute-start | bytes 196616 | tf_op jit(solution)/shard_map/ppermute | solution.py:300
  30.4 4.4 %collective-permute-start.7 = (bf16[128,256]{1,0:T(8,128)(2,1)S(1)}, bf16[128,256]{1,0:T(8,128)(2,1)S(1)}, u32[]{:S(2)}, u32[]{:S(2)}) collective-permute-start(bf16[128,256]{1,0:T(8,128)(2,1)S(1)} %get-tuple-element.72), channel_id=1, source_target_pairs={{0,3},{1,2},{2,1},{3,0},{4,7},{5,6},{6,5},{7,4},{8,11},{9,10},{10,... | collective-permute-start | bytes 196616 | tf_op jit(solution)/shard_map/ppermute | solution.py:300
  31.7 11.1 %collective-permute-start.11 = (bf16[128,1024]{1,0:T(8,128)(2,1)S(1)}, bf16[128,1024]{1,0:T(8,128)(2,1)S(1)}, u32[]{:S(2)}, u32[]{:S(2)}) collective-permute-start(bf16[128,1024]{1,0:T(8,128)(2,1)S(1)} %get-tuple-element.67.g0.grad_mix), channel_id=1, source_target_pairs={{8,0},{12,4},{16,8},{20,12},{24,16},{28,20},{9,1},{13,5},{17,9},{2... | collective-permute-start | bytes 786440 | tf_op jit(solution)/shard_map/ppermute | solution.py:296
  35.8 9.7 %collective-permute-start.12 = (bf16[64,1024]{1,0:T(8,128)(2,1)S(1)}, bf16[64,1024]{1,0:T(8,128)(2,1)S(1)}, u32[]{:S(2)}, u32[]{:S(2)}) collective-permute-start(bf16[64,1024]{1,0:T(8,128)(2,1)S(1)} %get-tuple-element.79), channel_id=1, source_target_pairs={{0,4},{4,0},{8,12},{12,8},{16,20},{20,16},{24,28},{28,24},{1,5},{5... | collective-permute-start | bytes 393224 | tf_op jit(solution)/shard_map/ppermute | solution.py:300
  37.4 8.2 %collective-permute-start.13 = (bf16[64,1024]{1,0:T(8,128)(2,1)S(1)}, bf16[64,1024]{1,0:T(8,128)(2,1)S(1)}, u32[]{:S(2)}, u32[]{:S(2)}) collective-permute-start(bf16[64,1024]{1,0:T(8,128)(2,1)S(1)} %get-tuple-element.80), channel_id=1, source_target_pairs={{0,8},{4,12},{8,0},{12,4},{16,24},{20,28},{24,16},{28,20},{1,9},{5... | collective-permute-start | bytes 393224 | tf_op jit(solution)/shard_map/ppermute | solution.py:300
  39.6 9.7 %collective-permute-start.14 = (bf16[64,1024]{1,0:T(8,128)(2,1)S(1)}, bf16[64,1024]{1,0:T(8,128)(2,1)S(1)}, u32[]{:S(2)}, u32[]{:S(2)}) collective-permute-start(bf16[64,1024]{1,0:T(8,128)(2,1)S(1)} %get-tuple-element.81), channel_id=1, source_target_pairs={{0,12},{4,8},{8,4},{12,0},{16,28},{20,24},{24,20},{28,16},{1,13},{... | collective-permute-start | bytes 393224 | tf_op jit(solution)/shard_map/ppermute | solution.py:300
  39.7 21.6 %collective-permute-start.16 = (bf16[128,1024]{1,0:T(8,128)(2,1)S(1)}, bf16[128,1024]{1,0:T(8,128)(2,1)S(1)}, u32[]{:S(2)}, u32[]{:S(2)}) collective-permute-start(bf16[128,1024]{1,0:T(8,128)(2,1)S(1)} %broadcast_select_fusion.1), channel_id=1, source_target_pairs={{0,4},{4,0},{8,12},{12,8},{16,20},{20,16},{24,28},{28,24},{1,5},{5... | collective-permute-start | bytes 786440 | tf_op jit(solution)/shard_map/ppermute | solution.py:300
  49.4 11.9 %collective-permute-start.17 = (bf16[128,1024]{1,0:T(8,128)(2,1)S(1)}, bf16[128,1024]{1,0:T(8,128)(2,1)S(1)}, u32[]{:S(2)}, u32[]{:S(2)}) collective-permute-start(bf16[128,1024]{1,0:T(8,128)(2,1)S(1)} %broadcast_select_fusion), channel_id=1, source_target_pairs={{0,4},{4,0},{8,12},{12,8},{16,20},{20,16},{24,28},{28,24},{1,5},{5... | collective-permute-start | bytes 786440 | tf_op jit(solution)/shard_map/ppermute | solution.py:300
  49.9 7.8 %collective-permute-start.15 = (bf16[64,1024]{1,0:T(8,128)(2,1)S(1)}, bf16[64,1024]{1,0:T(8,128)(2,1)S(1)}, u32[]{:S(2)}, u32[]{:S(2)}) collective-permute-start(bf16[64,1024]{1,0:T(8,128)(2,1)S(1)} %shard_map.126.mine), channel_id=1, source_target_pairs={{0,16},{4,20},{8,24},{12,28},{16,0},{20,4},{24,8},{28,12},{1,17},{... | collective-permute-start | bytes 393224 | tf_op jit(solution)/shard_map/ppermute | solution.py:300
  57.7 6.5 %collective-permute-start.18 = (bf16[64,1024]{1,0:T(8,128)(2,1)S(1)}, bf16[64,1024]{1,0:T(8,128)(2,1)S(1)}, u32[]{:S(2)}, u32[]{:S(2)}) collective-permute-start(bf16[64,1024]{1,0:T(8,128)(2,1)S(1)} %shard_map.128.refs_0_), channel_id=1, source_target_pairs={{0,4},{4,0},{8,12},{12,8},{16,20},{20,16},{24,28},{28,24},{1,5},{5... | collective-permute-start | bytes 393224 | tf_op jit(solution)/shard_map/ppermute | solution.py:300
  58.3 6.4 %collective-permute-start.19 = (bf16[64,1024]{1,0:T(8,128)(2,1)S(1)}, bf16[64,1024]{1,0:T(8,128)(2,1)S(1)}, u32[]{:S(2)}, u32[]{:S(2)}) collective-permute-start(bf16[64,1024]{1,0:T(8,128)(2,1)S(1)} %shard_map.128.refs_0_), channel_id=1, source_target_pairs={{0,8},{4,12},{8,0},{12,4},{16,24},{20,28},{24,16},{28,20},{1,9},{5... | collective-permute-start | bytes 393224 | tf_op jit(solution)/shard_map/ppermute | solution.py:300
  58.3 8.9 %collective-permute-start.20 = (bf16[64,1024]{1,0:T(8,128)(2,1)S(1)}, bf16[64,1024]{1,0:T(8,128)(2,1)S(1)}, u32[]{:S(2)}, u32[]{:S(2)}) collective-permute-start(bf16[64,1024]{1,0:T(8,128)(2,1)S(1)} %shard_map.128.refs_0_), channel_id=1, source_target_pairs={{0,12},{4,8},{8,4},{12,0},{16,28},{20,24},{24,20},{28,16},{1,13},{... | collective-permute-start | bytes 393224 | tf_op jit(solution)/shard_map/ppermute | solution.py:300

commit v8 on v7

--- a/solution.py
+++ b/solution.py
@@ -172,7 +172,7 @@
     hidden[...] = (normed[...] * gates[...].astype(F32)).astype(BF16)
     part = width // groups
     for d, ref in enumerate(slices):
-        at = pl.multiple_of((place_ref[1] ^ d) * part, 128)
+        at = pl.multiple_of((place_ref[1] // 2 ^ d) * part, 128)
         ref[...] = hidden[:, pl.ds(at, part)]
 
 
@@ -245,15 +245,22 @@
 def weight_kernel(groups, place_ref, *refs):
     hidden = jnp.concatenate([ref[...] for ref in refs[:groups]], axis=0)
     grads = jnp.concatenate([ref[...] for ref in refs[groups : 2 * groups]], axis=0)
-    own = refs[2 * groups]
-    sends = refs[2 * groups + 1 : -1]
-    total = refs[-1]
+    own, send, total = refs[2 * groups :]
+    rows = own.shape[0]
+    side = place_ref[1] & 1
     total[...] = dot_tn(hidden, grads)
-    if not sends:
-        own[...] = total[...]
+    own[...] = total[pl.ds(pl.multiple_of(side * rows, rows), rows), :]
+    send[...] = total[pl.ds(pl.multiple_of((1 - side) * rows, rows), rows), :].astype(BF16)
+
+
+def join_kernel(corners, place_ref, mine, got, own, *rest):
+    if not rest:
+        own[...] = mine[...] + got[...].astype(F32)
         return
+    sends, total = rest[:-1], rest[-1]
+    total[...] = mine[...] + got[...].astype(F32)
     rows = own.shape[0]
-    corner = place_ref[0] & len(sends)
+    corner = place_ref[0] & (corners - 1)
     own[...] = total[pl.ds(pl.multiple_of(corner * rows, rows), rows), :]
     for e, ref in enumerate(sends):
         at = pl.multiple_of((corner ^ (e + 1)) * rows, rows)
@@ -322,48 +329,45 @@
 
     k2 = shifted(keys[0], 2)
     v2 = shifted(values[0], 2)
+    passed = jnp.where(even, keys[0], k2)
+    k1 = swapped(passed, "seq", 1)
     q, k, v, mixed_own, slope0 = call(
         own_kernel,
         [near, near, near, wide, wide],
         scalars,
-        (in_hbm(queries[0]), in_hbm(keys[0]), in_hbm(values[0])),
+        (in_hbm(after(queries[0], passed)), in_hbm(keys[0]), in_hbm(values[0])),
         2 * block_flops,
         [pltpu.SemaphoreType.DMA((3,))],
         [hbm] * 3,
     )
-    passed = jnp.where(even, k, k2)
-    k1 = swapped(passed, "seq", 1)
     v1 = shifted(values[0], 1)
     grad, w, gate, grad_hidden = call(
         project_kernel,
         [near, kept(w_out.shape, BF16), near, wide],
         (),
-        (in_hbm(after(out_grad[0], passed)), in_hbm(w_out), in_hbm(gates[0])),
+        (in_hbm(after(out_grad[0], mixed_own)), in_hbm(w_out), in_hbm(gates[0])),
         proj_flops,
         [pltpu.SemaphoreType.DMA((CHUNKS + 2,))],
         [hbm] * 3,
     )
-    grads = [grad]
-    for d in range(1, batch):
-        low = d & -d
-        source = after(out_grad[0], passed) if d == 1 else out_grad[0] if d == low else grads[d ^ low]
-        grads.append(swapped(source, "batch", low))
+    pairs = batch // 2
+    grads = [grad] + [swapped(out_grad[0], "batch", 2 * d) for d in range(1, pairs)]
     mixed_far, slope2 = call(
-        second_kernel, [wide, wide], scalars, (after(q, v1, grad_hidden), k2, v2, mixed_own), 2 * block_flops
-    )
-    q2 = shifted(after(q, grads[2]), -2)
+        second_kernel, [wide, wide], scalars, (after(q, grad_hidden), k2, v2, mixed_own), 2 * block_flops
+    )
+    q2 = shifted(after(q, grad_hidden), -2)
     passed_q = jnp.where(even, q2, q)
     q1 = swapped(passed_q, "seq", 1)
-    attention1, slope1 = call(first_kernel, [near, wide], scalars, (after(q, v1), k1), block_flops)
+    attention1, slope1 = call(first_kernel, [near, wide], scalars, (after(q, mixed_far), k1), block_flops)
     hidden, normed, inv_std, *slices = call(
-        functools.partial(forward_kernel, batch),
-        [near, wide, kept((rows, 128), F32)] + [kept((rows, part), BF16)] * batch,
+        functools.partial(forward_kernel, pairs),
+        [near, wide, kept((rows, 128), F32)] + [kept((rows, 2 * part), BF16)] * pairs,
         (place,),
         (attention1, v1, after(mixed_far, grads[1]), gate),
         block_flops,
         [pltpu.VMEM((rows, width), F32)],
     )
-    hiddens = [slices[0]] + [swapped(slices[d], "batch", d) for d in range(1, batch)]
+    hiddens = [slices[0]] + [swapped(slices[d], "batch", 2 * d) for d in range(1, pairs)]
     grad_gates, grad_mix = call(
         mix_kernel, [full, near], (), (grad_hidden, gate, normed, inv_std), block_flops // 4
     )
@@ -375,13 +379,21 @@
     rows_w = part // corners if direct else part
     share = kept((rows_w, width), BF16)
     scale = (rows * seq * batch) ** (-0.5)
+    mine, send = call(
+        functools.partial(weight_kernel, pairs),
+        [kept((part, width), F32), kept((part, width), BF16)],
+        (place,),
+        (after(hiddens[0], passed_q), *hiddens[1:], *grads),
+        proj_flops,
+        [pltpu.VMEM((2 * part, width), F32)],
+    )
     own, *sends = call(
-        functools.partial(weight_kernel, batch),
+        functools.partial(join_kernel, corners),
         [kept((rows_w, width), F32)] + [share] * (corners - 1 if direct else 0),
         (place,),
-        (*hiddens, *grads),
-        proj_flops,
-        [pltpu.VMEM((part, width), F32)],
+        (mine, swapped(send, "batch", 1)),
+        part * width,
+        [pltpu.VMEM((part, width), F32)] if direct else [],
     )
     keys_part, values_part = call(
         key_kernel,

time: 69 us -> 72.7 us (1.054)
  waiting for transfers between devices: 13.4 us -> 16.4 us
  starting transfers between devices: 31.8 us -> 30.7 us
  other arithmetic: 0.16 us -> 1.12 us
  Pallas kernels: 21.9 us -> 22.8 us
    ppermute x5, waiting for transfers between devices: 1.58 us -> 6.88 us  [shifted(): return lax.ppermute(block, 'seq', route)]
    ppermute x16 -> x13, waiting for transfers between devices: 11.8 us -> 9.48 us  [swapped(): return lax.ppermute(block, axis, xor_route(lax.axis_size(axis), mask))]
    ppermute x16 -> x13, starting transfers between devices: 17.4 us -> 16.3 us  [swapped(): return lax.ppermute(block, axis, xor_route(lax.axis_size(axis), mask))]
    select_n x1, other arithmetic: 0.03 us -> 0.98 us  [on_device(): passed = jnp.where(even, keys[0], k2)]
    pallas_call x13 -> x14, Pallas kernels: 21.9 us -> 22.8 us  [call(): pl.pallas_call(kernel, out_shape=outs, in_specs=[SMEM] * len(scalars) + (...]
  transfers between devices with their start and end apart: 21 -> 18, of which waited for: 10 -> 8; matrix products, arithmetic and copies ran while one was open for 0% -> 2% of each run, Pallas kernels for 30% -> 28%
where the time goes in v8:
time: 72.7 us; the launch traced here: 72.4 us
  starting transfers between devices  30.7 us (42%)
  Pallas kernels  22.8 us (31%)
  waiting for transfers between devices  16.4 us (23%)
  other arithmetic  1.12 us (2%)
  between operations  0.81 us (1%)
    pallas_call x14, Pallas kernels, call(): pl.pallas_call(kernel, out_shape=outs, in_specs=[SMEM] * len(scalars) + (...  22.8 us
    ppermute x13, starting transfers between devices, swapped(): return lax.ppermute(block, axis, xor_route(lax.axis_size(axis), mask))  16.3 us
    ppermute x5, starting transfers between devices, shifted(): return lax.ppermute(block, 'seq', route)  14.4 us
    ppermute x13, waiting for transfers between devices, swapped(): return lax.ppermute(block, axis, xor_route(lax.axis_size(axis), mask))  9.48 us
    ppermute x5, waiting for transfers between devices, shifted(): return lax.ppermute(block, 'seq', route)  6.88 us
  transfers between devices with their start and end apart: 18, of which 8 were waited for; matrix products, arithmetic and copies ran while one was open for 2% of the time, Pallas kernels for 28%

profile of v8, /device:TPU:0, one launch (start us, length us, event | category | flops | bytes accessed | tf_op | source)
XLA Modules:
  0.0 72.4 jit_solution(6310748536705873649)
XLA Ops:
  0.6 4.9 %collective-permute-start = (bf16[128,1024]{1,0:T(8,128)(2,1)}, bf16[128,1024]{1,0:T(8,128)(2,1)S(1)}, u32[]{:S(2)}, u32[]{:S(2)}) collective-permute-start(bf16[128,1024]{1,0:T(8,128)(2,1)} %bitcast.13), channel_id=1, source_target_pairs={{0,8},{4,12},{8,16},{12,20},{16,24},{20,28},{1,9},{5,13},{9,17},{1... | collective-permute-start | bytes 786440 | tf_op jit(solution)/shard_map/ppermute | solution.py:303
  5.6 3.4 %collective-permute-start.2 = (bf16[128,1024]{1,0:T(8,128)(2,1)}, bf16[128,1024]{1,0:T(8,128)(2,1)S(1)}, u32[]{:S(2)}, u32[]{:S(2)}) collective-permute-start(bf16[128,1024]{1,0:T(8,128)(2,1)} %bitcast.19), channel_id=1, source_target_pairs={{0,4},{4,8},{8,12},{12,16},{16,20},{20,24},{24,28},{1,5},{5,9},{9,... | collective-permute-start | bytes 786440 | tf_op jit(solution)/shard_map/ppermute | solution.py:303
  9.0 3.5 %collective-permute-start.3 = (bf16[128,1024]{1,0:T(8,128)(2,1)}, bf16[128,1024]{1,0:T(8,128)(2,1)S(1)}, u32[]{:S(2)}, u32[]{:S(2)}) collective-permute-start(bf16[128,1024]{1,0:T(8,128)(2,1)} %bitcast.20), channel_id=1, source_target_pairs={{0,8},{4,12},{8,16},{12,20},{16,24},{20,28},{1,9},{5,13},{9,17},{1... | collective-permute-start | bytes 786440 | tf_op jit(solution)/shard_map/ppermute | solution.py:303
  12.5 1.6 %collective-permute-start.4 = (bf16[128,1024]{1,0:T(8,128)(2,1)}, bf16[128,1024]{1,0:T(8,128)(2,1)S(1)}, u32[]{:S(2)}, u32[]{:S(2)}) collective-permute-start(bf16[128,1024]{1,0:T(8,128)(2,1)} %bitcast.16), channel_id=1, source_target_pairs={{0,2},{1,3},{2,0},{3,1},{4,6},{5,7},{6,4},{7,5},{8,10},{9,11},{10,... | collective-permute-start | bytes 786440 | tf_op jit(solution)/shard_map/ppermute | solution.py:307
  14.1 0.1 pad_add_fusion.place_ref
  14.1 0.0 collective-permute-done.keys.k2
  14.2 1.0 %broadcast_select_fusion.2 = bf16[128,1024]{1,0:T(8,128)(2,1)S(1)} fusion(bf16[128,1024]{1,0:T(8,128)(2,1)S(1)} %collective-permute-done.keys.k2, pred[]{:T(512)S(6)} %eq.3, bf16[1,128,1024]{2,1,0:T(8,128)(2,1)} %param.8), kind=kLoop, calls=%fused_computation.2 | loop fusion | flops 131072 | bytes 786433 | tf_op jit(solution)/shard_map/jit(_where)/select_n | solution.py:332
  15.1 1.6 %collective-permute-start.1 = (bf16[128,1024]{1,0:T(8,128)(2,1)S(1)}, bf16[128,1024]{1,0:T(8,128)(2,1)S(1)}, u32[]{:S(2)}, u32[]{:S(2)}) collective-permute-start(bf16[128,1024]{1,0:T(8,128)(2,1)S(1)} %broadcast_select_fusion.2), channel_id=1, source_target_pairs={{0,4},{4,0},{8,12},{12,8},{16,20},{20,16},{24,28},{28,24},{1,5},{5... | collective-permute-start | bytes 786440 | tf_op jit(solution)/shard_map/ppermute | solution.py:307
  16.8 0.7 copy-done
  17.4 3.1 %shard_map.118 = (bf16[128,1024]{1,0:T(8,128)(2,1)S(1)}, bf16[128,1024]{1,0:T(8,128)(2,1)S(1)}, bf16[128,1024]{1,0:T(8,128)(2,1)S(1)}, f32[128,1024]{1,0:T(8,128)S(1)}, f32[128,1024]{1,0:T(8,128)S(1)}) custom-call(s32[1,4]{1,0:T(1,128)S(1)} %copy-done, s32[2]{0:T(128)S(1)} %pad_add_fusion.place_ref, bf16[128,1024]{1,0:T(8,128)(2,1)} %bitcast.18, ...), custom_call_target="tpu_custom_call" | custom-call | flops 67108864 | bytes 2621440 | tf_op jit(solution)/shard_map/pallas_call | solution.py:79
  20.5 2.9 %shard_map.119 = (bf16[128,1024]{1,0:T(8,128)(2,1)S(1)}, bf16[1024,1024]{1,0:T(8,128)(2,1)S(1)}, bf16[128,1024]{1,0:T(8,128)(2,1)S(1)}, f32[128,1024]{1,0:T(8,128)S(1)}) custom-call(bf16[128,1024]{1,0:T(8,128)(2,1)} %bitcast.17, bf16[1024,1024]{1,0:T(8,128)(2,1)} %w_in.1, bf16[128,1024]{1,0:T(8,128)(2,1)} %bitcast.15), custom_call_target="tpu_custom_call" | custom-call | flops 268435456 | bytes 5767168 | tf_op jit(solution)/shard_map/pallas_call | solution.py:79
  23.4 1.3 %collective-permute-start.5 = (bf16[128,1024]{1,0:T(8,128)(2,1)S(1)}, bf16[128,1024]{1,0:T(8,128)(2,1)S(1)}, u32[]{:S(2)}, u32[]{:S(2)}) collective-permute-start(bf16[128,1024]{1,0:T(8,128)(2,1)S(1)} %get-tuple-element.61.q.q0), channel_id=1, source_target_pairs={{8,0},{12,4},{16,8},{20,12},{24,16},{28,20},{9,1},{13,5},{17,9},{2... | collective-permute-start | bytes 786440 | tf_op jit(solution)/shard_map/ppermute | solution.py:303
  24.7 0.0 collective-permute-done.3.vals.v2
  24.7 2.0 %shard_map.120 = (f32[128,1024]{1,0:T(8,128)S(1)}, f32[128,1024]{1,0:T(8,128)S(1)}) custom-call(s32[1,4]{1,0:T(1,128)S(1)} %copy-done, s32[2]{0:T(128)S(1)} %pad_add_fusion.place_ref, bf16[128,1024]{1,0:T(8,128)(2,1)S(1)} %get-tuple-element.61.q.q0, bf16[128,1024]{1,0:T(8,128)(2,1)S(1)} %collective-permute-done.keys.k2, ...), custom_call_target="tpu_custom_call" | custom-call | flops 67108864 | bytes 2359296 | tf_op jit(solution)/shard_map/pallas_call | solution.py:79
  26.7 0.0 collective-permute-done.4.refs_3_
  26.8 1.0 %shard_map.121 = (bf16[128,1024]{1,0:T(8,128)(2,1)S(1)}, f32[128,1024]{1,0:T(8,128)S(1)}) custom-call(s32[1,4]{1,0:T(1,128)S(1)} %copy-done, s32[2]{0:T(128)S(1)} %pad_add_fusion.place_ref, bf16[128,1024]{1,0:T(8,128)(2,1)S(1)} %get-tuple-element.61.q.q0, bf16[128,1024]{1,0:T(8,128)(2,1)S(1)} %collective-permute-done.1.keys.k1), custom_call_target="tpu_custom_call" | custom-call | flops 33554432 | bytes 1310720 | tf_op jit(solution)/shard_map/pallas_call | solution.py:79
  27.8 1.0 %shard_map.122 = (bf16[128,1024]{1,0:T(8,128)(2,1)S(1)}, f32[128,1024]{1,0:T(8,128)S(1)}, f32[128,128]{1,0:T(8,128)S(1)}, bf16[128,512]{1,0:T(8,128)(2,1)S(1)}, bf16[128,512]{1,0:T(8,128)(2,1)S(1)}) custom-call(s32[2]{0:T(128)S(1)} %pad_add_fusion.place_ref, bf16[128,1024]{1,0:T(8,128)(2,1)S(1)} %get-tuple-element.65.attention, ...), custom_call_target="tpu_custom_call" | custom-call | flops 33554432 | bytes 2424832 | tf_op jit(solution)/shard_map/pallas_call | solution.py:79
  28.8 0.6 collective-permute-start.6
  29.4 2.6 %collective-permute-done.5.q2 = bf16[128,1024]{1,0:T(8,128)(2,1)S(1)} collective-permute-done((bf16[128,1024]{1,0:T(8,128)(2,1)S(1)}, bf16[128,1024]{1,0:T(8,128)(2,1)S(1)}, u32[]{:S(2)}, u32[]{:S(2)}) %collective-permute-start.5) | collective-permute-done | bytes 262176 | tf_op jit(solution)/shard_map/ppermute | solution.py:303
  32.0 1.8 %collective-permute-done.6.refs_1_ = bf16[128,512]{1,0:T(8,128)(2,1)S(1)} collective-permute-done((bf16[128,512]{1,0:T(8,128)(2,1)S(1)}, bf16[128,512]{1,0:T(8,128)(2,1)S(1)}, u32[]{:S(2)}, u32[]{:S(2)}) %collective-permute-start.6) | collective-permute-done | bytes 131104 | tf_op jit(solution)/shard_map/ppermute | solution.py:307
  33.8 1.2 %shard_map.124 = (f32[256,1024]{1,0:T(8,128)S(1)}, bf16[256,1024]{1,0:T(8,128)(2,1)S(1)}) custom-call(s32[2]{0:T(128)S(1)} %pad_add_fusion.place_ref, bf16[128,512]{1,0:T(8,128)(2,1)S(1)} %get-tuple-element.72.refs_0_, bf16[128,512]{1,0:T(8,128)(2,1)S(1)} %collective-permute-done.6.refs_1_, bf16[128,1024]{1,0:T(8,128)(2,1)S(1)} %get-tuple-element.74.refs_2_, ...), custom_call_target="tpu_custom_call" | custom-call | flops 268435456 | bytes 2359296 | tf_op jit(solution)/shard_map/pallas_call | solution.py:79
  35.1 0.1 collective-permute-start.7
  35.1 0.8 %shard_map.123 = (bf16[128,1024]{1,0:T(8,128)(2,1)}, bf16[128,1024]{1,0:T(8,128)(2,1)S(1)}) custom-call(f32[128,1024]{1,0:T(8,128)S(1)} %get-tuple-element.58.grad_hidden, bf16[128,1024]{1,0:T(8,128)(2,1)S(1)} %get-tuple-element.64.gates, f32[128,1024]{1,0:T(8,128)S(1)} %get-tuple-element.67.normed, f32[128,128]{1,0:T(8,128)S(1)} %get-tuple-element.68.inv_std), custom_call_target="tpu_custom_call" | custom-call | flops 8388608 | bytes 1900544 | tf_op jit(solution)/shard_map/pallas_call | solution.py:79
  36.0 1.3 %collective-permute-start.8 = (bf16[128,1024]{1,0:T(8,128)(2,1)S(1)}, bf16[128,1024]{1,0:T(8,128)(2,1)S(1)}, u32[]{:S(2)}, u32[]{:S(2)}) collective-permute-start(bf16[128,1024]{1,0:T(8,128)(2,1)S(1)} %get-tuple-element.69.g0.grad_mix), channel_id=1, source_target_pairs={{8,0},{12,4},{16,8},{20,12},{24,16},{28,20},{9,1},{13,5},{17,9},{2... | collective-permute-start | bytes 786440 | tf_op jit(solution)/shard_map/ppermute | solution.py:303
  37.3 0.0 collective-permute-done.7.got
  37.3 0.7 %shard_map.125 = (f32[64,1024]{1,0:T(8,128)S(1)}, bf16[64,1024]{1,0:T(8,128)(2,1)S(1)}, bf16[64,1024]{1,0:T(8,128)(2,1)S(1)}, bf16[64,1024]{1,0:T(8,128)(2,1)S(1)}) custom-call(s32[2]{0:T(128)S(1)} %pad_add_fusion.place_ref, f32[256,1024]{1,0:T(8,128)S(1)} %get-tuple-element.75.mine, bf16[256,1024]{1,0:T(8,128)(2,1)S(1)} %collective-permute-done.7.got), custom_call_target="tpu_custom_call" | custom-call | flops 262144 | bytes 2228224 | tf_op jit(solution)/shard_map/pallas_call | solution.py:79
  38.0 0.5 collective-permute-start.9
  38.6 3.3 %collective-permute-start.10 = (bf16[64,1024]{1,0:T(8,128)(2,1)S(1)}, bf16[64,1024]{1,0:T(8,128)(2,1)S(1)}, u32[]{:S(2)}, u32[]{:S(2)}) collective-permute-start(bf16[64,1024]{1,0:T(8,128)(2,1)S(1)} %get-tuple-element.82), channel_id=1, source_target_pairs={{0,8},{4,12},{8,0},{12,4},{16,24},{20,28},{24,16},{28,20},{1,9},{5... | collective-permute-start | bytes 393224 | tf_op jit(solution)/shard_map/ppermute | solution.py:307
  41.8 1.0 %collective-permute-start.11 = (bf16[64,1024]{1,0:T(8,128)(2,1)S(1)}, bf16[64,1024]{1,0:T(8,128)(2,1)S(1)}, u32[]{:S(2)}, u32[]{:S(2)}) collective-permute-start(bf16[64,1024]{1,0:T(8,128)(2,1)S(1)} %get-tuple-element.83), channel_id=1, source_target_pairs={{0,12},{4,8},{8,4},{12,0},{16,28},{20,24},{24,20},{28,16},{1,13},{... | collective-permute-start | bytes 393224 | tf_op jit(solution)/shard_map/ppermute | solution.py:307
  42.8 0.6 collective-permute-start.13
  43.4 4.3 %collective-permute-done.8.g2 = bf16[128,1024]{1,0:T(8,128)(2,1)S(1)} collective-permute-done((bf16[128,1024]{1,0:T(8,128)(2,1)S(1)}, bf16[128,1024]{1,0:T(8,128)(2,1)S(1)}, u32[]{:S(2)}, u32[]{:S(2)}) %collective-permute-start.8) | collective-permute-done | bytes 262176 | tf_op jit(solution)/shard_map/ppermute | solution.py:303
  47.7 2.7 %shard_map.126 = (f32[128,1024]{1,0:T(8,128)S(1)}, f32[128,1024]{1,0:T(8,128)S(1)}) custom-call(s32[1,4]{1,0:T(1,128)S(1)} %copy-done, s32[2]{0:T(128)S(1)} %pad_add_fusion.place_ref, bf16[128,1024]{1,0:T(8,128)(2,1)S(1)} %get-tuple-element.52.k.k0, bf16[128,1024]{1,0:T(8,128)(2,1)S(1)} %get-tuple-element.89.v.v0, ...), custom_call_target="tpu_custom_call" | custom-call | flops 268435456 | bytes 2621440 | tf_op jit(solution)/shard_map/pallas_call | solution.py:79
  50.4 0.0 collective-permute-done.9.refs_0_
  50.4 0.1 collective-permute-done.10.refs_1_
  50.5 2.6 %collective-permute-done.11.refs_2_ = bf16[64,1024]{1,0:T(8,128)(2,1)S(1)} collective-permute-done((bf16[64,1024]{1,0:T(8,128)(2,1)S(1)}, bf16[64,1024]{1,0:T(8,128)(2,1)S(1)}, u32[]{:S(2)}, u32[]{:S(2)}) %collective-permute-start.11) | collective-permute-done | bytes 131104 | tf_op jit(solution)/shard_map/ppermute | solution.py:307
  53.1 0.1 shard_map.127.mine
  53.2 1.5 %collective-permute-start.14 = (bf16[128,1024]{1,0:T(8,128)(2,1)S(1)}, bf16[128,1024]{1,0:T(8,128)(2,1)S(1)}, u32[]{:S(2)}, u32[]{:S(2)}) collective-permute-start(bf16[128,1024]{1,0:T(8,128)(2,1)S(1)} %broadcast_select_fusion), channel_id=1, source_target_pairs={{0,4},{4,0},{8,12},{12,8},{16,20},{20,16},{24,28},{28,24},{1,5},{5... | collective-permute-start | bytes 786440 | tf_op jit(solution)/shard_map/ppermute | solution.py:307
  54.7 2.0 %collective-permute-start.12 = (bf16[64,1024]{1,0:T(8,128)(2,1)S(1)}, bf16[64,1024]{1,0:T(8,128)(2,1)S(1)}, u32[]{:S(2)}, u32[]{:S(2)}) collective-permute-start(bf16[64,1024]{1,0:T(8,128)(2,1)S(1)} %shard_map.127.mine), channel_id=1, source_target_pairs={{0,16},{4,20},{8,24},{12,28},{16,0},{20,4},{24,8},{28,12},{1,17},{... | collective-permute-start | bytes 393224 | tf_op jit(solution)/shard_map/ppermute | solution.py:307
  56.7 2.7 %shard_map.128 = (bf16[128,1024]{1,0:T(8,128)(2,1)}, bf16[128,1024]{1,0:T(8,128)(2,1)}) custom-call(bf16[128,1024]{1,0:T(8,128)(2,1)S(1)} %get-tuple-element.52.k.k0, bf16[128,1024]{1,0:T(8,128)(2,1)S(1)} %collective-permute-done.1.keys.k1, bf16[128,1024]{1,0:T(8,128)(2,1)S(1)} %collective-permute-done.keys.k2, ...), custom_call_target="tpu_custom_call" | custom-call | flops 469762048 | bytes 6291456 | tf_op jit(solution)/shard_map/pallas_call | solution.py:79
  59.5 2.1 %collective-permute-done.12.other = bf16[64,1024]{1,0:T(8,128)(2,1)S(1)} collective-permute-done((bf16[64,1024]{1,0:T(8,128)(2,1)S(1)}, bf16[64,1024]{1,0:T(8,128)(2,1)S(1)}, u32[]{:S(2)}, u32[]{:S(2)}) %collective-permute-start.12) | collective-permute-done | bytes 131104 | tf_op jit(solution)/shard_map/ppermute | solution.py:307
  61.6 1.6 %collective-permute-start.15 = (bf16[64,1024]{1,0:T(8,128)(2,1)S(1)}, bf16[64,1024]{1,0:T(8,128)(2,1)S(1)}, u32[]{:S(2)}, u32[]{:S(2)}) collective-permute-start(bf16[64,1024]{1,0:T(8,128)(2,1)S(1)} %shard_map.129.refs_0_), channel_id=1, source_target_pairs={{0,4},{4,0},{8,12},{12,8},{16,20},{20,16},{24,28},{28,24},{1,5},{5... | collective-permute-start | bytes 393224 | tf_op jit(solution)/shard_map/ppermute | solution.py:307
  63.1 0.0 collective-permute-start.16
  63.1 2.0 %collective-permute-start.17 = (bf16[64,1024]{1,0:T(8,128)(2,1)S(1)}, bf16[64,1024]{1,0:T(8,128)(2,1)S(1)}, u32[]{:S(2)}, u32[]{:S(2)}) collective-permute-start(bf16[64,1024]{1,0:T(8,128)(2,1)S(1)} %shard_map.129.refs_0_), channel_id=1, source_target_pairs={{0,12},{4,8},{8,4},{12,0},{16,28},{20,24},{24,20},{28,16},{1,13},{... | collective-permute-start | bytes 393224 | tf_op jit(solution)/shard_map/ppermute | solution.py:307
  65.1 0.0 collective-permute-done.13.q1
  65.1 2.9 %shard_map.130 = (bf16[128,1024]{1,0:T(8,128)(2,1)}, bf16[128,1024]{1,0:T(8,128)(2,1)}) custom-call(s32[1,4]{1,0:T(1,128)S(1)} %copy-done, s32[2]{0:T(128)S(1)} %pad_add_fusion.place_ref, bf16[128,1024]{1,0:T(8,128)(2,1)S(1)} %get-tuple-element.52.k.k0, bf16[128,1024]{1,0:T(8,128)(2,1)S(1)} %get-tuple-element.89.v.v0, ...), custom_call_target="tpu_custom_call" | custom-call | flops 134217728 | bytes 2621440 | tf_op jit(solution)/shard_map/pallas_call | solution.py:79
  68.0 1.5 %collective-permute-done.16.refs_2_ = bf16[64,1024]{1,0:T(8,128)(2,1)S(1)} collective-permute-done((bf16[64,1024]{1,0:T(8,128)(2,1)S(1)}, bf16[64,1024]{1,0:T(8,128)(2,1)S(1)}, u32[]{:S(2)}, u32[]{:S(2)}) %collective-permute-start.16) | collective-permute-done | bytes 131104 | tf_op jit(solution)/shard_map/ppermute | solution.py:307
  69.5 1.3 %collective-permute-done.17.refs_3_ = bf16[64,1024]{1,0:T(8,128)(2,1)S(1)} collective-permute-done((bf16[64,1024]{1,0:T(8,128)(2,1)S(1)}, bf16[64,1024]{1,0:T(8,128)(2,1)S(1)}, u32[]{:S(2)}, u32[]{:S(2)}) %collective-permute-start.17) | collective-permute-done | bytes 131104 | tf_op jit(solution)/shard_map/ppermute | solution.py:307
  70.9 1.6 %shard_map.131 = f32[256,1024]{1,0:T(8,128)} custom-call(s32[2]{0:T(128)S(1)} %pad_add_fusion.place_ref, bf16[64,1024]{1,0:T(8,128)(2,1)S(1)} %shard_map.129.refs_0_, bf16[64,1024]{1,0:T(8,128)(2,1)S(1)} %collective-permute-done.15.refs_1_, bf16[64,1024]{1,0:T(8,128)(2,1)S(1)} %collective-permute-done.16.refs_2_, ...), custom_call_target="tpu_custom_call" | custom-call | flops 262144 | bytes 1572864 | tf_op jit(solution)/shard_map/pallas_call | solution.py:79
  (8 shorter events, 0.1 us)
Async XLA Ops:
  0.6 13.5 %collective-permute-start = (bf16[128,1024]{1,0:T(8,128)(2,1)}, bf16[128,1024]{1,0:T(8,128)(2,1)S(1)}, u32[]{:S(2)}, u32[]{:S(2)}) collective-permute-start(bf16[128,1024]{1,0:T(8,128)(2,1)} %bitcast.13), channel_id=1, source_target_pairs={{0,8},{4,12},{8,16},{12,20},{16,24},{20,28},{1,9},{5,13},{9,17},{1... | collective-permute-start | bytes 786440 | tf_op jit(solution)/shard_map/ppermute | solution.py:303
  5.6 22.2 %collective-permute-start.2 = (bf16[128,1024]{1,0:T(8,128)(2,1)}, bf16[128,1024]{1,0:T(8,128)(2,1)S(1)}, u32[]{:S(2)}, u32[]{:S(2)}) collective-permute-start(bf16[128,1024]{1,0:T(8,128)(2,1)} %bitcast.19), channel_id=1, source_target_pairs={{0,4},{4,8},{8,12},{12,16},{16,20},{20,24},{24,28},{1,5},{5,9},{9,... | collective-permute-start | bytes 786440 | tf_op jit(solution)/shard_map/ppermute | solution.py:303
  9.0 15.7 %collective-permute-start.3 = (bf16[128,1024]{1,0:T(8,128)(2,1)}, bf16[128,1024]{1,0:T(8,128)(2,1)S(1)}, u32[]{:S(2)}, u32[]{:S(2)}) collective-permute-start(bf16[128,1024]{1,0:T(8,128)(2,1)} %bitcast.20), channel_id=1, source_target_pairs={{0,8},{4,12},{8,16},{12,20},{16,24},{20,28},{1,9},{5,13},{9,17},{1... | collective-permute-start | bytes 786440 | tf_op jit(solution)/shard_map/ppermute | solution.py:303
  12.5 14.2 %collective-permute-start.4 = (bf16[128,1024]{1,0:T(8,128)(2,1)}, bf16[128,1024]{1,0:T(8,128)(2,1)S(1)}, u32[]{:S(2)}, u32[]{:S(2)}) collective-permute-start(bf16[128,1024]{1,0:T(8,128)(2,1)} %bitcast.16), channel_id=1, source_target_pairs={{0,2},{1,3},{2,0},{3,1},{4,6},{5,7},{6,4},{7,5},{8,10},{9,11},{10,... | collective-permute-start | bytes 786440 | tf_op jit(solution)/shard_map/ppermute | solution.py:307
  15.1 11.6 %collective-permute-start.1 = (bf16[128,1024]{1,0:T(8,128)(2,1)S(1)}, bf16[128,1024]{1,0:T(8,128)(2,1)S(1)}, u32[]{:S(2)}, u32[]{:S(2)}) collective-permute-start(bf16[128,1024]{1,0:T(8,128)(2,1)S(1)} %broadcast_select_fusion.2), channel_id=1, source_target_pairs={{0,4},{4,0},{8,12},{12,8},{16,20},{20,16},{24,28},{28,24},{1,5},{5... | collective-permute-start | bytes 786440 | tf_op jit(solution)/shard_map/ppermute | solution.py:307
  16.7 0.7 copy-start
  23.4 8.5 %collective-permute-start.5 = (bf16[128,1024]{1,0:T(8,128)(2,1)S(1)}, bf16[128,1024]{1,0:T(8,128)(2,1)S(1)}, u32[]{:S(2)}, u32[]{:S(2)}) collective-permute-start(bf16[128,1024]{1,0:T(8,128)(2,1)S(1)} %get-tuple-element.61.q.q0), channel_id=1, source_target_pairs={{8,0},{12,4},{16,8},{20,12},{24,16},{28,20},{9,1},{13,5},{17,9},{2... | collective-permute-start | bytes 786440 | tf_op jit(solution)/shard_map/ppermute | solution.py:303
  28.8 5.0 %collective-permute-start.6 = (bf16[128,512]{1,0:T(8,128)(2,1)S(1)}, bf16[128,512]{1,0:T(8,128)(2,1)S(1)}, u32[]{:S(2)}, u32[]{:S(2)}) collective-permute-start(bf16[128,512]{1,0:T(8,128)(2,1)S(1)} %get-tuple-element.73), channel_id=1, source_target_pairs={{0,2},{1,3},{2,0},{3,1},{4,6},{5,7},{6,4},{7,5},{8,10},{9,11},{10,... | collective-permute-start | bytes 393224 | tf_op jit(solution)/shard_map/ppermute | solution.py:307
  35.1 2.2 %collective-permute-start.7 = (bf16[256,1024]{1,0:T(8,128)(2,1)S(1)}, bf16[256,1024]{1,0:T(8,128)(2,1)S(1)}, u32[]{:S(2)}, u32[]{:S(2)}) collective-permute-start(bf16[256,1024]{1,0:T(8,128)(2,1)S(1)} %get-tuple-element.76), channel_id=1, source_target_pairs={{0,1},{1,0},{2,3},{3,2},{4,5},{5,4},{6,7},{7,6},{8,9},{9,8},{10,11... | collective-permute-start | bytes 1572872 | tf_op jit(solution)/shard_map/ppermute | solution.py:307
  36.0 11.7 %collective-permute-start.8 = (bf16[128,1024]{1,0:T(8,128)(2,1)S(1)}, bf16[128,1024]{1,0:T(8,128)(2,1)S(1)}, u32[]{:S(2)}, u32[]{:S(2)}) collective-permute-start(bf16[128,1024]{1,0:T(8,128)(2,1)S(1)} %get-tuple-element.69.g0.grad_mix), channel_id=1, source_target_pairs={{8,0},{12,4},{16,8},{20,12},{24,16},{28,20},{9,1},{13,5},{17,9},{2... | collective-permute-start | bytes 786440 | tf_op jit(solution)/shard_map/ppermute | solution.py:303
  38.0 12.4 %collective-permute-start.9 = (bf16[64,1024]{1,0:T(8,128)(2,1)S(1)}, bf16[64,1024]{1,0:T(8,128)(2,1)S(1)}, u32[]{:S(2)}, u32[]{:S(2)}) collective-permute-start(bf16[64,1024]{1,0:T(8,128)(2,1)S(1)} %get-tuple-element.81), channel_id=1, source_target_pairs={{0,4},{4,0},{8,12},{12,8},{16,20},{20,16},{24,28},{28,24},{1,5},{5... | collective-permute-start | bytes 393224 | tf_op jit(solution)/shard_map/ppermute | solution.py:307
  38.6 11.9 %collective-permute-start.10 = (bf16[64,1024]{1,0:T(8,128)(2,1)S(1)}, bf16[64,1024]{1,0:T(8,128)(2,1)S(1)}, u32[]{:S(2)}, u32[]{:S(2)}) collective-permute-start(bf16[64,1024]{1,0:T(8,128)(2,1)S(1)} %get-tuple-element.82), channel_id=1, source_target_pairs={{0,8},{4,12},{8,0},{12,4},{16,24},{20,28},{24,16},{28,20},{1,9},{5... | collective-permute-start | bytes 393224 | tf_op jit(solution)/shard_map/ppermute | solution.py:307
  41.8 11.3 %collective-permute-start.11 = (bf16[64,1024]{1,0:T(8,128)(2,1)S(1)}, bf16[64,1024]{1,0:T(8,128)(2,1)S(1)}, u32[]{:S(2)}, u32[]{:S(2)}) collective-permute-start(bf16[64,1024]{1,0:T(8,128)(2,1)S(1)} %get-tuple-element.83), channel_id=1, source_target_pairs={{0,12},{4,8},{8,4},{12,0},{16,28},{20,24},{24,20},{28,16},{1,13},{... | collective-permute-start | bytes 393224 | tf_op jit(solution)/shard_map/ppermute | solution.py:307
  42.8 22.3 %collective-permute-start.13 = (bf16[128,1024]{1,0:T(8,128)(2,1)S(1)}, bf16[128,1024]{1,0:T(8,128)(2,1)S(1)}, u32[]{:S(2)}, u32[]{:S(2)}) collective-permute-start(bf16[128,1024]{1,0:T(8,128)(2,1)S(1)} %broadcast_select_fusion.1), channel_id=1, source_target_pairs={{0,4},{4,0},{8,12},{12,8},{16,20},{20,16},{24,28},{28,24},{1,5},{5... | collective-permute-start | bytes 786440 | tf_op jit(solution)/shard_map/ppermute | solution.py:307
  53.2 11.9 %collective-permute-start.14 = (bf16[128,1024]{1,0:T(8,128)(2,1)S(1)}, bf16[128,1024]{1,0:T(8,128)(2,1)S(1)}, u32[]{:S(2)}, u32[]{:S(2)}) collective-permute-start(bf16[128,1024]{1,0:T(8,128)(2,1)S(1)} %broadcast_select_fusion), channel_id=1, source_target_pairs={{0,4},{4,0},{8,12},{12,8},{16,20},{20,16},{24,28},{28,24},{1,5},{5... | collective-permute-start | bytes 786440 | tf_op jit(solution)/shard_map/ppermute | solution.py:307
  54.7 6.8 %collective-permute-start.12 = (bf16[64,1024]{1,0:T(8,128)(2,1)S(1)}, bf16[64,1024]{1,0:T(8,128)(2,1)S(1)}, u32[]{:S(2)}, u32[]{:S(2)}) collective-permute-start(bf16[64,1024]{1,0:T(8,128)(2,1)S(1)} %shard_map.127.mine), channel_id=1, source_target_pairs={{0,16},{4,20},{8,24},{12,28},{16,0},{20,4},{24,8},{28,12},{1,17},{... | collective-permute-start | bytes 393224 | tf_op jit(solution)/shard_map/ppermute | solution.py:307
  61.6 6.5 %collective-permute-start.15 = (bf16[64,1024]{1,0:T(8,128)(2,1)S(1)}, bf16[64,1024]{1,0:T(8,128)(2,1)S(1)}, u32[]{:S(2)}, u32[]{:S(2)}) collective-permute-start(bf16[64,1024]{1,0:T(8,128)(2,1)S(1)} %shard_map.129.refs_0_), channel_id=1, source_target_pairs={{0,4},{4,0},{8,12},{12,8},{16,20},{20,16},{24,28},{28,24},{1,5},{5... | collective-permute-start | bytes 393224 | tf_op jit(solution)/shard_map/ppermute | solution.py:307
  63.1 6.4 %collective-permute-start.16 = (bf16[64,1024]{1,0:T(8,128)(2,1)S(1)}, bf16[64,1024]{1,0:T(8,128)(2,1)S(1)}, u32[]{:S(2)}, u32[]{:S(2)}) collective-permute-start(bf16[64,1024]{1,0:T(8,128)(2,1)S(1)} %shard_map.129.refs_0_), channel_id=1, source_target_pairs={{0,8},{4,12},{8,0},{12,4},{16,24},{20,28},{24,16},{28,20},{1,9},{5... | collective-permute-start | bytes 393224 | tf_op jit(solution)/shard_map/ppermute | solution.py:307
  63.1 7.7 %collective-permute-start.17 = (bf16[64,1024]{1,0:T(8,128)(2,1)S(1)}, bf16[64,1024]{1,0:T(8,128)(2,1)S(1)}, u32[]{:S(2)}, u32[]{:S(2)}) collective-permute-start(bf16[64,1024]{1,0:T(8,128)(2,1)S(1)} %shard_map.129.refs_0_), channel_id=1, source_target_pairs={{0,12},{4,8},{8,4},{12,0},{16,28},{20,24},{24,20},{28,16},{1,13},{... | collective-permute-start | bytes 393224 | tf_op jit(solution)/shard_map/ppermute | solution.py:307

commit v9 on v7

--- a/solution.py
+++ b/solution.py
@@ -90,41 +90,39 @@
     )(*scalars, *arrays)
 
 
-def own_kernel(len_ref, place_ref, q_in, k_in, v_in, q, k, v, mixed, slope, sems):
+def own_kernel(
+    len_ref, place_ref, q_in, k_in, v_in, grad_in, w_in, gate_in,
+    q, k, v, grad, w, gates, mixed, grad_hidden, slope, sems,
+):
+    pairs = ((q_in, q), (k_in, k), (v_in, v), (grad_in, grad), (gate_in, gates))
     moves = [
-        pltpu.make_async_copy(src, dst, sems.at[i])
-        for i, (src, dst) in enumerate(((q_in, q), (k_in, k), (v_in, v)))
+        pltpu.make_async_copy(src, dst, sems.at[i]) for i, (src, dst) in enumerate(pairs)
     ]
-    for move in moves:
+    rows, width = q.shape
+    part = width // CHUNKS
+    parts = []
+    for c in range(CHUNKS):
+        here = pl.ds(c * part, part)
+        parts.append(
+            pltpu.make_async_copy(w_in.at[here, :], w.at[here, :], sems.at[len(pairs) + c])
+        )
+    for move in moves[:4] + parts + moves[4:]:
         move.start()
-    rows, width = q.shape
     size = width // HEADS
     first = place_ref[0] * rows
     allowed = allowed_block(rows, first, first, len_ref, 0)
-    for move in moves:
+    for move in moves[:3]:
         move.wait()
     for h in range(HEADS):
         cols = head_slice(h, size)
         attention = block_scores(h, allowed, q, k, slope)
         mixed[:, cols] = dot(attention, v[:, cols])
-
-
-def project_kernel(grad_in, w_in, gate_in, grad, w, gates, grad_hidden, sems):
-    width = w.shape[0]
-    part = width // CHUNKS
-    moves = [pltpu.make_async_copy(grad_in, grad, sems.at[0])]
+    moves[3].wait()
     for c in range(CHUNKS):
-        here = pl.ds(c * part, part)
-        moves.append(pltpu.make_async_copy(w_in.at[here, :], w.at[here, :], sems.at[c + 1]))
-    moves.append(pltpu.make_async_copy(gate_in, gates, sems.at[CHUNKS + 1]))
-    for move in moves:
-        move.start()
-    moves[0].wait()
-    for c in range(CHUNKS):
-        moves[c + 1].wait()
+        parts[c].wait()
         here = slice(c * part, (c + 1) * part)
         grad_hidden[:, here] = dot_nt(grad[...], w[here, :])
-    moves[-1].wait()
+    moves[4].wait()
 
 
 def block_scores(h, allowed, q, keys, slope):
@@ -322,44 +320,38 @@
 
     k2 = shifted(keys[0], 2)
     v2 = shifted(values[0], 2)
-    q, k, v, mixed_own, slope0 = call(
+    passed = jnp.where(even, keys[0], k2)
+    k1 = swapped(passed, "seq", 1)
+    q, k, v, grad, w, gate, mixed_own, grad_hidden, slope0 = call(
         own_kernel,
-        [near, near, near, wide, wide],
+        [near, near, near, near, kept(w_out.shape, BF16), near, wide, wide, wide],
         scalars,
-        (in_hbm(queries[0]), in_hbm(keys[0]), in_hbm(values[0])),
-        2 * block_flops,
-        [pltpu.SemaphoreType.DMA((3,))],
-        [hbm] * 3,
-    )
-    passed = jnp.where(even, k, k2)
-    k1 = swapped(passed, "seq", 1)
+        tuple(
+            in_hbm(a)
+            for a in (after(queries[0], passed), keys[0], values[0], out_grad[0], w_out, gates[0])
+        ),
+        proj_flops + 2 * block_flops,
+        [pltpu.SemaphoreType.DMA((5 + CHUNKS,))],
+        [hbm] * 6,
+    )
     v1 = shifted(values[0], 1)
-    grad, w, gate, grad_hidden = call(
-        project_kernel,
-        [near, kept(w_out.shape, BF16), near, wide],
-        (),
-        (in_hbm(after(out_grad[0], passed)), in_hbm(w_out), in_hbm(gates[0])),
-        proj_flops,
-        [pltpu.SemaphoreType.DMA((CHUNKS + 2,))],
-        [hbm] * 3,
-    )
     grads = [grad]
     for d in range(1, batch):
         low = d & -d
-        source = after(out_grad[0], passed) if d == 1 else out_grad[0] if d == low else grads[d ^ low]
+        source = out_grad[0] if d == 1 else out_grad[0] if d == low else after(grads[d ^ low], grad)
         grads.append(swapped(source, "batch", low))
     mixed_far, slope2 = call(
-        second_kernel, [wide, wide], scalars, (after(q, v1, grad_hidden), k2, v2, mixed_own), 2 * block_flops
-    )
-    q2 = shifted(after(q, grads[2]), -2)
+        second_kernel, [wide, wide], scalars, (after(q, passed), k2, v2, mixed_own), 2 * block_flops
+    )
+    q2 = shifted(after(queries[0], passed), -2)
     passed_q = jnp.where(even, q2, q)
     q1 = swapped(passed_q, "seq", 1)
-    attention1, slope1 = call(first_kernel, [near, wide], scalars, (after(q, v1), k1), block_flops)
+    attention1, slope1 = call(first_kernel, [near, wide], scalars, (after(q, mixed_far), k1), block_flops)
     hidden, normed, inv_std, *slices = call(
         functools.partial(forward_kernel, batch),
         [near, wide, kept((rows, 128), F32)] + [kept((rows, part), BF16)] * batch,
         (place,),
-        (attention1, v1, after(mixed_far, grads[1]), gate),
+        (attention1, v1, after(mixed_far, q2, grads[1]), gate),
         block_flops,
         [pltpu.VMEM((rows, width), F32)],
     )

time: 69 us -> 67.3 us (0.975)
  Pallas kernels: 21.9 us -> 20.9 us
  starting transfers between devices: 31.8 us -> 30.8 us
  other arithmetic: 0.16 us -> 1.13 us
    ppermute x16, waiting for transfers between devices: 11.8 us -> 8.36 us  [swapped(): return lax.ppermute(block, axis, xor_route(lax.axis_size(axis), mask))]
    ppermute x5, waiting for transfers between devices: 1.58 us -> 4.39 us  [shifted(): return lax.ppermute(block, 'seq', route)]
    pallas_call x13 -> x12, Pallas kernels: 21.9 us -> 20.9 us  [call(): pl.pallas_call(kernel, out_shape=outs, in_specs=[SMEM] * len(scalars) + (...]
    ppermute x16, starting transfers between devices: 17.4 us -> 16.4 us  [swapped(): return lax.ppermute(block, axis, xor_route(lax.axis_size(axis), mask))]
    select_n x1, other arithmetic: 0.03 us -> 0.98 us  [on_device(): passed = jnp.where(even, keys[0], k2)]
  transfers between devices with their start and end apart: 21 -> 21, of which waited for: 10 -> 9; matrix products, arithmetic and copies ran while one was open for 0% -> 2% of each run, Pallas kernels for 30% -> 29%
where the time goes in v9:
time: 67.3 us; the launch traced here: 67 us
  starting transfers between devices  30.8 us (46%)
  Pallas kernels  20.9 us (31%)
  waiting for transfers between devices  12.8 us (19%)
  other arithmetic  1.13 us (2%)
  between operations  0.83 us (1%)
    pallas_call x12, Pallas kernels, call(): pl.pallas_call(kernel, out_shape=outs, in_specs=[SMEM] * len(scalars) + (...  20.9 us
    ppermute x16, starting transfers between devices, swapped(): return lax.ppermute(block, axis, xor_route(lax.axis_size(axis), mask))  16.4 us
    ppermute x5, starting transfers between devices, shifted(): return lax.ppermute(block, 'seq', route)  14.4 us
    ppermute x16, waiting for transfers between devices, swapped(): return lax.ppermute(block, axis, xor_route(lax.axis_size(axis), mask))  8.36 us
    ppermute x5, waiting for transfers between devices, shifted(): return lax.ppermute(block, 'seq', route)  4.39 us
  transfers between devices with their start and end apart: 21, of which 9 were waited for; matrix products, arithmetic and copies ran while one was open for 2% of the time, Pallas kernels for 29%

profile of v9, /device:TPU:0, one launch (start us, length us, event | category | flops | bytes accessed | tf_op | source)
XLA Modules:
  0.0 67.0 jit_solution(17287902525624711999)
XLA Ops:
  0.6 4.9 %collective-permute-start = (bf16[128,1024]{1,0:T(8,128)(2,1)}, bf16[128,1024]{1,0:T(8,128)(2,1)S(1)}, u32[]{:S(2)}, u32[]{:S(2)}) collective-permute-start(bf16[128,1024]{1,0:T(8,128)(2,1)} %bitcast.13), channel_id=1, source_target_pairs={{0,8},{4,12},{8,16},{12,20},{16,24},{20,28},{1,9},{5,13},{9,17},{1... | collective-permute-start | bytes 786440 | tf_op jit(solution)/shard_map/ppermute | solution.py:294
  5.6 1.6 %collective-permute-start.9 = (bf16[128,1024]{1,0:T(8,128)(2,1)}, bf16[128,1024]{1,0:T(8,128)(2,1)S(1)}, u32[]{:S(2)}, u32[]{:S(2)}) collective-permute-start(bf16[128,1024]{1,0:T(8,128)(2,1)} %bitcast.16), channel_id=1, source_target_pairs={{0,2},{1,3},{2,0},{3,1},{4,6},{5,7},{6,4},{7,5},{8,10},{9,11},{10,... | collective-permute-start | bytes 786440 | tf_op jit(solution)/shard_map/ppermute | solution.py:298
  7.2 3.4 %collective-permute-start.2 = (bf16[128,1024]{1,0:T(8,128)(2,1)}, bf16[128,1024]{1,0:T(8,128)(2,1)S(1)}, u32[]{:S(2)}, u32[]{:S(2)}) collective-permute-start(bf16[128,1024]{1,0:T(8,128)(2,1)} %bitcast.21), channel_id=1, source_target_pairs={{0,4},{4,8},{8,12},{12,16},{16,20},{20,24},{24,28},{1,5},{5,9},{9,... | collective-permute-start | bytes 786440 | tf_op jit(solution)/shard_map/ppermute | solution.py:294
  10.6 3.5 %collective-permute-start.3 = (bf16[128,1024]{1,0:T(8,128)(2,1)}, bf16[128,1024]{1,0:T(8,128)(2,1)S(1)}, u32[]{:S(2)}, u32[]{:S(2)}) collective-permute-start(bf16[128,1024]{1,0:T(8,128)(2,1)} %bitcast.22), channel_id=1, source_target_pairs={{0,8},{4,12},{8,16},{12,20},{16,24},{20,28},{1,9},{5,13},{9,17},{1... | collective-permute-start | bytes 786440 | tf_op jit(solution)/shard_map/ppermute | solution.py:294
  14.1 0.1 collective-permute-start.5
  14.2 1.0 %broadcast_select_fusion.2 = bf16[128,1024]{1,0:T(8,128)(2,1)S(1)} fusion(bf16[128,1024]{1,0:T(8,128)(2,1)S(1)} %collective-permute-done.keys.k2, pred[]{:T(512)S(6)} %eq.3, bf16[1,128,1024]{2,1,0:T(8,128)(2,1)} %param.8), kind=kLoop, calls=%fused_computation.2 | loop fusion | flops 131072 | bytes 786433 | tf_op jit(solution)/shard_map/jit(_where)/select_n | solution.py:323
  15.1 1.6 %collective-permute-start.1 = (bf16[128,1024]{1,0:T(8,128)(2,1)S(1)}, bf16[128,1024]{1,0:T(8,128)(2,1)S(1)}, u32[]{:S(2)}, u32[]{:S(2)}) collective-permute-start(bf16[128,1024]{1,0:T(8,128)(2,1)S(1)} %broadcast_select_fusion.2), channel_id=1, source_target_pairs={{0,4},{4,0},{8,12},{12,8},{16,20},{20,16},{24,28},{28,24},{1,5},{5... | collective-permute-start | bytes 786440 | tf_op jit(solution)/shard_map/ppermute | solution.py:298
  16.8 0.0 collective-permute-done.9.refs_6_
  16.8 1.3 %collective-permute-start.4 = (bf16[128,1024]{1,0:T(8,128)(2,1)}, bf16[128,1024]{1,0:T(8,128)(2,1)S(1)}, u32[]{:S(2)}, u32[]{:S(2)}) collective-permute-start(bf16[128,1024]{1,0:T(8,128)(2,1)} %bitcast.19), channel_id=1, source_target_pairs={{8,0},{12,4},{16,8},{20,12},{24,16},{28,20},{9,1},{13,5},{17,9},{2... | collective-permute-start | bytes 786440 | tf_op jit(solution)/shard_map/ppermute | solution.py:294
  18.1 0.1 pad_add_fusion.place_ref
  18.1 0.7 copy-done
  18.8 4.9 %shard_map.118 = (bf16[128,1024]{1,0:T(8,128)(2,1)S(1)}, bf16[128,1024]{1,0:T(8,128)(2,1)S(1)}, bf16[128,1024]{1,0:T(8,128)(2,1)S(1)}, bf16[128,1024]{1,0:T(8,12...) custom-call(s32[1,4]{1,0:T(1,128)S(1)} %copy-done, ...), custom_call_target="tpu_custom_call" | custom-call | flops 335544320 | bytes 8388608 | tf_op jit(solution)/shard_map/pallas_call | solution.py:79
  23.7 0.3 collective-permute-start.10
  24.0 2.0 %shard_map.119 = (f32[128,1024]{1,0:T(8,128)S(1)}, f32[128,1024]{1,0:T(8,128)S(1)}) custom-call(s32[1,4]{1,0:T(1,128)S(1)} %copy-done, s32[2]{0:T(128)S(1)} %pad_add_fusion.place_ref, bf16[128,1024]{1,0:T(8,128)(2,1)S(1)} %get-tuple-element.58.q.q0, bf16[128,1024]{1,0:T(8,128)(2,1)S(1)} %collective-permute-done.keys.k2, ...), custom_call_target="tpu_custom_call" | custom-call | flops 67108864 | bytes 2359296 | tf_op jit(solution)/shard_map/pallas_call | solution.py:79
  26.0 1.3 %collective-permute-done.4.q2 = bf16[128,1024]{1,0:T(8,128)(2,1)S(1)} collective-permute-done((bf16[128,1024]{1,0:T(8,128)(2,1)}, bf16[128,1024]{1,0:T(8,128)(2,1)S(1)}, u32[]{:S(2)}, u32[]{:S(2)}) %collective-permute-start.4) | collective-permute-done | bytes 262176 | tf_op jit(solution)/shard_map/ppermute | solution.py:294
  27.3 0.0 collective-permute-done.1.keys.k1
  27.3 1.0 %shard_map.120 = (bf16[128,1024]{1,0:T(8,128)(2,1)S(1)}, f32[128,1024]{1,0:T(8,128)S(1)}) custom-call(s32[1,4]{1,0:T(1,128)S(1)} %copy-done, s32[2]{0:T(128)S(1)} %pad_add_fusion.place_ref, bf16[128,1024]{1,0:T(8,128)(2,1)S(1)} %get-tuple-element.58.q.q0, bf16[128,1024]{1,0:T(8,128)(2,1)S(1)} %collective-permute-done.1.keys.k1), custom_call_target="tpu_custom_call" | custom-call | flops 33554432 | bytes 1310720 | tf_op jit(solution)/shard_map/pallas_call | solution.py:79
  28.3 1.0 %shard_map.121 = (bf16[128,1024]{1,0:T(8,128)(2,1)S(1)}, f32[128,1024]{1,0:T(8,128)S(1)}, f32[128,128]{1,0:T(8,128)S(1)}, bf16[128,256]{1,0:T(8,128)(2,1)S(1)}, ...) custom-call(s32[2]{0:T(128)S(1)} %pad_add_fusion.place_ref, ...), custom_call_target="tpu_custom_call" | custom-call | flops 33554432 | bytes 2424832 | tf_op jit(solution)/shard_map/pallas_call | solution.py:79
  29.4 0.1 collective-permute-start.6
  29.4 0.6 collective-permute-start.7
  30.0 1.3 %collective-permute-start.8 = (bf16[128,256]{1,0:T(8,128)(2,1)S(1)}, bf16[128,256]{1,0:T(8,128)(2,1)S(1)}, u32[]{:S(2)}, u32[]{:S(2)}) collective-permute-start(bf16[128,256]{1,0:T(8,128)(2,1)S(1)} %get-tuple-element.72), channel_id=1, source_target_pairs={{0,3},{1,2},{2,1},{3,0},{4,7},{5,6},{6,5},{7,4},{8,11},{9,10},{10,... | collective-permute-start | bytes 196616 | tf_op jit(solution)/shard_map/ppermute | solution.py:298
  31.3 0.9 %shard_map.122 = (bf16[128,1024]{1,0:T(8,128)(2,1)}, bf16[128,1024]{1,0:T(8,128)(2,1)S(1)}) custom-call(f32[128,1024]{1,0:T(8,128)S(1)} %get-tuple-element.61.grad_hidden, bf16[128,1024]{1,0:T(8,128)(2,1)S(1)} %get-tuple-element.62.gates, f32[128,1024]{1,0:T(8,128)S(1)} %get-tuple-element.65.normed, f32[128,128]{1,0:T(8,128)S(1)} %get-tuple-element.66.inv_std), custom_call_target="tpu_custom_call" | custom-call | flops 8388608 | bytes 1900544 | tf_op jit(solution)/shard_map/pallas_call | solution.py:79
  32.2 1.3 %collective-permute-start.11 = (bf16[128,1024]{1,0:T(8,128)(2,1)S(1)}, bf16[128,1024]{1,0:T(8,128)(2,1)S(1)}, u32[]{:S(2)}, u32[]{:S(2)}) collective-permute-start(bf16[128,1024]{1,0:T(8,128)(2,1)S(1)} %get-tuple-element.67.g0.grad_mix), channel_id=1, source_target_pairs={{8,0},{12,4},{16,8},{20,12},{24,16},{28,20},{9,1},{13,5},{17,9},{2... | collective-permute-start | bytes 786440 | tf_op jit(solution)/shard_map/ppermute | solution.py:294
  33.5 0.0 collective-permute-done.10.refs_7_
  33.5 0.0 collective-permute-done.6.refs_1_
  33.5 0.9 %collective-permute-done.7.refs_2_ = bf16[128,256]{1,0:T(8,128)(2,1)S(1)} collective-permute-done((bf16[128,256]{1,0:T(8,128)(2,1)S(1)}, bf16[128,256]{1,0:T(8,128)(2,1)S(1)}, u32[]{:S(2)}, u32[]{:S(2)}) %collective-permute-start.7) | collective-permute-done | bytes 65568 | tf_op jit(solution)/shard_map/ppermute | solution.py:298
  34.4 0.5 collective-permute-done.8.refs_3_
  34.9 1.1 %shard_map.123 = (f32[64,1024]{1,0:T(8,128)S(1)}, bf16[64,1024]{1,0:T(8,128)(2,1)S(1)}, bf16[64,1024]{1,0:T(8,128)(2,1)S(1)}, bf16[64,1024]{1,0:T(8,128)(2,1)S(1)}) custom-call(s32[2]{0:T(128)S(1)} %pad_add_fusion.place_ref, bf16[128,256]{1,0:T(8,128)(2,1)S(1)} %get-tuple-element.69.refs_0_, bf16[128,256]{1,0:T(8,128)(2,1)S(1)} %collective-permute-done.6.refs_1_, ...), custom_call_target="tpu_custom_call" | custom-call | flops 268435456 | bytes 1966080 | tf_op jit(solution)/shard_map/pallas_call | solution.py:79
  36.0 0.5 collective-permute-start.12
  36.5 1.7 %collective-permute-start.13 = (bf16[64,1024]{1,0:T(8,128)(2,1)S(1)}, bf16[64,1024]{1,0:T(8,128)(2,1)S(1)}, u32[]{:S(2)}, u32[]{:S(2)}) collective-permute-start(bf16[64,1024]{1,0:T(8,128)(2,1)S(1)} %get-tuple-element.80), channel_id=1, source_target_pairs={{0,8},{4,12},{8,0},{12,4},{16,24},{20,28},{24,16},{28,20},{1,9},{5... | collective-permute-start | bytes 393224 | tf_op jit(solution)/shard_map/ppermute | solution.py:298
  38.2 1.3 %collective-permute-start.14 = (bf16[64,1024]{1,0:T(8,128)(2,1)S(1)}, bf16[64,1024]{1,0:T(8,128)(2,1)S(1)}, u32[]{:S(2)}, u32[]{:S(2)}) collective-permute-start(bf16[64,1024]{1,0:T(8,128)(2,1)S(1)} %get-tuple-element.81), channel_id=1, source_target_pairs={{0,12},{4,8},{8,4},{12,0},{16,28},{20,24},{24,20},{28,16},{1,13},{... | collective-permute-start | bytes 393224 | tf_op jit(solution)/shard_map/ppermute | solution.py:298
  39.6 0.5 collective-permute-start.16
  40.1 3.1 %collective-permute-done.11.g2 = bf16[128,1024]{1,0:T(8,128)(2,1)S(1)} collective-permute-done((bf16[128,1024]{1,0:T(8,128)(2,1)S(1)}, bf16[128,1024]{1,0:T(8,128)(2,1)S(1)}, u32[]{:S(2)}, u32[]{:S(2)}) %collective-permute-start.11) | collective-permute-done | bytes 262176 | tf_op jit(solution)/shard_map/ppermute | solution.py:294
  43.2 2.7 %shard_map.124 = (f32[128,1024]{1,0:T(8,128)S(1)}, f32[128,1024]{1,0:T(8,128)S(1)}) custom-call(s32[1,4]{1,0:T(1,128)S(1)} %copy-done, s32[2]{0:T(128)S(1)} %pad_add_fusion.place_ref, bf16[128,1024]{1,0:T(8,128)(2,1)S(1)} %get-tuple-element.51.k.k0, bf16[128,1024]{1,0:T(8,128)(2,1)S(1)} %get-tuple-element.87.v.v0, ...), custom_call_target="tpu_custom_call" | custom-call | flops 268435456 | bytes 2621440 | tf_op jit(solution)/shard_map/pallas_call | solution.py:79
  45.9 0.1 collective-permute-done.13.refs_1_
  46.0 2.3 %collective-permute-done.14.refs_2_ = bf16[64,1024]{1,0:T(8,128)(2,1)S(1)} collective-permute-done((bf16[64,1024]{1,0:T(8,128)(2,1)S(1)}, bf16[64,1024]{1,0:T(8,128)(2,1)S(1)}, u32[]{:S(2)}, u32[]{:S(2)}) %collective-permute-start.14) | collective-permute-done | bytes 131104 | tf_op jit(solution)/shard_map/ppermute | solution.py:298
  48.2 0.1 shard_map.125.mine
  48.4 1.6 %collective-permute-start.17 = (bf16[128,1024]{1,0:T(8,128)(2,1)S(1)}, bf16[128,1024]{1,0:T(8,128)(2,1)S(1)}, u32[]{:S(2)}, u32[]{:S(2)}) collective-permute-start(bf16[128,1024]{1,0:T(8,128)(2,1)S(1)} %broadcast_select_fusion), channel_id=1, source_target_pairs={{0,4},{4,0},{8,12},{12,8},{16,20},{20,16},{24,28},{28,24},{1,5},{5... | collective-permute-start | bytes 786440 | tf_op jit(solution)/shard_map/ppermute | solution.py:298
  50.0 1.7 %collective-permute-start.15 = (bf16[64,1024]{1,0:T(8,128)(2,1)S(1)}, bf16[64,1024]{1,0:T(8,128)(2,1)S(1)}, u32[]{:S(2)}, u32[]{:S(2)}) collective-permute-start(bf16[64,1024]{1,0:T(8,128)(2,1)S(1)} %shard_map.125.mine), channel_id=1, source_target_pairs={{0,16},{4,20},{8,24},{12,28},{16,0},{20,4},{24,8},{28,12},{1,17},{... | collective-permute-start | bytes 393224 | tf_op jit(solution)/shard_map/ppermute | solution.py:298
  51.7 2.7 %shard_map.126 = (bf16[128,1024]{1,0:T(8,128)(2,1)}, bf16[128,1024]{1,0:T(8,128)(2,1)}) custom-call(bf16[128,1024]{1,0:T(8,128)(2,1)S(1)} %get-tuple-element.51.k.k0, bf16[128,1024]{1,0:T(8,128)(2,1)S(1)} %collective-permute-done.1.keys.k1, bf16[128,1024]{1,0:T(8,128)(2,1)S(1)} %collective-permute-done.keys.k2, ...), custom_call_target="tpu_custom_call" | custom-call | flops 469762048 | bytes 6291456 | tf_op jit(solution)/shard_map/pallas_call | solution.py:79
  54.4 2.2 %collective-permute-done.15.other = bf16[64,1024]{1,0:T(8,128)(2,1)S(1)} collective-permute-done((bf16[64,1024]{1,0:T(8,128)(2,1)S(1)}, bf16[64,1024]{1,0:T(8,128)(2,1)S(1)}, u32[]{:S(2)}, u32[]{:S(2)}) %collective-permute-start.15) | collective-permute-done | bytes 131104 | tf_op jit(solution)/shard_map/ppermute | solution.py:298
  56.6 1.3 %collective-permute-start.18 = (bf16[64,1024]{1,0:T(8,128)(2,1)S(1)}, bf16[64,1024]{1,0:T(8,128)(2,1)S(1)}, u32[]{:S(2)}, u32[]{:S(2)}) collective-permute-start(bf16[64,1024]{1,0:T(8,128)(2,1)S(1)} %shard_map.127.refs_0_), channel_id=1, source_target_pairs={{0,4},{4,0},{8,12},{12,8},{16,20},{20,16},{24,28},{28,24},{1,5},{5... | collective-permute-start | bytes 393224 | tf_op jit(solution)/shard_map/ppermute | solution.py:298
  57.9 2.2 %collective-permute-start.20 = (bf16[64,1024]{1,0:T(8,128)(2,1)S(1)}, bf16[64,1024]{1,0:T(8,128)(2,1)S(1)}, u32[]{:S(2)}, u32[]{:S(2)}) collective-permute-start(bf16[64,1024]{1,0:T(8,128)(2,1)S(1)} %shard_map.127.refs_0_), channel_id=1, source_target_pairs={{0,12},{4,8},{8,4},{12,0},{16,28},{20,24},{24,20},{28,16},{1,13},{... | collective-permute-start | bytes 393224 | tf_op jit(solution)/shard_map/ppermute | solution.py:298
  60.2 0.0 collective-permute-done.16.q1
  60.2 2.9 %shard_map.128 = (bf16[128,1024]{1,0:T(8,128)(2,1)}, bf16[128,1024]{1,0:T(8,128)(2,1)}) custom-call(s32[1,4]{1,0:T(1,128)S(1)} %copy-done.1, s32[2]{0:T(128)S(1)} %pad_add_fusion.place_ref, bf16[128,1024]{1,0:T(8,128)(2,1)S(1)} %get-tuple-element.51.k.k0, bf16[128,1024]{1,0:T(8,128)(2,1)S(1)} %get-tuple-element.87.v.v0, ...), custom_call_target="tpu_custom_call" | custom-call | flops 134217728 | bytes 2621440 | tf_op jit(solution)/shard_map/pallas_call | solution.py:79
  63.1 1.2 %collective-permute-done.19.refs_2_ = bf16[64,1024]{1,0:T(8,128)(2,1)S(1)} collective-permute-done((bf16[64,1024]{1,0:T(8,128)(2,1)S(1)}, bf16[64,1024]{1,0:T(8,128)(2,1)S(1)}, u32[]{:S(2)}, u32[]{:S(2)}) %collective-permute-start.19) | collective-permute-done | bytes 131104 | tf_op jit(solution)/shard_map/ppermute | solution.py:298
  64.3 1.2 %collective-permute-done.20.refs_3_ = bf16[64,1024]{1,0:T(8,128)(2,1)S(1)} collective-permute-done((bf16[64,1024]{1,0:T(8,128)(2,1)S(1)}, bf16[64,1024]{1,0:T(8,128)(2,1)S(1)}, u32[]{:S(2)}, u32[]{:S(2)}) %collective-permute-start.20) | collective-permute-done | bytes 131104 | tf_op jit(solution)/shard_map/ppermute | solution.py:298
  65.5 1.6 %shard_map.129 = f32[256,1024]{1,0:T(8,128)} custom-call(s32[2]{0:T(128)S(1)} %pad_add_fusion.place_ref, bf16[64,1024]{1,0:T(8,128)(2,1)S(1)} %shard_map.127.refs_0_, bf16[64,1024]{1,0:T(8,128)(2,1)S(1)} %collective-permute-done.18.refs_1_, bf16[64,1024]{1,0:T(8,128)(2,1)S(1)} %collective-permute-done.19.refs_2_, ...), custom_call_target="tpu_custom_call" | custom-call | flops 262144 | bytes 1572864 | tf_op jit(solution)/shard_map/pallas_call | solution.py:79
  (14 shorter events, 0.1 us)
Async XLA Ops:
  0.6 13.5 %collective-permute-start = (bf16[128,1024]{1,0:T(8,128)(2,1)}, bf16[128,1024]{1,0:T(8,128)(2,1)S(1)}, u32[]{:S(2)}, u32[]{:S(2)}) collective-permute-start(bf16[128,1024]{1,0:T(8,128)(2,1)} %bitcast.13), channel_id=1, source_target_pairs={{0,8},{4,12},{8,16},{12,20},{16,24},{20,28},{1,9},{5,13},{9,17},{1... | collective-permute-start | bytes 786440 | tf_op jit(solution)/shard_map/ppermute | solution.py:294
  5.6 11.2 %collective-permute-start.9 = (bf16[128,1024]{1,0:T(8,128)(2,1)}, bf16[128,1024]{1,0:T(8,128)(2,1)S(1)}, u32[]{:S(2)}, u32[]{:S(2)}) collective-permute-start(bf16[128,1024]{1,0:T(8,128)(2,1)} %bitcast.16), channel_id=1, source_target_pairs={{0,2},{1,3},{2,0},{3,1},{4,6},{5,7},{6,4},{7,5},{8,10},{9,11},{10,... | collective-permute-start | bytes 786440 | tf_op jit(solution)/shard_map/ppermute | solution.py:298
  7.2 21.1 %collective-permute-start.2 = (bf16[128,1024]{1,0:T(8,128)(2,1)}, bf16[128,1024]{1,0:T(8,128)(2,1)S(1)}, u32[]{:S(2)}, u32[]{:S(2)}) collective-permute-start(bf16[128,1024]{1,0:T(8,128)(2,1)} %bitcast.21), channel_id=1, source_target_pairs={{0,4},{4,8},{8,12},{12,16},{16,20},{20,24},{24,28},{1,5},{5,9},{9,... | collective-permute-start | bytes 786440 | tf_op jit(solution)/shard_map/ppermute | solution.py:294
  10.6 13.1 %collective-permute-start.3 = (bf16[128,1024]{1,0:T(8,128)(2,1)}, bf16[128,1024]{1,0:T(8,128)(2,1)S(1)}, u32[]{:S(2)}, u32[]{:S(2)}) collective-permute-start(bf16[128,1024]{1,0:T(8,128)(2,1)} %bitcast.22), channel_id=1, source_target_pairs={{0,8},{4,12},{8,16},{12,20},{16,24},{20,28},{1,9},{5,13},{9,17},{1... | collective-permute-start | bytes 786440 | tf_op jit(solution)/shard_map/ppermute | solution.py:294
  14.1 11.9 %collective-permute-start.5 = (bf16[128,1024]{1,0:T(8,128)(2,1)}, bf16[128,1024]{1,0:T(8,128)(2,1)S(1)}, u32[]{:S(2)}, u32[]{:S(2)}) collective-permute-start(bf16[128,1024]{1,0:T(8,128)(2,1)} %bitcast.17), channel_id=1, source_target_pairs={{0,1},{1,0},{2,3},{3,2},{4,5},{5,4},{6,7},{7,6},{8,9},{9,8},{10,11... | collective-permute-start | bytes 786440 | tf_op jit(solution)/shard_map/ppermute | solution.py:298
  15.1 12.1 %collective-permute-start.1 = (bf16[128,1024]{1,0:T(8,128)(2,1)S(1)}, bf16[128,1024]{1,0:T(8,128)(2,1)S(1)}, u32[]{:S(2)}, u32[]{:S(2)}) collective-permute-start(bf16[128,1024]{1,0:T(8,128)(2,1)S(1)} %broadcast_select_fusion.2), channel_id=1, source_target_pairs={{0,4},{4,0},{8,12},{12,8},{16,20},{20,16},{24,28},{28,24},{1,5},{5... | collective-permute-start | bytes 786440 | tf_op jit(solution)/shard_map/ppermute | solution.py:298
  16.8 10.5 %collective-permute-start.4 = (bf16[128,1024]{1,0:T(8,128)(2,1)}, bf16[128,1024]{1,0:T(8,128)(2,1)S(1)}, u32[]{:S(2)}, u32[]{:S(2)}) collective-permute-start(bf16[128,1024]{1,0:T(8,128)(2,1)} %bitcast.19), channel_id=1, source_target_pairs={{8,0},{12,4},{16,8},{20,12},{24,16},{28,20},{9,1},{13,5},{17,9},{2... | collective-permute-start | bytes 786440 | tf_op jit(solution)/shard_map/ppermute | solution.py:294
  18.1 0.7 copy-start
  23.7 9.8 %collective-permute-start.10 = (bf16[128,1024]{1,0:T(8,128)(2,1)S(1)}, bf16[128,1024]{1,0:T(8,128)(2,1)S(1)}, u32[]{:S(2)}, u32[]{:S(2)}) collective-permute-start(bf16[128,1024]{1,0:T(8,128)(2,1)S(1)} %collective-permute-done.9.refs_6_), channel_id=1, source_target_pairs={{0,1},{1,0},{2,3},{3,2},{4,5},{5,4},{6,7},{7,6},{8,9},{9,8},{10,11... | collective-permute-start | bytes 786440 | tf_op jit(solution)/shard_map/ppermute | solution.py:298
  29.4 4.1 %collective-permute-start.6 = (bf16[128,256]{1,0:T(8,128)(2,1)S(1)}, bf16[128,256]{1,0:T(8,128)(2,1)S(1)}, u32[]{:S(2)}, u32[]{:S(2)}) collective-permute-start(bf16[128,256]{1,0:T(8,128)(2,1)S(1)} %get-tuple-element.70), channel_id=1, source_target_pairs={{0,1},{1,0},{2,3},{3,2},{4,5},{5,4},{6,7},{7,6},{8,9},{9,8},{10,11... | collective-permute-start | bytes 196616 | tf_op jit(solution)/shard_map/ppermute | solution.py:298
  29.4 5.0 %collective-permute-start.7 = (bf16[128,256]{1,0:T(8,128)(2,1)S(1)}, bf16[128,256]{1,0:T(8,128)(2,1)S(1)}, u32[]{:S(2)}, u32[]{:S(2)}) collective-permute-start(bf16[128,256]{1,0:T(8,128)(2,1)S(1)} %get-tuple-element.71), channel_id=1, source_target_pairs={{0,2},{1,3},{2,0},{3,1},{4,6},{5,7},{6,4},{7,5},{8,10},{9,11},{10,... | collective-permute-start | bytes 196616 | tf_op jit(solution)/shard_map/ppermute | solution.py:298
  30.0 4.9 %collective-permute-start.8 = (bf16[128,256]{1,0:T(8,128)(2,1)S(1)}, bf16[128,256]{1,0:T(8,128)(2,1)S(1)}, u32[]{:S(2)}, u32[]{:S(2)}) collective-permute-start(bf16[128,256]{1,0:T(8,128)(2,1)S(1)} %get-tuple-element.72), channel_id=1, source_target_pairs={{0,3},{1,2},{2,1},{3,0},{4,7},{5,6},{6,5},{7,4},{8,11},{9,10},{10,... | collective-permute-start | bytes 196616 | tf_op jit(solution)/shard_map/ppermute | solution.py:298
  32.2 11.0 %collective-permute-start.11 = (bf16[128,1024]{1,0:T(8,128)(2,1)S(1)}, bf16[128,1024]{1,0:T(8,128)(2,1)S(1)}, u32[]{:S(2)}, u32[]{:S(2)}) collective-permute-start(bf16[128,1024]{1,0:T(8,128)(2,1)S(1)} %get-tuple-element.67.g0.grad_mix), channel_id=1, source_target_pairs={{8,0},{12,4},{16,8},{20,12},{24,16},{28,20},{9,1},{13,5},{17,9},{2... | collective-permute-start | bytes 786440 | tf_op jit(solution)/shard_map/ppermute | solution.py:294
  36.0 9.9 %collective-permute-start.12 = (bf16[64,1024]{1,0:T(8,128)(2,1)S(1)}, bf16[64,1024]{1,0:T(8,128)(2,1)S(1)}, u32[]{:S(2)}, u32[]{:S(2)}) collective-permute-start(bf16[64,1024]{1,0:T(8,128)(2,1)S(1)} %get-tuple-element.79), channel_id=1, source_target_pairs={{0,4},{4,0},{8,12},{12,8},{16,20},{20,16},{24,28},{28,24},{1,5},{5... | collective-permute-start | bytes 393224 | tf_op jit(solution)/shard_map/ppermute | solution.py:298
  36.5 9.5 %collective-permute-start.13 = (bf16[64,1024]{1,0:T(8,128)(2,1)S(1)}, bf16[64,1024]{1,0:T(8,128)(2,1)S(1)}, u32[]{:S(2)}, u32[]{:S(2)}) collective-permute-start(bf16[64,1024]{1,0:T(8,128)(2,1)S(1)} %get-tuple-element.80), channel_id=1, source_target_pairs={{0,8},{4,12},{8,0},{12,4},{16,24},{20,28},{24,16},{28,20},{1,9},{5... | collective-permute-start | bytes 393224 | tf_op jit(solution)/shard_map/ppermute | solution.py:298
  38.2 10.0 %collective-permute-start.14 = (bf16[64,1024]{1,0:T(8,128)(2,1)S(1)}, bf16[64,1024]{1,0:T(8,128)(2,1)S(1)}, u32[]{:S(2)}, u32[]{:S(2)}) collective-permute-start(bf16[64,1024]{1,0:T(8,128)(2,1)S(1)} %get-tuple-element.81), channel_id=1, source_target_pairs={{0,12},{4,8},{8,4},{12,0},{16,28},{20,24},{24,20},{28,16},{1,13},{... | collective-permute-start | bytes 393224 | tf_op jit(solution)/shard_map/ppermute | solution.py:298
  39.6 20.6 %collective-permute-start.16 = (bf16[128,1024]{1,0:T(8,128)(2,1)S(1)}, bf16[128,1024]{1,0:T(8,128)(2,1)S(1)}, u32[]{:S(2)}, u32[]{:S(2)}) collective-permute-start(bf16[128,1024]{1,0:T(8,128)(2,1)S(1)} %broadcast_select_fusion.1), channel_id=1, source_target_pairs={{0,4},{4,0},{8,12},{12,8},{16,20},{20,16},{24,28},{28,24},{1,5},{5... | collective-permute-start | bytes 786440 | tf_op jit(solution)/shard_map/ppermute | solution.py:298
  48.4 11.8 %collective-permute-start.17 = (bf16[128,1024]{1,0:T(8,128)(2,1)S(1)}, bf16[128,1024]{1,0:T(8,128)(2,1)S(1)}, u32[]{:S(2)}, u32[]{:S(2)}) collective-permute-start(bf16[128,1024]{1,0:T(8,128)(2,1)S(1)} %broadcast_select_fusion), channel_id=1, source_target_pairs={{0,4},{4,0},{8,12},{12,8},{16,20},{20,16},{24,28},{28,24},{1,5},{5... | collective-permute-start | bytes 786440 | tf_op jit(solution)/shard_map/ppermute | solution.py:298
  50.0 6.6 %collective-permute-start.15 = (bf16[64,1024]{1,0:T(8,128)(2,1)S(1)}, bf16[64,1024]{1,0:T(8,128)(2,1)S(1)}, u32[]{:S(2)}, u32[]{:S(2)}) collective-permute-start(bf16[64,1024]{1,0:T(8,128)(2,1)S(1)} %shard_map.125.mine), channel_id=1, source_target_pairs={{0,16},{4,20},{8,24},{12,28},{16,0},{20,4},{24,8},{28,12},{1,17},{... | collective-permute-start | bytes 393224 | tf_op jit(solution)/shard_map/ppermute | solution.py:298
  51.7 8.5 %copy-start.1 = (s32[1,4]{1,0:T(1,128)S(1)}, s32[1,4]{1,0:T(1,128)}, u32[]{:S(2)}) copy-start(s32[1,4]{1,0:T(1,128)} %len_ref.9) | copy-start | bytes 52
  56.6 6.5 %collective-permute-start.18 = (bf16[64,1024]{1,0:T(8,128)(2,1)S(1)}, bf16[64,1024]{1,0:T(8,128)(2,1)S(1)}, u32[]{:S(2)}, u32[]{:S(2)}) collective-permute-start(bf16[64,1024]{1,0:T(8,128)(2,1)S(1)} %shard_map.127.refs_0_), channel_id=1, source_target_pairs={{0,4},{4,0},{8,12},{12,8},{16,20},{20,16},{24,28},{28,24},{1,5},{5... | collective-permute-start | bytes 393224 | tf_op jit(solution)/shard_map/ppermute | solution.py:298
  57.9 6.3 %collective-permute-start.19 = (bf16[64,1024]{1,0:T(8,128)(2,1)S(1)}, bf16[64,1024]{1,0:T(8,128)(2,1)S(1)}, u32[]{:S(2)}, u32[]{:S(2)}) collective-permute-start(bf16[64,1024]{1,0:T(8,128)(2,1)S(1)} %shard_map.127.refs_0_), channel_id=1, source_target_pairs={{0,8},{4,12},{8,0},{12,4},{16,24},{20,28},{24,16},{28,20},{1,9},{5... | collective-permute-start | bytes 393224 | tf_op jit(solution)/shard_map/ppermute | solution.py:298
  57.9 7.5 %collective-permute-start.20 = (bf16[64,1024]{1,0:T(8,128)(2,1)S(1)}, bf16[64,1024]{1,0:T(8,128)(2,1)S(1)}, u32[]{:S(2)}, u32[]{:S(2)}) collective-permute-start(bf16[64,1024]{1,0:T(8,128)(2,1)S(1)} %shard_map.127.refs_0_), channel_id=1, source_target_pairs={{0,12},{4,8},{8,4},{12,0},{16,28},{20,24},{24,20},{28,16},{1,13},{... | collective-permute-start | bytes 393224 | tf_op jit(solution)/shard_map/ppermute | solution.py:298

commit v10 on v9

--- a/solution.py
+++ b/solution.py
@@ -135,33 +135,26 @@
     return jnp.where(allowed, scores * gate, 0.0).astype(BF16)
 
 
-def second_kernel(len_ref, place_ref, q, keys, vals, mixed_own, mixed, slope):
+def far_kernel(distance, len_ref, place_ref, q, keys, attention, slope):
     rows, width = q.shape
     size = width // HEADS
     first = place_ref[0] * rows
-    allowed = allowed_block(rows, first, first - 2 * rows, len_ref, 0)
+    allowed = allowed_block(rows, first, first - distance * rows, len_ref, 0)
+    for h in range(HEADS):
+        attention[:, head_slice(h, size)] = block_scores(h, allowed, q, keys, slope)
+
+
+def forward_kernel(groups, place_ref, attention1, attention2, v1, v2, mixed_own, gates, hidden, normed, inv_std, *rest):
+    slices, mixed = rest[:-1], rest[-1]
+    rows, width = v1.shape
+    size = width // HEADS
     for h in range(HEADS):
         cols = head_slice(h, size)
-        attention = block_scores(h, allowed, q, keys, slope)
-        mixed[:, cols] = mixed_own[:, cols] + dot(attention, vals[:, cols])
-
-
-def first_kernel(len_ref, place_ref, q, keys, attention, slope):
-    rows, width = q.shape
-    size = width // HEADS
-    first = place_ref[0] * rows
-    allowed = allowed_block(rows, first, first - rows, len_ref, 0)
-    for h in range(HEADS):
-        attention[:, head_slice(h, size)] = block_scores(h, allowed, q, keys, slope)
-
-
-def forward_kernel(groups, place_ref, attention, vals, mixed_far, gates, hidden, normed, inv_std, *rest):
-    slices, mixed = rest[:-1], rest[-1]
-    rows, width = vals.shape
-    size = width // HEADS
-    for h in range(HEADS):
-        cols = head_slice(h, size)
-        mixed[:, cols] = mixed_far[:, cols] + dot(attention[:, cols], vals[:, cols])
+        mixed[:, cols] = (
+            mixed_own[:, cols]
+            + dot(attention1[:, cols], v1[:, cols])
+            + dot(attention2[:, cols], v2[:, cols])
+        )
     values = mixed[...]
     centered = values - jnp.mean(values, axis=1, keepdims=True)
     inverse = lax.rsqrt(jnp.mean(centered * centered, axis=1, keepdims=True) + 1e-05)
@@ -338,20 +331,22 @@
     grads = [grad]
     for d in range(1, batch):
         low = d & -d
-        source = out_grad[0] if d == 1 else out_grad[0] if d == low else after(grads[d ^ low], grad)
+        source = out_grad[0] if d == 1 else out_grad[0] if d == low else grads[d ^ low]
         grads.append(swapped(source, "batch", low))
-    mixed_far, slope2 = call(
-        second_kernel, [wide, wide], scalars, (after(q, passed), k2, v2, mixed_own), 2 * block_flops
-    )
-    q2 = shifted(after(queries[0], passed), -2)
+    attention2, slope2 = call(
+        functools.partial(far_kernel, 2), [near, wide], scalars, (after(q, passed), k2), block_flops
+    )
+    q2 = shifted(after(q, attention2), -2)
     passed_q = jnp.where(even, q2, q)
     q1 = swapped(passed_q, "seq", 1)
-    attention1, slope1 = call(first_kernel, [near, wide], scalars, (after(q, mixed_far), k1), block_flops)
+    attention1, slope1 = call(
+        functools.partial(far_kernel, 1), [near, wide], scalars, (after(q, v1), k1), block_flops
+    )
     hidden, normed, inv_std, *slices = call(
         functools.partial(forward_kernel, batch),
         [near, wide, kept((rows, 128), F32)] + [kept((rows, part), BF16)] * batch,
         (place,),
-        (attention1, v1, after(mixed_far, q2, grads[1]), gate),
+        (attention1, attention2, v1, v2, after(mixed_own, grads[1], grads[3]), gate),
         block_flops,
         [pltpu.VMEM((rows, width), F32)],
     )
@@ -375,26 +370,26 @@
         proj_flops,
         [pltpu.VMEM((part, width), F32)],
     )
+    output, grad_queries = call(
+        query_kernel,
+        [full, full],
+        (),
+        (k, k1, k2, v, v1, v2, slope0, slope1, slope2, grad_mix, after(hidden, own), w),
+        proj_flops + 6 * block_flops,
+    )
+    if direct:
+        got = [swapped(s, "seq", e + 1) for e, s in enumerate(sends)]
+        (mine,) = call(corner_kernel, [share], (), (after(own, output), *got), own.size * 4)
+        other = swapped(mine, "seq", corners)
+        g2_late = after(g2, mine)
+    else:
+        mine = own
     keys_part, values_part = call(
         key_kernel,
         [wide, wide],
         scalars,
-        (k, after(v, own), q, q2, grad_mix, g2),
+        (k, after(v, mine), q, q2, grad_mix, g2),
         8 * block_flops,
-    )
-    if direct:
-        got = [swapped(s, "seq", e + 1) for e, s in enumerate(sends)]
-        (mine,) = call(corner_kernel, [share], (), (after(own, keys_part), *got), own.size * 4)
-        other = swapped(mine, "seq", corners)
-        g2_late = after(g2, mine)
-    else:
-        mine = own
-    output, grad_queries = call(
-        query_kernel,
-        [full, full],
-        (),
-        (k, k1, k2, v, v1, v2, slope0, slope1, slope2, grad_mix, after(hidden, mine), w),
-        proj_flops + 6 * block_flops,
     )
     g1 = swapped(jnp.where(even, g2_late, grad_mix), "seq", 1)
     if direct:
@@ -402,7 +397,7 @@
             functools.partial(pair_kernel, scale),
             [share],
             (),
-            (after(mine, output), other),
+            (after(mine, keys_part), other),
             own.size * 2,
         )
     else:

time: 67.3 us -> 66.4 us (0.987)
  Pallas kernels: 20.9 us -> 19.9 us
  starting transfers between devices: 30.8 us -> 31.8 us
  waiting for transfers between devices: 12.8 us -> 11.8 us
    ppermute x5, waiting for transfers between devices: 4.39 us -> 0.01 us  [shifted(): return lax.ppermute(block, 'seq', route)]
    ppermute x16, waiting for transfers between devices: 8.36 us -> 11.8 us  [swapped(): return lax.ppermute(block, axis, xor_route(lax.axis_size(axis), mask))]
    ppermute x16, starting transfers between devices: 16.4 us -> 17.4 us  [swapped(): return lax.ppermute(block, axis, xor_route(lax.axis_size(axis), mask))]
    pallas_call x12, Pallas kernels: 20.9 us -> 19.9 us  [call(): pl.pallas_call(kernel, out_shape=outs, in_specs=[SMEM] * len(scalars) + (...]
  transfers between devices with their start and end apart: 21 -> 21, of which waited for: 9 -> 6; matrix products, arithmetic and copies ran while one was open for 2% -> 2% of each run, Pallas kernels for 29% -> 28%
where the time goes in v10:
time: 66.4 us; the launch traced here: 66.1 us
  starting transfers between devices  31.8 us (48%)
  Pallas kernels  19.9 us (30%)
  waiting for transfers between devices  11.8 us (18%)
  other arithmetic  1.12 us (2%)
  between operations  0.84 us (1%)
    pallas_call x12, Pallas kernels, call(): pl.pallas_call(kernel, out_shape=outs, in_specs=[SMEM] * len(scalars) + (...  19.9 us
    ppermute x16, starting transfers between devices, swapped(): return lax.ppermute(block, axis, xor_route(lax.axis_size(axis), mask))  17.4 us
    ppermute x5, starting transfers between devices, shifted(): return lax.ppermute(block, 'seq', route)  14.4 us
    ppermute x16, waiting for transfers between devices, swapped(): return lax.ppermute(block, axis, xor_route(lax.axis_size(axis), mask))  11.8 us
  transfers between devices with their start and end apart: 21, of which 6 were waited for; matrix products, arithmetic and copies ran while one was open for 2% of the time, Pallas kernels for 28%

profile of v10, /device:TPU:0, one launch (start us, length us, event | category | flops | bytes accessed | tf_op | source)
XLA Modules:
  0.0 66.1 jit_solution(699466865658322108)
XLA Ops:
  0.6 4.9 %collective-permute-start = (bf16[128,1024]{1,0:T(8,128)(2,1)}, bf16[128,1024]{1,0:T(8,128)(2,1)S(1)}, u32[]{:S(2)}, u32[]{:S(2)}) collective-permute-start(bf16[128,1024]{1,0:T(8,128)(2,1)} %bitcast.13), channel_id=1, source_target_pairs={{0,8},{4,12},{8,16},{12,20},{16,24},{20,28},{1,9},{5,13},{9,17},{1... | collective-permute-start | bytes 786440 | tf_op jit(solution)/shard_map/ppermute | solution.py:287
  5.6 1.6 %collective-permute-start.5 = (bf16[128,1024]{1,0:T(8,128)(2,1)}, bf16[128,1024]{1,0:T(8,128)(2,1)S(1)}, u32[]{:S(2)}, u32[]{:S(2)}) collective-permute-start(bf16[128,1024]{1,0:T(8,128)(2,1)} %bitcast.17), channel_id=1, source_target_pairs={{0,2},{1,3},{2,0},{3,1},{4,6},{5,7},{6,4},{7,5},{8,10},{9,11},{10,... | collective-permute-start | bytes 786440 | tf_op jit(solution)/shard_map/ppermute | solution.py:291
  7.2 3.4 %collective-permute-start.2 = (bf16[128,1024]{1,0:T(8,128)(2,1)}, bf16[128,1024]{1,0:T(8,128)(2,1)S(1)}, u32[]{:S(2)}, u32[]{:S(2)}) collective-permute-start(bf16[128,1024]{1,0:T(8,128)(2,1)} %bitcast.20), channel_id=1, source_target_pairs={{0,4},{4,8},{8,12},{12,16},{16,20},{20,24},{24,28},{1,5},{5,9},{9,... | collective-permute-start | bytes 786440 | tf_op jit(solution)/shard_map/ppermute | solution.py:287
  10.6 3.5 %collective-permute-start.3 = (bf16[128,1024]{1,0:T(8,128)(2,1)}, bf16[128,1024]{1,0:T(8,128)(2,1)S(1)}, u32[]{:S(2)}, u32[]{:S(2)}) collective-permute-start(bf16[128,1024]{1,0:T(8,128)(2,1)} %bitcast.21), channel_id=1, source_target_pairs={{0,8},{4,12},{8,16},{12,20},{16,24},{20,28},{1,9},{5,13},{9,17},{1... | collective-permute-start | bytes 786440 | tf_op jit(solution)/shard_map/ppermute | solution.py:287
  14.1 0.1 collective-permute-start.4
  14.2 0.0 collective-permute-done.keys.k2
  14.2 1.0 %broadcast_select_fusion.2 = bf16[128,1024]{1,0:T(8,128)(2,1)S(1)} fusion(bf16[128,1024]{1,0:T(8,128)(2,1)S(1)} %collective-permute-done.keys.k2, pred[]{:T(512)S(6)} %eq.3, bf16[1,128,1024]{2,1,0:T(8,128)(2,1)} %param.8), kind=kLoop, calls=%fused_computation.2 | loop fusion | flops 131072 | bytes 786433 | tf_op jit(solution)/shard_map/jit(_where)/select_n | solution.py:316
  15.1 1.6 %collective-permute-start.1 = (bf16[128,1024]{1,0:T(8,128)(2,1)S(1)}, bf16[128,1024]{1,0:T(8,128)(2,1)S(1)}, u32[]{:S(2)}, u32[]{:S(2)}) collective-permute-start(bf16[128,1024]{1,0:T(8,128)(2,1)S(1)} %broadcast_select_fusion.2), channel_id=1, source_target_pairs={{0,4},{4,0},{8,12},{12,8},{16,20},{20,16},{24,28},{28,24},{1,5},{5... | collective-permute-start | bytes 786440 | tf_op jit(solution)/shard_map/ppermute | solution.py:291
  16.8 0.2 collective-permute-start.6
  17.0 0.1 pad_add_fusion.place_ref
  17.0 0.7 copy-done
  17.7 4.9 %shard_map.118 = (bf16[128,1024]{1,0:T(8,128)(2,1)S(1)}, bf16[128,1024]{1,0:T(8,128)(2,1)S(1)}, bf16[128,1024]{1,0:T(8,128)(2,1)S(1)}, bf16[128,1024]{1,0:T(8,12...) custom-call(s32[1,4]{1,0:T(1,128)S(1)} %copy-done, ...), custom_call_target="tpu_custom_call" | custom-call | flops 335544320 | bytes 8388608 | tf_op jit(solution)/shard_map/pallas_call | solution.py:79
  22.6 1.0 %shard_map.120 = (bf16[128,1024]{1,0:T(8,128)(2,1)S(1)}, f32[128,1024]{1,0:T(8,128)S(1)}) custom-call(s32[1,4]{1,0:T(1,128)S(1)} %copy-done, s32[2]{0:T(128)S(1)} %pad_add_fusion.place_ref, bf16[128,1024]{1,0:T(8,128)(2,1)S(1)} %get-tuple-element.84.q.q0, bf16[128,1024]{1,0:T(8,128)(2,1)S(1)} %collective-permute-done.keys.k2), custom_call_target="tpu_custom_call" | custom-call | flops 33554432 | bytes 1310720 | tf_op jit(solution)/shard_map/pallas_call | solution.py:79
  23.6 0.0 collective-permute-done.2.v1
  23.6 1.3 %collective-permute-start.13 = (bf16[128,1024]{1,0:T(8,128)(2,1)S(1)}, bf16[128,1024]{1,0:T(8,128)(2,1)S(1)}, u32[]{:S(2)}, u32[]{:S(2)}) collective-permute-start(bf16[128,1024]{1,0:T(8,128)(2,1)S(1)} %get-tuple-element.84.q.q0), channel_id=1, source_target_pairs={{8,0},{12,4},{16,8},{20,12},{24,16},{28,20},{9,1},{13,5},{17,9},{2... | collective-permute-start | bytes 786440 | tf_op jit(solution)/shard_map/ppermute | solution.py:287
  24.9 0.0 collective-permute-done.4.refs_5_
  24.9 0.0 collective-permute-done.1.keys.k1
  24.9 1.0 %shard_map.119 = (bf16[128,1024]{1,0:T(8,128)(2,1)S(1)}, f32[128,1024]{1,0:T(8,128)S(1)}) custom-call(s32[1,4]{1,0:T(1,128)S(1)} %copy-done, s32[2]{0:T(128)S(1)} %pad_add_fusion.place_ref, bf16[128,1024]{1,0:T(8,128)(2,1)S(1)} %get-tuple-element.84.q.q0, bf16[128,1024]{1,0:T(8,128)(2,1)S(1)} %collective-permute-done.1.keys.k1), custom_call_target="tpu_custom_call" | custom-call | flops 33554432 | bytes 1310720 | tf_op jit(solution)/shard_map/pallas_call | solution.py:79
  26.0 0.0 collective-permute-done.3.v2
  26.0 1.1 %shard_map.121 = (bf16[128,1024]{1,0:T(8,128)(2,1)S(1)}, f32[128,1024]{1,0:T(8,128)S(1)}, f32[128,128]{1,0:T(8,128)S(1)}, bf16[128,256]{1,0:T(8,128)(2,1)S(1)}, ...) custom-call(s32[2]{0:T(128)S(1)} %pad_add_fusion.place_ref, ...), custom_call_target="tpu_custom_call" | custom-call | flops 33554432 | bytes 2949120 | tf_op jit(solution)/shard_map/pallas_call | solution.py:79
  27.1 0.4 collective-permute-start.7
  27.5 0.5 collective-permute-start.8
  28.0 1.0 %collective-permute-start.9 = (bf16[128,256]{1,0:T(8,128)(2,1)S(1)}, bf16[128,256]{1,0:T(8,128)(2,1)S(1)}, u32[]{:S(2)}, u32[]{:S(2)}) collective-permute-start(bf16[128,256]{1,0:T(8,128)(2,1)S(1)} %get-tuple-element.72), channel_id=1, source_target_pairs={{0,3},{1,2},{2,1},{3,0},{4,7},{5,6},{6,5},{7,4},{8,11},{9,10},{10,... | collective-permute-start | bytes 196616 | tf_op jit(solution)/shard_map/ppermute | solution.py:291
  29.0 0.9 %shard_map.122 = (bf16[128,1024]{1,0:T(8,128)(2,1)}, bf16[128,1024]{1,0:T(8,128)(2,1)S(1)}) custom-call(f32[128,1024]{1,0:T(8,128)S(1)} %get-tuple-element.59.grad_hidden, bf16[128,1024]{1,0:T(8,128)(2,1)S(1)} %get-tuple-element.60.gates, f32[128,1024]{1,0:T(8,128)S(1)} %get-tuple-element.65.normed, f32[128,128]{1,0:T(8,128)S(1)} %get-tuple-element.66.inv_std), custom_call_target="tpu_custom_call" | custom-call | flops 8388608 | bytes 1900544 | tf_op jit(solution)/shard_map/pallas_call | solution.py:79
  29.9 1.3 %collective-permute-start.14 = (bf16[128,1024]{1,0:T(8,128)(2,1)S(1)}, bf16[128,1024]{1,0:T(8,128)(2,1)S(1)}, u32[]{:S(2)}, u32[]{:S(2)}) collective-permute-start(bf16[128,1024]{1,0:T(8,128)(2,1)S(1)} %get-tuple-element.67.grad_mix.g0), channel_id=1, source_target_pairs={{8,0},{12,4},{16,8},{20,12},{24,16},{28,20},{9,1},{13,5},{17,9},{2... | collective-permute-start | bytes 786440 | tf_op jit(solution)/shard_map/ppermute | solution.py:287
  31.2 0.0 collective-permute-done.7.refs_1_
  31.2 1.2 %collective-permute-done.8.refs_2_ = bf16[128,256]{1,0:T(8,128)(2,1)S(1)} collective-permute-done((bf16[128,256]{1,0:T(8,128)(2,1)S(1)}, bf16[128,256]{1,0:T(8,128)(2,1)S(1)}, u32[]{:S(2)}, u32[]{:S(2)}) %collective-permute-start.8) | collective-permute-done | bytes 65568 | tf_op jit(solution)/shard_map/ppermute | solution.py:291
  32.4 0.0 collective-permute-done.9.refs_3_
  32.4 1.1 %shard_map.123 = (f32[64,1024]{1,0:T(8,128)S(1)}, bf16[64,1024]{1,0:T(8,128)(2,1)S(1)}, bf16[64,1024]{1,0:T(8,128)(2,1)S(1)}, bf16[64,1024]{1,0:T(8,128)(2,1)S(1)}) custom-call(s32[2]{0:T(128)S(1)} %pad_add_fusion.place_ref, bf16[128,256]{1,0:T(8,128)(2,1)S(1)} %get-tuple-element.69.refs_0_, bf16[128,256]{1,0:T(8,128)(2,1)S(1)} %collective-permute-done.7.refs_1_, ...), custom_call_target="tpu_custom_call" | custom-call | flops 268435456 | bytes 1966080 | tf_op jit(solution)/shard_map/pallas_call | solution.py:79
  33.5 0.6 collective-permute-start.10
  34.0 2.9 %collective-permute-start.11 = (bf16[64,1024]{1,0:T(8,128)(2,1)S(1)}, bf16[64,1024]{1,0:T(8,128)(2,1)S(1)}, u32[]{:S(2)}, u32[]{:S(2)}) collective-permute-start(bf16[64,1024]{1,0:T(8,128)(2,1)S(1)} %get-tuple-element.81), channel_id=1, source_target_pairs={{0,8},{4,12},{8,0},{12,4},{16,24},{20,28},{24,16},{28,20},{1,9},{5... | collective-permute-start | bytes 393224 | tf_op jit(solution)/shard_map/ppermute | solution.py:291
  36.9 1.0 %collective-permute-start.12 = (bf16[64,1024]{1,0:T(8,128)(2,1)S(1)}, bf16[64,1024]{1,0:T(8,128)(2,1)S(1)}, u32[]{:S(2)}, u32[]{:S(2)}) collective-permute-start(bf16[64,1024]{1,0:T(8,128)(2,1)S(1)} %get-tuple-element.82), channel_id=1, source_target_pairs={{0,12},{4,8},{8,4},{12,0},{16,28},{20,24},{24,20},{28,16},{1,13},{... | collective-permute-start | bytes 393224 | tf_op jit(solution)/shard_map/ppermute | solution.py:291
  37.9 0.0 collective-permute-done.13.q2
  37.9 0.6 collective-permute-start.16
  38.5 2.7 %shard_map.124 = (bf16[128,1024]{1,0:T(8,128)(2,1)}, bf16[128,1024]{1,0:T(8,128)(2,1)}) custom-call(bf16[128,1024]{1,0:T(8,128)(2,1)S(1)} %get-tuple-element.51.k0.k, bf16[128,1024]{1,0:T(8,128)(2,1)S(1)} %collective-permute-done.1.keys.k1, bf16[128,1024]{1,0:T(8,128)(2,1)S(1)} %collective-permute-done.keys.k2, ...), custom_call_target="tpu_custom_call" | custom-call | flops 469762048 | bytes 6291456 | tf_op jit(solution)/shard_map/pallas_call | solution.py:79
  41.2 3.2 %collective-permute-done.11.refs_1_ = bf16[64,1024]{1,0:T(8,128)(2,1)S(1)} collective-permute-done((bf16[64,1024]{1,0:T(8,128)(2,1)S(1)}, bf16[64,1024]{1,0:T(8,128)(2,1)S(1)}, u32[]{:S(2)}, u32[]{:S(2)}) %collective-permute-start.11) | collective-permute-done | bytes 131104 | tf_op jit(solution)/shard_map/ppermute | solution.py:291
  44.4 2.5 %collective-permute-done.12.refs_2_ = bf16[64,1024]{1,0:T(8,128)(2,1)S(1)} collective-permute-done((bf16[64,1024]{1,0:T(8,128)(2,1)S(1)}, bf16[64,1024]{1,0:T(8,128)(2,1)S(1)}, u32[]{:S(2)}, u32[]{:S(2)}) %collective-permute-start.12) | collective-permute-done | bytes 131104 | tf_op jit(solution)/shard_map/ppermute | solution.py:291
  46.9 0.1 shard_map.125.mine
  47.0 1.6 %collective-permute-start.17 = (bf16[128,1024]{1,0:T(8,128)(2,1)S(1)}, bf16[128,1024]{1,0:T(8,128)(2,1)S(1)}, u32[]{:S(2)}, u32[]{:S(2)}) collective-permute-start(bf16[128,1024]{1,0:T(8,128)(2,1)S(1)} %broadcast_select_fusion), channel_id=1, source_target_pairs={{0,4},{4,0},{8,12},{12,8},{16,20},{20,16},{24,28},{28,24},{1,5},{5... | collective-permute-start | bytes 786440 | tf_op jit(solution)/shard_map/ppermute | solution.py:291
  48.6 1.8 %collective-permute-start.15 = (bf16[64,1024]{1,0:T(8,128)(2,1)S(1)}, bf16[64,1024]{1,0:T(8,128)(2,1)S(1)}, u32[]{:S(2)}, u32[]{:S(2)}) collective-permute-start(bf16[64,1024]{1,0:T(8,128)(2,1)S(1)} %shard_map.125.mine), channel_id=1, source_target_pairs={{0,16},{4,20},{8,24},{12,28},{16,0},{20,4},{24,8},{28,12},{1,17},{... | collective-permute-start | bytes 393224 | tf_op jit(solution)/shard_map/ppermute | solution.py:291
  50.4 2.7 %shard_map.126 = (f32[128,1024]{1,0:T(8,128)S(1)}, f32[128,1024]{1,0:T(8,128)S(1)}) custom-call(s32[1,4]{1,0:T(1,128)S(1)} %copy-done.1, s32[2]{0:T(128)S(1)} %pad_add_fusion.place_ref, bf16[128,1024]{1,0:T(8,128)(2,1)S(1)} %get-tuple-element.51.k0.k, bf16[128,1024]{1,0:T(8,128)(2,1)S(1)} %get-tuple-element.87.v0.v, ...), custom_call_target="tpu_custom_call" | custom-call | flops 268435456 | bytes 2621440 | tf_op jit(solution)/shard_map/pallas_call | solution.py:79
  53.1 2.1 %collective-permute-done.15.other = bf16[64,1024]{1,0:T(8,128)(2,1)S(1)} collective-permute-done((bf16[64,1024]{1,0:T(8,128)(2,1)S(1)}, bf16[64,1024]{1,0:T(8,128)(2,1)S(1)}, u32[]{:S(2)}, u32[]{:S(2)}) %collective-permute-start.15) | collective-permute-done | bytes 131104 | tf_op jit(solution)/shard_map/ppermute | solution.py:291
  55.3 1.5 %collective-permute-start.18 = (bf16[64,1024]{1,0:T(8,128)(2,1)S(1)}, bf16[64,1024]{1,0:T(8,128)(2,1)S(1)}, u32[]{:S(2)}, u32[]{:S(2)}) collective-permute-start(bf16[64,1024]{1,0:T(8,128)(2,1)S(1)} %shard_map.127.refs_0_), channel_id=1, source_target_pairs={{0,4},{4,0},{8,12},{12,8},{16,20},{20,16},{24,28},{28,24},{1,5},{5... | collective-permute-start | bytes 393224 | tf_op jit(solution)/shard_map/ppermute | solution.py:291
  56.8 2.0 %collective-permute-start.20 = (bf16[64,1024]{1,0:T(8,128)(2,1)S(1)}, bf16[64,1024]{1,0:T(8,128)(2,1)S(1)}, u32[]{:S(2)}, u32[]{:S(2)}) collective-permute-start(bf16[64,1024]{1,0:T(8,128)(2,1)S(1)} %shard_map.127.refs_0_), channel_id=1, source_target_pairs={{0,12},{4,8},{8,4},{12,0},{16,28},{20,24},{24,20},{28,16},{1,13},{... | collective-permute-start | bytes 393224 | tf_op jit(solution)/shard_map/ppermute | solution.py:291
  58.8 2.9 %shard_map.128 = (bf16[128,1024]{1,0:T(8,128)(2,1)}, bf16[128,1024]{1,0:T(8,128)(2,1)}) custom-call(s32[1,4]{1,0:T(1,128)S(1)} %copy-done.1, s32[2]{0:T(128)S(1)} %pad_add_fusion.place_ref, bf16[128,1024]{1,0:T(8,128)(2,1)S(1)} %get-tuple-element.51.k0.k, bf16[128,1024]{1,0:T(8,128)(2,1)S(1)} %get-tuple-element.87.v0.v, ...), custom_call_target="tpu_custom_call" | custom-call | flops 134217728 | bytes 2621440 | tf_op jit(solution)/shard_map/pallas_call | solution.py:79
  61.7 1.5 %collective-permute-done.19.refs_2_ = bf16[64,1024]{1,0:T(8,128)(2,1)S(1)} collective-permute-done((bf16[64,1024]{1,0:T(8,128)(2,1)S(1)}, bf16[64,1024]{1,0:T(8,128)(2,1)S(1)}, u32[]{:S(2)}, u32[]{:S(2)}) %collective-permute-start.19) | collective-permute-done | bytes 131104 | tf_op jit(solution)/shard_map/ppermute | solution.py:291
  63.2 1.3 %collective-permute-done.20.refs_3_ = bf16[64,1024]{1,0:T(8,128)(2,1)S(1)} collective-permute-done((bf16[64,1024]{1,0:T(8,128)(2,1)S(1)}, bf16[64,1024]{1,0:T(8,128)(2,1)S(1)}, u32[]{:S(2)}, u32[]{:S(2)}) %collective-permute-start.20) | collective-permute-done | bytes 131104 | tf_op jit(solution)/shard_map/ppermute | solution.py:291
  64.6 1.6 %shard_map.129 = f32[256,1024]{1,0:T(8,128)} custom-call(s32[2]{0:T(128)S(1)} %pad_add_fusion.place_ref, bf16[64,1024]{1,0:T(8,128)(2,1)S(1)} %shard_map.127.refs_0_, bf16[64,1024]{1,0:T(8,128)(2,1)S(1)} %collective-permute-done.18.refs_1_, bf16[64,1024]{1,0:T(8,128)(2,1)S(1)} %collective-permute-done.19.refs_2_, ...), custom_call_target="tpu_custom_call" | custom-call | flops 262144 | bytes 1572864 | tf_op jit(solution)/shard_map/pallas_call | solution.py:79
  (14 shorter events, 0.1 us)
Async XLA Ops:
  0.6 13.5 %collective-permute-start = (bf16[128,1024]{1,0:T(8,128)(2,1)}, bf16[128,1024]{1,0:T(8,128)(2,1)S(1)}, u32[]{:S(2)}, u32[]{:S(2)}) collective-permute-start(bf16[128,1024]{1,0:T(8,128)(2,1)} %bitcast.13), channel_id=1, source_target_pairs={{0,8},{4,12},{8,16},{12,20},{16,24},{20,28},{1,9},{5,13},{9,17},{1... | collective-permute-start | bytes 786440 | tf_op jit(solution)/shard_map/ppermute | solution.py:287
  5.6 11.2 %collective-permute-start.5 = (bf16[128,1024]{1,0:T(8,128)(2,1)}, bf16[128,1024]{1,0:T(8,128)(2,1)S(1)}, u32[]{:S(2)}, u32[]{:S(2)}) collective-permute-start(bf16[128,1024]{1,0:T(8,128)(2,1)} %bitcast.17), channel_id=1, source_target_pairs={{0,2},{1,3},{2,0},{3,1},{4,6},{5,7},{6,4},{7,5},{8,10},{9,11},{10,... | collective-permute-start | bytes 786440 | tf_op jit(solution)/shard_map/ppermute | solution.py:291
  7.2 16.4 %collective-permute-start.2 = (bf16[128,1024]{1,0:T(8,128)(2,1)}, bf16[128,1024]{1,0:T(8,128)(2,1)S(1)}, u32[]{:S(2)}, u32[]{:S(2)}) collective-permute-start(bf16[128,1024]{1,0:T(8,128)(2,1)} %bitcast.20), channel_id=1, source_target_pairs={{0,4},{4,8},{8,12},{12,16},{16,20},{20,24},{24,28},{1,5},{5,9},{9,... | collective-permute-start | bytes 786440 | tf_op jit(solution)/shard_map/ppermute | solution.py:287
  10.6 15.4 %collective-permute-start.3 = (bf16[128,1024]{1,0:T(8,128)(2,1)}, bf16[128,1024]{1,0:T(8,128)(2,1)S(1)}, u32[]{:S(2)}, u32[]{:S(2)}) collective-permute-start(bf16[128,1024]{1,0:T(8,128)(2,1)} %bitcast.21), channel_id=1, source_target_pairs={{0,8},{4,12},{8,16},{12,20},{16,24},{20,28},{1,9},{5,13},{9,17},{1... | collective-permute-start | bytes 786440 | tf_op jit(solution)/shard_map/ppermute | solution.py:287
  14.1 10.9 %collective-permute-start.4 = (bf16[128,1024]{1,0:T(8,128)(2,1)}, bf16[128,1024]{1,0:T(8,128)(2,1)S(1)}, u32[]{:S(2)}, u32[]{:S(2)}) collective-permute-start(bf16[128,1024]{1,0:T(8,128)(2,1)} %bitcast.18), channel_id=1, source_target_pairs={{0,1},{1,0},{2,3},{3,2},{4,5},{5,4},{6,7},{7,6},{8,9},{9,8},{10,11... | collective-permute-start | bytes 786440 | tf_op jit(solution)/shard_map/ppermute | solution.py:291
  15.1 9.8 %collective-permute-start.1 = (bf16[128,1024]{1,0:T(8,128)(2,1)S(1)}, bf16[128,1024]{1,0:T(8,128)(2,1)S(1)}, u32[]{:S(2)}, u32[]{:S(2)}) collective-permute-start(bf16[128,1024]{1,0:T(8,128)(2,1)S(1)} %broadcast_select_fusion.2), channel_id=1, source_target_pairs={{0,4},{4,0},{8,12},{12,8},{16,20},{20,16},{24,28},{28,24},{1,5},{5... | collective-permute-start | bytes 786440 | tf_op jit(solution)/shard_map/ppermute | solution.py:291
  16.8 8.2 %collective-permute-start.6 = (bf16[128,1024]{1,0:T(8,128)(2,1)S(1)}, bf16[128,1024]{1,0:T(8,128)(2,1)S(1)}, u32[]{:S(2)}, u32[]{:S(2)}) collective-permute-start(bf16[128,1024]{1,0:T(8,128)(2,1)S(1)} %collective-permute-done.5.refs_6_), channel_id=1, source_target_pairs={{0,1},{1,0},{2,3},{3,2},{4,5},{5,4},{6,7},{7,6},{8,9},{9,8},{10,11... | collective-permute-start | bytes 786440 | tf_op jit(solution)/shard_map/ppermute | solution.py:291
  17.0 0.7 copy-start
  23.6 14.3 %collective-permute-start.13 = (bf16[128,1024]{1,0:T(8,128)(2,1)S(1)}, bf16[128,1024]{1,0:T(8,128)(2,1)S(1)}, u32[]{:S(2)}, u32[]{:S(2)}) collective-permute-start(bf16[128,1024]{1,0:T(8,128)(2,1)S(1)} %get-tuple-element.84.q.q0), channel_id=1, source_target_pairs={{8,0},{12,4},{16,8},{20,12},{24,16},{28,20},{9,1},{13,5},{17,9},{2... | collective-permute-start | bytes 786440 | tf_op jit(solution)/shard_map/ppermute | solution.py:287
  27.1 4.1 %collective-permute-start.7 = (bf16[128,256]{1,0:T(8,128)(2,1)S(1)}, bf16[128,256]{1,0:T(8,128)(2,1)S(1)}, u32[]{:S(2)}, u32[]{:S(2)}) collective-permute-start(bf16[128,256]{1,0:T(8,128)(2,1)S(1)} %get-tuple-element.70), channel_id=1, source_target_pairs={{0,1},{1,0},{2,3},{3,2},{4,5},{5,4},{6,7},{7,6},{8,9},{9,8},{10,11... | collective-permute-start | bytes 196616 | tf_op jit(solution)/shard_map/ppermute | solution.py:291
  27.5 4.9 %collective-permute-start.8 = (bf16[128,256]{1,0:T(8,128)(2,1)S(1)}, bf16[128,256]{1,0:T(8,128)(2,1)S(1)}, u32[]{:S(2)}, u32[]{:S(2)}) collective-permute-start(bf16[128,256]{1,0:T(8,128)(2,1)S(1)} %get-tuple-element.71), channel_id=1, source_target_pairs={{0,2},{1,3},{2,0},{3,1},{4,6},{5,7},{6,4},{7,5},{8,10},{9,11},{10,... | collective-permute-start | bytes 196616 | tf_op jit(solution)/shard_map/ppermute | solution.py:291
  28.0 4.4 %collective-permute-start.9 = (bf16[128,256]{1,0:T(8,128)(2,1)S(1)}, bf16[128,256]{1,0:T(8,128)(2,1)S(1)}, u32[]{:S(2)}, u32[]{:S(2)}) collective-permute-start(bf16[128,256]{1,0:T(8,128)(2,1)S(1)} %get-tuple-element.72), channel_id=1, source_target_pairs={{0,3},{1,2},{2,1},{3,0},{4,7},{5,6},{6,5},{7,4},{8,11},{9,10},{10,... | collective-permute-start | bytes 196616 | tf_op jit(solution)/shard_map/ppermute | solution.py:291
  29.9 17.1 %collective-permute-start.14 = (bf16[128,1024]{1,0:T(8,128)(2,1)S(1)}, bf16[128,1024]{1,0:T(8,128)(2,1)S(1)}, u32[]{:S(2)}, u32[]{:S(2)}) collective-permute-start(bf16[128,1024]{1,0:T(8,128)(2,1)S(1)} %get-tuple-element.67.grad_mix.g0), channel_id=1, source_target_pairs={{8,0},{12,4},{16,8},{20,12},{24,16},{28,20},{9,1},{13,5},{17,9},{2... | collective-permute-start | bytes 786440 | tf_op jit(solution)/shard_map/ppermute | solution.py:287
  33.5 7.8 %collective-permute-start.10 = (bf16[64,1024]{1,0:T(8,128)(2,1)S(1)}, bf16[64,1024]{1,0:T(8,128)(2,1)S(1)}, u32[]{:S(2)}, u32[]{:S(2)}) collective-permute-start(bf16[64,1024]{1,0:T(8,128)(2,1)S(1)} %get-tuple-element.80), channel_id=1, source_target_pairs={{0,4},{4,0},{8,12},{12,8},{16,20},{20,16},{24,28},{28,24},{1,5},{5... | collective-permute-start | bytes 393224 | tf_op jit(solution)/shard_map/ppermute | solution.py:291
  34.0 10.4 %collective-permute-start.11 = (bf16[64,1024]{1,0:T(8,128)(2,1)S(1)}, bf16[64,1024]{1,0:T(8,128)(2,1)S(1)}, u32[]{:S(2)}, u32[]{:S(2)}) collective-permute-start(bf16[64,1024]{1,0:T(8,128)(2,1)S(1)} %get-tuple-element.81), channel_id=1, source_target_pairs={{0,8},{4,12},{8,0},{12,4},{16,24},{20,28},{24,16},{28,20},{1,9},{5... | collective-permute-start | bytes 393224 | tf_op jit(solution)/shard_map/ppermute | solution.py:291
  36.9 10.0 %collective-permute-start.12 = (bf16[64,1024]{1,0:T(8,128)(2,1)S(1)}, bf16[64,1024]{1,0:T(8,128)(2,1)S(1)}, u32[]{:S(2)}, u32[]{:S(2)}) collective-permute-start(bf16[64,1024]{1,0:T(8,128)(2,1)S(1)} %get-tuple-element.82), channel_id=1, source_target_pairs={{0,12},{4,8},{8,4},{12,0},{16,28},{20,24},{24,20},{28,16},{1,13},{... | collective-permute-start | bytes 393224 | tf_op jit(solution)/shard_map/ppermute | solution.py:291
  37.9 20.9 %collective-permute-start.16 = (bf16[128,1024]{1,0:T(8,128)(2,1)S(1)}, bf16[128,1024]{1,0:T(8,128)(2,1)S(1)}, u32[]{:S(2)}, u32[]{:S(2)}) collective-permute-start(bf16[128,1024]{1,0:T(8,128)(2,1)S(1)} %broadcast_select_fusion.1), channel_id=1, source_target_pairs={{0,4},{4,0},{8,12},{12,8},{16,20},{20,16},{24,28},{28,24},{1,5},{5... | collective-permute-start | bytes 786440 | tf_op jit(solution)/shard_map/ppermute | solution.py:291
  38.5 11.9 %copy-start.1 = (s32[1,4]{1,0:T(1,128)S(1)}, s32[1,4]{1,0:T(1,128)}, u32[]{:S(2)}) copy-start(s32[1,4]{1,0:T(1,128)} %len_ref.9) | copy-start | bytes 52
  47.0 11.8 %collective-permute-start.17 = (bf16[128,1024]{1,0:T(8,128)(2,1)S(1)}, bf16[128,1024]{1,0:T(8,128)(2,1)S(1)}, u32[]{:S(2)}, u32[]{:S(2)}) collective-permute-start(bf16[128,1024]{1,0:T(8,128)(2,1)S(1)} %broadcast_select_fusion), channel_id=1, source_target_pairs={{0,4},{4,0},{8,12},{12,8},{16,20},{20,16},{24,28},{28,24},{1,5},{5... | collective-permute-start | bytes 786440 | tf_op jit(solution)/shard_map/ppermute | solution.py:291
  48.6 6.6 %collective-permute-start.15 = (bf16[64,1024]{1,0:T(8,128)(2,1)S(1)}, bf16[64,1024]{1,0:T(8,128)(2,1)S(1)}, u32[]{:S(2)}, u32[]{:S(2)}) collective-permute-start(bf16[64,1024]{1,0:T(8,128)(2,1)S(1)} %shard_map.125.mine), channel_id=1, source_target_pairs={{0,16},{4,20},{8,24},{12,28},{16,0},{20,4},{24,8},{28,12},{1,17},{... | collective-permute-start | bytes 393224 | tf_op jit(solution)/shard_map/ppermute | solution.py:291
  55.3 6.5 %collective-permute-start.18 = (bf16[64,1024]{1,0:T(8,128)(2,1)S(1)}, bf16[64,1024]{1,0:T(8,128)(2,1)S(1)}, u32[]{:S(2)}, u32[]{:S(2)}) collective-permute-start(bf16[64,1024]{1,0:T(8,128)(2,1)S(1)} %shard_map.127.refs_0_), channel_id=1, source_target_pairs={{0,4},{4,0},{8,12},{12,8},{16,20},{20,16},{24,28},{28,24},{1,5},{5... | collective-permute-start | bytes 393224 | tf_op jit(solution)/shard_map/ppermute | solution.py:291
  56.8 6.4 %collective-permute-start.19 = (bf16[64,1024]{1,0:T(8,128)(2,1)S(1)}, bf16[64,1024]{1,0:T(8,128)(2,1)S(1)}, u32[]{:S(2)}, u32[]{:S(2)}) collective-permute-start(bf16[64,1024]{1,0:T(8,128)(2,1)S(1)} %shard_map.127.refs_0_), channel_id=1, source_target_pairs={{0,8},{4,12},{8,0},{12,4},{16,24},{20,28},{24,16},{28,20},{1,9},{5... | collective-permute-start | bytes 393224 | tf_op jit(solution)/shard_map/ppermute | solution.py:291
  56.8 7.7 %collective-permute-start.20 = (bf16[64,1024]{1,0:T(8,128)(2,1)S(1)}, bf16[64,1024]{1,0:T(8,128)(2,1)S(1)}, u32[]{:S(2)}, u32[]{:S(2)}) collective-permute-start(bf16[64,1024]{1,0:T(8,128)(2,1)S(1)} %shard_map.127.refs_0_), channel_id=1, source_target_pairs={{0,12},{4,8},{8,4},{12,0},{16,28},{20,24},{24,20},{28,16},{1,13},{... | collective-permute-start | bytes 393224 | tf_op jit(solution)/shard_map/ppermute | solution.py:291

commit v11 on v10

--- a/solution.py
+++ b/solution.py
@@ -283,7 +283,7 @@
 
 def shifted(block, distance):
     count = lax.axis_size("seq")
-    route = [(i, i + distance) for i in range(count) if 0 <= i + distance < count]
+    route = [(i, (i + distance) % count) for i in range(count)]
     return lax.ppermute(block, "seq", route)
 
 

time: 66.4 us -> 64 us (0.964)
  starting transfers between devices: 31.8 us -> 24.9 us
  waiting for transfers between devices: 11.8 us -> 16.6 us
    ppermute x5, waiting for transfers between devices: 0.01 us -> 4.79 us  [shifted(): return lax.ppermute(block, 'seq', route)]
    ppermute x5, starting transfers between devices: 14.4 us -> 9.76 us  [shifted(): return lax.ppermute(block, 'seq', route)]
    ppermute x16, starting transfers between devices: 17.4 us -> 15.1 us  [swapped(): return lax.ppermute(block, axis, xor_route(lax.axis_size(axis), mask))]
  transfers between devices with their start and end apart: 21 -> 21, of which waited for: 6 -> 6; matrix products, arithmetic and copies ran while one was open for 2% -> 2% of each run, Pallas kernels for 28% -> 29%
where the time goes in v11:
time: 64 us; the launch traced here: 63.9 us
  starting transfers between devices  24.9 us (39%)
  Pallas kernels  19.9 us (31%)
  waiting for transfers between devices  16.6 us (26%)
  other arithmetic  1.11 us (2%)
  between operations  0.75 us (1%)
  local copies, waits for them, and re-layouts  0.66 us (1%)
    pallas_call x12, Pallas kernels, call(): pl.pallas_call(kernel, out_shape=outs, in_specs=[SMEM] * len(scalars) + (...  19.9 us
    ppermute x16, starting transfers between devices, swapped(): return lax.ppermute(block, axis, xor_route(lax.axis_size(axis), mask))  15.1 us
    ppermute x16, waiting for transfers between devices, swapped(): return lax.ppermute(block, axis, xor_route(lax.axis_size(axis), mask))  11.8 us
    ppermute x5, starting transfers between devices, shifted(): return lax.ppermute(block, 'seq', route)  9.76 us
    ppermute x5, waiting for transfers between devices, shifted(): return lax.ppermute(block, 'seq', route)  4.79 us
  transfers between devices with their start and end apart: 21, of which 6 were waited for; matrix products, arithmetic and copies ran while one was open for 2% of the time, Pallas kernels for 29%

profile of v11, /device:TPU:0, one launch (start us, length us, event | category | flops | bytes accessed | tf_op | source)
XLA Modules:
  0.0 63.9 jit_solution(582866233560574039)
XLA Ops:
  0.6 3.1 %collective-permute-start = (bf16[128,1024]{1,0:T(8,128)(2,1)}, bf16[128,1024]{1,0:T(8,128)(2,1)S(1)}, u32[]{:S(2)}, u32[]{:S(2)}) collective-permute-start(bf16[128,1024]{1,0:T(8,128)(2,1)} %bitcast.13), channel_id=1, source_target_pairs={{0,8},{4,12},{8,16},{12,20},{16,24},{20,28},{24,0},{28,4},{1,9},{5... | collective-permute-start | bytes 786440 | tf_op jit(solution)/shard_map/ppermute | solution.py:287
  3.7 1.5 %collective-permute-start.5 = (bf16[128,1024]{1,0:T(8,128)(2,1)}, bf16[128,1024]{1,0:T(8,128)(2,1)S(1)}, u32[]{:S(2)}, u32[]{:S(2)}) collective-permute-start(bf16[128,1024]{1,0:T(8,128)(2,1)} %bitcast.17), channel_id=1, source_target_pairs={{0,2},{1,3},{2,0},{3,1},{4,6},{5,7},{6,4},{7,5},{8,10},{9,11},{10,... | collective-permute-start | bytes 786440 | tf_op jit(solution)/shard_map/ppermute | solution.py:291
  5.2 1.5 %collective-permute-start.2 = (bf16[128,1024]{1,0:T(8,128)(2,1)}, bf16[128,1024]{1,0:T(8,128)(2,1)S(1)}, u32[]{:S(2)}, u32[]{:S(2)}) collective-permute-start(bf16[128,1024]{1,0:T(8,128)(2,1)} %bitcast.20), channel_id=1, source_target_pairs={{0,4},{4,8},{8,12},{12,16},{16,20},{20,24},{24,28},{28,0},{1,5},{5... | collective-permute-start | bytes 786440 | tf_op jit(solution)/shard_map/ppermute | solution.py:287
  6.7 1.6 %collective-permute-start.3 = (bf16[128,1024]{1,0:T(8,128)(2,1)}, bf16[128,1024]{1,0:T(8,128)(2,1)S(1)}, u32[]{:S(2)}, u32[]{:S(2)}) collective-permute-start(bf16[128,1024]{1,0:T(8,128)(2,1)} %bitcast.21), channel_id=1, source_target_pairs={{0,8},{4,12},{8,16},{12,20},{16,24},{20,28},{24,0},{28,4},{1,9},{5... | collective-permute-start | bytes 786440 | tf_op jit(solution)/shard_map/ppermute | solution.py:287
  8.3 0.0 collective-permute-start.4
  8.3 4.8 %collective-permute-done.keys.k2 = bf16[128,1024]{1,0:T(8,128)(2,1)S(1)} collective-permute-done((bf16[128,1024]{1,0:T(8,128)(2,1)}, bf16[128,1024]{1,0:T(8,128)(2,1)S(1)}, u32[]{:S(2)}, u32[]{:S(2)}) %collective-permute-start) | collective-permute-done | bytes 262176 | tf_op jit(solution)/shard_map/ppermute | solution.py:287
  13.1 1.0 %broadcast_select_fusion.2 = bf16[128,1024]{1,0:T(8,128)(2,1)S(1)} fusion(bf16[128,1024]{1,0:T(8,128)(2,1)S(1)} %collective-permute-done.keys.k2, pred[]{:T(512)S(6)} %eq.3, bf16[1,128,1024]{2,1,0:T(8,128)(2,1)} %param.8), kind=kLoop, calls=%fused_computation.2 | loop fusion | flops 131072 | bytes 786433 | tf_op jit(solution)/shard_map/jit(_where)/select_n | solution.py:316
  14.1 1.8 %collective-permute-start.1 = (bf16[128,1024]{1,0:T(8,128)(2,1)S(1)}, bf16[128,1024]{1,0:T(8,128)(2,1)S(1)}, u32[]{:S(2)}, u32[]{:S(2)}) collective-permute-start(bf16[128,1024]{1,0:T(8,128)(2,1)S(1)} %broadcast_select_fusion.2), channel_id=1, source_target_pairs={{0,4},{4,0},{8,12},{12,8},{16,20},{20,16},{24,28},{28,24},{1,5},{5... | collective-permute-start | bytes 786440 | tf_op jit(solution)/shard_map/ppermute | solution.py:291
  15.9 0.1 pad_add_fusion.place_ref
  15.9 0.7 %copy-done = s32[1,4]{1,0:T(1,128)S(1)} copy-done((s32[1,4]{1,0:T(1,128)S(1)}, s32[1,4]{1,0:T(1,128)}, u32[]{:S(2)}) %copy-start) | copy-done | bytes 40
  16.6 4.9 %shard_map.118 = (bf16[128,1024]{1,0:T(8,128)(2,1)S(1)}, bf16[128,1024]{1,0:T(8,128)(2,1)S(1)}, bf16[128,1024]{1,0:T(8,128)(2,1)S(1)}, bf16[128,1024]{1,0:T(8,12...) custom-call(s32[1,4]{1,0:T(1,128)S(1)} %copy-done, ...), custom_call_target="tpu_custom_call" | custom-call | flops 335544320 | bytes 8388608 | tf_op jit(solution)/shard_map/pallas_call | solution.py:79
  21.5 1.0 %shard_map.120 = (bf16[128,1024]{1,0:T(8,128)(2,1)S(1)}, f32[128,1024]{1,0:T(8,128)S(1)}) custom-call(s32[1,4]{1,0:T(1,128)S(1)} %copy-done, s32[2]{0:T(128)S(1)} %pad_add_fusion.place_ref, bf16[128,1024]{1,0:T(8,128)(2,1)S(1)} %get-tuple-element.84.q.q0, bf16[128,1024]{1,0:T(8,128)(2,1)S(1)} %collective-permute-done.keys.k2), custom_call_target="tpu_custom_call" | custom-call | flops 33554432 | bytes 1310720 | tf_op jit(solution)/shard_map/pallas_call | solution.py:79
  22.5 0.0 collective-permute-done.2.v1
  22.5 1.9 %collective-permute-start.13 = (bf16[128,1024]{1,0:T(8,128)(2,1)S(1)}, bf16[128,1024]{1,0:T(8,128)(2,1)S(1)}, u32[]{:S(2)}, u32[]{:S(2)}) collective-permute-start(bf16[128,1024]{1,0:T(8,128)(2,1)S(1)} %get-tuple-element.84.q.q0), channel_id=1, source_target_pairs={{0,24},{4,28},{8,0},{12,4},{16,8},{20,12},{24,16},{28,20},{1,25},{... | collective-permute-start | bytes 786440 | tf_op jit(solution)/shard_map/ppermute | solution.py:287
  24.4 0.0 collective-permute-done.4.refs_5_
  24.4 0.0 collective-permute-done.6.refs_7_
  24.4 0.0 collective-permute-done.1.keys.k1
  24.4 1.0 %shard_map.119 = (bf16[128,1024]{1,0:T(8,128)(2,1)S(1)}, f32[128,1024]{1,0:T(8,128)S(1)}) custom-call(s32[1,4]{1,0:T(1,128)S(1)} %copy-done, s32[2]{0:T(128)S(1)} %pad_add_fusion.place_ref, bf16[128,1024]{1,0:T(8,128)(2,1)S(1)} %get-tuple-element.84.q.q0, bf16[128,1024]{1,0:T(8,128)(2,1)S(1)} %collective-permute-done.1.keys.k1), custom_call_target="tpu_custom_call" | custom-call | flops 33554432 | bytes 1310720 | tf_op jit(solution)/shard_map/pallas_call | solution.py:79
  25.4 1.1 %shard_map.121 = (bf16[128,1024]{1,0:T(8,128)(2,1)S(1)}, f32[128,1024]{1,0:T(8,128)S(1)}, f32[128,128]{1,0:T(8,128)S(1)}, bf16[128,256]{1,0:T(8,128)(2,1)S(1)}, ...) custom-call(s32[2]{0:T(128)S(1)} %pad_add_fusion.place_ref, ...), custom_call_target="tpu_custom_call" | custom-call | flops 33554432 | bytes 2949120 | tf_op jit(solution)/shard_map/pallas_call | solution.py:79
  26.6 0.3 collective-permute-start.7
  26.9 1.5 %collective-permute-start.8 = (bf16[128,256]{1,0:T(8,128)(2,1)S(1)}, bf16[128,256]{1,0:T(8,128)(2,1)S(1)}, u32[]{:S(2)}, u32[]{:S(2)}) collective-permute-start(bf16[128,256]{1,0:T(8,128)(2,1)S(1)} %get-tuple-element.71), channel_id=1, source_target_pairs={{0,2},{1,3},{2,0},{3,1},{4,6},{5,7},{6,4},{7,5},{8,10},{9,11},{10,... | collective-permute-start | bytes 196616 | tf_op jit(solution)/shard_map/ppermute | solution.py:291
  28.4 0.1 collective-permute-start.9
  28.5 0.9 %shard_map.122 = (bf16[128,1024]{1,0:T(8,128)(2,1)}, bf16[128,1024]{1,0:T(8,128)(2,1)S(1)}) custom-call(f32[128,1024]{1,0:T(8,128)S(1)} %get-tuple-element.59.grad_hidden, bf16[128,1024]{1,0:T(8,128)(2,1)S(1)} %get-tuple-element.60.gates, f32[128,1024]{1,0:T(8,128)S(1)} %get-tuple-element.65.normed, f32[128,128]{1,0:T(8,128)S(1)} %get-tuple-element.66.inv_std), custom_call_target="tpu_custom_call" | custom-call | flops 8388608 | bytes 1900544 | tf_op jit(solution)/shard_map/pallas_call | solution.py:79
  29.4 1.7 %collective-permute-start.14 = (bf16[128,1024]{1,0:T(8,128)(2,1)S(1)}, bf16[128,1024]{1,0:T(8,128)(2,1)S(1)}, u32[]{:S(2)}, u32[]{:S(2)}) collective-permute-start(bf16[128,1024]{1,0:T(8,128)(2,1)S(1)} %get-tuple-element.67.grad_mix.g0), channel_id=1, source_target_pairs={{0,24},{4,28},{8,0},{12,4},{16,8},{20,12},{24,16},{28,20},{1,25},{... | collective-permute-start | bytes 786440 | tf_op jit(solution)/shard_map/ppermute | solution.py:287
  31.1 0.0 collective-permute-done.7.refs_1_
  31.1 0.0 collective-permute-done.8.refs_2_
  31.1 1.4 %collective-permute-done.9.refs_3_ = bf16[128,256]{1,0:T(8,128)(2,1)S(1)} collective-permute-done((bf16[128,256]{1,0:T(8,128)(2,1)S(1)}, bf16[128,256]{1,0:T(8,128)(2,1)S(1)}, u32[]{:S(2)}, u32[]{:S(2)}) %collective-permute-start.9) | collective-permute-done | bytes 65568 | tf_op jit(solution)/shard_map/ppermute | solution.py:291
  32.6 1.1 %shard_map.123 = (f32[64,1024]{1,0:T(8,128)S(1)}, bf16[64,1024]{1,0:T(8,128)(2,1)S(1)}, bf16[64,1024]{1,0:T(8,128)(2,1)S(1)}, bf16[64,1024]{1,0:T(8,128)(2,1)S(1)}) custom-call(s32[2]{0:T(128)S(1)} %pad_add_fusion.place_ref, bf16[128,256]{1,0:T(8,128)(2,1)S(1)} %get-tuple-element.69.refs_0_, bf16[128,256]{1,0:T(8,128)(2,1)S(1)} %collective-permute-done.7.refs_1_, ...), custom_call_target="tpu_custom_call" | custom-call | flops 268435456 | bytes 1966080 | tf_op jit(solution)/shard_map/pallas_call | solution.py:79
  33.6 0.6 collective-permute-start.10
  34.2 0.2 collective-permute-start.11
  34.5 2.7 %collective-permute-start.12 = (bf16[64,1024]{1,0:T(8,128)(2,1)S(1)}, bf16[64,1024]{1,0:T(8,128)(2,1)S(1)}, u32[]{:S(2)}, u32[]{:S(2)}) collective-permute-start(bf16[64,1024]{1,0:T(8,128)(2,1)S(1)} %get-tuple-element.82), channel_id=1, source_target_pairs={{0,12},{4,8},{8,4},{12,0},{16,28},{20,24},{24,20},{28,16},{1,13},{... | collective-permute-start | bytes 393224 | tf_op jit(solution)/shard_map/ppermute | solution.py:291
  37.2 0.0 collective-permute-done.13.q2
  37.2 0.6 collective-permute-start.16
  37.8 2.7 %shard_map.124 = (bf16[128,1024]{1,0:T(8,128)(2,1)}, bf16[128,1024]{1,0:T(8,128)(2,1)}) custom-call(bf16[128,1024]{1,0:T(8,128)(2,1)S(1)} %get-tuple-element.51.k0.k, bf16[128,1024]{1,0:T(8,128)(2,1)S(1)} %collective-permute-done.1.keys.k1, bf16[128,1024]{1,0:T(8,128)(2,1)S(1)} %collective-permute-done.keys.k2, ...), custom_call_target="tpu_custom_call" | custom-call | flops 469762048 | bytes 6291456 | tf_op jit(solution)/shard_map/pallas_call | solution.py:79
  40.5 0.0 collective-permute-done.10.refs_0_
  40.5 0.7 %collective-permute-done.11.refs_1_ = bf16[64,1024]{1,0:T(8,128)(2,1)S(1)} collective-permute-done((bf16[64,1024]{1,0:T(8,128)(2,1)S(1)}, bf16[64,1024]{1,0:T(8,128)(2,1)S(1)}, u32[]{:S(2)}, u32[]{:S(2)}) %collective-permute-start.11) | collective-permute-done | bytes 131104 | tf_op jit(solution)/shard_map/ppermute | solution.py:291
  41.3 2.5 %collective-permute-done.12.refs_2_ = bf16[64,1024]{1,0:T(8,128)(2,1)S(1)} collective-permute-done((bf16[64,1024]{1,0:T(8,128)(2,1)S(1)}, bf16[64,1024]{1,0:T(8,128)(2,1)S(1)}, u32[]{:S(2)}, u32[]{:S(2)}) %collective-permute-start.12) | collective-permute-done | bytes 131104 | tf_op jit(solution)/shard_map/ppermute | solution.py:291
  43.8 0.1 shard_map.125.mine
  43.9 1.6 %collective-permute-start.17 = (bf16[128,1024]{1,0:T(8,128)(2,1)S(1)}, bf16[128,1024]{1,0:T(8,128)(2,1)S(1)}, u32[]{:S(2)}, u32[]{:S(2)}) collective-permute-start(bf16[128,1024]{1,0:T(8,128)(2,1)S(1)} %broadcast_select_fusion), channel_id=1, source_target_pairs={{0,4},{4,0},{8,12},{12,8},{16,20},{20,16},{24,28},{28,24},{1,5},{5... | collective-permute-start | bytes 786440 | tf_op jit(solution)/shard_map/ppermute | solution.py:291
  45.4 0.6 collective-permute-start.15
  46.0 2.7 %shard_map.126 = (f32[128,1024]{1,0:T(8,128)S(1)}, f32[128,1024]{1,0:T(8,128)S(1)}) custom-call(s32[1,4]{1,0:T(1,128)S(1)} %copy-done.1, s32[2]{0:T(128)S(1)} %pad_add_fusion.place_ref, bf16[128,1024]{1,0:T(8,128)(2,1)S(1)} %get-tuple-element.51.k0.k, bf16[128,1024]{1,0:T(8,128)(2,1)S(1)} %get-tuple-element.87.v0.v, ...), custom_call_target="tpu_custom_call" | custom-call | flops 268435456 | bytes 2621440 | tf_op jit(solution)/shard_map/pallas_call | solution.py:79
  48.7 5.2 %collective-permute-done.15.other = bf16[64,1024]{1,0:T(8,128)(2,1)S(1)} collective-permute-done((bf16[64,1024]{1,0:T(8,128)(2,1)S(1)}, bf16[64,1024]{1,0:T(8,128)(2,1)S(1)}, u32[]{:S(2)}, u32[]{:S(2)}) %collective-permute-start.15) | collective-permute-done | bytes 131104 | tf_op jit(solution)/shard_map/ppermute | solution.py:291
  54.0 0.4 collective-permute-start.18
  54.4 0.1 collective-permute-start.19
  54.5 3.0 %collective-permute-start.20 = (bf16[64,1024]{1,0:T(8,128)(2,1)S(1)}, bf16[64,1024]{1,0:T(8,128)(2,1)S(1)}, u32[]{:S(2)}, u32[]{:S(2)}) collective-permute-start(bf16[64,1024]{1,0:T(8,128)(2,1)S(1)} %shard_map.127.refs_0_), channel_id=1, source_target_pairs={{0,12},{4,8},{8,4},{12,0},{16,28},{20,24},{24,20},{28,16},{1,13},{... | collective-permute-start | bytes 393224 | tf_op jit(solution)/shard_map/ppermute | solution.py:291
  57.5 2.9 %shard_map.128 = (bf16[128,1024]{1,0:T(8,128)(2,1)}, bf16[128,1024]{1,0:T(8,128)(2,1)}) custom-call(s32[1,4]{1,0:T(1,128)S(1)} %copy-done.1, s32[2]{0:T(128)S(1)} %pad_add_fusion.place_ref, bf16[128,1024]{1,0:T(8,128)(2,1)S(1)} %get-tuple-element.51.k0.k, bf16[128,1024]{1,0:T(8,128)(2,1)S(1)} %get-tuple-element.87.v0.v, ...), custom_call_target="tpu_custom_call" | custom-call | flops 134217728 | bytes 2621440 | tf_op jit(solution)/shard_map/pallas_call | solution.py:79
  60.4 1.9 %collective-permute-done.20.refs_3_ = bf16[64,1024]{1,0:T(8,128)(2,1)S(1)} collective-permute-done((bf16[64,1024]{1,0:T(8,128)(2,1)S(1)}, bf16[64,1024]{1,0:T(8,128)(2,1)S(1)}, u32[]{:S(2)}, u32[]{:S(2)}) %collective-permute-start.20) | collective-permute-done | bytes 131104 | tf_op jit(solution)/shard_map/ppermute | solution.py:291
  62.3 1.6 %shard_map.129 = f32[256,1024]{1,0:T(8,128)} custom-call(s32[2]{0:T(128)S(1)} %pad_add_fusion.place_ref, bf16[64,1024]{1,0:T(8,128)(2,1)S(1)} %shard_map.127.refs_0_, bf16[64,1024]{1,0:T(8,128)(2,1)S(1)} %collective-permute-done.18.refs_1_, bf16[64,1024]{1,0:T(8,128)(2,1)S(1)} %collective-permute-done.19.refs_2_, ...), custom_call_target="tpu_custom_call" | custom-call | flops 262144 | bytes 1572864 | tf_op jit(solution)/shard_map/pallas_call | solution.py:79
  (14 shorter events, 0.1 us)
Async XLA Ops:
  0.6 12.4 %collective-permute-start = (bf16[128,1024]{1,0:T(8,128)(2,1)}, bf16[128,1024]{1,0:T(8,128)(2,1)S(1)}, u32[]{:S(2)}, u32[]{:S(2)}) collective-permute-start(bf16[128,1024]{1,0:T(8,128)(2,1)} %bitcast.13), channel_id=1, source_target_pairs={{0,8},{4,12},{8,16},{12,20},{16,24},{20,28},{24,0},{28,4},{1,9},{5... | collective-permute-start | bytes 786440 | tf_op jit(solution)/shard_map/ppermute | solution.py:287
  3.7 12.2 %collective-permute-start.5 = (bf16[128,1024]{1,0:T(8,128)(2,1)}, bf16[128,1024]{1,0:T(8,128)(2,1)S(1)}, u32[]{:S(2)}, u32[]{:S(2)}) collective-permute-start(bf16[128,1024]{1,0:T(8,128)(2,1)} %bitcast.17), channel_id=1, source_target_pairs={{0,2},{1,3},{2,0},{3,1},{4,6},{5,7},{6,4},{7,5},{8,10},{9,11},{10,... | collective-permute-start | bytes 786440 | tf_op jit(solution)/shard_map/ppermute | solution.py:291
  5.2 17.3 %collective-permute-start.2 = (bf16[128,1024]{1,0:T(8,128)(2,1)}, bf16[128,1024]{1,0:T(8,128)(2,1)S(1)}, u32[]{:S(2)}, u32[]{:S(2)}) collective-permute-start(bf16[128,1024]{1,0:T(8,128)(2,1)} %bitcast.20), channel_id=1, source_target_pairs={{0,4},{4,8},{8,12},{12,16},{16,20},{20,24},{24,28},{28,0},{1,5},{5... | collective-permute-start | bytes 786440 | tf_op jit(solution)/shard_map/ppermute | solution.py:287
  6.7 18.7 %collective-permute-start.3 = (bf16[128,1024]{1,0:T(8,128)(2,1)}, bf16[128,1024]{1,0:T(8,128)(2,1)S(1)}, u32[]{:S(2)}, u32[]{:S(2)}) collective-permute-start(bf16[128,1024]{1,0:T(8,128)(2,1)} %bitcast.21), channel_id=1, source_target_pairs={{0,8},{4,12},{8,16},{12,20},{16,24},{20,28},{24,0},{28,4},{1,9},{5... | collective-permute-start | bytes 786440 | tf_op jit(solution)/shard_map/ppermute | solution.py:287
  8.3 16.1 %collective-permute-start.4 = (bf16[128,1024]{1,0:T(8,128)(2,1)}, bf16[128,1024]{1,0:T(8,128)(2,1)S(1)}, u32[]{:S(2)}, u32[]{:S(2)}) collective-permute-start(bf16[128,1024]{1,0:T(8,128)(2,1)} %bitcast.18), channel_id=1, source_target_pairs={{0,1},{1,0},{2,3},{3,2},{4,5},{5,4},{6,7},{7,6},{8,9},{9,8},{10,11... | collective-permute-start | bytes 786440 | tf_op jit(solution)/shard_map/ppermute | solution.py:291
  14.1 10.4 %collective-permute-start.1 = (bf16[128,1024]{1,0:T(8,128)(2,1)S(1)}, bf16[128,1024]{1,0:T(8,128)(2,1)S(1)}, u32[]{:S(2)}, u32[]{:S(2)}) collective-permute-start(bf16[128,1024]{1,0:T(8,128)(2,1)S(1)} %broadcast_select_fusion.2), channel_id=1, source_target_pairs={{0,4},{4,0},{8,12},{12,8},{16,20},{20,16},{24,28},{28,24},{1,5},{5... | collective-permute-start | bytes 786440 | tf_op jit(solution)/shard_map/ppermute | solution.py:291
  15.9 8.5 %collective-permute-start.6 = (bf16[128,1024]{1,0:T(8,128)(2,1)S(1)}, bf16[128,1024]{1,0:T(8,128)(2,1)S(1)}, u32[]{:S(2)}, u32[]{:S(2)}) collective-permute-start(bf16[128,1024]{1,0:T(8,128)(2,1)S(1)} %collective-permute-done.5.refs_6_), channel_id=1, source_target_pairs={{0,1},{1,0},{2,3},{3,2},{4,5},{5,4},{6,7},{7,6},{8,9},{9,8},{10,11... | collective-permute-start | bytes 786440 | tf_op jit(solution)/shard_map/ppermute | solution.py:291
  15.9 0.7 %copy-start = (s32[1,4]{1,0:T(1,128)S(1)}, s32[1,4]{1,0:T(1,128)}, u32[]{:S(2)}) copy-start(s32[1,4]{1,0:T(1,128)} %len_ref.9) | copy-start | bytes 52
  22.5 14.7 %collective-permute-start.13 = (bf16[128,1024]{1,0:T(8,128)(2,1)S(1)}, bf16[128,1024]{1,0:T(8,128)(2,1)S(1)}, u32[]{:S(2)}, u32[]{:S(2)}) collective-permute-start(bf16[128,1024]{1,0:T(8,128)(2,1)S(1)} %get-tuple-element.84.q.q0), channel_id=1, source_target_pairs={{0,24},{4,28},{8,0},{12,4},{16,8},{20,12},{24,16},{28,20},{1,25},{... | collective-permute-start | bytes 786440 | tf_op jit(solution)/shard_map/ppermute | solution.py:287
  26.6 4.5 %collective-permute-start.7 = (bf16[128,256]{1,0:T(8,128)(2,1)S(1)}, bf16[128,256]{1,0:T(8,128)(2,1)S(1)}, u32[]{:S(2)}, u32[]{:S(2)}) collective-permute-start(bf16[128,256]{1,0:T(8,128)(2,1)S(1)} %get-tuple-element.70), channel_id=1, source_target_pairs={{0,1},{1,0},{2,3},{3,2},{4,5},{5,4},{6,7},{7,6},{8,9},{9,8},{10,11... | collective-permute-start | bytes 196616 | tf_op jit(solution)/shard_map/ppermute | solution.py:291
  26.9 4.3 %collective-permute-start.8 = (bf16[128,256]{1,0:T(8,128)(2,1)S(1)}, bf16[128,256]{1,0:T(8,128)(2,1)S(1)}, u32[]{:S(2)}, u32[]{:S(2)}) collective-permute-start(bf16[128,256]{1,0:T(8,128)(2,1)S(1)} %get-tuple-element.71), channel_id=1, source_target_pairs={{0,2},{1,3},{2,0},{3,1},{4,6},{5,7},{6,4},{7,5},{8,10},{9,11},{10,... | collective-permute-start | bytes 196616 | tf_op jit(solution)/shard_map/ppermute | solution.py:291
  28.4 4.2 %collective-permute-start.9 = (bf16[128,256]{1,0:T(8,128)(2,1)S(1)}, bf16[128,256]{1,0:T(8,128)(2,1)S(1)}, u32[]{:S(2)}, u32[]{:S(2)}) collective-permute-start(bf16[128,256]{1,0:T(8,128)(2,1)S(1)} %get-tuple-element.72), channel_id=1, source_target_pairs={{0,3},{1,2},{2,1},{3,0},{4,7},{5,6},{6,5},{7,4},{8,11},{9,10},{10,... | collective-permute-start | bytes 196616 | tf_op jit(solution)/shard_map/ppermute | solution.py:291
  29.4 14.5 %collective-permute-start.14 = (bf16[128,1024]{1,0:T(8,128)(2,1)S(1)}, bf16[128,1024]{1,0:T(8,128)(2,1)S(1)}, u32[]{:S(2)}, u32[]{:S(2)}) collective-permute-start(bf16[128,1024]{1,0:T(8,128)(2,1)S(1)} %get-tuple-element.67.grad_mix.g0), channel_id=1, source_target_pairs={{0,24},{4,28},{8,0},{12,4},{16,8},{20,12},{24,16},{28,20},{1,25},{... | collective-permute-start | bytes 786440 | tf_op jit(solution)/shard_map/ppermute | solution.py:287
  33.6 6.9 %collective-permute-start.10 = (bf16[64,1024]{1,0:T(8,128)(2,1)S(1)}, bf16[64,1024]{1,0:T(8,128)(2,1)S(1)}, u32[]{:S(2)}, u32[]{:S(2)}) collective-permute-start(bf16[64,1024]{1,0:T(8,128)(2,1)S(1)} %get-tuple-element.80), channel_id=1, source_target_pairs={{0,4},{4,0},{8,12},{12,8},{16,20},{20,16},{24,28},{28,24},{1,5},{5... | collective-permute-start | bytes 393224 | tf_op jit(solution)/shard_map/ppermute | solution.py:291
  34.2 7.0 %collective-permute-start.11 = (bf16[64,1024]{1,0:T(8,128)(2,1)S(1)}, bf16[64,1024]{1,0:T(8,128)(2,1)S(1)}, u32[]{:S(2)}, u32[]{:S(2)}) collective-permute-start(bf16[64,1024]{1,0:T(8,128)(2,1)S(1)} %get-tuple-element.81), channel_id=1, source_target_pairs={{0,8},{4,12},{8,0},{12,4},{16,24},{20,28},{24,16},{28,20},{1,9},{5... | collective-permute-start | bytes 393224 | tf_op jit(solution)/shard_map/ppermute | solution.py:291
  34.5 9.3 %collective-permute-start.12 = (bf16[64,1024]{1,0:T(8,128)(2,1)S(1)}, bf16[64,1024]{1,0:T(8,128)(2,1)S(1)}, u32[]{:S(2)}, u32[]{:S(2)}) collective-permute-start(bf16[64,1024]{1,0:T(8,128)(2,1)S(1)} %get-tuple-element.82), channel_id=1, source_target_pairs={{0,12},{4,8},{8,4},{12,0},{16,28},{20,24},{24,20},{28,16},{1,13},{... | collective-permute-start | bytes 393224 | tf_op jit(solution)/shard_map/ppermute | solution.py:291
  37.2 20.3 %collective-permute-start.16 = (bf16[128,1024]{1,0:T(8,128)(2,1)S(1)}, bf16[128,1024]{1,0:T(8,128)(2,1)S(1)}, u32[]{:S(2)}, u32[]{:S(2)}) collective-permute-start(bf16[128,1024]{1,0:T(8,128)(2,1)S(1)} %broadcast_select_fusion.1), channel_id=1, source_target_pairs={{0,4},{4,0},{8,12},{12,8},{16,20},{20,16},{24,28},{28,24},{1,5},{5... | collective-permute-start | bytes 786440 | tf_op jit(solution)/shard_map/ppermute | solution.py:291
  37.8 8.2 %copy-start.1 = (s32[1,4]{1,0:T(1,128)S(1)}, s32[1,4]{1,0:T(1,128)}, u32[]{:S(2)}) copy-start(s32[1,4]{1,0:T(1,128)} %len_ref.9) | copy-start | bytes 52
  43.9 13.6 %collective-permute-start.17 = (bf16[128,1024]{1,0:T(8,128)(2,1)S(1)}, bf16[128,1024]{1,0:T(8,128)(2,1)S(1)}, u32[]{:S(2)}, u32[]{:S(2)}) collective-permute-start(bf16[128,1024]{1,0:T(8,128)(2,1)S(1)} %broadcast_select_fusion), channel_id=1, source_target_pairs={{0,4},{4,0},{8,12},{12,8},{16,20},{20,16},{24,28},{28,24},{1,5},{5... | collective-permute-start | bytes 786440 | tf_op jit(solution)/shard_map/ppermute | solution.py:291
  45.4 8.5 %collective-permute-start.15 = (bf16[64,1024]{1,0:T(8,128)(2,1)S(1)}, bf16[64,1024]{1,0:T(8,128)(2,1)S(1)}, u32[]{:S(2)}, u32[]{:S(2)}) collective-permute-start(bf16[64,1024]{1,0:T(8,128)(2,1)S(1)} %shard_map.125.mine), channel_id=1, source_target_pairs={{0,16},{4,20},{8,24},{12,28},{16,0},{20,4},{24,8},{28,12},{1,17},{... | collective-permute-start | bytes 393224 | tf_op jit(solution)/shard_map/ppermute | solution.py:291
  54.0 6.5 %collective-permute-start.18 = (bf16[64,1024]{1,0:T(8,128)(2,1)S(1)}, bf16[64,1024]{1,0:T(8,128)(2,1)S(1)}, u32[]{:S(2)}, u32[]{:S(2)}) collective-permute-start(bf16[64,1024]{1,0:T(8,128)(2,1)S(1)} %shard_map.127.refs_0_), channel_id=1, source_target_pairs={{0,4},{4,0},{8,12},{12,8},{16,20},{20,16},{24,28},{28,24},{1,5},{5... | collective-permute-start | bytes 393224 | tf_op jit(solution)/shard_map/ppermute | solution.py:291
  54.4 6.0 %collective-permute-start.19 = (bf16[64,1024]{1,0:T(8,128)(2,1)S(1)}, bf16[64,1024]{1,0:T(8,128)(2,1)S(1)}, u32[]{:S(2)}, u32[]{:S(2)}) collective-permute-start(bf16[64,1024]{1,0:T(8,128)(2,1)S(1)} %shard_map.127.refs_0_), channel_id=1, source_target_pairs={{0,8},{4,12},{8,0},{12,4},{16,24},{20,28},{24,16},{28,20},{1,9},{5... | collective-permute-start | bytes 393224 | tf_op jit(solution)/shard_map/ppermute | solution.py:291
  54.5 7.8 %collective-permute-start.20 = (bf16[64,1024]{1,0:T(8,128)(2,1)S(1)}, bf16[64,1024]{1,0:T(8,128)(2,1)S(1)}, u32[]{:S(2)}, u32[]{:S(2)}) collective-permute-start(bf16[64,1024]{1,0:T(8,128)(2,1)S(1)} %shard_map.127.refs_0_), channel_id=1, source_target_pairs={{0,12},{4,8},{8,4},{12,0},{16,28},{20,24},{24,20},{28,16},{1,13},{... | collective-permute-start | bytes 393224 | tf_op jit(solution)/shard_map/ppermute | solution.py:291

commit v12 on v11

--- a/solution.py
+++ b/solution.py
@@ -313,20 +313,20 @@
 
     k2 = shifted(keys[0], 2)
     v2 = shifted(values[0], 2)
-    passed = jnp.where(even, keys[0], k2)
-    k1 = swapped(passed, "seq", 1)
     q, k, v, grad, w, gate, mixed_own, grad_hidden, slope0 = call(
         own_kernel,
         [near, near, near, near, kept(w_out.shape, BF16), near, wide, wide, wide],
         scalars,
         tuple(
             in_hbm(a)
-            for a in (after(queries[0], passed), keys[0], values[0], out_grad[0], w_out, gates[0])
+            for a in (queries[0], keys[0], values[0], out_grad[0], w_out, gates[0])
         ),
         proj_flops + 2 * block_flops,
         [pltpu.SemaphoreType.DMA((5 + CHUNKS,))],
         [hbm] * 6,
     )
+    passed = jnp.where(even, k, k2)
+    k1 = swapped(passed, "seq", 1)
     v1 = shifted(values[0], 1)
     grads = [grad]
     for d in range(1, batch):
@@ -334,9 +334,9 @@
         source = out_grad[0] if d == 1 else out_grad[0] if d == low else grads[d ^ low]
         grads.append(swapped(source, "batch", low))
     attention2, slope2 = call(
-        functools.partial(far_kernel, 2), [near, wide], scalars, (after(q, passed), k2), block_flops
-    )
-    q2 = shifted(after(q, attention2), -2)
+        functools.partial(far_kernel, 2), [near, wide], scalars, (after(q, grads[2]), k2), block_flops
+    )
+    q2 = shifted(after(q, grads[2]), -2)
     passed_q = jnp.where(even, q2, q)
     q1 = swapped(passed_q, "seq", 1)
     attention1, slope1 = call(
@@ -346,7 +346,7 @@
         functools.partial(forward_kernel, batch),
         [near, wide, kept((rows, 128), F32)] + [kept((rows, part), BF16)] * batch,
         (place,),
-        (attention1, attention2, v1, v2, after(mixed_own, grads[1], grads[3]), gate),
+        (attention1, attention2, v1, v2, after(mixed_own, grads[1]), gate),
         block_flops,
         [pltpu.VMEM((rows, width), F32)],
     )

time: 64 us -> 67.1 us (1.048)
  starting transfers between devices: 24.9 us -> 30.6 us
  waiting for transfers between devices: 16.6 us -> 14.8 us
  other arithmetic: 1.11 us -> 0.16 us
    ppermute x16, starting transfers between devices: 15.1 us -> 21.8 us  [swapped(): return lax.ppermute(block, axis, xor_route(lax.axis_size(axis), mask))]
    ppermute x16, waiting for transfers between devices: 11.8 us -> 10.5 us  [swapped(): return lax.ppermute(block, axis, xor_route(lax.axis_size(axis), mask))]
    ppermute x5, starting transfers between devices: 9.76 us -> 8.78 us  [shifted(): return lax.ppermute(block, 'seq', route)]
    select_n x1, other arithmetic: 0.98 us -> 0.03 us  [on_device(): passed = jnp.where(even, k, k2)]
  transfers between devices with their start and end apart: 21 -> 21, of which waited for: 6 -> 9; matrix products, arithmetic and copies ran while one was open for 2% -> 0% of each run, Pallas kernels for 29% -> 27%
where the time goes in v12:
time: 67.1 us; the launch traced here: 66.9 us
  starting transfers between devices  30.6 us (46%)
  Pallas kernels  19.9 us (30%)
  waiting for transfers between devices  14.8 us (22%)
  between operations  0.76 us (1%)
    ppermute x16, starting transfers between devices, swapped(): return lax.ppermute(block, axis, xor_route(lax.axis_size(axis), mask))  21.8 us
    pallas_call x12, Pallas kernels, call(): pl.pallas_call(kernel, out_shape=outs, in_specs=[SMEM] * len(scalars) + (...  19.9 us
    ppermute x16, waiting for transfers between devices, swapped(): return lax.ppermute(block, axis, xor_route(lax.axis_size(axis), mask))  10.5 us
    ppermute x5, starting transfers between devices, shifted(): return lax.ppermute(block, 'seq', route)  8.78 us
    ppermute x5, waiting for transfers between devices, shifted(): return lax.ppermute(block, 'seq', route)  4.35 us
  transfers between devices with their start and end apart: 21, of which 9 were waited for; matrix products, arithmetic and copies ran while one was open for 0% of the time, Pallas kernels for 27%

profile of v12, /device:TPU:0, one launch (start us, length us, event | category | flops | bytes accessed | tf_op | source)
XLA Modules:
  0.0 66.9 jit_solution(5909969589493369823)
XLA Ops:
  0.6 3.1 %collective-permute-start = (bf16[128,1024]{1,0:T(8,128)(2,1)}, bf16[128,1024]{1,0:T(8,128)(2,1)S(1)}, u32[]{:S(2)}, u32[]{:S(2)}) collective-permute-start(bf16[128,1024]{1,0:T(8,128)(2,1)} %bitcast.14), channel_id=1, source_target_pairs={{0,8},{4,12},{8,16},{12,20},{16,24},{20,28},{24,0},{28,4},{1,9},{5... | collective-permute-start | bytes 786440 | tf_op jit(solution)/shard_map/ppermute | solution.py:287
  3.7 1.5 %collective-permute-start.4 = (bf16[128,1024]{1,0:T(8,128)(2,1)}, bf16[128,1024]{1,0:T(8,128)(2,1)S(1)}, u32[]{:S(2)}, u32[]{:S(2)}) collective-permute-start(bf16[128,1024]{1,0:T(8,128)(2,1)} %bitcast.16), channel_id=1, source_target_pairs={{0,2},{1,3},{2,0},{3,1},{4,6},{5,7},{6,4},{7,5},{8,10},{9,11},{10,... | collective-permute-start | bytes 786440 | tf_op jit(solution)/shard_map/ppermute | solution.py:291
  5.2 0.0 collective-permute-start.5
  5.2 1.5 %collective-permute-start.2 = (bf16[128,1024]{1,0:T(8,128)(2,1)}, bf16[128,1024]{1,0:T(8,128)(2,1)S(1)}, u32[]{:S(2)}, u32[]{:S(2)}) collective-permute-start(bf16[128,1024]{1,0:T(8,128)(2,1)} %bitcast.19), channel_id=1, source_target_pairs={{0,4},{4,8},{8,12},{12,16},{16,20},{20,24},{24,28},{28,0},{1,5},{5... | collective-permute-start | bytes 786440 | tf_op jit(solution)/shard_map/ppermute | solution.py:287
  6.7 0.1 pad_add_fusion.place_ref
  6.8 0.7 copy-done
  7.5 4.9 %shard_map.118 = (bf16[128,1024]{1,0:T(8,128)(2,1)S(1)}, bf16[128,1024]{1,0:T(8,128)(2,1)S(1)}, bf16[128,1024]{1,0:T(8,128)(2,1)S(1)}, bf16[128,1024]{1,0:T(8,12...) custom-call(s32[1,4]{1,0:T(1,128)S(1)} %copy-done, ...), custom_call_target="tpu_custom_call" | custom-call | flops 335544320 | bytes 8388608 | tf_op jit(solution)/shard_map/pallas_call | solution.py:79
  12.3 0.0 collective-permute-done.keys.k2
  12.4 2.5 %collective-permute-start.1 = (bf16[128,1024]{1,0:T(8,128)(2,1)S(1)}, bf16[128,1024]{1,0:T(8,128)(2,1)S(1)}, u32[]{:S(2)}, u32[]{:S(2)}) collective-permute-start(bf16[128,1024]{1,0:T(8,128)(2,1)S(1)} %broadcast_select_fusion.2), channel_id=1, source_target_pairs={{0,4},{4,0},{8,12},{12,8},{16,20},{20,16},{24,28},{28,24},{1,5},{5... | collective-permute-start | bytes 786440 | tf_op jit(solution)/shard_map/ppermute | solution.py:291
  14.9 0.7 %collective-permute-start.3 = (bf16[128,1024]{1,0:T(8,128)(2,1)S(1)}, bf16[128,1024]{1,0:T(8,128)(2,1)S(1)}, u32[]{:S(2)}, u32[]{:S(2)}) collective-permute-start(bf16[128,1024]{1,0:T(8,128)(2,1)S(1)} %bitcast.21), channel_id=1, source_target_pairs={{0,8},{4,12},{8,16},{12,20},{16,24},{20,28},{24,0},{28,4},{1,9},{5... | collective-permute-start | bytes 786440 | tf_op jit(solution)/shard_map/ppermute | solution.py:287
  15.6 0.0 collective-permute-done.4.refs_6_
  15.6 0.0 collective-permute-start.9
  15.6 3.8 %collective-permute-done.2.v1 = bf16[128,1024]{1,0:T(8,128)(2,1)S(1)} collective-permute-done((bf16[128,1024]{1,0:T(8,128)(2,1)}, bf16[128,1024]{1,0:T(8,128)(2,1)S(1)}, u32[]{:S(2)}, u32[]{:S(2)}) %collective-permute-start.2) | collective-permute-done | bytes 262176 | tf_op jit(solution)/shard_map/ppermute | solution.py:287
  19.4 2.4 %collective-permute-start.13 = (bf16[128,1024]{1,0:T(8,128)(2,1)S(1)}, bf16[128,1024]{1,0:T(8,128)(2,1)S(1)}, u32[]{:S(2)}, u32[]{:S(2)}) collective-permute-start(bf16[128,1024]{1,0:T(8,128)(2,1)S(1)} %get-tuple-element.54.q.q0), channel_id=1, source_target_pairs={{0,24},{4,28},{8,0},{12,4},{16,8},{20,12},{24,16},{28,20},{1,25},{... | collective-permute-start | bytes 786440 | tf_op jit(solution)/shard_map/ppermute | solution.py:287
  21.7 1.0 %shard_map.120 = (bf16[128,1024]{1,0:T(8,128)(2,1)S(1)}, f32[128,1024]{1,0:T(8,128)S(1)}) custom-call(s32[1,4]{1,0:T(1,128)S(1)} %copy-done, s32[2]{0:T(128)S(1)} %pad_add_fusion.place_ref, bf16[128,1024]{1,0:T(8,128)(2,1)S(1)} %get-tuple-element.54.q.q0, bf16[128,1024]{1,0:T(8,128)(2,1)S(1)} %collective-permute-done.keys.k2), custom_call_target="tpu_custom_call" | custom-call | flops 33554432 | bytes 1310720 | tf_op jit(solution)/shard_map/pallas_call | solution.py:79
  22.7 1.7 %collective-permute-done.1.keys.k1 = bf16[128,1024]{1,0:T(8,128)(2,1)S(1)} collective-permute-done((bf16[128,1024]{1,0:T(8,128)(2,1)S(1)}, bf16[128,1024]{1,0:T(8,128)(2,1)S(1)}, u32[]{:S(2)}, u32[]{:S(2)}) %collective-permute-start.1) | collective-permute-done | bytes 262176 | tf_op jit(solution)/shard_map/ppermute | solution.py:291
  24.4 1.0 %shard_map.119 = (bf16[128,1024]{1,0:T(8,128)(2,1)S(1)}, f32[128,1024]{1,0:T(8,128)S(1)}) custom-call(s32[1,4]{1,0:T(1,128)S(1)} %copy-done, s32[2]{0:T(128)S(1)} %pad_add_fusion.place_ref, bf16[128,1024]{1,0:T(8,128)(2,1)S(1)} %get-tuple-element.54.q.q0, bf16[128,1024]{1,0:T(8,128)(2,1)S(1)} %collective-permute-done.1.keys.k1), custom_call_target="tpu_custom_call" | custom-call | flops 33554432 | bytes 1310720 | tf_op jit(solution)/shard_map/pallas_call | solution.py:79
  25.4 0.6 collective-permute-done.3.v2
  26.0 1.1 %shard_map.121 = (bf16[128,1024]{1,0:T(8,128)(2,1)S(1)}, f32[128,1024]{1,0:T(8,128)S(1)}, f32[128,128]{1,0:T(8,128)S(1)}, bf16[128,256]{1,0:T(8,128)(2,1)S(1)}, ...) custom-call(s32[2]{0:T(128)S(1)} %pad_add_fusion.place_ref, ...), custom_call_target="tpu_custom_call" | custom-call | flops 33554432 | bytes 2949120 | tf_op jit(solution)/shard_map/pallas_call | solution.py:79
  27.1 0.1 collective-permute-start.6
  27.2 1.2 %collective-permute-start.7 = (bf16[128,256]{1,0:T(8,128)(2,1)S(1)}, bf16[128,256]{1,0:T(8,128)(2,1)S(1)}, u32[]{:S(2)}, u32[]{:S(2)}) collective-permute-start(bf16[128,256]{1,0:T(8,128)(2,1)S(1)} %get-tuple-element.68), channel_id=1, source_target_pairs={{0,2},{1,3},{2,0},{3,1},{4,6},{5,7},{6,4},{7,5},{8,10},{9,11},{10,... | collective-permute-start | bytes 196616 | tf_op jit(solution)/shard_map/ppermute | solution.py:291
  28.4 0.6 collective-permute-start.8
  29.1 0.9 %shard_map.122 = (bf16[128,1024]{1,0:T(8,128)(2,1)}, bf16[128,1024]{1,0:T(8,128)(2,1)S(1)}) custom-call(f32[128,1024]{1,0:T(8,128)S(1)} %get-tuple-element.56.grad_hidden, bf16[128,1024]{1,0:T(8,128)(2,1)S(1)} %get-tuple-element.57.gates, f32[128,1024]{1,0:T(8,128)S(1)} %get-tuple-element.62.normed, f32[128,128]{1,0:T(8,128)S(1)} %get-tuple-element.63.inv_std), custom_call_target="tpu_custom_call" | custom-call | flops 8388608 | bytes 1900544 | tf_op jit(solution)/shard_map/pallas_call | solution.py:79
  29.9 0.0 collective-permute-done.9.refs_7_
  29.9 1.2 %collective-permute-start.14 = (bf16[128,1024]{1,0:T(8,128)(2,1)S(1)}, bf16[128,1024]{1,0:T(8,128)(2,1)S(1)}, u32[]{:S(2)}, u32[]{:S(2)}) collective-permute-start(bf16[128,1024]{1,0:T(8,128)(2,1)S(1)} %get-tuple-element.64.grad_mix.g0), channel_id=1, source_target_pairs={{0,24},{4,28},{8,0},{12,4},{16,8},{20,12},{24,16},{28,20},{1,25},{... | collective-permute-start | bytes 786440 | tf_op jit(solution)/shard_map/ppermute | solution.py:287
  31.1 0.0 collective-permute-done.6.refs_1_
  31.1 0.9 %collective-permute-done.7.refs_2_ = bf16[128,256]{1,0:T(8,128)(2,1)S(1)} collective-permute-done((bf16[128,256]{1,0:T(8,128)(2,1)S(1)}, bf16[128,256]{1,0:T(8,128)(2,1)S(1)}, u32[]{:S(2)}, u32[]{:S(2)}) %collective-permute-start.7) | collective-permute-done | bytes 65568 | tf_op jit(solution)/shard_map/ppermute | solution.py:291
  32.0 0.7 %collective-permute-done.8.refs_3_ = bf16[128,256]{1,0:T(8,128)(2,1)S(1)} collective-permute-done((bf16[128,256]{1,0:T(8,128)(2,1)S(1)}, bf16[128,256]{1,0:T(8,128)(2,1)S(1)}, u32[]{:S(2)}, u32[]{:S(2)}) %collective-permute-start.8) | collective-permute-done | bytes 65568 | tf_op jit(solution)/shard_map/ppermute | solution.py:291
  32.8 1.1 %shard_map.123 = (f32[64,1024]{1,0:T(8,128)S(1)}, bf16[64,1024]{1,0:T(8,128)(2,1)S(1)}, bf16[64,1024]{1,0:T(8,128)(2,1)S(1)}, bf16[64,1024]{1,0:T(8,128)(2,1)S(1)}) custom-call(s32[2]{0:T(128)S(1)} %pad_add_fusion.place_ref, bf16[128,256]{1,0:T(8,128)(2,1)S(1)} %get-tuple-element.66.refs_0_, bf16[128,256]{1,0:T(8,128)(2,1)S(1)} %collective-permute-done.6.refs_1_, ...), custom_call_target="tpu_custom_call" | custom-call | flops 268435456 | bytes 1966080 | tf_op jit(solution)/shard_map/pallas_call | solution.py:79
  33.8 3.6 %collective-permute-start.10 = (bf16[64,1024]{1,0:T(8,128)(2,1)S(1)}, bf16[64,1024]{1,0:T(8,128)(2,1)S(1)}, u32[]{:S(2)}, u32[]{:S(2)}) collective-permute-start(bf16[64,1024]{1,0:T(8,128)(2,1)S(1)} %get-tuple-element.77), channel_id=1, source_target_pairs={{0,4},{4,0},{8,12},{12,8},{16,20},{20,16},{24,28},{28,24},{1,5},{5... | collective-permute-start | bytes 393224 | tf_op jit(solution)/shard_map/ppermute | solution.py:291
  37.4 0.0 collective-permute-start.11
  37.5 1.5 %collective-permute-start.12 = (bf16[64,1024]{1,0:T(8,128)(2,1)S(1)}, bf16[64,1024]{1,0:T(8,128)(2,1)S(1)}, u32[]{:S(2)}, u32[]{:S(2)}) collective-permute-start(bf16[64,1024]{1,0:T(8,128)(2,1)S(1)} %get-tuple-element.79), channel_id=1, source_target_pairs={{0,12},{4,8},{8,4},{12,0},{16,28},{20,24},{24,20},{28,16},{1,13},{... | collective-permute-start | bytes 393224 | tf_op jit(solution)/shard_map/ppermute | solution.py:291
  39.0 0.0 collective-permute-done.13.q2
  39.0 2.0 %collective-permute-start.16 = (bf16[128,1024]{1,0:T(8,128)(2,1)S(1)}, bf16[128,1024]{1,0:T(8,128)(2,1)S(1)}, u32[]{:S(2)}, u32[]{:S(2)}) collective-permute-start(bf16[128,1024]{1,0:T(8,128)(2,1)S(1)} %broadcast_select_fusion.1), channel_id=1, source_target_pairs={{0,4},{4,0},{8,12},{12,8},{16,20},{20,16},{24,28},{28,24},{1,5},{5... | collective-permute-start | bytes 786440 | tf_op jit(solution)/shard_map/ppermute | solution.py:291
  41.0 2.7 %shard_map.124 = (bf16[128,1024]{1,0:T(8,128)(2,1)}, bf16[128,1024]{1,0:T(8,128)(2,1)}) custom-call(bf16[128,1024]{1,0:T(8,128)(2,1)S(1)} %get-tuple-element.48.k0.k, bf16[128,1024]{1,0:T(8,128)(2,1)S(1)} %collective-permute-done.1.keys.k1, bf16[128,1024]{1,0:T(8,128)(2,1)S(1)} %collective-permute-done.keys.k2, ...), custom_call_target="tpu_custom_call" | custom-call | flops 469762048 | bytes 6291456 | tf_op jit(solution)/shard_map/pallas_call | solution.py:79
  43.7 0.1 collective-permute-done.11.refs_1_
  43.8 1.5 %collective-permute-done.12.refs_2_ = bf16[64,1024]{1,0:T(8,128)(2,1)S(1)} collective-permute-done((bf16[64,1024]{1,0:T(8,128)(2,1)S(1)}, bf16[64,1024]{1,0:T(8,128)(2,1)S(1)}, u32[]{:S(2)}, u32[]{:S(2)}) %collective-permute-start.12) | collective-permute-done | bytes 131104 | tf_op jit(solution)/shard_map/ppermute | solution.py:291
  45.3 0.1 shard_map.125.mine
  45.5 2.8 %collective-permute-start.17 = (bf16[128,1024]{1,0:T(8,128)(2,1)S(1)}, bf16[128,1024]{1,0:T(8,128)(2,1)S(1)}, u32[]{:S(2)}, u32[]{:S(2)}) collective-permute-start(bf16[128,1024]{1,0:T(8,128)(2,1)S(1)} %broadcast_select_fusion), channel_id=1, source_target_pairs={{0,4},{4,0},{8,12},{12,8},{16,20},{20,16},{24,28},{28,24},{1,5},{5... | collective-permute-start | bytes 786440 | tf_op jit(solution)/shard_map/ppermute | solution.py:291
  48.2 2.4 %collective-permute-start.15 = (bf16[64,1024]{1,0:T(8,128)(2,1)S(1)}, bf16[64,1024]{1,0:T(8,128)(2,1)S(1)}, u32[]{:S(2)}, u32[]{:S(2)}) collective-permute-start(bf16[64,1024]{1,0:T(8,128)(2,1)S(1)} %shard_map.125.mine), channel_id=1, source_target_pairs={{0,16},{4,20},{8,24},{12,28},{16,0},{20,4},{24,8},{28,12},{1,17},{... | collective-permute-start | bytes 393224 | tf_op jit(solution)/shard_map/ppermute | solution.py:291
  50.6 2.7 %shard_map.126 = (f32[128,1024]{1,0:T(8,128)S(1)}, f32[128,1024]{1,0:T(8,128)S(1)}) custom-call(s32[1,4]{1,0:T(1,128)S(1)} %copy-done.1, s32[2]{0:T(128)S(1)} %pad_add_fusion.place_ref, bf16[128,1024]{1,0:T(8,128)(2,1)S(1)} %get-tuple-element.48.k0.k, bf16[128,1024]{1,0:T(8,128)(2,1)S(1)} %get-tuple-element.83.v0.v, ...), custom_call_target="tpu_custom_call" | custom-call | flops 268435456 | bytes 2621440 | tf_op jit(solution)/shard_map/pallas_call | solution.py:79
  53.3 3.6 %collective-permute-done.15.other = bf16[64,1024]{1,0:T(8,128)(2,1)S(1)} collective-permute-done((bf16[64,1024]{1,0:T(8,128)(2,1)S(1)}, bf16[64,1024]{1,0:T(8,128)(2,1)S(1)}, u32[]{:S(2)}, u32[]{:S(2)}) %collective-permute-start.15) | collective-permute-done | bytes 131104 | tf_op jit(solution)/shard_map/ppermute | solution.py:291
  56.9 0.1 collective-permute-start.18
  57.0 1.2 %collective-permute-start.19 = (bf16[64,1024]{1,0:T(8,128)(2,1)S(1)}, bf16[64,1024]{1,0:T(8,128)(2,1)S(1)}, u32[]{:S(2)}, u32[]{:S(2)}) collective-permute-start(bf16[64,1024]{1,0:T(8,128)(2,1)S(1)} %shard_map.127.refs_0_), channel_id=1, source_target_pairs={{0,8},{4,12},{8,0},{12,4},{16,24},{20,28},{24,16},{28,20},{1,9},{5... | collective-permute-start | bytes 393224 | tf_op jit(solution)/shard_map/ppermute | solution.py:291
  58.2 2.3 %collective-permute-start.20 = (bf16[64,1024]{1,0:T(8,128)(2,1)S(1)}, bf16[64,1024]{1,0:T(8,128)(2,1)S(1)}, u32[]{:S(2)}, u32[]{:S(2)}) collective-permute-start(bf16[64,1024]{1,0:T(8,128)(2,1)S(1)} %shard_map.127.refs_0_), channel_id=1, source_target_pairs={{0,12},{4,8},{8,4},{12,0},{16,28},{20,24},{24,20},{28,16},{1,13},{... | collective-permute-start | bytes 393224 | tf_op jit(solution)/shard_map/ppermute | solution.py:291
  60.5 2.9 %shard_map.128 = (bf16[128,1024]{1,0:T(8,128)(2,1)}, bf16[128,1024]{1,0:T(8,128)(2,1)}) custom-call(s32[1,4]{1,0:T(1,128)S(1)} %copy-done.1, s32[2]{0:T(128)S(1)} %pad_add_fusion.place_ref, bf16[128,1024]{1,0:T(8,128)(2,1)S(1)} %get-tuple-element.48.k0.k, bf16[128,1024]{1,0:T(8,128)(2,1)S(1)} %get-tuple-element.83.v0.v, ...), custom_call_target="tpu_custom_call" | custom-call | flops 134217728 | bytes 2621440 | tf_op jit(solution)/shard_map/pallas_call | solution.py:79
  63.4 1.9 %collective-permute-done.20.refs_3_ = bf16[64,1024]{1,0:T(8,128)(2,1)S(1)} collective-permute-done((bf16[64,1024]{1,0:T(8,128)(2,1)S(1)}, bf16[64,1024]{1,0:T(8,128)(2,1)S(1)}, u32[]{:S(2)}, u32[]{:S(2)}) %collective-permute-start.20) | collective-permute-done | bytes 131104 | tf_op jit(solution)/shard_map/ppermute | solution.py:291
  65.4 1.6 %shard_map.129 = f32[256,1024]{1,0:T(8,128)} custom-call(s32[2]{0:T(128)S(1)} %pad_add_fusion.place_ref, bf16[64,1024]{1,0:T(8,128)(2,1)S(1)} %shard_map.127.refs_0_, bf16[64,1024]{1,0:T(8,128)(2,1)S(1)} %collective-permute-done.18.refs_1_, bf16[64,1024]{1,0:T(8,128)(2,1)S(1)} %collective-permute-done.19.refs_2_, ...), custom_call_target="tpu_custom_call" | custom-call | flops 262144 | bytes 1572864 | tf_op jit(solution)/shard_map/pallas_call | solution.py:79
  (16 shorter events, 0.2 us)
Async XLA Ops:
  0.6 11.7 %collective-permute-start = (bf16[128,1024]{1,0:T(8,128)(2,1)}, bf16[128,1024]{1,0:T(8,128)(2,1)S(1)}, u32[]{:S(2)}, u32[]{:S(2)}) collective-permute-start(bf16[128,1024]{1,0:T(8,128)(2,1)} %bitcast.14), channel_id=1, source_target_pairs={{0,8},{4,12},{8,16},{12,20},{16,24},{20,28},{24,0},{28,4},{1,9},{5... | collective-permute-start | bytes 786440 | tf_op jit(solution)/shard_map/ppermute | solution.py:287
  3.7 11.9 %collective-permute-start.4 = (bf16[128,1024]{1,0:T(8,128)(2,1)}, bf16[128,1024]{1,0:T(8,128)(2,1)S(1)}, u32[]{:S(2)}, u32[]{:S(2)}) collective-permute-start(bf16[128,1024]{1,0:T(8,128)(2,1)} %bitcast.16), channel_id=1, source_target_pairs={{0,2},{1,3},{2,0},{3,1},{4,6},{5,7},{6,4},{7,5},{8,10},{9,11},{10,... | collective-permute-start | bytes 786440 | tf_op jit(solution)/shard_map/ppermute | solution.py:291
  5.2 16.5 %collective-permute-start.5 = (bf16[128,1024]{1,0:T(8,128)(2,1)}, bf16[128,1024]{1,0:T(8,128)(2,1)S(1)}, u32[]{:S(2)}, u32[]{:S(2)}) collective-permute-start(bf16[128,1024]{1,0:T(8,128)(2,1)} %bitcast.17), channel_id=1, source_target_pairs={{0,1},{1,0},{2,3},{3,2},{4,5},{5,4},{6,7},{7,6},{8,9},{9,8},{10,11... | collective-permute-start | bytes 786440 | tf_op jit(solution)/shard_map/ppermute | solution.py:291
  5.2 14.1 %collective-permute-start.2 = (bf16[128,1024]{1,0:T(8,128)(2,1)}, bf16[128,1024]{1,0:T(8,128)(2,1)S(1)}, u32[]{:S(2)}, u32[]{:S(2)}) collective-permute-start(bf16[128,1024]{1,0:T(8,128)(2,1)} %bitcast.19), channel_id=1, source_target_pairs={{0,4},{4,8},{8,12},{12,16},{16,20},{20,24},{24,28},{28,0},{1,5},{5... | collective-permute-start | bytes 786440 | tf_op jit(solution)/shard_map/ppermute | solution.py:287
  6.8 0.7 copy-start
  7.5 7.5 %copy-start.2 = (bf16[1,128,1024]{2,1,0:T(8,128)(2,1)S(1)}, bf16[1,128,1024]{2,1,0:T(8,128)(2,1)}, u32[]{:S(2)}) copy-start(bf16[1,128,1024]{2,1,0:T(8,128)(2,1)} %param.9) | copy-start | bytes 786436
  12.4 12.0 %collective-permute-start.1 = (bf16[128,1024]{1,0:T(8,128)(2,1)S(1)}, bf16[128,1024]{1,0:T(8,128)(2,1)S(1)}, u32[]{:S(2)}, u32[]{:S(2)}) collective-permute-start(bf16[128,1024]{1,0:T(8,128)(2,1)S(1)} %broadcast_select_fusion.2), channel_id=1, source_target_pairs={{0,4},{4,0},{8,12},{12,8},{16,20},{20,16},{24,28},{28,24},{1,5},{5... | collective-permute-start | bytes 786440 | tf_op jit(solution)/shard_map/ppermute | solution.py:291
  14.9 11.1 %collective-permute-start.3 = (bf16[128,1024]{1,0:T(8,128)(2,1)S(1)}, bf16[128,1024]{1,0:T(8,128)(2,1)S(1)}, u32[]{:S(2)}, u32[]{:S(2)}) collective-permute-start(bf16[128,1024]{1,0:T(8,128)(2,1)S(1)} %bitcast.21), channel_id=1, source_target_pairs={{0,8},{4,12},{8,16},{12,20},{16,24},{20,28},{24,0},{28,4},{1,9},{5... | collective-permute-start | bytes 786440 | tf_op jit(solution)/shard_map/ppermute | solution.py:287
  15.6 14.3 %collective-permute-start.9 = (bf16[128,1024]{1,0:T(8,128)(2,1)S(1)}, bf16[128,1024]{1,0:T(8,128)(2,1)S(1)}, u32[]{:S(2)}, u32[]{:S(2)}) collective-permute-start(bf16[128,1024]{1,0:T(8,128)(2,1)S(1)} %collective-permute-done.4.refs_6_), channel_id=1, source_target_pairs={{0,1},{1,0},{2,3},{3,2},{4,5},{5,4},{6,7},{7,6},{8,9},{9,8},{10,11... | collective-permute-start | bytes 786440 | tf_op jit(solution)/shard_map/ppermute | solution.py:291
  19.4 19.6 %collective-permute-start.13 = (bf16[128,1024]{1,0:T(8,128)(2,1)S(1)}, bf16[128,1024]{1,0:T(8,128)(2,1)S(1)}, u32[]{:S(2)}, u32[]{:S(2)}) collective-permute-start(bf16[128,1024]{1,0:T(8,128)(2,1)S(1)} %get-tuple-element.54.q.q0), channel_id=1, source_target_pairs={{0,24},{4,28},{8,0},{12,4},{16,8},{20,12},{24,16},{28,20},{1,25},{... | collective-permute-start | bytes 786440 | tf_op jit(solution)/shard_map/ppermute | solution.py:287
  27.1 4.0 %collective-permute-start.6 = (bf16[128,256]{1,0:T(8,128)(2,1)S(1)}, bf16[128,256]{1,0:T(8,128)(2,1)S(1)}, u32[]{:S(2)}, u32[]{:S(2)}) collective-permute-start(bf16[128,256]{1,0:T(8,128)(2,1)S(1)} %get-tuple-element.67), channel_id=1, source_target_pairs={{0,1},{1,0},{2,3},{3,2},{4,5},{5,4},{6,7},{7,6},{8,9},{9,8},{10,11... | collective-permute-start | bytes 196616 | tf_op jit(solution)/shard_map/ppermute | solution.py:291
  27.2 4.8 %collective-permute-start.7 = (bf16[128,256]{1,0:T(8,128)(2,1)S(1)}, bf16[128,256]{1,0:T(8,128)(2,1)S(1)}, u32[]{:S(2)}, u32[]{:S(2)}) collective-permute-start(bf16[128,256]{1,0:T(8,128)(2,1)S(1)} %get-tuple-element.68), channel_id=1, source_target_pairs={{0,2},{1,3},{2,0},{3,1},{4,6},{5,7},{6,4},{7,5},{8,10},{9,11},{10,... | collective-permute-start | bytes 196616 | tf_op jit(solution)/shard_map/ppermute | solution.py:291
  28.4 4.3 %collective-permute-start.8 = (bf16[128,256]{1,0:T(8,128)(2,1)S(1)}, bf16[128,256]{1,0:T(8,128)(2,1)S(1)}, u32[]{:S(2)}, u32[]{:S(2)}) collective-permute-start(bf16[128,256]{1,0:T(8,128)(2,1)S(1)} %get-tuple-element.69), channel_id=1, source_target_pairs={{0,3},{1,2},{2,1},{3,0},{4,7},{5,6},{6,5},{7,4},{8,11},{9,10},{10,... | collective-permute-start | bytes 196616 | tf_op jit(solution)/shard_map/ppermute | solution.py:291
  29.9 15.5 %collective-permute-start.14 = (bf16[128,1024]{1,0:T(8,128)(2,1)S(1)}, bf16[128,1024]{1,0:T(8,128)(2,1)S(1)}, u32[]{:S(2)}, u32[]{:S(2)}) collective-permute-start(bf16[128,1024]{1,0:T(8,128)(2,1)S(1)} %get-tuple-element.64.grad_mix.g0), channel_id=1, source_target_pairs={{0,24},{4,28},{8,0},{12,4},{16,8},{20,12},{24,16},{28,20},{1,25},{... | collective-permute-start | bytes 786440 | tf_op jit(solution)/shard_map/ppermute | solution.py:287
  33.8 9.9 %collective-permute-start.10 = (bf16[64,1024]{1,0:T(8,128)(2,1)S(1)}, bf16[64,1024]{1,0:T(8,128)(2,1)S(1)}, u32[]{:S(2)}, u32[]{:S(2)}) collective-permute-start(bf16[64,1024]{1,0:T(8,128)(2,1)S(1)} %get-tuple-element.77), channel_id=1, source_target_pairs={{0,4},{4,0},{8,12},{12,8},{16,20},{20,16},{24,28},{28,24},{1,5},{5... | collective-permute-start | bytes 393224 | tf_op jit(solution)/shard_map/ppermute | solution.py:291
  37.4 6.4 %collective-permute-start.11 = (bf16[64,1024]{1,0:T(8,128)(2,1)S(1)}, bf16[64,1024]{1,0:T(8,128)(2,1)S(1)}, u32[]{:S(2)}, u32[]{:S(2)}) collective-permute-start(bf16[64,1024]{1,0:T(8,128)(2,1)S(1)} %get-tuple-element.78), channel_id=1, source_target_pairs={{0,8},{4,12},{8,0},{12,4},{16,24},{20,28},{24,16},{28,20},{1,9},{5... | collective-permute-start | bytes 393224 | tf_op jit(solution)/shard_map/ppermute | solution.py:291
  37.5 7.9 %collective-permute-start.12 = (bf16[64,1024]{1,0:T(8,128)(2,1)S(1)}, bf16[64,1024]{1,0:T(8,128)(2,1)S(1)}, u32[]{:S(2)}, u32[]{:S(2)}) collective-permute-start(bf16[64,1024]{1,0:T(8,128)(2,1)S(1)} %get-tuple-element.79), channel_id=1, source_target_pairs={{0,12},{4,8},{8,4},{12,0},{16,28},{20,24},{24,20},{28,16},{1,13},{... | collective-permute-start | bytes 393224 | tf_op jit(solution)/shard_map/ppermute | solution.py:291
  39.0 21.5 %collective-permute-start.16 = (bf16[128,1024]{1,0:T(8,128)(2,1)S(1)}, bf16[128,1024]{1,0:T(8,128)(2,1)S(1)}, u32[]{:S(2)}, u32[]{:S(2)}) collective-permute-start(bf16[128,1024]{1,0:T(8,128)(2,1)S(1)} %broadcast_select_fusion.1), channel_id=1, source_target_pairs={{0,4},{4,0},{8,12},{12,8},{16,20},{20,16},{24,28},{28,24},{1,5},{5... | collective-permute-start | bytes 786440 | tf_op jit(solution)/shard_map/ppermute | solution.py:291
  41.0 9.6 %copy-start.1 = (s32[1,4]{1,0:T(1,128)S(1)}, s32[1,4]{1,0:T(1,128)}, u32[]{:S(2)}) copy-start(s32[1,4]{1,0:T(1,128)} %len_ref.9) | copy-start | bytes 52
  45.5 15.0 %collective-permute-start.17 = (bf16[128,1024]{1,0:T(8,128)(2,1)S(1)}, bf16[128,1024]{1,0:T(8,128)(2,1)S(1)}, u32[]{:S(2)}, u32[]{:S(2)}) collective-permute-start(bf16[128,1024]{1,0:T(8,128)(2,1)S(1)} %broadcast_select_fusion), channel_id=1, source_target_pairs={{0,4},{4,0},{8,12},{12,8},{16,20},{20,16},{24,28},{28,24},{1,5},{5... | collective-permute-start | bytes 786440 | tf_op jit(solution)/shard_map/ppermute | solution.py:291
  48.2 8.7 %collective-permute-start.15 = (bf16[64,1024]{1,0:T(8,128)(2,1)S(1)}, bf16[64,1024]{1,0:T(8,128)(2,1)S(1)}, u32[]{:S(2)}, u32[]{:S(2)}) collective-permute-start(bf16[64,1024]{1,0:T(8,128)(2,1)S(1)} %shard_map.125.mine), channel_id=1, source_target_pairs={{0,16},{4,20},{8,24},{12,28},{16,0},{20,4},{24,8},{28,12},{1,17},{... | collective-permute-start | bytes 393224 | tf_op jit(solution)/shard_map/ppermute | solution.py:291
  56.9 6.5 %collective-permute-start.18 = (bf16[64,1024]{1,0:T(8,128)(2,1)S(1)}, bf16[64,1024]{1,0:T(8,128)(2,1)S(1)}, u32[]{:S(2)}, u32[]{:S(2)}) collective-permute-start(bf16[64,1024]{1,0:T(8,128)(2,1)S(1)} %shard_map.127.refs_0_), channel_id=1, source_target_pairs={{0,4},{4,0},{8,12},{12,8},{16,20},{20,16},{24,28},{28,24},{1,5},{5... | collective-permute-start | bytes 393224 | tf_op jit(solution)/shard_map/ppermute | solution.py:291
  57.0 6.4 %collective-permute-start.19 = (bf16[64,1024]{1,0:T(8,128)(2,1)S(1)}, bf16[64,1024]{1,0:T(8,128)(2,1)S(1)}, u32[]{:S(2)}, u32[]{:S(2)}) collective-permute-start(bf16[64,1024]{1,0:T(8,128)(2,1)S(1)} %shard_map.127.refs_0_), channel_id=1, source_target_pairs={{0,8},{4,12},{8,0},{12,4},{16,24},{20,28},{24,16},{28,20},{1,9},{5... | collective-permute-start | bytes 393224 | tf_op jit(solution)/shard_map/ppermute | solution.py:291
  58.2 7.2 %collective-permute-start.20 = (bf16[64,1024]{1,0:T(8,128)(2,1)S(1)}, bf16[64,1024]{1,0:T(8,128)(2,1)S(1)}, u32[]{:S(2)}, u32[]{:S(2)}) collective-permute-start(bf16[64,1024]{1,0:T(8,128)(2,1)S(1)} %shard_map.127.refs_0_), channel_id=1, source_target_pairs={{0,12},{4,8},{8,4},{12,0},{16,28},{20,24},{24,20},{28,16},{1,13},{... | collective-permute-start | bytes 393224 | tf_op jit(solution)/shard_map/ppermute | solution.py:291
